TPU v7x, 128 devices: a whole 4x4x4 slice. The times are simulated.
128 devices in a mesh: rows: 32 (over y, x_lo, z), cols: 4 (over x_hi, core).
Axes of the slice: x: 4 (x_hi: 2, x_lo: 2; x = x_hi * 2 + x_lo), y: 4, z: 4, core: 2. Of those that a mesh axis runs over, the one named last changes fastest.
Arguments:
- fmap_left: bfloat16 [64, 2048, 256], P('rows', 'cols'), may hold values from -6 to 6
- fmap_right: bfloat16 [64, 2048, 256], P('rows', 'cols'), may hold values from -6 to 6
- hidden_init: bfloat16 [64, 2048, 128], P('rows', 'cols'), may hold values from -3 to 3
- disp_init: int32 [64], P('rows'), may hold values from 0 to 191
- level_offset: int32 [64, 4], P('rows'), may hold values from -4 to 4
- motion_weight: bfloat16 [36, 128], replicated, may hold values from -1 to 1
- gate_weight: bfloat16 [2304, 256], replicated, may hold values from -0.125 to 0.125
- cand_weight: bfloat16 [2304, 128], replicated, may hold values from -0.125 to 0.125
- grad_hidden: bfloat16 [64, 2048, 128], P('rows', 'cols'), may hold values from -6 to 6
Outputs:
- grad_left: bfloat16 [64, 2048, 256], P('rows', 'cols')
- grad_right: bfloat16 [64, 2048, 256], P('rows', 'cols')
- grad_hidden_init: bfloat16 [64, 2048, 128], P('rows', 'cols')
- grad_motion_w: float32 [36, 128], replicated
- grad_gate_w: float32 [2304, 256], replicated
- grad_cand_w: float32 [2304, 128], replicated
All inputs are finite; a program needn't handle non-finite values.
Results may differ from a plain program's by a relative error of at most 0.011.
Values may be sent and summed in bfloat16 or wider, within the bound.
No kernel may reach another device: no remote copies, remote signals or barrier semaphores. Data moves between devices by JAX's collectives and lax.ppermute only.
A program may use at most 64 MiB of HBM per device.

v0:
```python
import math

import jax
import jax.numpy as jnp
from jax import lax
from jax.experimental import pallas as pl
from jax.experimental.pallas import tpu as pltpu
from jax.sharding import PartitionSpec as P

LEVELS = 4
RADIUS = 4
DISP = 192
TAPS = 2 * RADIUS + 1
HALO = 16
LANES = 128
CHUNK_ROWS = 64

BF16 = jnp.bfloat16
F32 = jnp.float32
VMEM = pl.BlockSpec(memory_space=pltpu.VMEM)
SMEM = pl.BlockSpec(memory_space=pltpu.SMEM)


def dot(a, b):
    return jnp.dot(a, b, preferred_element_type=F32)


def dot_nt(a, b):
    return lax.dot_general(a, b, (((1,), (1,)), ((), ())), preferred_element_type=F32)


def dot_tn(a, b):
    return lax.dot_general(a, b, (((0,), (0,)), ((), ())), preferred_element_type=F32)


def split_dot(a, table, contract):
    high = a.astype(BF16)
    low = (a - high.astype(F32)).astype(BF16)
    return contract(high, table) + contract(low, table)


def kernel_call(body, outs, ins, scalars, scratch, flops):
    bytes_moved = sum(x.size * x.dtype.itemsize for x in ins) + sum(
        math.prod(o.shape) * o.dtype.itemsize for o in outs
    )
    return pl.pallas_call(
        body,
        out_shape=outs,
        in_specs=[SMEM] * scalars + [VMEM] * (len(ins) - scalars),
        out_specs=[VMEM] * len(outs),
        scratch_shapes=scratch,
        compiler_params=pltpu.CompilerParams(vmem_limit_bytes=48 * 2**20),
        cost_estimate=pl.CostEstimate(flops=flops, bytes_accessed=bytes_moved, transcendentals=0),
    )(*ins)


def array(shape, dtype):
    return jax.ShapeDtypeStruct(shape, dtype)


def lookup_rows(position, valid, disparity, offsets, row):
    count = position.shape[0]
    feature = lax.broadcasted_iota(jnp.int32, (count, LANES), 1)
    table = jnp.zeros((count, LANES), F32)
    for level in range(LEVELS):
        centre = (disparity[row] >> level) + offsets[row, level]
        tap = feature - level * TAPS
        matches = (position >> level) == tap + (centre - RADIUS)
        matches = matches & (tap >= 0) & (tap < TAPS) & valid
        table = jnp.where(matches, 1.0 / 2**level, table)
    return table.astype(BF16)


def sides(odd, first, second):
    return jnp.where(odd, first, second), jnp.where(odd, second, first)


def store_taps(ref, row, lane, step, value, forward):
    wide = value.shape[0]
    left = pltpu.roll(value, 1, 0).astype(BF16)
    right = pltpu.roll(value, wide - 1, 0).astype(BF16)
    taps = (left, value.astype(BF16), right) if forward else (right, value.astype(BF16), left)
    for tap in range(3):
        start = lane + tap * step
        ref[row, :, start : start + LANES] = taps[tap]


def motion_kernel(place, disparity, offsets, left, right, got_a, got_b, weight, motion, pre, feats, ext, window, flipped):
    odd = place[1] % 2 == 1
    cols = left.shape[1]
    wide = cols + 2 * HALO
    block = wide // 2
    span = 512
    tail = DISP + HALO
    flat = (lax.broadcasted_iota(jnp.int32, (LANES, LANES), 0)
            + lax.broadcasted_iota(jnp.int32, (LANES, LANES), 1))
    mirror = jnp.where(flat == LANES - 1, 1.0, 0.0).astype(BF16)
    total = window.shape[0]
    position = lax.broadcasted_iota(jnp.int32, (span, LANES), 0) - (block - 1)
    valid = (position >= 0) & (position < DISP)
    for row in range(2):
        from_left, from_right = sides(odd, got_a[row], got_b[row])
        ext[0:HALO] = from_left[tail : tail + HALO]
        ext[HALO : HALO + cols] = left[row]
        ext[HALO + cols : wide] = from_right[tail + HALO : tail + 2 * HALO]
        window[0:tail] = from_left[0:tail]
        window[tail : tail + cols] = right[row]
        window[tail + cols : tail + cols + HALO] = from_right[tail + 2 * HALO :]
        window[tail + cols + HALO :] = jnp.zeros((total - tail - cols - HALO, window.shape[1]), BF16)
        parts = total // LANES
        for part in range(parts):
            source = window[(parts - 1 - part) * LANES : (parts - part) * LANES]
            flipped[part * LANES : (part + 1) * LANES] = dot(mirror, source).astype(BF16)
        flipped[total:] = jnp.zeros((flipped.shape[0] - total, window.shape[1]), BF16)
        table = lookup_rows(position, valid, disparity, offsets, row)
        for part in range(2):
            start = part * block
            base = total - DISP - start - block
            scores = dot_nt(ext[start : start + block], flipped[base : base + span])
            scores = scores * (1.0 / math.sqrt(left.shape[2]))
            band = pltpu.roll(scores, 0, 1, stride=1, stride_axis=0)
            found = split_dot(band, table, dot).astype(BF16)
            value = dot(found, weight[...])
            feats[row, start : start + block] = found
            pre[row, start : start + block] = value
            motion[row, start : start + block] = (value * jax.nn.sigmoid(value)).astype(BF16)


def image_columns(place, wide, cols, cols_axis):
    column = lax.broadcasted_iota(jnp.int32, (wide, LANES), 0) - HALO + place[1] * cols
    return (column >= 0) & (column < cols * cols_axis)


def fill_rows(store, odd, own, first, second):
    for row in range(2):
        above, below = sides(odd, first[row], second[row])
        store(row, above.astype(F32))
        store(4 + row, below.astype(F32))
        store(2 + row, own[row].astype(F32))


def gates(fields, resets, gate_w, update, reset, reset_hidden, wide):
    block = wide // 2
    deep = gate_w.shape[0] // 3

    def gate_part(step, carry):
        row, start = step // 2, pl.multiple_of((step % 2) * block, 16)
        here = pl.ds(start, block)
        total = sum(dot(fields[row + a, here], gate_w[a * deep : (a + 1) * deep]) for a in range(3))
        reset_part = jax.nn.sigmoid(total[:, LANES:])
        update[row, here] = jax.nn.sigmoid(total[:, :LANES])
        reset[row, here] = reset_part
        hidden = fields[row + 1, here, 2 * LANES : 3 * LANES].astype(F32)
        reset_hidden[row, here] = (reset_part * hidden).astype(BF16)
        return carry

    lax.fori_loop(0, 8, gate_part, 0)
    for row in range(4):
        store_taps(resets, row, 0, 2 * LANES, reset_hidden[row].astype(F32), True)
        for tap in range(3):
            start = (2 * tap + 1) * LANES
            resets[row, :, start : start + LANES] = fields[row + 1, :, start : start + LANES]


def load_fields(odd, fields, hidden, hidden_a, hidden_b, motion, motion_a, motion_b):
    fill_rows(lambda r, v: store_taps(fields, r, 0, 2 * LANES, v, True), odd, hidden, hidden_a, hidden_b)
    fill_rows(lambda r, v: store_taps(fields, r, LANES, 2 * LANES, v, True), odd, motion, motion_a, motion_b)


def candidate_part(resets, cand_w, row, here):
    deep = cand_w.shape[0] // 3
    total = sum(dot(resets[row + a, here], cand_w[a * deep : (a + 1) * deep]) for a in range(3))
    return jnp.tanh(total)


def first_kernel(cols_axis, place, hidden, hidden_a, hidden_b, motion, motion_a, motion_b, gate_w, cand_w,
                 later, update, reset, reset_hidden, candidate, fields, resets):
    odd = place[0] % 2 == 1
    wide = hidden.shape[1]
    block = wide // 2
    load_fields(odd, fields, hidden, hidden_a, hidden_b, motion, motion_a, motion_b)
    gates(fields, resets, gate_w, update, reset, reset_hidden, wide)
    inside = image_columns(place, wide, wide - 2 * HALO, cols_axis)
    for row in range(2):
        for start in (0, block):
            here = pl.ds(start, block)
            new = candidate_part(resets, cand_w, row, here)
            candidate[row, here] = new
            gate = update[row + 1, here]
            old = hidden[row, here].astype(F32)
            value = (1.0 - gate) * old + gate * new
            later[row, here] = jnp.where(inside[start : start + block], value, 0.0).astype(BF16)


def gradients_out(odd, grad, gate, new, old, row, here, grad_cand, grad_update, send_a, send_b):
    cand_part = (grad * gate * (1.0 - new * new)).astype(BF16)
    update_part = (grad * (new - old) * gate * (1.0 - gate)).astype(BF16)
    grad_cand[row, here] = cand_part
    grad_update[row, here] = update_part
    send_a[row, here] = cand_part
    send_b[row, here] = cand_part

    @pl.when(odd == (row == 0))
    def _():
        send_a[2, here] = update_part

    @pl.when(odd == (row == 1))
    def _():
        send_b[2, here] = update_part


def second_kernel(place, hidden, hidden_a, hidden_b, motion, motion_a, motion_b, gate_w, cand_w, grad_hidden,
                  update, reset, reset_hidden, grad_cand, grad_update, send_a, send_b, fields, resets):
    odd = place[0] % 2 == 1
    wide = hidden.shape[1]
    block = wide // 2
    load_fields(odd, fields, hidden, hidden_a, hidden_b, motion, motion_a, motion_b)
    gates(fields, resets, gate_w, update, reset, reset_hidden, wide)
    for row in range(2):
        for start in (0, block):
            here = pl.ds(start, block)
            new = candidate_part(resets, cand_w, row, here)
            gradients_out(odd, grad_hidden[row, here].astype(F32), update[row + 1, here], new,
                          hidden[row, here].astype(F32), row, here, grad_cand, grad_update, send_a, send_b)


def back_step(place, grad_cand, grad_a, grad_b, grad_update, hidden, hidden_a, hidden_b, reset, cand_wt, gate_wt,
              grad_gate, cand_taps, gate_taps, inner, grad_motion, finish):
    odd = place[0] % 2 == 1
    wide = hidden.shape[1]
    block = wide // 2
    fill_rows(lambda r, v: store_taps(cand_taps, r, 0, LANES, v, False), odd, grad_cand, grad_a, grad_b)
    deep = cand_wt.shape[0] // 3
    deeper = gate_wt.shape[0] // 3

    def cand_back(step, carry):
        row, start = step // 2, pl.multiple_of((step % 2) * block, 16)
        here = pl.ds(start, block)
        total = sum(dot(cand_taps[row + 2 - a, here], cand_wt[a * deep : (a + 1) * deep]) for a in range(3))
        inner[row, here] = total[:, :LANES]

        @pl.when((row == 1) | (row == 2))
        def _():
            grad_motion[row - 1, here] = total[:, LANES:]

        return carry

    lax.fori_loop(0, 8, cand_back, 0)
    above_h, below_h = sides(odd, hidden_a[1], hidden_b[1])[0], sides(odd, hidden_a[0], hidden_b[0])[1]
    above_u, below_u = sides(odd, grad_a[2], grad_b[2])
    hiddens = (above_h, hidden[0], hidden[1], below_h)
    updates = (above_u, grad_update[0], grad_update[1], below_u)
    for row in range(4):
        gate = reset[row]
        value = (inner[row] * hiddens[row].astype(F32) * gate * (1.0 - gate)).astype(BF16)
        store_taps(gate_taps, row, 0, 2 * LANES, updates[row].astype(F32), False)
        store_taps(gate_taps, row, LANES, 2 * LANES, value.astype(F32), False)
        if row in (1, 2):
            grad_gate[row - 1, :, :LANES] = updates[row]
            grad_gate[row - 1, :, LANES:] = value
    for row in range(2):
        for start in (0, block):
            here = pl.ds(start, block)
            total = sum(
                dot(gate_taps[row + 2 - a, here], gate_wt[a * deeper : (a + 1) * deeper]) for a in range(3)
            )
            grad_motion[row, here] += total[:, LANES:]
            finish(row, start, here, inner[row + 1, here] * reset[row + 1, here] + total[:, :LANES])


def later_back_kernel(cols_axis, place, grad_cand, grad_a, grad_b, grad_update, hidden, hidden_a, hidden_b, reset,
                      cand_wt, gate_wt, update, grad_hidden, older_hidden, older_update, older_candidate,
                      grad_gate, grad_state, grad_motion, older_cand, older_upd, send_a, send_b,
                      cand_taps, gate_taps, inner):
    odd = place[0] % 2 == 1
    wide = hidden.shape[1]
    block = wide // 2
    inside = image_columns(place, wide, wide - 2 * HALO, cols_axis)

    def finish(row, start, here, terms):
        gate = update[row + 1, here]
        grad = grad_hidden[row, here].astype(F32) * (1.0 - gate) + terms
        grad = jnp.where(inside[start : start + block], grad, 0.0)
        grad_state[row, here] = grad
        gradients_out(odd, grad, older_update[row + 1, here], older_candidate[row, here],
                      older_hidden[row, here].astype(F32), row, here, older_cand, older_upd, send_a, send_b)

    back_step(place, grad_cand, grad_a, grad_b, grad_update, hidden, hidden_a, hidden_b, reset, cand_wt, gate_wt,
              grad_gate, cand_taps, gate_taps, inner, grad_motion, finish)


def first_back_kernel(place, grad_cand, grad_a, grad_b, grad_update, hidden, hidden_a, hidden_b, reset,
                      cand_wt, gate_wt, update, grad_state, motion_so_far,
                      grad_gate, grad_first, grad_motion, cand_taps, gate_taps, inner):
    def finish(row, start, here, terms):
        gate = update[row + 1, here]
        grad = grad_state[row, here] * (1.0 - gate) + terms
        grad_first[row, here] = grad.astype(BF16)
        grad_motion[row, here] += motion_so_far[row, here]

    back_step(place, grad_cand, grad_a, grad_b, grad_update, hidden, hidden_a, hidden_b, reset, cand_wt, gate_wt,
              grad_gate, cand_taps, gate_taps, inner, grad_motion, finish)


def load_pixels(odd, pixels, hiddens, motion, motion_a, motion_b):
    wide = motion.shape[1]
    above, below = sides(odd, motion_a[1], motion_b[1])[0], sides(odd, motion_a[0], motion_b[0])[1]
    for row, value in enumerate((above, motion[0], motion[1], below)):
        pixels[row * wide : (row + 1) * wide, LANES:] = value
    for row, value in enumerate(hiddens):
        pixels[row * wide : (row + 1) * wide, :LANES] = value


def load_grads(taps, grads):
    wide = grads.shape[1]
    column = lax.broadcasted_iota(jnp.int32, (wide, LANES), 0)
    own = (column >= HALO) & (column < wide - HALO)
    depth = grads.shape[2]
    for row in range(2):
        for part in range(depth // LANES):
            value = jnp.where(own, grads[row, :, part * LANES : (part + 1) * LANES].astype(F32), 0.0)
            shifted = (pltpu.roll(value, wide - 1, 0), value, pltpu.roll(value, 1, 0))
            for tap in range(3):
                start = tap * depth + part * LANES
                taps[row * wide : (row + 1) * wide, start : start + LANES] = shifted[tap].astype(BF16)


def weight_products(pixels, taps, wide, depth, finish):
    def one_row(a, carry):
        rows = pixels[pl.ds(pl.multiple_of(a * wide, 16), 2 * wide), :]
        total = dot_tn(rows, taps[...])
        for b in range(3):
            finish(pl.multiple_of((3 * a + b) * 2 * LANES, LANES), total[:, b * depth : (b + 1) * depth])
        return carry

    lax.fori_loop(0, 3, one_row, 0)


def hidden_rows(odd, hidden, hidden_a, hidden_b):
    above, below = sides(odd, hidden_a[1], hidden_b[1])[0], sides(odd, hidden_a[0], hidden_b[0])[1]
    return (above, hidden[0], hidden[1], below)


def cand_weights_kernel(place, resets, motion, motion_a, motion_b, grads, out, pixels, taps):
    odd = place[0] % 2 == 1
    load_pixels(odd, pixels, [resets[row] for row in range(4)], motion, motion_a, motion_b)
    load_grads(taps, grads)

    def finish(start, value):
        out[pl.ds(start, 2 * LANES)] = value

    weight_products(pixels, taps, motion.shape[1], LANES, finish)


def middle_weights_kernel(place, resets, hidden, hidden_a, hidden_b, motion, motion_a, motion_b, cand_grads, gate_grads,
                          so_far, cand_out, gate_out, pixels, cand_taps, gate_taps):
    odd = place[0] % 2 == 1
    wide = motion.shape[1]
    load_pixels(odd, pixels, [resets[row] for row in range(4)], motion, motion_a, motion_b)
    load_grads(cand_taps, cand_grads)
    load_grads(gate_taps, gate_grads)

    def cand_finish(start, value):
        here = pl.ds(start, 2 * LANES)
        cand_out[here] = so_far[here] + value

    weight_products(pixels, cand_taps, wide, LANES, cand_finish)
    for row, value in enumerate(hidden_rows(odd, hidden, hidden_a, hidden_b)):
        pixels[row * wide : (row + 1) * wide, :LANES] = value

    def gate_finish(start, value):
        here = pl.ds(start, 2 * LANES)
        for half in range(2):
            gate_out[half, here] = value[:, half * LANES : (half + 1) * LANES]

    weight_products(pixels, gate_taps, wide, 2 * LANES, gate_finish)


def last_weights_kernel(place, hidden, hidden_a, hidden_b, motion, motion_a, motion_b, gate_grads, gate_so_far, cand,
                        motion_w, out, pixels, taps):
    odd = place[0] % 2 == 1
    load_pixels(odd, pixels, hidden_rows(odd, hidden, hidden_a, hidden_b), motion, motion_a, motion_b)
    load_grads(taps, gate_grads)
    rows = cand.shape[0]

    def finish(start, value):
        here = pl.ds(start, 2 * LANES)
        for half in range(2):
            there = pl.ds(pl.multiple_of(half * rows + start, LANES), 2 * LANES)
            part = value[:, half * LANES : (half + 1) * LANES] + gate_so_far[half, here]
            out[there] = part.astype(BF16)

    weight_products(pixels, taps, motion.shape[1], 2 * LANES, finish)
    out[2 * rows : 3 * rows] = cand[...].astype(BF16)
    out[3 * rows : 3 * rows + LANES] = motion_w[...].astype(BF16)
    out[3 * rows + LANES :] = jnp.zeros((out.shape[0] - 3 * rows - LANES, LANES), BF16)


def band_back_kernel(place, disparity, offsets, left, right, got_a, got_b, weight, grad_motion, pre, feats,
                     grad_left, back, own, motion_w, window, grad_window):
    odd = place[1] % 2 == 1
    cols = left.shape[1]
    block = cols // 2
    span = 512
    scaling = 1.0 / math.sqrt(left.shape[2])
    position = DISP - lax.broadcasted_iota(jnp.int32, (span, LANES), 0)
    valid = (position >= 0) & (position < DISP)
    inner = slice(HALO, HALO + cols)
    total_w = jnp.zeros((LANES, LANES), F32)
    for row in range(2):
        from_left = sides(odd, got_a[row], got_b[row])[0]
        window[0:DISP] = from_left[HALO : HALO + DISP]
        window[DISP : DISP + cols] = right[row]
        window[DISP + cols :] = jnp.zeros((window.shape[0] - DISP - cols, window.shape[1]), BF16)
        grad_window[...] = jnp.zeros(grad_window.shape, F32)
        value = pre[row, inner]
        gate = jax.nn.sigmoid(value)
        slope = gate * (1.0 + value * (1.0 - gate))
        grad_pre = (grad_motion[row, inner] * slope).astype(BF16)
        total_w = total_w + dot_tn(feats[row, inner], grad_pre)
        grad_feats = dot_nt(grad_pre, weight[...])
        table = lookup_rows(position, valid, disparity, offsets, row)
        for part in range(2):
            here = slice(part * block, (part + 1) * block)
            there = slice(part * block, part * block + span)
            band = split_dot(grad_feats[here], table, dot_nt)
            scores = (pltpu.roll(band, 0, 1, stride=1, stride_axis=0) * scaling).astype(BF16)
            grad_left[row, here] = dot(scores, window[there]).astype(BF16)
            grad_window[there] += dot_tn(scores, left[row, here])
        back[row] = grad_window[0:DISP].astype(BF16)
        own[row] = grad_window[DISP : DISP + cols]
    motion_w[...] = total_w


def pairings(count):
    first = [(2 * k, 2 * k + 1) for k in range(count // 2)]
    second = [(2 * k + 1, 2 * k + 2) for k in range(count // 2 - 1)]
    both = lambda pairs: pairs + [(b, a) for a, b in pairs]
    return both(first), both(second)


def exchanged(value, axis):
    first, second = pairings(lax.axis_size(axis))
    return lax.ppermute(value, axis, first), lax.ppermute(value, axis, second)


def exchanged_pair(value_a, value_b, axis):
    first, second = pairings(lax.axis_size(axis))
    return lax.ppermute(value_a, axis, first), lax.ppermute(value_b, axis, second)


def summed_everywhere(parts, cols_index, axes):
    cols_count = lax.axis_size("cols")
    devices = lax.axis_size("rows") * cols_count
    core = cols_index % 2
    swap = [(i, i ^ 1) for i in range(cols_count)]
    groups = [[i for i in range(devices) if i % 2 == c] for c in range(2)]
    kept = lax.dynamic_index_in_dim(parts, core, 0, keepdims=False)
    given = lax.dynamic_index_in_dim(parts, 1 - core, 0, keepdims=False)
    got = lax.ppermute(given, "cols", swap)
    half = (kept.astype(F32) + got.astype(F32)).astype(BF16)
    pieces = lax.all_to_all(half, axes, 0, 0, tiled=True, axis_index_groups=groups)
    piece = jnp.sum(pieces.astype(F32), axis=0).astype(BF16)
    spread = jnp.broadcast_to(piece[None], pieces.shape)
    half = lax.all_to_all(spread, axes, 0, 0, tiled=True, axis_index_groups=groups)
    other = lax.ppermute(half, "cols", swap)
    first = jnp.where(core == 0, half, other)
    second = jnp.where(core == 0, other, half)
    return jnp.stack([first, second])


def on_device(
    fmap_left,
    fmap_right,
    hidden_init,
    disp_init,
    level_offset,
    motion_weight,
    gate_weight,
    cand_weight,
    grad_hidden,
):
    rows, cols, channels = fmap_left.shape
    wide = cols + 2 * HALO
    state = hidden_init.shape[2]
    feats_count = motion_weight.shape[0]
    rows_axis, cols_axis = lax.axis_size("rows"), lax.axis_size("cols")
    rows_index, cols_index = lax.axis_index("rows"), lax.axis_index("cols")
    place = jnp.stack([rows_index, cols_index]).astype(jnp.int32)
    odd_col = cols_index % 2 == 1

    maps = jnp.concatenate(
        [fmap_right[:, cols - DISP - HALO :], fmap_left[:, cols - HALO :], fmap_left[:, :HALO], fmap_right[:, :HALO]],
        axis=1,
    )
    states = jnp.concatenate(
        [hidden_init[:, cols - HALO :], hidden_init[:, :HALO], grad_hidden[:, cols - HALO :], grad_hidden[:, :HALO]],
        axis=1,
    )
    states_a, states_b = exchanged(states, "cols")
    maps_a, maps_b = exchanged(maps, "cols")
    state_left = jnp.where(odd_col, states_a, states_b)
    state_right = jnp.where(odd_col, states_b, states_a)
    hidden = jnp.concatenate(
        [state_left[:, :HALO], hidden_init, state_right[:, HALO : 2 * HALO]], axis=1
    )
    grads = jnp.concatenate(
        [state_left[:, 2 * HALO : 3 * HALO], grad_hidden, state_right[:, 3 * HALO :]], axis=1
    )
    hidden_a, hidden_b = exchanged(hidden, "rows")

    motion_w = jnp.pad(motion_weight, ((0, LANES - feats_count), (0, 0)))
    gate_wt = jnp.transpose(gate_weight.reshape(3, 3, 2 * state, 2 * state), (0, 1, 3, 2)).reshape(-1, 2 * state)
    cand_wt = jnp.transpose(cand_weight.reshape(3, 3, 2 * state, state), (0, 1, 3, 2)).reshape(-1, 2 * state)

    field = lambda count, dtype: array((count, wide, LANES), dtype)
    band_flops = 2 * rows * wide * 512 * channels
    motion, motion_pre, feats = kernel_call(
        motion_kernel,
        [field(2, BF16), field(2, F32), field(2, BF16)],
        [place, disp_init, level_offset, fmap_left, fmap_right, maps_a, maps_b, motion_w],
        3,
        [pltpu.VMEM((wide, channels), BF16), pltpu.VMEM((768, channels), BF16), pltpu.VMEM((832, channels), BF16)],
        2 * band_flops,
    )
    motion_a, motion_b = exchanged(motion, "rows")
    motions = (motion, motion_a, motion_b)
    unit = 2 * wide * 9 * 2 * state * state
    fields = [pltpu.VMEM((6, wide, 6 * LANES), BF16), pltpu.VMEM((4, wide, 6 * LANES), BF16)]

    hidden_1, update_0, reset_0, reset_hidden_0, candidate_0 = kernel_call(
        lambda *refs: first_kernel(cols_axis, *refs),
        [field(2, BF16), field(4, F32), field(4, F32), field(4, BF16), field(2, F32)],
        [place, hidden, hidden_a, hidden_b, *motions, gate_weight, cand_weight],
        1,
        fields,
        10 * unit,
    )
    hidden_1a, hidden_1b = exchanged(hidden_1, "rows")
    update_1, reset_1, reset_hidden_1, grad_cand_1, grad_update_1, send_a, send_b = kernel_call(
        second_kernel,
        [field(4, F32), field(4, F32), field(4, BF16), field(2, BF16), field(2, BF16), field(3, BF16), field(3, BF16)],
        [place, hidden_1, hidden_1a, hidden_1b, *motions, gate_weight, cand_weight, grads],
        1,
        fields,
        10 * unit,
    )
    got_a, got_b = exchanged_pair(send_a, send_b, "rows")
    pixels = pltpu.VMEM((4 * wide, 2 * LANES), BF16)
    cand_taps = pltpu.VMEM((2 * wide, 3 * LANES), BF16)
    gate_taps = pltpu.VMEM((2 * wide, 6 * LANES), BF16)
    (cand_sum_1,) = kernel_call(
        cand_weights_kernel,
        [array(cand_weight.shape, F32)],
        [place, reset_hidden_1, *motions, grad_cand_1],
        1,
        [pixels, cand_taps],
        2 * unit,
    )
    back_scratch = [
        pltpu.VMEM((6, wide, 3 * LANES), BF16),
        pltpu.VMEM((4, wide, 6 * LANES), BF16),
        pltpu.VMEM((4, wide, LANES), F32),
    ]
    grad_gate_1, grad_state, grad_motion_1, grad_cand_0, grad_update_0, send_a, send_b = kernel_call(
        lambda *refs: later_back_kernel(cols_axis, *refs),
        [array((2, wide, 2 * LANES), BF16), field(2, F32), field(2, F32), field(2, BF16), field(2, BF16),
         field(3, BF16), field(3, BF16)],
        [place, grad_cand_1, got_a, got_b, grad_update_1, hidden_1, hidden_1a, hidden_1b, reset_1, cand_wt, gate_wt,
         update_1, grads, hidden, update_0, candidate_0],
        1,
        back_scratch,
        8 * unit,
    )
    got_a, got_b = exchanged_pair(send_a, send_b, "rows")
    cand_sum, gate_sum_1 = kernel_call(
        middle_weights_kernel,
        [array(cand_weight.shape, F32), array((2,) + cand_weight.shape, F32)],
        [place, reset_hidden_0, hidden_1, hidden_1a, hidden_1b, *motions, grad_cand_0, grad_gate_1, cand_sum_1],
        1,
        [pixels, cand_taps, gate_taps],
        6 * unit,
    )
    grad_gate_0, grad_first, grad_motion = kernel_call(
        first_back_kernel,
        [array((2, wide, 2 * LANES), BF16), field(2, BF16), field(2, F32)],
        [place, grad_cand_0, got_a, got_b, grad_update_0, hidden, hidden_a, hidden_b, reset_0, cand_wt, gate_wt,
         update_0, grad_state, grad_motion_1],
        1,
        back_scratch,
        8 * unit,
    )
    grad_left, back, own, motion_sum = kernel_call(
        band_back_kernel,
        [array((2, cols, channels), BF16), array((2, DISP, channels), BF16), array((2, cols, channels), F32),
         array((LANES, LANES), F32)],
        [place, disp_init, level_offset, fmap_left, fmap_right, maps_a, maps_b, motion_w, grad_motion, motion_pre, feats],
        3,
        [pltpu.VMEM((768, channels), BF16), pltpu.VMEM((768, channels), F32)],
        3 * band_flops,
    )
    back_a, back_b = exchanged(back, "cols")
    devices = rows_axis * cols_axis
    (parts,) = kernel_call(
        last_weights_kernel,
        [array((devices * CHUNK_ROWS, LANES), BF16)],
        [place, hidden, hidden_a, hidden_b, *motions, grad_gate_0, gate_sum_1, cand_sum, motion_sum],
        1,
        [pixels, gate_taps],
        4 * unit,
    )
    sums = summed_everywhere(
        parts.reshape(2, devices // 2, CHUNK_ROWS, LANES), cols_index, ("rows", "cols")
    ).reshape(devices * CHUNK_ROWS, LANES)
    returned = jnp.where(odd_col, back_b, back_a).astype(F32)
    grad_right = jnp.concatenate(
        [own[:, : cols - DISP], own[:, cols - DISP :] + returned], axis=1
    ).astype(BF16)
    normaliser = 1.0 / math.sqrt(rows * rows_axis * cols * cols_axis)
    depth = cand_weight.shape[0]
    scaled = lambda start, count: sums[start : start + count].astype(F32) * normaliser
    return (
        grad_left,
        grad_right,
        grad_first[:, HALO : HALO + cols],
        scaled(3 * depth, feats_count),
        jnp.concatenate([scaled(0, depth), scaled(depth, depth)], axis=1),
        scaled(2 * depth, depth),
    )


def solution(mesh):
    in_specs = (
        P("rows", "cols", None),
        P("rows", "cols", None),
        P("rows", "cols", None),
        P("rows"),
        P("rows", None),
        P(),
        P(),
        P(),
        P("rows", "cols", None),
    )
    out_specs = (
        P("rows", "cols", None),
        P("rows", "cols", None),
        P("rows", "cols", None),
        P(),
        P(),
        P(),
    )
    return jax.shard_map(
        on_device, mesh=mesh, in_specs=in_specs, out_specs=out_specs, check_vma=False
    )
```

profile of v0, /device:TPU:1, one launch (start us, length us, event | category | flops | bytes accessed | tf_op | source)
XLA Modules:
  0.0 205.7 jit_solution(5138712494179378151)
XLA Ops:
  0.7 0.8 slice.61
  1.5 0.9 slice.58
  2.5 0.7 fusion.1
  3.2 1.5 collective-permute-start
  4.7 4.6 %collective-permute-start.1 = (bf16[2,256,256]{2,1,0:T(8,128)(2,1)S(1)}, bf16[2,256,256]{2,1,0:T(8,128)(2,1)S(1)}, u32[]{:S(2)}, u32[]{:S(2)}) collective-permute-start(bf16[2,256,256]{2,1,0:T(8,128)(2,1)S(1)} %pad_maximum_fusion.5), channel_id=1, source_target_pairs={{1,2},{2,1},{5,6},{6,5},{9,10},{10,9},{13,14},{14,13},{17,18},{18,... | collective-permute-start | bytes 786440 | tf_op jit(solution)/shard_map/ppermute | solution.py:444
  9.4 0.8 fusion.2
  10.2 2.4 %collective-permute-start.3 = (bf16[2,64,128]{2,1,0:T(8,128)(2,1)S(1)}, bf16[2,64,128]{2,1,0:T(8,128)(2,1)S(1)}, u32[]{:S(2)}, u32[]{:S(2)}) collective-permute-start(bf16[2,64,128]{2,1,0:T(8,128)(2,1)S(1)} %pad_maximum_fusion.6), channel_id=1, source_target_pairs={{1,2},{2,1},{5,6},{6,5},{9,10},{10,9},{13,14},{14,13},{17,18},{18,... | collective-permute-start | bytes 98312 | tf_op jit(solution)/shard_map/ppermute | solution.py:444
  12.7 0.7 pad.4.weight
  13.4 3.5 %collective-permute-done.3 = bf16[2,64,128]{2,1,0:T(8,128)(2,1)S(1)} collective-permute-done((bf16[2,64,128]{2,1,0:T(8,128)(2,1)S(1)}, bf16[2,64,128]{2,1,0:T(8,128)(2,1)S(1)}, u32[]{:S(2)}, u32[]{:S(2)}) %collective-permute-start.3) | collective-permute-done | bytes 32800 | tf_op jit(solution)/shard_map/ppermute | solution.py:444
  17.0 1.7 collective-permute-start.4
  18.8 0.7 collective-permute-start.5
  19.5 4.0 %shard_map.136 = (bf16[2,544,128]{2,1,0:T(8,128)(2,1)S(1)}, f32[2,544,128]{2,1,0:T(8,128)S(1)}, bf16[2,544,128]{2,1,0:T(8,128)(2,1)S(1)}) custom-call(s32[2]{0:T(128)S(1)} %pad_add_fusion.place.refs_0_, s32[2]{0:T(128)S(1)} %copy-done.28, s32[2,4]{1,0:T(2,128)S(1)} %copy-done.27, bf16[2,512,256]{2,1,0:T(8,128)(2,1)S(1)} %copy-done.10, ...), custom_call_target="tpu_custom_call" | custom-call | flops 570425344 | bytes 2719792 | tf_op jit(solution)/shard_map/pallas_call | solution.py:46
  23.6 4.3 %collective-permute-start.6 = (bf16[2,544,128]{2,1,0:T(8,128)(2,1)S(1)}, bf16[2,544,128]{2,1,0:T(8,128)(2,1)S(1)}, u32[]{:S(2)}, u32[]{:S(2)}) collective-permute-start(bf16[2,544,128]{2,1,0:T(8,128)(2,1)S(1)} %get-tuple-element.37.refs_4_.motion), channel_id=1, source_target_pairs={{0,4},{8,12},{16,20},{24,28},{32,36},{40,44},{48,52},{56,60},{64,6... | collective-permute-start | bytes 835592 | tf_op jit(solution)/shard_map/ppermute | solution.py:444
  27.9 0.7 collective-permute-start.7
  28.6 3.2 %collective-permute-done.6.refs_5_.motion_a = bf16[2,544,128]{2,1,0:T(8,128)(2,1)S(1)} collective-permute-done((bf16[2,544,128]{2,1,0:T(8,128)(2,1)S(1)}, bf16[2,544,128]{2,1,0:T(8,128)(2,1)S(1)}, u32[]{:S(2)}, u32[]{:S(2)}) %collective-permute-start.6) | collective-permute-done | bytes 278560 | tf_op jit(solution)/shard_map/ppermute | solution.py:444
  31.8 8.0 %shard_map.137 = (bf16[2,544,128]{2,1,0:T(8,128)(2,1)S(1)}, f32[4,544,128]{2,1,0:T(8,128)S(1)}, f32[4,544,128]{2,1,0:T(8,128)S(1)}, bf16[4,544,128]{2,1,0:T(8,128)(2,1)S(1)}, f32[2,544,128]{2,1,0:T(8,128)S(1)}) custom-call(s32[2]{0:T(128)S(1)} %pad_add_fusion.place.refs_0_, bf16[2,544,128]{2,1,0:T(8,128)(2,1)S(1)} %pad_maximum_fusion.3.refs_1_.refs_13_.hidden, ...), custom_call_target="tpu_custom_call" | custom-call | flops 3208642560 | bytes 7061512 | tf_op jit(solution)/shard_map/pallas_call | solution.py:46
  39.9 1.0 copy-done.33
  40.9 0.8 copy-done.35
  41.7 1.0 copy-done.48
  42.7 0.8 copy-done.49
  43.5 3.5 %collective-permute-start.8 = (bf16[2,544,128]{2,1,0:T(8,128)(2,1)S(1)}, bf16[2,544,128]{2,1,0:T(8,128)(2,1)S(1)}, u32[]{:S(2)}, u32[]{:S(2)}) collective-permute-start(bf16[2,544,128]{2,1,0:T(8,128)(2,1)S(1)} %get-tuple-element.38.hidden.refs_5_), channel_id=1, source_target_pairs={{0,4},{8,12},{16,20},{24,28},{32,36},{40,44},{48,52},{56,60},{64,6... | collective-permute-start | bytes 835592 | tf_op jit(solution)/shard_map/ppermute | solution.py:444
  47.0 0.7 collective-permute-start.9
  47.7 3.3 %collective-permute-done.8.hidden_a.refs_6_ = bf16[2,544,128]{2,1,0:T(8,128)(2,1)S(1)} collective-permute-done((bf16[2,544,128]{2,1,0:T(8,128)(2,1)S(1)}, bf16[2,544,128]{2,1,0:T(8,128)(2,1)S(1)}, u32[]{:S(2)}, u32[]{:S(2)}) %collective-permute-start.8) | collective-permute-done | bytes 278560 | tf_op jit(solution)/shard_map/ppermute | solution.py:444
  51.0 11.5 %shard_map.138 = (f32[4,544,128]{2,1,0:T(8,128)S(1)}, f32[4,544,128]{2,1,0:T(8,128)}, bf16[4,544,128]{2,1,0:T(8,128)(2,1)S(1)}, bf16[2,544,128]{2,1,0:T(8,128)(2...) custom-call(s32[2]{0:T(128)S(1)} %pad_add_fusion.place.refs_0_, ...), custom_call_target="tpu_custom_call" | custom-call | flops 3208642560 | bytes 7897096 | tf_op jit(solution)/shard_map/pallas_call | solution.py:46
  62.6 1.0 copy-done.34
  63.5 0.7 copy-done.46
  64.3 5.5 %collective-permute-start.10 = (bf16[3,544,128]{2,1,0:T(8,128)(2,1)}, bf16[3,544,128]{2,1,0:T(8,128)(2,1)}, u32[]{:S(2)}, u32[]{:S(2)}) collective-permute-start(bf16[3,544,128]{2,1,0:T(8,128)(2,1)} %get-tuple-element.40), channel_id=1, source_target_pairs={{0,4},{8,12},{16,20},{24,28},{32,36},{40,44},{48,52},{56,60},{64,6... | collective-permute-start | bytes 1253384 | tf_op jit(solution)/shard_map/ppermute | solution.py:449
  69.8 1.4 collective-permute-start.11
  71.2 1.1 copy.15
  72.3 2.4 %copy.16 = bf16[3,3,256,256]{2,3,1,0:T(8,128)(2,1)} copy(bf16[3,3,256,256]{3,2,1,0:T(8,128)(2,1)} %bitcast.28) | data formatting | bytes 2359296 | tf_op jit(solution)/shard_map/reshape | solution.py:513
  74.7 3.5 %collective-permute-done.10.refs_2_ = bf16[3,544,128]{2,1,0:T(8,128)(2,1)} collective-permute-done((bf16[3,544,128]{2,1,0:T(8,128)(2,1)}, bf16[3,544,128]{2,1,0:T(8,128)(2,1)}, u32[]{:S(2)}, u32[]{:S(2)}) %collective-permute-start.10) | collective-permute-done | bytes 417824 | tf_op jit(solution)/shard_map/ppermute | solution.py:449
  78.2 0.9 copy-done.19
  79.1 1.0 copy-done.47
  80.1 11.2 %shard_map.139 = (bf16[2,544,256]{2,1,0:T(8,128)(2,1)S(1)}, f32[2,544,128]{2,1,0:T(8,128)S(1)}, f32[2,544,128]{2,1,0:T(8,128)S(1)}, bf16[2,544,128]{2,1,0:T(8,12...) custom-call(s32[2]{0:T(128)S(1)} %pad_add_fusion.place.refs_0_, ...), custom_call_target="tpu_custom_call" | custom-call | flops 2566914048 | bytes 11517960 | tf_op jit(solution)/shard_map/pallas_call | solution.py:46
  91.3 0.8 copy-done.36
  92.1 0.8 copy-done.38
  92.9 0.8 copy-done.40
  93.7 0.7 copy-done.42
  94.5 0.7 copy-done.44
  95.2 5.7 %collective-permute-start.12 = (bf16[3,544,128]{2,1,0:T(8,128)(2,1)}, bf16[3,544,128]{2,1,0:T(8,128)(2,1)S(1)}, u32[]{:S(2)}, u32[]{:S(2)}) collective-permute-start(bf16[3,544,128]{2,1,0:T(8,128)(2,1)} %get-tuple-element.48), channel_id=1, source_target_pairs={{0,4},{8,12},{16,20},{24,28},{32,36},{40,44},{48,52},{56,60},{64,6... | collective-permute-start | bytes 1253384 | tf_op jit(solution)/shard_map/ppermute | solution.py:449
  100.9 1.4 collective-permute-start.13
  102.3 2.5 %shard_map.142.so_far = f32[2304,128]{1,0:T(8,128)S(1)} custom-call(s32[2]{0:T(128)S(1)} %pad_add_fusion.place.refs_0_, bf16[4,544,128]{2,1,0:T(8,128)(2,1)S(1)} %get-tuple-element.64.resets, bf16[2,544,128]{2,1,0:T(8,128)(2,1)S(1)} %get-tuple-element.37.refs_4_.motion, bf16[2,544,128]{2,1,0:T(8,128)(2,1)S(1)} %collective-permute-done.6.refs_5_.motion_a, ...), custom_call_target="tpu_custom_call" | custom-call | flops 641728512 | bytes 2850824 | tf_op jit(solution)/shard_map/pallas_call | solution.py:46
  105.0 6.5 %shard_map.143 = (f32[2304,128]{1,0:T(8,128)S(1)}, f32[2,2304,128]{2,1,0:T(8,128)}) custom-call(s32[2]{0:T(128)S(1)} %pad_add_fusion.place.refs_0_, bf16[4,544,128]{2,1,0:T(8,128)(2,1)S(1)} %copy-done.50, bf16[2,544,128]{2,1,0:T(8,128)(2,1)S(1)} %copy-done.14, bf16[2,544,128]{2,1,0:T(8,128)(2,1)S(1)} %copy-done.17, bf16[2,544,128]{2,1,0:T(8,128)(2,1)S(1)} %copy-done.20, ...), custom_call_target="tpu_custom_call" | custom-call | flops 1925185536 | bytes 7782408 | tf_op jit(solution)/shard_map/pallas_call | solution.py:46
  111.6 7.6 %shard_map.140 = (bf16[2,544,256]{2,1,0:T(8,128)(2,1)S(1)}, bf16[2,544,128]{2,1,0:T(8,128)(2,1)S(1)}, f32[2,544,128]{2,1,0:T(8,128)S(1)}) custom-call(s32[2]{0:T(128)S(1)} %pad_add_fusion.place.refs_0_, bf16[2,544,128]{2,1,0:T(8,128)(2,1)S(1)} %copy-done.43, bf16[3,544,128]{2,1,0:T(8,128)(2,1)S(1)} %collective-permute-done.12.grad_a, ...), custom_call_target="tpu_custom_call" | custom-call | flops 2566914048 | bytes 8732680 | tf_op jit(solution)/shard_map/pallas_call | solution.py:46
  119.3 3.5 %shard_map.141 = (bf16[2,512,256]{2,1,0:T(8,128)(2,1)}, bf16[2,192,256]{2,1,0:T(8,128)(2,1)S(1)}, f32[2,512,256]{2,1,0:T(8,128)S(1)}, f32[128,128]{1,0:T(8,128)S(1)}) custom-call(s32[2]{0:T(128)S(1)} %pad_add_fusion.place.refs_0_, s32[2]{0:T(128)S(1)} %copy-done.28, s32[2,4]{1,0:T(2,128)S(1)} %copy-done.27, bf16[2,512,256]{2,1,0:T(8,128)(2,1)S(1)} %copy-done.11, ...), custom_call_target="tpu_custom_call" | custom-call | flops 855638016 | bytes 4833328 | tf_op jit(solution)/shard_map/pallas_call | solution.py:46
  122.8 5.0 %shard_map.144 = bf16[8192,128]{1,0:T(8,128)(2,1)S(1)} custom-call(s32[2]{0:T(128)S(1)} %pad_add_fusion.place.refs_0_, bf16[2,544,128]{2,1,0:T(8,128)(2,1)S(1)} %pad_maximum_fusion.3.refs_1_.refs_13_.hidden, bf16[2,544,128]{2,1,0:T(8,128)(2,1)S(1)} %collective-permute-done.4.refs_2_.hidden_a, bf16[2,544,128]{2,1,0:T(8,128)(2,1)S(1)} %copy-done.5, ...), custom_call_target="tpu_custom_call" | custom-call | flops 1283457024 | bytes 7929864 | tf_op jit(solution)/shard_map/pallas_call | solution.py:46
  127.9 0.1 collective-permute-start.16
  128.0 2.8 %collective-permute-done.16 = bf16[64,64,128]{2,1,0:T(8,128)(2,1)} collective-permute-done((bf16[64,64,128]{2,1,0:T(8,128)(2,1)S(1)}, bf16[64,64,128]{2,1,0:T(8,128)(2,1)}, u32[]{:S(2)}, u32[]{:S(2)}) %collective-permute-start.16) | collective-permute-done | bytes 1048608 | tf_op jit(solution)/shard_map/ppermute | solution.py:460
  130.7 1.6 fusion
  132.4 33.8 %all_to_all.10 = bf16[64,64,128]{2,1,0:T(8,128)(2,1)S(1)} all-to-all(bf16[64,64,128]{2,1,0:T(8,128)(2,1)S(1)} %fusion), channel_id=1, replica_groups={{0,2,4,6,8,10,12,14,16,18,20,22,24,26,28,30,32,34,36,38,40,42,44,46,48,..., dimensions={0} | all-to-all | bytes 2097152 | tf_op jit(solution)/shard_map/all_to_all | solution.py:462
  166.2 0.2 reduce_sum.12
  166.4 0.2 broadcast_in_dim.2
  166.7 21.1 %all_to_all.11 = bf16[64,64,128]{2,1,0:T(8,128)(2,1)S(1)} all-to-all(bf16[64,64,128]{2,1,0:T(8,128)(2,1)S(1)} %broadcast_in_dim.2), channel_id=1, replica_groups={{0,2,4,6,8,10,12,14,16,18,20,22,24,26,28,30,32,34,36,38,40,42,44,46,48,..., dimensions={0} | all-to-all | bytes 2097152 | tf_op jit(solution)/shard_map/all_to_all | solution.py:465
  187.8 3.5 %collective-permute-start.17 = (bf16[64,64,128]{2,1,0:T(8,128)(2,1)S(1)}, bf16[64,64,128]{2,1,0:T(8,128)(2,1)}, u32[]{:S(2)}, u32[]{:S(2)}) collective-permute-start(bf16[64,64,128]{2,1,0:T(8,128)(2,1)S(1)} %all_to_all.11), channel_id=1, source_target_pairs={{0,1},{1,0},{2,3},{3,2},{4,5},{5,4},{6,7},{7,6},{8,9},{9,8},{10,11... | collective-permute-start | bytes 3145736 | tf_op jit(solution)/shard_map/ppermute | solution.py:466
  191.3 2.8 %collective-permute-start.14 = (bf16[2,192,256]{2,1,0:T(8,128)(2,1)S(1)}, bf16[2,192,256]{2,1,0:T(8,128)(2,1)S(1)}, u32[]{:S(2)}, u32[]{:S(2)}) collective-permute-start(bf16[2,192,256]{2,1,0:T(8,128)(2,1)S(1)} %copy-done.26), channel_id=1, source_target_pairs={{1,2},{2,1},{5,6},{6,5},{9,10},{10,9},{13,14},{14,13},{17,18},{18,... | collective-permute-start | bytes 589832 | tf_op jit(solution)/shard_map/ppermute | solution.py:444
  194.1 0.1 collective-permute-start.15
  194.2 0.7 slice.72
  194.9 4.8 %collective-permute-done.14 = bf16[2,192,256]{2,1,0:T(8,128)(2,1)S(1)} collective-permute-done((bf16[2,192,256]{2,1,0:T(8,128)(2,1)S(1)}, bf16[2,192,256]{2,1,0:T(8,128)(2,1)S(1)}, u32[]{:S(2)}, u32[]{:S(2)}) %collective-permute-start.14) | collective-permute-done | bytes 196640 | tf_op jit(solution)/shard_map/ppermute | solution.py:444
  199.8 0.8 pad_maximum_fusion.2
  200.7 1.4 select_bitcast_fusion.1
  202.0 0.2 pad_maximum_fusion.1
  202.2 0.6 convert_multiply_fusion.3
  202.8 1.3 convert_multiply_fusion
  204.1 1.6 pad_maximum_fusion
  (117 shorter events, 0.6 us)
Async XLA Ops:
  0.6 18.8 %copy-start.8 = (bf16[2,512,256]{2,1,0:T(8,128)(2,1)S(1)}, bf16[2,512,256]{2,1,0:T(8,128)(2,1)}, u32[]{:S(2)}) copy-start(bf16[2,512,256]{2,1,0:T(8,128)(2,1)} %right.3) | copy-start | bytes 1572868
  0.6 18.8 %copy-start.10 = (bf16[2,512,256]{2,1,0:T(8,128)(2,1)S(1)}, bf16[2,512,256]{2,1,0:T(8,128)(2,1)}, u32[]{:S(2)}) copy-start(bf16[2,512,256]{2,1,0:T(8,128)(2,1)} %left.3) | copy-start | bytes 1572868
  0.7 16.3 %copy-start.51 = (bf16[2,512,128]{2,1,0:T(8,128)(2,1)S(1)}, bf16[2,512,128]{2,1,0:T(8,128)(2,1)}, u32[]{:S(2)}) copy-start(bf16[2,512,128]{2,1,0:T(8,128)(2,1)} %param.11) | copy-start | bytes 786436
  0.7 18.8 %copy-start.28 = (s32[2]{0:T(128)S(1)}, s32[2]{0:T(128)}, u32[]{:S(2)}) copy-start(s32[2]{0:T(128)} %disparity.3) | copy-start | bytes 28
  0.7 18.8 %copy-start.27 = (s32[2,4]{1,0:T(2,128)S(1)}, s32[2,4]{1,0:T(2,128)}, u32[]{:S(2)}) copy-start(s32[2,4]{1,0:T(2,128)} %offsets.3) | copy-start | bytes 100
  3.2 16.2 %collective-permute-start = (bf16[2,256,256]{2,1,0:T(8,128)(2,1)S(1)}, bf16[2,256,256]{2,1,0:T(8,128)(2,1)S(1)}, u32[]{:S(2)}, u32[]{:S(2)}) collective-permute-start(bf16[2,256,256]{2,1,0:T(8,128)(2,1)S(1)} %pad_maximum_fusion.5), channel_id=1, source_target_pairs={{0,1},{2,3},{1,0},{3,2},{4,5},{6,7},{5,4},{7,6},{8,9},{10,11},{9,8... | collective-permute-start | bytes 786440 | tf_op jit(solution)/shard_map/ppermute | solution.py:444
  4.7 14.7 %collective-permute-start.1 = (bf16[2,256,256]{2,1,0:T(8,128)(2,1)S(1)}, bf16[2,256,256]{2,1,0:T(8,128)(2,1)S(1)}, u32[]{:S(2)}, u32[]{:S(2)}) collective-permute-start(bf16[2,256,256]{2,1,0:T(8,128)(2,1)S(1)} %pad_maximum_fusion.5), channel_id=1, source_target_pairs={{1,2},{2,1},{5,6},{6,5},{9,10},{10,9},{13,14},{14,13},{17,18},{18,... | collective-permute-start | bytes 786440 | tf_op jit(solution)/shard_map/ppermute | solution.py:444
  10.1 3.3 %collective-permute-start.2 = (bf16[2,64,128]{2,1,0:T(8,128)(2,1)S(1)}, bf16[2,64,128]{2,1,0:T(8,128)(2,1)S(1)}, u32[]{:S(2)}, u32[]{:S(2)}) collective-permute-start(bf16[2,64,128]{2,1,0:T(8,128)(2,1)S(1)} %pad_maximum_fusion.6), channel_id=1, source_target_pairs={{0,1},{2,3},{1,0},{3,2},{4,5},{6,7},{5,4},{7,6},{8,9},{10,11},{9,8... | collective-permute-start | bytes 98312 | tf_op jit(solution)/shard_map/ppermute | solution.py:444
  10.2 6.7 %collective-permute-start.3 = (bf16[2,64,128]{2,1,0:T(8,128)(2,1)S(1)}, bf16[2,64,128]{2,1,0:T(8,128)(2,1)S(1)}, u32[]{:S(2)}, u32[]{:S(2)}) collective-permute-start(bf16[2,64,128]{2,1,0:T(8,128)(2,1)S(1)} %pad_maximum_fusion.6), channel_id=1, source_target_pairs={{1,2},{2,1},{5,6},{6,5},{9,10},{10,9},{13,14},{14,13},{17,18},{18,... | collective-permute-start | bytes 98312 | tf_op jit(solution)/shard_map/ppermute | solution.py:444
  17.0 14.8 %copy-start = (bf16[2304,128]{1,0:T(8,128)(2,1)S(1)}, bf16[2304,128]{1,0:T(8,128)(2,1)}, u32[]{:S(2)}) copy-start(bf16[2304,128]{1,0:T(8,128)(2,1)} %cand_w.1) | copy-start | bytes 1769476
  17.0 11.5 %collective-permute-start.4 = (bf16[2,544,128]{2,1,0:T(8,128)(2,1)S(1)}, bf16[2,544,128]{2,1,0:T(8,128)(2,1)S(1)}, u32[]{:S(2)}, u32[]{:S(2)}) collective-permute-start(bf16[2,544,128]{2,1,0:T(8,128)(2,1)S(1)} %pad_maximum_fusion.3.refs_1_.refs_13_.hidden), channel_id=1, source_target_pairs={{0,4},{8,12},{16,20},{24,28},{32,36},{40,44},{48,52},{56,60},{64,6... | collective-permute-start | bytes 835592 | tf_op jit(solution)/shard_map/ppermute | solution.py:444
  18.8 9.8 %collective-permute-start.5 = (bf16[2,544,128]{2,1,0:T(8,128)(2,1)S(1)}, bf16[2,544,128]{2,1,0:T(8,128)(2,1)S(1)}, u32[]{:S(2)}, u32[]{:S(2)}) collective-permute-start(bf16[2,544,128]{2,1,0:T(8,128)(2,1)S(1)} %pad_maximum_fusion.3.refs_1_.refs_13_.hidden), channel_id=1, source_target_pairs={{4,8},{12,16},{20,24},{28,32},{36,40},{44,48},{52,56},{60,64},{68,... | collective-permute-start | bytes 835592 | tf_op jit(solution)/shard_map/ppermute | solution.py:444
  19.4 4.1 %copy-start.21 = (bf16[2,256,256]{2,1,0:T(8,128)(2,1)}, bf16[2,256,256]{2,1,0:T(8,128)(2,1)S(1)}, u32[]{:S(2)}) copy-start(bf16[2,256,256]{2,1,0:T(8,128)(2,1)S(1)} %collective-permute-done.got_a) | copy-start | bytes 786436
  19.5 4.0 %copy-start.23 = (bf16[2,256,256]{2,1,0:T(8,128)(2,1)}, bf16[2,256,256]{2,1,0:T(8,128)(2,1)S(1)}, u32[]{:S(2)}) copy-start(bf16[2,256,256]{2,1,0:T(8,128)(2,1)S(1)} %collective-permute-done.1.got_b) | copy-start | bytes 786436
  23.5 16.3 %copy-start.29 = (f32[2,544,128]{2,1,0:T(8,128)}, f32[2,544,128]{2,1,0:T(8,128)S(1)}, u32[]{:S(2)}) copy-start(f32[2,544,128]{2,1,0:T(8,128)S(1)} %get-tuple-element.55.pre) | copy-start | bytes 1671172
  23.5 16.3 %copy-start.31 = (bf16[2,544,128]{2,1,0:T(8,128)(2,1)}, bf16[2,544,128]{2,1,0:T(8,128)(2,1)S(1)}, u32[]{:S(2)}) copy-start(bf16[2,544,128]{2,1,0:T(8,128)(2,1)S(1)} %get-tuple-element.56.feats) | copy-start | bytes 835588
  23.6 24.1 %copy-start.52 = (bf16[2,512,128]{2,1,0:T(8,128)(2,1)S(1)}, bf16[2,512,128]{2,1,0:T(8,128)(2,1)}, u32[]{:S(2)}) copy-start(bf16[2,512,128]{2,1,0:T(8,128)(2,1)} %param.17) | copy-start | bytes 786436
  23.6 8.2 %collective-permute-start.6 = (bf16[2,544,128]{2,1,0:T(8,128)(2,1)S(1)}, bf16[2,544,128]{2,1,0:T(8,128)(2,1)S(1)}, u32[]{:S(2)}, u32[]{:S(2)}) collective-permute-start(bf16[2,544,128]{2,1,0:T(8,128)(2,1)S(1)} %get-tuple-element.37.refs_4_.motion), channel_id=1, source_target_pairs={{0,4},{8,12},{16,20},{24,28},{32,36},{40,44},{48,52},{56,60},{64,6... | collective-permute-start | bytes 835592 | tf_op jit(solution)/shard_map/ppermute | solution.py:444
  27.9 3.9 %collective-permute-start.7 = (bf16[2,544,128]{2,1,0:T(8,128)(2,1)S(1)}, bf16[2,544,128]{2,1,0:T(8,128)(2,1)S(1)}, u32[]{:S(2)}, u32[]{:S(2)}) collective-permute-start(bf16[2,544,128]{2,1,0:T(8,128)(2,1)S(1)} %get-tuple-element.37.refs_4_.motion), channel_id=1, source_target_pairs={{4,8},{12,16},{20,24},{28,32},{36,40},{44,48},{52,56},{60,64},{68,... | collective-permute-start | bytes 835592 | tf_op jit(solution)/shard_map/ppermute | solution.py:444
  28.6 82.9 %copy-start.4 = (bf16[2,544,128]{2,1,0:T(8,128)(2,1)}, bf16[2,544,128]{2,1,0:T(8,128)(2,1)S(1)}, u32[]{:S(2)}) copy-start(bf16[2,544,128]{2,1,0:T(8,128)(2,1)S(1)} %collective-permute-done.5.refs_3_.hidden_b) | copy-start | bytes 835588
  39.9 1.0 copy-start.33
  40.9 0.8 copy-start.35
  41.7 1.0 copy-start.48
  43.5 19.0 %copy-start.12 = (bf16[2,544,128]{2,1,0:T(8,128)(2,1)}, bf16[2,544,128]{2,1,0:T(8,128)(2,1)S(1)}, u32[]{:S(2)}) copy-start(bf16[2,544,128]{2,1,0:T(8,128)(2,1)S(1)} %get-tuple-element.38.hidden.refs_5_) | copy-start | bytes 835588
  43.5 7.5 %collective-permute-start.8 = (bf16[2,544,128]{2,1,0:T(8,128)(2,1)S(1)}, bf16[2,544,128]{2,1,0:T(8,128)(2,1)S(1)}, u32[]{:S(2)}, u32[]{:S(2)}) collective-permute-start(bf16[2,544,128]{2,1,0:T(8,128)(2,1)S(1)} %get-tuple-element.38.hidden.refs_5_), channel_id=1, source_target_pairs={{0,4},{8,12},{16,20},{24,28},{32,36},{40,44},{48,52},{56,60},{64,6... | collective-permute-start | bytes 835592 | tf_op jit(solution)/shard_map/ppermute | solution.py:444
  47.0 4.0 %collective-permute-start.9 = (bf16[2,544,128]{2,1,0:T(8,128)(2,1)S(1)}, bf16[2,544,128]{2,1,0:T(8,128)(2,1)S(1)}, u32[]{:S(2)}, u32[]{:S(2)}) collective-permute-start(bf16[2,544,128]{2,1,0:T(8,128)(2,1)S(1)} %get-tuple-element.38.hidden.refs_5_), channel_id=1, source_target_pairs={{4,8},{12,16},{20,24},{28,32},{36,40},{44,48},{52,56},{60,64},{68,... | collective-permute-start | bytes 835592 | tf_op jit(solution)/shard_map/ppermute | solution.py:444
  51.0 11.5 %copy-start.15 = (bf16[2,544,128]{2,1,0:T(8,128)(2,1)}, bf16[2,544,128]{2,1,0:T(8,128)(2,1)S(1)}, u32[]{:S(2)}) copy-start(bf16[2,544,128]{2,1,0:T(8,128)(2,1)S(1)} %collective-permute-done.8.hidden_a.refs_6_) | copy-start | bytes 835588
  51.0 11.5 %copy-start.18 = (bf16[2,544,128]{2,1,0:T(8,128)(2,1)}, bf16[2,544,128]{2,1,0:T(8,128)(2,1)S(1)}, u32[]{:S(2)}) copy-start(bf16[2,544,128]{2,1,0:T(8,128)(2,1)S(1)} %collective-permute-done.9.hidden_b.refs_7_) | copy-start | bytes 835588
  62.5 1.0 copy-start.34
  64.3 13.9 %collective-permute-start.10 = (bf16[3,544,128]{2,1,0:T(8,128)(2,1)}, bf16[3,544,128]{2,1,0:T(8,128)(2,1)}, u32[]{:S(2)}, u32[]{:S(2)}) collective-permute-start(bf16[3,544,128]{2,1,0:T(8,128)(2,1)} %get-tuple-element.40), channel_id=1, source_target_pairs={{0,4},{8,12},{16,20},{24,28},{32,36},{40,44},{48,52},{56,60},{64,6... | collective-permute-start | bytes 1253384 | tf_op jit(solution)/shard_map/ppermute | solution.py:449
  69.8 8.4 %collective-permute-start.11 = (bf16[3,544,128]{2,1,0:T(8,128)(2,1)}, bf16[3,544,128]{2,1,0:T(8,128)(2,1)}, u32[]{:S(2)}, u32[]{:S(2)}) collective-permute-start(bf16[3,544,128]{2,1,0:T(8,128)(2,1)} %get-tuple-element.41), channel_id=1, source_target_pairs={{4,8},{12,16},{20,24},{28,32},{36,40},{44,48},{52,56},{60,64},{68,... | collective-permute-start | bytes 1253384 | tf_op jit(solution)/shard_map/ppermute | solution.py:449
  72.2 5.9 %copy-start.13 = (bf16[2,544,128]{2,1,0:T(8,128)(2,1)S(1)}, bf16[2,544,128]{2,1,0:T(8,128)(2,1)}, u32[]{:S(2)}) copy-start(bf16[2,544,128]{2,1,0:T(8,128)(2,1)} %copy-done.12) | copy-start | bytes 835588
  72.3 5.9 %copy-start.16 = (bf16[2,544,128]{2,1,0:T(8,128)(2,1)S(1)}, bf16[2,544,128]{2,1,0:T(8,128)(2,1)}, u32[]{:S(2)}) copy-start(bf16[2,544,128]{2,1,0:T(8,128)(2,1)} %copy-done.15) | copy-start | bytes 835588
  78.2 1.0 copy-start.19
  79.1 1.0 copy-start.47
  95.2 16.3 %collective-permute-start.12 = (bf16[3,544,128]{2,1,0:T(8,128)(2,1)}, bf16[3,544,128]{2,1,0:T(8,128)(2,1)S(1)}, u32[]{:S(2)}, u32[]{:S(2)}) collective-permute-start(bf16[3,544,128]{2,1,0:T(8,128)(2,1)} %get-tuple-element.48), channel_id=1, source_target_pairs={{0,4},{8,12},{16,20},{24,28},{32,36},{40,44},{48,52},{56,60},{64,6... | collective-permute-start | bytes 1253384 | tf_op jit(solution)/shard_map/ppermute | solution.py:449
  100.9 10.6 %collective-permute-start.13 = (bf16[3,544,128]{2,1,0:T(8,128)(2,1)}, bf16[3,544,128]{2,1,0:T(8,128)(2,1)}, u32[]{:S(2)}, u32[]{:S(2)}) collective-permute-start(bf16[3,544,128]{2,1,0:T(8,128)(2,1)} %get-tuple-element.49), channel_id=1, source_target_pairs={{4,8},{12,16},{20,24},{28,32},{36,40},{44,48},{52,56},{60,64},{68,... | collective-permute-start | bytes 1253384 | tf_op jit(solution)/shard_map/ppermute | solution.py:449
  102.3 2.5 %copy-start.14 = (bf16[2,544,128]{2,1,0:T(8,128)(2,1)S(1)}, bf16[2,544,128]{2,1,0:T(8,128)(2,1)}, u32[]{:S(2)}) copy-start(bf16[2,544,128]{2,1,0:T(8,128)(2,1)} %copy-done.12) | copy-start | bytes 835588
  102.3 2.5 %copy-start.17 = (bf16[2,544,128]{2,1,0:T(8,128)(2,1)S(1)}, bf16[2,544,128]{2,1,0:T(8,128)(2,1)}, u32[]{:S(2)}) copy-start(bf16[2,544,128]{2,1,0:T(8,128)(2,1)} %copy-done.15) | copy-start | bytes 835588
  102.3 2.5 %copy-start.20 = (bf16[2,544,128]{2,1,0:T(8,128)(2,1)S(1)}, bf16[2,544,128]{2,1,0:T(8,128)(2,1)}, u32[]{:S(2)}) copy-start(bf16[2,544,128]{2,1,0:T(8,128)(2,1)} %copy-done.18) | copy-start | bytes 835588
  102.3 2.6 %copy-start.41 = (bf16[2,544,256]{2,1,0:T(8,128)(2,1)S(1)}, bf16[2,544,256]{2,1,0:T(8,128)(2,1)}, u32[]{:S(2)}) copy-start(bf16[2,544,256]{2,1,0:T(8,128)(2,1)} %copy-done.40) | copy-start | bytes 1671172
  102.3 2.6 %copy-start.43 = (bf16[2,544,128]{2,1,0:T(8,128)(2,1)S(1)}, bf16[2,544,128]{2,1,0:T(8,128)(2,1)}, u32[]{:S(2)}) copy-start(bf16[2,544,128]{2,1,0:T(8,128)(2,1)} %copy-done.42) | copy-start | bytes 835588
  102.3 2.6 %copy-start.50 = (bf16[4,544,128]{2,1,0:T(8,128)(2,1)S(1)}, bf16[4,544,128]{2,1,0:T(8,128)(2,1)}, u32[]{:S(2)}) copy-start(bf16[4,544,128]{2,1,0:T(8,128)(2,1)} %copy-done.49) | copy-start | bytes 1671172
  104.9 6.6 %copy-start.1 = (bf16[3,3,256,128]{2,3,1,0:T(8,128)(2,1)S(1)}, bf16[3,3,256,128]{2,3,1,0:T(8,128)(2,1)}, u32[]{:S(2)}) copy-start(bf16[3,3,256,128]{2,3,1,0:T(8,128)(2,1)} %copy.15) | copy-start | bytes 1769476
  104.9 6.6 %copy-start.37 = (f32[2,544,128]{2,1,0:T(8,128)S(1)}, f32[2,544,128]{2,1,0:T(8,128)}, u32[]{:S(2)}) copy-start(f32[2,544,128]{2,1,0:T(8,128)} %copy-done.36) | copy-start | bytes 1671172
  104.9 6.6 %copy-start.39 = (f32[2,544,128]{2,1,0:T(8,128)S(1)}, f32[2,544,128]{2,1,0:T(8,128)}, u32[]{:S(2)}) copy-start(f32[2,544,128]{2,1,0:T(8,128)} %copy-done.38) | copy-start | bytes 1671172
  104.9 6.6 %copy-start.45 = (bf16[2,544,128]{2,1,0:T(8,128)(2,1)S(1)}, bf16[2,544,128]{2,1,0:T(8,128)(2,1)}, u32[]{:S(2)}) copy-start(bf16[2,544,128]{2,1,0:T(8,128)(2,1)} %copy-done.44) | copy-start | bytes 835588
  111.5 7.6 %copy-start.9 = (bf16[2,512,256]{2,1,0:T(8,128)(2,1)S(1)}, bf16[2,512,256]{2,1,0:T(8,128)(2,1)}, u32[]{:S(2)}) copy-start(bf16[2,512,256]{2,1,0:T(8,128)(2,1)} %right.3) | copy-start | bytes 1572868
  111.5 7.6 %copy-start.11 = (bf16[2,512,256]{2,1,0:T(8,128)(2,1)S(1)}, bf16[2,512,256]{2,1,0:T(8,128)(2,1)}, u32[]{:S(2)}) copy-start(bf16[2,512,256]{2,1,0:T(8,128)(2,1)} %left.3) | copy-start | bytes 1572868
  111.6 7.6 %copy-start.22 = (bf16[2,256,256]{2,1,0:T(8,128)(2,1)S(1)}, bf16[2,256,256]{2,1,0:T(8,128)(2,1)}, u32[]{:S(2)}) copy-start(bf16[2,256,256]{2,1,0:T(8,128)(2,1)} %copy-done.21) | copy-start | bytes 786436
  111.6 7.6 %copy-start.24 = (bf16[2,256,256]{2,1,0:T(8,128)(2,1)S(1)}, bf16[2,256,256]{2,1,0:T(8,128)(2,1)}, u32[]{:S(2)}) copy-start(bf16[2,256,256]{2,1,0:T(8,128)(2,1)} %copy-done.23) | copy-start | bytes 786436
  111.6 7.6 %copy-start.30 = (f32[2,544,128]{2,1,0:T(8,128)S(1)}, f32[2,544,128]{2,1,0:T(8,128)}, u32[]{:S(2)}) copy-start(f32[2,544,128]{2,1,0:T(8,128)} %copy-done.29) | copy-start | bytes 1671172
  111.6 7.6 %copy-start.32 = (bf16[2,544,128]{2,1,0:T(8,128)(2,1)S(1)}, bf16[2,544,128]{2,1,0:T(8,128)(2,1)}, u32[]{:S(2)}) copy-start(bf16[2,544,128]{2,1,0:T(8,128)(2,1)} %copy-done.31) | copy-start | bytes 835588
  119.2 3.6 %copy-start.6 = (bf16[2,544,128]{2,1,0:T(8,128)(2,1)}, bf16[2,544,128]{2,1,0:T(8,128)(2,1)S(1)}, u32[]{:S(2)}) copy-start(bf16[2,544,128]{2,1,0:T(8,128)(2,1)S(1)} %get-tuple-element.60) | copy-start | bytes 835588
  119.2 3.5 %copy-start.5 = (bf16[2,544,128]{2,1,0:T(8,128)(2,1)S(1)}, bf16[2,544,128]{2,1,0:T(8,128)(2,1)}, u32[]{:S(2)}) copy-start(bf16[2,544,128]{2,1,0:T(8,128)(2,1)} %copy-done.4) | copy-start | bytes 835588
  122.8 5.0 %copy-start.2 = (f32[2,512,256]{2,1,0:T(8,128)}, f32[2,512,256]{2,1,0:T(8,128)S(1)}, u32[]{:S(2)}) copy-start(f32[2,512,256]{2,1,0:T(8,128)S(1)} %get-tuple-element.58) | copy-start | bytes 3145732
  122.8 5.0 %copy-start.25 = (bf16[2,192,256]{2,1,0:T(8,128)(2,1)}, bf16[2,192,256]{2,1,0:T(8,128)(2,1)S(1)}, u32[]{:S(2)}) copy-start(bf16[2,192,256]{2,1,0:T(8,128)(2,1)S(1)} %get-tuple-element.59) | copy-start | bytes 589828
  127.9 2.9 %collective-permute-start.16 = (bf16[64,64,128]{2,1,0:T(8,128)(2,1)S(1)}, bf16[64,64,128]{2,1,0:T(8,128)(2,1)}, u32[]{:S(2)}, u32[]{:S(2)}) collective-permute-start(bf16[64,64,128]{2,1,0:T(8,128)(2,1)S(1)} %dynamic-slice_bitcast_fusion), channel_id=1, source_target_pairs={{0,1},{1,0},{2,3},{3,2},{4,5},{5,4},{6,7},{7,6},{8,9},{9,8},{10,11... | collective-permute-start | bytes 3145736 | tf_op jit(solution)/shard_map/ppermute | solution.py:460
  166.6 24.7 %copy-start.26 = (bf16[2,192,256]{2,1,0:T(8,128)(2,1)S(1)}, bf16[2,192,256]{2,1,0:T(8,128)(2,1)}, u32[]{:S(2)}) copy-start(bf16[2,192,256]{2,1,0:T(8,128)(2,1)} %copy-done.25) | copy-start | bytes 589828
  166.6 27.5 %copy-start.3 = (f32[2,512,256]{2,1,0:T(8,128)S(1)}, f32[2,512,256]{2,1,0:T(8,128)}, u32[]{:S(2)}) copy-start(f32[2,512,256]{2,1,0:T(8,128)} %copy-done.2) | copy-start | bytes 3145732
  166.6 27.6 %copy-start.7 = (bf16[2,544,128]{2,1,0:T(8,128)(2,1)S(1)}, bf16[2,544,128]{2,1,0:T(8,128)(2,1)}, u32[]{:S(2)}) copy-start(bf16[2,544,128]{2,1,0:T(8,128)(2,1)} %copy-done.6) | copy-start | bytes 835588
  187.8 12.9 %collective-permute-start.17 = (bf16[64,64,128]{2,1,0:T(8,128)(2,1)S(1)}, bf16[64,64,128]{2,1,0:T(8,128)(2,1)}, u32[]{:S(2)}, u32[]{:S(2)}) collective-permute-start(bf16[64,64,128]{2,1,0:T(8,128)(2,1)S(1)} %all_to_all.11), channel_id=1, source_target_pairs={{0,1},{1,0},{2,3},{3,2},{4,5},{5,4},{6,7},{7,6},{8,9},{9,8},{10,11... | collective-permute-start | bytes 3145736 | tf_op jit(solution)/shard_map/ppermute | solution.py:466
  191.3 8.5 %collective-permute-start.14 = (bf16[2,192,256]{2,1,0:T(8,128)(2,1)S(1)}, bf16[2,192,256]{2,1,0:T(8,128)(2,1)S(1)}, u32[]{:S(2)}, u32[]{:S(2)}) collective-permute-start(bf16[2,192,256]{2,1,0:T(8,128)(2,1)S(1)} %copy-done.26), channel_id=1, source_target_pairs={{1,2},{2,1},{5,6},{6,5},{9,10},{10,9},{13,14},{14,13},{17,18},{18,... | collective-permute-start | bytes 589832 | tf_op jit(solution)/shard_map/ppermute | solution.py:444
  194.1 5.7 %collective-permute-start.15 = (bf16[2,192,256]{2,1,0:T(8,128)(2,1)S(1)}, bf16[2,192,256]{2,1,0:T(8,128)(2,1)S(1)}, u32[]{:S(2)}, u32[]{:S(2)}) collective-permute-start(bf16[2,192,256]{2,1,0:T(8,128)(2,1)S(1)} %copy-done.26), channel_id=1, source_target_pairs={{0,1},{2,3},{1,0},{3,2},{4,5},{6,7},{5,4},{7,6},{8,9},{10,11},{9,8... | collective-permute-start | bytes 589832 | tf_op jit(solution)/shard_map/ppermute | solution.py:444
  (7 other events, 5.4 us)
where the time goes:
time: 207 us; the launch traced here: 206 us
  Pallas kernels  59.8 us (29%)
  blocking collectives  54.9 us (27%)
  starting transfers between devices  40.6 us (20%)
  waiting for transfers between devices  21.2 us (10%)
  local copies, waits for them, and re-layouts  19.9 us (10%)
  other arithmetic  7.84 us (4%)
    pallas_call x9, Pallas kernels, kernel_call(): pl.pallas_call(body, out_shape=outs, in_specs=[SMEM] * scalars + [VMEM] *...  59.8 us
    all_to_all x1, blocking collectives, summed_everywhere(): lax.all_to_all(half, axes, 0, 0, tiled=True, axis_index_groups=groups)  33.8 us
    ppermute x12, starting transfers between devices, exchanged(): return (lax.ppermute(value, axis, first), lax.ppermute(value, axis, second))  23 us
    all_to_all x1, blocking collectives, summed_everywhere(): lax.all_to_all(spread, axes, 0, 0, tiled=True, axis_index_groups=groups)  21.1 us
    ppermute x12, waiting for transfers between devices, exchanged(): return (lax.ppermute(value, axis, first), lax.ppermute(value, axis, second))  14.9 us
    unnamed x106, local copies, waits for them, and re-layouts  11.3 us
    ppermute x2, starting transfers between devices, exchanged_pair(): lax.ppermute(value_a, axis, first)  11.2 us
  transfers between devices with their start and end apart: 18, of which 6 were waited for; matrix products, arithmetic and copies ran while one was open for 3% of the time, Pallas kernels for 6%

commit v1 on v0

--- a/solution.py
+++ b/solution.py
@@ -13,7 +13,7 @@
 TAPS = 2 * RADIUS + 1
 HALO = 16
 LANES = 128
-CHUNK_ROWS = 64
+CHUNK_ROWS = 56
 
 BF16 = jnp.bfloat16
 F32 = jnp.float32
@@ -40,16 +40,15 @@
 
 
 def kernel_call(body, outs, ins, scalars, scratch, flops):
-    bytes_moved = sum(x.size * x.dtype.itemsize for x in ins) + sum(
-        math.prod(o.shape) * o.dtype.itemsize for o in outs
-    )
+    bytes_moved = sum(math.prod(x.shape) * x.dtype.itemsize for x in (*ins, *outs))
+    held = sum(math.prod(x.shape) * jnp.dtype(x.dtype).itemsize for x in scratch)
     return pl.pallas_call(
         body,
         out_shape=outs,
         in_specs=[SMEM] * scalars + [VMEM] * (len(ins) - scalars),
         out_specs=[VMEM] * len(outs),
         scratch_shapes=scratch,
-        compiler_params=pltpu.CompilerParams(vmem_limit_bytes=48 * 2**20),
+        compiler_params=pltpu.CompilerParams(vmem_limit_bytes=bytes_moved + held + 4 * 2**20),
         cost_estimate=pl.CostEstimate(flops=flops, bytes_accessed=bytes_moved, transcendentals=0),
     )(*ins)
 
@@ -83,6 +82,83 @@
     for tap in range(3):
         start = lane + tap * step
         ref[row, :, start : start + LANES] = taps[tap]
+
+
+def pack_kernel(left, right, hidden, grads, out, sems):
+    cols = left.shape[1]
+    tail = DISP + HALO
+    first, last = pl.ds(0, HALO), pl.ds(cols - HALO, HALO)
+    low, high = pl.ds(0, LANES), pl.ds(LANES, LANES)
+    every = pl.ds(0, 2 * LANES)
+    moves = (
+        (right, pl.ds(cols - tail, tail), pl.ds(0, tail), every),
+        (left, last, pl.ds(tail, HALO), every),
+        (left, first, pl.ds(tail + HALO, HALO), every),
+        (right, first, pl.ds(tail + 2 * HALO, HALO), every),
+        (hidden, last, pl.ds(tail + 3 * HALO, HALO), low),
+        (hidden, first, pl.ds(tail + 3 * HALO, HALO), high),
+        (grads, last, pl.ds(tail + 4 * HALO, HALO), low),
+        (grads, first, pl.ds(tail + 4 * HALO, HALO), high),
+    )
+    copies = [
+        pltpu.make_async_copy(source.at[:, start], out.at[:, stop, lanes], sems.at[number])
+        for number, (source, start, stop, lanes) in enumerate(moves)
+    ]
+    for copy in copies:
+        copy.start()
+    for copy in copies:
+        copy.wait()
+
+
+def packed(left, right, hidden, grads):
+    rows, cols, channels = left.shape
+    count = DISP + 6 * HALO
+    return pl.pallas_call(
+        pack_kernel,
+        out_shape=array((rows, count, channels), BF16),
+        in_specs=[pl.BlockSpec(memory_space=pltpu.HBM)] * 4,
+        out_specs=VMEM,
+        scratch_shapes=[pltpu.SemaphoreType.DMA((8,))],
+        compiler_params=pltpu.CompilerParams(vmem_limit_bytes=4 * 2**20),
+        cost_estimate=pl.CostEstimate(flops=0, bytes_accessed=4 * rows * count * channels, transcendentals=0),
+    )(left, right, hidden, grads)
+
+
+def unpack_kernel(count, scale, place, half, other, gate, cand, motion):
+    core = place[1] % 2
+    block = gate.shape[0]
+    per_half = half.shape[0] // block
+    step = pl.program_id(0)
+
+    def part(number):
+        start = pl.multiple_of((number % per_half) * block, block)
+        mine = half[pl.ds(start, block)]
+        theirs = other[pl.ds(start, block)]
+        return jnp.where(number // per_half == core, mine, theirs).astype(F32) * scale
+
+    gate[:, :LANES] = part(step)
+    gate[:, LANES:] = part(step + count)
+    cand[...] = part(step + 2 * count)
+    motion[...] = part(3 * count)[: motion.shape[0]]
+
+
+def unpacked(place, half, other, depth, feats_count, scale):
+    block = 256
+    count = depth // block
+    whole = lambda i: (0, 0)
+    return pl.pallas_call(
+        lambda *refs: unpack_kernel(count, scale, *refs),
+        grid=(count,),
+        out_shape=[array((depth, 2 * LANES), F32), array((depth, LANES), F32), array((feats_count, LANES), F32)],
+        in_specs=[SMEM, pl.BlockSpec(half.shape, whole), pl.BlockSpec(half.shape, whole)],
+        out_specs=[
+            pl.BlockSpec((block, 2 * LANES), lambda i: (i, 0)),
+            pl.BlockSpec((block, LANES), lambda i: (i, 0)),
+            pl.BlockSpec((feats_count, LANES), whole),
+        ],
+        compiler_params=pltpu.CompilerParams(vmem_limit_bytes=12 * 2**20),
+        cost_estimate=pl.CostEstimate(flops=0, bytes_accessed=6 * depth * 384, transcendentals=0),
+    )(place, half, other)
 
 
 def motion_kernel(place, disparity, offsets, left, right, got_a, got_b, weight, motion, pre, feats, ext, window, flipped):
@@ -105,7 +181,7 @@
         ext[HALO + cols : wide] = from_right[tail + HALO : tail + 2 * HALO]
         window[0:tail] = from_left[0:tail]
         window[tail : tail + cols] = right[row]
-        window[tail + cols : tail + cols + HALO] = from_right[tail + 2 * HALO :]
+        window[tail + cols : tail + cols + HALO] = from_right[tail + 2 * HALO : tail + 3 * HALO]
         window[tail + cols + HALO :] = jnp.zeros((total - tail - cols - HALO, window.shape[1]), BF16)
         parts = total // LANES
         for part in range(parts):
@@ -225,7 +301,7 @@
 
 
 def back_step(place, grad_cand, grad_a, grad_b, grad_update, hidden, hidden_a, hidden_b, reset, cand_wt, gate_wt,
-              grad_gate, cand_taps, gate_taps, inner, grad_motion, finish):
+              grad_reset, cand_taps, gate_taps, inner, grad_motion, finish):
     odd = place[0] % 2 == 1
     wide = hidden.shape[1]
     block = wide // 2
@@ -256,8 +332,7 @@
         store_taps(gate_taps, row, 0, 2 * LANES, updates[row].astype(F32), False)
         store_taps(gate_taps, row, LANES, 2 * LANES, value.astype(F32), False)
         if row in (1, 2):
-            grad_gate[row - 1, :, :LANES] = updates[row]
-            grad_gate[row - 1, :, LANES:] = value
+            grad_reset[row - 1] = value
     for row in range(2):
         for start in (0, block):
             here = pl.ds(start, block)
@@ -270,7 +345,7 @@
 
 def later_back_kernel(cols_axis, place, grad_cand, grad_a, grad_b, grad_update, hidden, hidden_a, hidden_b, reset,
                       cand_wt, gate_wt, update, grad_hidden, older_hidden, older_update, older_candidate,
-                      grad_gate, grad_state, grad_motion, older_cand, older_upd, send_a, send_b,
+                      grad_reset, grad_state, grad_motion, older_cand, older_upd, send_a, send_b,
                       cand_taps, gate_taps, inner):
     odd = place[0] % 2 == 1
     wide = hidden.shape[1]
@@ -286,20 +361,22 @@
                       older_hidden[row, here].astype(F32), row, here, older_cand, older_upd, send_a, send_b)
 
     back_step(place, grad_cand, grad_a, grad_b, grad_update, hidden, hidden_a, hidden_b, reset, cand_wt, gate_wt,
-              grad_gate, cand_taps, gate_taps, inner, grad_motion, finish)
+              grad_reset, cand_taps, gate_taps, inner, grad_motion, finish)
 
 
 def first_back_kernel(place, grad_cand, grad_a, grad_b, grad_update, hidden, hidden_a, hidden_b, reset,
                       cand_wt, gate_wt, update, grad_state, motion_so_far,
-                      grad_gate, grad_first, grad_motion, cand_taps, gate_taps, inner):
+                      grad_reset, grad_first, grad_motion, cand_taps, gate_taps, inner):
     def finish(row, start, here, terms):
         gate = update[row + 1, here]
         grad = grad_state[row, here] * (1.0 - gate) + terms
-        grad_first[row, here] = grad.astype(BF16)
+        skip = HALO if start == 0 else 0
+        count = grad.shape[0] - HALO
+        grad_first[row, (start + skip) - HALO : (start + skip) - HALO + count] = grad[skip : skip + count].astype(BF16)
         grad_motion[row, here] += motion_so_far[row, here]
 
     back_step(place, grad_cand, grad_a, grad_b, grad_update, hidden, hidden_a, hidden_b, reset, cand_wt, gate_wt,
-              grad_gate, cand_taps, gate_taps, inner, grad_motion, finish)
+              grad_reset, cand_taps, gate_taps, inner, grad_motion, finish)
 
 
 def load_pixels(odd, pixels, hiddens, motion, motion_a, motion_b):
@@ -341,59 +418,87 @@
     return (above, hidden[0], hidden[1], below)
 
 
-def cand_weights_kernel(place, resets, motion, motion_a, motion_b, grads, out, pixels, taps):
-    odd = place[0] % 2 == 1
-    load_pixels(odd, pixels, [resets[row] for row in range(4)], motion, motion_a, motion_b)
-    load_grads(taps, grads)
-
-    def finish(start, value):
-        out[pl.ds(start, 2 * LANES)] = value
-
-    weight_products(pixels, taps, motion.shape[1], LANES, finish)
-
-
-def middle_weights_kernel(place, resets, hidden, hidden_a, hidden_b, motion, motion_a, motion_b, cand_grads, gate_grads,
-                          so_far, cand_out, gate_out, pixels, cand_taps, gate_taps):
+def load_hidden(pixels, rows, wide):
+    for row, value in enumerate(rows):
+        pixels[row * wide : (row + 1) * wide, :LANES] = value
+
+
+def second_weights_kernel(place, resets, hidden, hidden_a, hidden_b, motion, motion_a, motion_b, cand_grads, update_grads,
+                          cand_out, update_out, pixels, taps):
     odd = place[0] % 2 == 1
     wide = motion.shape[1]
     load_pixels(odd, pixels, [resets[row] for row in range(4)], motion, motion_a, motion_b)
-    load_grads(cand_taps, cand_grads)
-    load_grads(gate_taps, gate_grads)
+    load_grads(taps, cand_grads)
+
+    def cand_finish(start, value):
+        cand_out[pl.ds(start, 2 * LANES)] = value
+
+    def update_finish(start, value):
+        update_out[pl.ds(start, 2 * LANES)] = value
+
+    weight_products(pixels, taps, wide, LANES, cand_finish)
+    load_hidden(pixels, hidden_rows(odd, hidden, hidden_a, hidden_b), wide)
+    load_grads(taps, update_grads)
+    weight_products(pixels, taps, wide, LANES, update_finish)
+
+
+def first_weights_kernel(place, resets, older, older_a, older_b, hidden, hidden_a, hidden_b, motion, motion_a, motion_b,
+                         cand_grads, update_grads, reset_grads, cand_sum, update_sum,
+                         cand_out, update_out, reset_out, pixels, taps):
+    odd = place[0] % 2 == 1
+    wide = motion.shape[1]
+    load_pixels(odd, pixels, [resets[row] for row in range(4)], motion, motion_a, motion_b)
+    load_grads(taps, cand_grads)
 
     def cand_finish(start, value):
         here = pl.ds(start, 2 * LANES)
-        cand_out[here] = so_far[here] + value
-
-    weight_products(pixels, cand_taps, wide, LANES, cand_finish)
-    for row, value in enumerate(hidden_rows(odd, hidden, hidden_a, hidden_b)):
-        pixels[row * wide : (row + 1) * wide, :LANES] = value
-
-    def gate_finish(start, value):
+        cand_out[here] = cand_sum[here] + value
+
+    def update_finish(start, value):
         here = pl.ds(start, 2 * LANES)
-        for half in range(2):
-            gate_out[half, here] = value[:, half * LANES : (half + 1) * LANES]
-
-    weight_products(pixels, gate_taps, wide, 2 * LANES, gate_finish)
-
-
-def last_weights_kernel(place, hidden, hidden_a, hidden_b, motion, motion_a, motion_b, gate_grads, gate_so_far, cand,
-                        motion_w, out, pixels, taps):
+        update_out[here] = update_sum[here] + value
+
+    def reset_finish(start, value):
+        reset_out[pl.ds(start, 2 * LANES)] = value
+
+    weight_products(pixels, taps, wide, LANES, cand_finish)
+    load_hidden(pixels, hidden_rows(odd, older, older_a, older_b), wide)
+    load_grads(taps, update_grads)
+    weight_products(pixels, taps, wide, LANES, update_finish)
+    load_hidden(pixels, hidden_rows(odd, hidden, hidden_a, hidden_b), wide)
+    load_grads(taps, reset_grads)
+    weight_products(pixels, taps, wide, LANES, reset_finish)
+
+
+def last_weights_kernel(place, hidden, hidden_a, hidden_b, motion, motion_a, motion_b, reset_grads, reset_sum,
+                        update_sum, cand_sum, motion_w, kept, given, pixels, taps, parts):
     odd = place[0] % 2 == 1
     load_pixels(odd, pixels, hidden_rows(odd, hidden, hidden_a, hidden_b), motion, motion_a, motion_b)
-    load_grads(taps, gate_grads)
-    rows = cand.shape[0]
+    load_grads(taps, reset_grads)
+    rows = cand_sum.shape[0]
 
     def finish(start, value):
-        here = pl.ds(start, 2 * LANES)
-        for half in range(2):
-            there = pl.ds(pl.multiple_of(half * rows + start, LANES), 2 * LANES)
-            part = value[:, half * LANES : (half + 1) * LANES] + gate_so_far[half, here]
-            out[there] = part.astype(BF16)
-
-    weight_products(pixels, taps, motion.shape[1], 2 * LANES, finish)
-    out[2 * rows : 3 * rows] = cand[...].astype(BF16)
-    out[3 * rows : 3 * rows + LANES] = motion_w[...].astype(BF16)
-    out[3 * rows + LANES :] = jnp.zeros((out.shape[0] - 3 * rows - LANES, LANES), BF16)
+        there = pl.ds(pl.multiple_of(rows + start, LANES), 2 * LANES)
+        parts[there] = (value + reset_sum[pl.ds(start, 2 * LANES)]).astype(BF16)
+
+    weight_products(pixels, taps, motion.shape[1], LANES, finish)
+    parts[0:rows] = update_sum[...].astype(BF16)
+    parts[2 * rows : 3 * rows] = cand_sum[...].astype(BF16)
+    parts[3 * rows : 3 * rows + LANES] = motion_w[...].astype(BF16)
+    parts[3 * rows + LANES :] = jnp.zeros((parts.shape[0] - 3 * rows - LANES, LANES), BF16)
+    half = parts.shape[0] // 2
+    core = place[1] % 2
+    kept[...] = parts[pl.ds(pl.multiple_of(core * half, LANES), half)]
+    given[...] = parts[pl.ds(pl.multiple_of((1 - core) * half, LANES), half)]
+
+
+def right_kernel(place, own, back_a, back_b, grad_right):
+    odd = place[1] % 2 == 1
+    split = own.shape[1] - DISP
+    for row in range(2):
+        grad_right[row, :split] = own[row, :split].astype(BF16)
+        returned = sides(odd, back_a[row], back_b[row])[1].astype(F32)
+        grad_right[row, split:] = (own[row, split:] + returned).astype(BF16)
 
 
 def band_back_kernel(place, disparity, offsets, left, right, got_a, got_b, weight, grad_motion, pre, feats,
@@ -449,24 +554,20 @@
     return lax.ppermute(value_a, axis, first), lax.ppermute(value_b, axis, second)
 
 
-def summed_everywhere(parts, cols_index, axes):
+def summed_everywhere(kept, given, axes, meanwhile):
     cols_count = lax.axis_size("cols")
     devices = lax.axis_size("rows") * cols_count
-    core = cols_index % 2
     swap = [(i, i ^ 1) for i in range(cols_count)]
     groups = [[i for i in range(devices) if i % 2 == c] for c in range(2)]
-    kept = lax.dynamic_index_in_dim(parts, core, 0, keepdims=False)
-    given = lax.dynamic_index_in_dim(parts, 1 - core, 0, keepdims=False)
     got = lax.ppermute(given, "cols", swap)
-    half = (kept.astype(F32) + got.astype(F32)).astype(BF16)
+    got, meanwhile = lax.optimization_barrier((got, meanwhile))
+    half = (kept.astype(F32) + got.astype(F32)).astype(BF16).reshape(devices // 2, -1, LANES)
     pieces = lax.all_to_all(half, axes, 0, 0, tiled=True, axis_index_groups=groups)
     piece = jnp.sum(pieces.astype(F32), axis=0).astype(BF16)
     spread = jnp.broadcast_to(piece[None], pieces.shape)
     half = lax.all_to_all(spread, axes, 0, 0, tiled=True, axis_index_groups=groups)
     other = lax.ppermute(half, "cols", swap)
-    first = jnp.where(core == 0, half, other)
-    second = jnp.where(core == 0, other, half)
-    return jnp.stack([first, second])
+    return half.reshape(-1, LANES), other.reshape(-1, LANES), meanwhile
 
 
 def on_device(
@@ -489,29 +590,22 @@
     place = jnp.stack([rows_index, cols_index]).astype(jnp.int32)
     odd_col = cols_index % 2 == 1
 
-    maps = jnp.concatenate(
-        [fmap_right[:, cols - DISP - HALO :], fmap_left[:, cols - HALO :], fmap_left[:, :HALO], fmap_right[:, :HALO]],
-        axis=1,
-    )
-    states = jnp.concatenate(
-        [hidden_init[:, cols - HALO :], hidden_init[:, :HALO], grad_hidden[:, cols - HALO :], grad_hidden[:, :HALO]],
-        axis=1,
-    )
-    states_a, states_b = exchanged(states, "cols")
-    maps_a, maps_b = exchanged(maps, "cols")
-    state_left = jnp.where(odd_col, states_a, states_b)
-    state_right = jnp.where(odd_col, states_b, states_a)
-    hidden = jnp.concatenate(
-        [state_left[:, :HALO], hidden_init, state_right[:, HALO : 2 * HALO]], axis=1
-    )
-    grads = jnp.concatenate(
-        [state_left[:, 2 * HALO : 3 * HALO], grad_hidden, state_right[:, 3 * HALO :]], axis=1
-    )
-    hidden_a, hidden_b = exchanged(hidden, "rows")
+    halos = packed(fmap_left, fmap_right, hidden_init, grad_hidden)
+    maps_a, maps_b = exchanged(halos, "cols")
+    init_a, init_b = exchanged(hidden_init, "rows")
+    base = DISP + 4 * HALO
+    from_left = jnp.where(odd_col, maps_a[:, base:], maps_b[:, base:])
+    from_right = jnp.where(odd_col, maps_b[:, base:], maps_a[:, base:])
+    edges = jnp.concatenate([from_left[:, :HALO, :state], from_right[:, :HALO, state:]], axis=1)
+    hidden = jnp.concatenate([edges[:, :HALO], hidden_init, edges[:, HALO:]], axis=1)
+    grads = jnp.concatenate([from_left[:, HALO:, :state], grad_hidden, from_right[:, HALO:, state:]], axis=1)
 
     motion_w = jnp.pad(motion_weight, ((0, LANES - feats_count), (0, 0)))
     gate_wt = jnp.transpose(gate_weight.reshape(3, 3, 2 * state, 2 * state), (0, 1, 3, 2)).reshape(-1, 2 * state)
     cand_wt = jnp.transpose(cand_weight.reshape(3, 3, 2 * state, state), (0, 1, 3, 2)).reshape(-1, 2 * state)
+    motion_w, gate_wt, cand_wt, init_a, init_b, edges, hidden, grads = lax.optimization_barrier(
+        (motion_w, gate_wt, cand_wt, init_a, init_b, edges, hidden, grads)
+    )
 
     field = lambda count, dtype: array((count, wide, LANES), dtype)
     band_flops = 2 * rows * wide * 512 * channels
@@ -523,7 +617,13 @@
         [pltpu.VMEM((wide, channels), BF16), pltpu.VMEM((768, channels), BF16), pltpu.VMEM((832, channels), BF16)],
         2 * band_flops,
     )
-    motion_a, motion_b = exchanged(motion, "rows")
+    sent = jnp.concatenate([motion, edges], axis=1)
+    sent_a, sent_b = exchanged(sent, "rows")
+    motion_a, motion_b = sent_a[:, :wide], sent_b[:, :wide]
+    with_edges = lambda inner, got: jnp.concatenate(
+        [got[:, wide : wide + HALO], inner, got[:, wide + HALO :]], axis=1
+    )
+    hidden_a, hidden_b = with_edges(init_a, sent_a), with_edges(init_b, sent_b)
     motions = (motion, motion_a, motion_b)
     unit = 2 * wide * 9 * 2 * state * state
     fields = [pltpu.VMEM((6, wide, 6 * LANES), BF16), pltpu.VMEM((4, wide, 6 * LANES), BF16)]
@@ -547,24 +647,25 @@
     )
     got_a, got_b = exchanged_pair(send_a, send_b, "rows")
     pixels = pltpu.VMEM((4 * wide, 2 * LANES), BF16)
-    cand_taps = pltpu.VMEM((2 * wide, 3 * LANES), BF16)
-    gate_taps = pltpu.VMEM((2 * wide, 6 * LANES), BF16)
-    (cand_sum_1,) = kernel_call(
-        cand_weights_kernel,
-        [array(cand_weight.shape, F32)],
-        [place, reset_hidden_1, *motions, grad_cand_1],
+    taps = pltpu.VMEM((2 * wide, 3 * LANES), BF16)
+    weights = array(cand_weight.shape, F32)
+    cand_sum, update_sum = kernel_call(
+        second_weights_kernel,
+        [weights, weights],
+        [place, reset_hidden_1, hidden_1, hidden_1a, hidden_1b, *motions, grad_cand_1, grad_update_1],
         1,
-        [pixels, cand_taps],
-        2 * unit,
-    )
+        [pixels, taps],
+        4 * unit,
+    )
+    got_a, got_b, cand_sum, update_sum = lax.optimization_barrier((got_a, got_b, cand_sum, update_sum))
     back_scratch = [
         pltpu.VMEM((6, wide, 3 * LANES), BF16),
         pltpu.VMEM((4, wide, 6 * LANES), BF16),
         pltpu.VMEM((4, wide, LANES), F32),
     ]
-    grad_gate_1, grad_state, grad_motion_1, grad_cand_0, grad_update_0, send_a, send_b = kernel_call(
+    grad_reset_1, grad_state, grad_motion_1, grad_cand_0, grad_update_0, send_a, send_b = kernel_call(
         lambda *refs: later_back_kernel(cols_axis, *refs),
-        [array((2, wide, 2 * LANES), BF16), field(2, F32), field(2, F32), field(2, BF16), field(2, BF16),
+        [field(2, BF16), field(2, F32), field(2, F32), field(2, BF16), field(2, BF16),
          field(3, BF16), field(3, BF16)],
         [place, grad_cand_1, got_a, got_b, grad_update_1, hidden_1, hidden_1a, hidden_1b, reset_1, cand_wt, gate_wt,
          update_1, grads, hidden, update_0, candidate_0],
@@ -573,17 +674,21 @@
         8 * unit,
     )
     got_a, got_b = exchanged_pair(send_a, send_b, "rows")
-    cand_sum, gate_sum_1 = kernel_call(
-        middle_weights_kernel,
-        [array(cand_weight.shape, F32), array((2,) + cand_weight.shape, F32)],
-        [place, reset_hidden_0, hidden_1, hidden_1a, hidden_1b, *motions, grad_cand_0, grad_gate_1, cand_sum_1],
+    cand_sum, update_sum, reset_sum = kernel_call(
+        first_weights_kernel,
+        [weights, weights, weights],
+        [place, reset_hidden_0, hidden, hidden_a, hidden_b, hidden_1, hidden_1a, hidden_1b, *motions,
+         grad_cand_0, grad_update_0, grad_reset_1, cand_sum, update_sum],
         1,
-        [pixels, cand_taps, gate_taps],
+        [pixels, taps],
         6 * unit,
     )
-    grad_gate_0, grad_first, grad_motion = kernel_call(
+    got_a, got_b, cand_sum, update_sum, reset_sum = lax.optimization_barrier(
+        (got_a, got_b, cand_sum, update_sum, reset_sum)
+    )
+    grad_reset_0, grad_first, grad_motion = kernel_call(
         first_back_kernel,
-        [array((2, wide, 2 * LANES), BF16), field(2, BF16), field(2, F32)],
+        [field(2, BF16), array((2, cols, LANES), BF16), field(2, F32)],
         [place, grad_cand_0, got_a, got_b, grad_update_0, hidden, hidden_a, hidden_b, reset_0, cand_wt, gate_wt,
          update_0, grad_state, grad_motion_1],
         1,
@@ -601,32 +706,26 @@
     )
     back_a, back_b = exchanged(back, "cols")
     devices = rows_axis * cols_axis
-    (parts,) = kernel_call(
+    total = devices * CHUNK_ROWS
+    kept, given = kernel_call(
         last_weights_kernel,
-        [array((devices * CHUNK_ROWS, LANES), BF16)],
-        [place, hidden, hidden_a, hidden_b, *motions, grad_gate_0, gate_sum_1, cand_sum, motion_sum],
+        [array((total // 2, LANES), BF16), array((total // 2, LANES), BF16)],
+        [place, hidden, hidden_a, hidden_b, *motions, grad_reset_0, reset_sum, update_sum, cand_sum, motion_sum],
         1,
-        [pixels, gate_taps],
-        4 * unit,
-    )
-    sums = summed_everywhere(
-        parts.reshape(2, devices // 2, CHUNK_ROWS, LANES), cols_index, ("rows", "cols")
-    ).reshape(devices * CHUNK_ROWS, LANES)
-    returned = jnp.where(odd_col, back_b, back_a).astype(F32)
-    grad_right = jnp.concatenate(
-        [own[:, : cols - DISP], own[:, cols - DISP :] + returned], axis=1
-    ).astype(BF16)
+        [pixels, taps, pltpu.VMEM((total, LANES), BF16)],
+        2 * unit,
+    )
+    (grad_right,) = kernel_call(
+        right_kernel, [array((2, cols, channels), BF16)], [place, own, back_a, back_b], 1, [], 0
+    )
+    half, other, (grad_left, grad_right, grad_first) = summed_everywhere(
+        kept, given, ("rows", "cols"), (grad_left, grad_right, grad_first)
+    )
     normaliser = 1.0 / math.sqrt(rows * rows_axis * cols * cols_axis)
-    depth = cand_weight.shape[0]
-    scaled = lambda start, count: sums[start : start + count].astype(F32) * normaliser
-    return (
-        grad_left,
-        grad_right,
-        grad_first[:, HALO : HALO + cols],
-        scaled(3 * depth, feats_count),
-        jnp.concatenate([scaled(0, depth), scaled(depth, depth)], axis=1),
-        scaled(2 * depth, depth),
-    )
+    grad_gate_w, grad_cand_w, grad_motion_w = unpacked(
+        place, half, other, cand_weight.shape[0], feats_count, normaliser
+    )
+    return (grad_left, grad_right, grad_first, grad_motion_w, grad_gate_w, grad_cand_w)
 
 
 def solution(mesh):

time: 207 us -> 185 us (0.89)
  local copies, waits for them, and re-layouts: 19.9 us -> 5.16 us
  blocking collectives: 54.9 us -> 49.8 us
  other arithmetic: 7.84 us -> 4.27 us
  starting transfers between devices: 40.6 us -> 43.8 us
    unnamed x106 -> x25, local copies, waits for them, and re-layouts: 11.3 us -> 3.19 us
    pallas_call x0 -> x2, Pallas kernels: none -> 5.54 us  [the longest x1 4.56 us: unpacked(): pl.pallas_call(lambda *refs: unpack_kernel(count, scale, *refs), grid=(co...]
    pallas_call x9 -> x10, Pallas kernels: 59.8 us -> 54.6 us  [kernel_call(): pl.pallas_call(body, out_shape=outs, in_specs=[SMEM] * scalars + [VMEM] *...]
    ppermute x1, starting transfers between devices: 0.09 us -> 4.44 us  [summed_everywhere(): got = lax.ppermute(given, 'cols', swap)]
    slice x8 -> x5, local copies, waits for them, and re-layouts: 4.04 us -> 0.05 us  [the longest x2 0.04 us: on_device(): motion_a, motion_b = (sent_a[:, :wide], sent_b[:, :wide])]
    all_to_all x1, blocking collectives: 33.8 us -> 30.1 us  [summed_everywhere(): lax.all_to_all(half, axes, 0, 0, tiled=True, axis_index_groups=groups)]
    ppermute x2, starting transfers between devices: 11.2 us -> 7.89 us  [exchanged_pair(): lax.ppermute(value_a, axis, first)]
    ppermute x1, waiting for transfers between devices: 2.77 us -> 0.01 us  [summed_everywhere(): got = lax.ppermute(given, 'cols', swap)]
  transfers between devices with their start and end apart: 18 -> 16, of which waited for: 6 -> 6; matrix products, arithmetic and copies ran while one was open for 3% -> 3% of each run, Pallas kernels for 6% -> 6%
where the time goes in v1:
time: 185 us; the launch traced here: 184 us
  Pallas kernels  60.1 us (32%)
  blocking collectives  49.8 us (27%)
  starting transfers between devices  43.8 us (24%)
  waiting for transfers between devices  20.4 us (11%)
  local copies, waits for them, and re-layouts  5.16 us (3%)
  other arithmetic  4.27 us (2%)
    pallas_call x10, Pallas kernels, kernel_call(): pl.pallas_call(body, out_shape=outs, in_specs=[SMEM] * scalars + [VMEM] *...  54.6 us
    all_to_all x1, blocking collectives, summed_everywhere(): lax.all_to_all(half, axes, 0, 0, tiled=True, axis_index_groups=groups)  30.1 us
    ppermute x10, starting transfers between devices, exchanged(): return (lax.ppermute(value, axis, first), lax.ppermute(value, axis, second))  25.7 us
    all_to_all x1, blocking collectives, summed_everywhere(): lax.all_to_all(spread, axes, 0, 0, tiled=True, axis_index_groups=groups)  19.7 us
    ppermute x10, waiting for transfers between devices, exchanged(): return (lax.ppermute(value, axis, first), lax.ppermute(value, axis, second))  16.4 us
    ppermute x2, starting transfers between devices, exchanged_pair(): lax.ppermute(value_a, axis, first)  7.89 us
    pallas_call x1, Pallas kernels, unpacked(): pl.pallas_call(lambda *refs: unpack_kernel(count, scale, *refs), grid=(co...  4.56 us
    ppermute x1, starting transfers between devices, summed_everywhere(): got = lax.ppermute(given, 'cols', swap)  4.44 us
  transfers between devices with their start and end apart: 16, of which 6 were waited for; matrix products, arithmetic and copies ran while one was open for 3% of the time, Pallas kernels for 6%

profile of v1, /device:TPU:1, one launch (start us, length us, event | category | flops | bytes accessed | tf_op | source)
XLA Modules:
  0.0 184.5 jit_solution(10873446907227987217)
XLA Ops:
  0.6 0.0 copy-start.1
  0.7 1.0 copy-done.1
  1.7 1.0 copy-done.5
  2.7 1.0 copy-done.7
  3.8 1.0 shard_map.136
  4.8 6.0 %collective-permute-start.3 = (bf16[2,288,256]{2,1,0:T(8,128)(2,1)S(1)}, bf16[2,288,256]{2,1,0:T(8,128)(2,1)}, u32[]{:S(2)}, u32[]{:S(2)}) collective-permute-start(bf16[2,288,256]{2,1,0:T(8,128)(2,1)S(1)} %shard_map.136), channel_id=1, source_target_pairs={{1,2},{2,1},{5,6},{6,5},{9,10},{10,9},{13,14},{14,13},{17,18},{18,... | collective-permute-start | bytes 884744 | tf_op jit(solution)/shard_map/ppermute | solution.py:549
  10.8 0.1 collective-permute-start.2
  10.9 1.4 collective-permute-start.1
  12.3 3.9 %collective-permute-start = (bf16[2,512,128]{2,1,0:T(8,128)(2,1)}, bf16[2,512,128]{2,1,0:T(8,128)(2,1)}, u32[]{:S(2)}, u32[]{:S(2)}) collective-permute-start(bf16[2,512,128]{2,1,0:T(8,128)(2,1)} %hidden.1), channel_id=1, source_target_pairs={{0,4},{8,12},{16,20},{24,28},{32,36},{40,44},{48,52},{56,60},{64,6... | collective-permute-start | bytes 786440 | tf_op jit(solution)/shard_map/ppermute | solution.py:549
  16.2 1.1 copy.16
  17.3 0.7 copy.15
  18.0 0.0 copy-start.6
  18.0 0.0 copy-start.8
  18.0 0.0 copy-start.9
  18.0 0.0 copy-start.10
  18.1 0.1 pad_add_fusion.place.refs_0_
  18.1 0.0 collective-permute-done.3.got_b
  18.1 0.0 collective-permute-done.2.got_a
  18.1 0.9 broadcast_select_fusion.1
  19.0 1.0 pad_maximum_fusion.refs_1_.refs_13_.older.hidden
  20.0 0.0 collective-permute-done.1
  20.0 2.4 %collective-permute-done = bf16[2,512,128]{2,1,0:T(8,128)(2,1)} collective-permute-done((bf16[2,512,128]{2,1,0:T(8,128)(2,1)}, bf16[2,512,128]{2,1,0:T(8,128)(2,1)}, u32[]{:S(2)}, u32[]{:S(2)}) %collective-permute-start) | collective-permute-done | bytes 262176 | tf_op jit(solution)/shard_map/ppermute | solution.py:549
  22.4 4.5 %shard_map.137 = (bf16[2,544,128]{2,1,0:T(8,128)(2,1)S(1)}, f32[2,544,128]{2,1,0:T(8,128)S(1)}, bf16[2,544,128]{2,1,0:T(8,128)(2,1)S(1)}) custom-call(s32[2]{0:T(128)S(1)} %pad_add_fusion.place.refs_0_, s32[2]{0:T(128)S(1)} %copy-done.10, s32[2,4]{1,0:T(2,128)S(1)} %copy-done.9, bf16[2,512,256]{2,1,0:T(8,128)(2,1)S(1)} %copy-done.6, ...), custom_call_target="tpu_custom_call" | custom-call | flops 570425344 | bytes 2785328 | tf_op jit(solution)/shard_map/pallas_call | solution.py:45
  27.0 0.7 collective-permute-start.5
  27.7 2.7 %collective-permute-start.4 = (bf16[2,576,128]{2,1,0:T(8,128)(2,1)S(1)}, bf16[2,576,128]{2,1,0:T(8,128)(2,1)S(1)}, u32[]{:S(2)}, u32[]{:S(2)}) collective-permute-start(bf16[2,576,128]{2,1,0:T(8,128)(2,1)S(1)} %constant_dynamic-update-slice_fusion), channel_id=1, source_target_pairs={{0,4},{8,12},{16,20},{24,28},{32,36},{40,44},{48,52},{56,60},{64,6... | collective-permute-start | bytes 884744 | tf_op jit(solution)/shard_map/ppermute | solution.py:549
  30.4 0.0 collective-permute-done.5
  30.4 1.0 pad_maximum_fusion.3.refs_3_.older_b.hidden_b
  31.3 4.6 %collective-permute-done.4 = bf16[2,576,128]{2,1,0:T(8,128)(2,1)S(1)} collective-permute-done((bf16[2,576,128]{2,1,0:T(8,128)(2,1)S(1)}, bf16[2,576,128]{2,1,0:T(8,128)(2,1)S(1)}, u32[]{:S(2)}, u32[]{:S(2)}) %collective-permute-start.4) | collective-permute-done | bytes 294944 | tf_op jit(solution)/shard_map/ppermute | solution.py:549
  36.0 1.0 pad_maximum_fusion.2.refs_2_.older_a.hidden_a
  37.0 7.3 %shard_map.138 = (bf16[2,544,128]{2,1,0:T(8,128)(2,1)S(1)}, f32[4,544,128]{2,1,0:T(8,128)S(1)}, f32[4,544,128]{2,1,0:T(8,128)S(1)}, bf16[4,544,128]{2,1,0:T(8,128)(2,1)S(1)}, f32[2,544,128]{2,1,0:T(8,128)S(1)}) custom-call(s32[2]{0:T(128)S(1)} %pad_add_fusion.place.refs_0_, bf16[2,544,128]{2,1,0:T(8,128)(2,1)S(1)} %pad_maximum_fusion.refs_1_.refs_13_.older.hidden, ...), custom_call_target="tpu_custom_call" | custom-call | flops 3208642560 | bytes 7061512 | tf_op jit(solution)/shard_map/pallas_call | solution.py:45
  44.3 0.7 collective-permute-start.7
  45.0 6.7 %collective-permute-start.6 = (bf16[2,544,128]{2,1,0:T(8,128)(2,1)S(1)}, bf16[2,544,128]{2,1,0:T(8,128)(2,1)S(1)}, u32[]{:S(2)}, u32[]{:S(2)}) collective-permute-start(bf16[2,544,128]{2,1,0:T(8,128)(2,1)S(1)} %get-tuple-element.72.hidden.refs_5_), channel_id=1, source_target_pairs={{0,4},{8,12},{16,20},{24,28},{32,36},{40,44},{48,52},{56,60},{64,6... | collective-permute-start | bytes 835592 | tf_op jit(solution)/shard_map/ppermute | solution.py:549
  51.7 0.0 collective-permute-done.7.hidden_b.refs_7_
  51.7 4.5 %collective-permute-done.6.hidden_a.refs_6_ = bf16[2,544,128]{2,1,0:T(8,128)(2,1)S(1)} collective-permute-done((bf16[2,544,128]{2,1,0:T(8,128)(2,1)S(1)}, bf16[2,544,128]{2,1,0:T(8,128)(2,1)S(1)}, u32[]{:S(2)}, u32[]{:S(2)}) %collective-permute-start.6) | collective-permute-done | bytes 278560 | tf_op jit(solution)/shard_map/ppermute | solution.py:549
  56.2 9.3 %shard_map.139 = (f32[4,544,128]{2,1,0:T(8,128)S(1)}, f32[4,544,128]{2,1,0:T(8,128)S(1)}, bf16[4,544,128]{2,1,0:T(8,128)(2,1)S(1)}, bf16[2,544,128]{2,1,0:T(8,12...) custom-call(s32[2]{0:T(128)S(1)} %pad_add_fusion.place.refs_0_, ...), custom_call_target="tpu_custom_call" | custom-call | flops 3208642560 | bytes 7897096 | tf_op jit(solution)/shard_map/pallas_call | solution.py:45
  65.5 1.4 collective-permute-start.8
  67.0 0.7 collective-permute-start.9
  67.7 0.0 copy-start.4
  67.7 4.4 %shard_map.140 = (f32[2304,128]{1,0:T(8,128)S(1)}, f32[2304,128]{1,0:T(8,128)S(1)}) custom-call(s32[2]{0:T(128)S(1)} %pad_add_fusion.place.refs_0_, bf16[4,544,128]{2,1,0:T(8,128)(2,1)S(1)} %get-tuple-element.77.resets, bf16[2,544,128]{2,1,0:T(8,128)(2,1)S(1)} %get-tuple-element.72.hidden.refs_5_, ...), custom_call_target="tpu_custom_call" | custom-call | flops 1283457024 | bytes 5144584 | tf_op jit(solution)/shard_map/pallas_call | solution.py:45
  72.0 1.8 collective-permute-done.8.refs_2_
  73.9 8.0 %shard_map.141 = (bf16[2,544,128]{2,1,0:T(8,128)(2,1)S(1)}, f32[2,544,128]{2,1,0:T(8,128)S(1)}, f32[2,544,128]{2,1,0:T(8,128)S(1)}, bf16[2,544,128]{2,1,0:T(8,12...) custom-call(s32[2]{0:T(128)S(1)} %pad_add_fusion.place.refs_0_, ...), custom_call_target="tpu_custom_call" | custom-call | flops 2566914048 | bytes 11239432 | tf_op jit(solution)/shard_map/pallas_call | solution.py:45
  81.9 6.4 %collective-permute-start.10 = (bf16[3,544,128]{2,1,0:T(8,128)(2,1)S(1)}, bf16[3,544,128]{2,1,0:T(8,128)(2,1)S(1)}, u32[]{:S(2)}, u32[]{:S(2)}) collective-permute-start(bf16[3,544,128]{2,1,0:T(8,128)(2,1)S(1)} %get-tuple-element.90), channel_id=1, source_target_pairs={{0,4},{8,12},{16,20},{24,28},{32,36},{40,44},{48,52},{56,60},{64,6... | collective-permute-start | bytes 1253384 | tf_op jit(solution)/shard_map/ppermute | solution.py:554
  88.4 0.9 collective-permute-start.11
  89.3 6.2 %shard_map.142 = (f32[2304,128]{1,0:T(8,128)S(1)}, f32[2304,128]{1,0:T(8,128)S(1)}, f32[2304,128]{1,0:T(8,128)S(1)}) custom-call(s32[2]{0:T(128)S(1)} %pad_add_fusion.place.refs_0_, bf16[4,544,128]{2,1,0:T(8,128)(2,1)S(1)} %get-tuple-element.92.resets, bf16[2,544,128]{2,1,0:T(8,128)(2,1)S(1)} %pad_maximum_fusion.refs_1_.refs_13_.older.hidden, ...), custom_call_target="tpu_custom_call" | custom-call | flops 1925185536 | bytes 9797640 | tf_op jit(solution)/shard_map/pallas_call | solution.py:45
  95.5 0.0 collective-permute-done.10.grad_a
  95.5 0.0 collective-permute-done.11.grad_b
  95.5 6.7 %shard_map.143 = (bf16[2,544,128]{2,1,0:T(8,128)(2,1)S(1)}, bf16[2,512,128]{2,1,0:T(8,128)(2,1)}, f32[2,544,128]{2,1,0:T(8,128)S(1)}) custom-call(s32[2]{0:T(128)S(1)} %pad_add_fusion.place.refs_0_, bf16[2,544,128]{2,1,0:T(8,128)(2,1)S(1)} %get-tuple-element.89.cand_grads.grad_cand, bf16[3,544,128]{2,1,0:T(8,128)(2,1)S(1)} %collective-permute-done.10.grad_a, ...), custom_call_target="tpu_custom_call" | custom-call | flops 2566914048 | bytes 8437768 | tf_op jit(solution)/shard_map/pallas_call | solution.py:45
  102.2 4.0 %shard_map.144 = (bf16[2,512,256]{2,1,0:T(8,128)(2,1)}, bf16[2,192,256]{2,1,0:T(8,128)(2,1)S(1)}, f32[2,512,256]{2,1,0:T(8,128)S(1)}, f32[128,128]{1,0:T(8,128)S(1)}) custom-call(s32[2]{0:T(128)S(1)} %pad_add_fusion.place.refs_0_, s32[2]{0:T(128)S(1)} %copy-done.10, s32[2,4]{1,0:T(2,128)S(1)} %copy-done.9, bf16[2,512,256]{2,1,0:T(8,128)(2,1)S(1)} %copy-done.6, ...), custom_call_target="tpu_custom_call" | custom-call | flops 855638016 | bytes 4898864 | tf_op jit(solution)/shard_map/pallas_call | solution.py:45
  106.2 2.8 %shard_map.145 = (bf16[3584,128]{1,0:T(8,128)(2,1)S(1)}, bf16[3584,128]{1,0:T(8,128)(2,1)S(1)}) custom-call(s32[2]{0:T(128)S(1)} %pad_add_fusion.place.refs_0_, bf16[2,544,128]{2,1,0:T(8,128)(2,1)S(1)} %pad_maximum_fusion.refs_1_.refs_13_.older.hidden, bf16[2,544,128]{2,1,0:T(8,128)(2,1)S(1)} %pad_maximum_fusion.2.refs_2_.older_a.hidden_a, ...), custom_call_target="tpu_custom_call" | custom-call | flops 641728512 | bytes 7389192 | tf_op jit(solution)/shard_map/pallas_call | solution.py:45
  109.0 4.4 %collective-permute-start.12 = (bf16[3584,128]{1,0:T(8,128)(2,1)S(1)}, bf16[3584,128]{1,0:T(8,128)(2,1)S(1)}, u32[]{:S(2)}, u32[]{:S(2)}) collective-permute-start(bf16[3584,128]{1,0:T(8,128)(2,1)S(1)} %get-tuple-element.113), channel_id=1, source_target_pairs={{0,1},{1,0},{2,3},{3,2},{4,5},{5,4},{6,7},{7,6},{8,9},{9,8},{10,11... | collective-permute-start | bytes 2752520 | tf_op jit(solution)/shard_map/ppermute | solution.py:562
  113.4 3.5 %collective-permute-start.14 = (bf16[2,192,256]{2,1,0:T(8,128)(2,1)S(1)}, bf16[2,192,256]{2,1,0:T(8,128)(2,1)S(1)}, u32[]{:S(2)}, u32[]{:S(2)}) collective-permute-start(bf16[2,192,256]{2,1,0:T(8,128)(2,1)S(1)} %get-tuple-element.116), channel_id=1, source_target_pairs={{1,2},{2,1},{5,6},{6,5},{9,10},{10,9},{13,14},{14,13},{17,18},{18,... | collective-permute-start | bytes 589832 | tf_op jit(solution)/shard_map/ppermute | solution.py:549
  116.9 0.1 collective-permute-start.13
  117.0 4.9 %collective-permute-done.14.back_b = bf16[2,192,256]{2,1,0:T(8,128)(2,1)S(1)} collective-permute-done((bf16[2,192,256]{2,1,0:T(8,128)(2,1)S(1)}, bf16[2,192,256]{2,1,0:T(8,128)(2,1)S(1)}, u32[]{:S(2)}, u32[]{:S(2)}) %collective-permute-start.14) | collective-permute-done | bytes 196640 | tf_op jit(solution)/shard_map/ppermute | solution.py:549
  121.9 0.0 collective-permute-done.13.back_a
  121.9 1.4 shard_map.146
  123.3 0.0 collective-permute-done.12
  123.3 0.2 add_convert_fusion
  123.5 30.1 %all_to_all.10 = bf16[64,56,128]{2,1,0:T(8,128)(2,1)S(1)} all-to-all(bf16[64,56,128]{2,1,0:T(8,128)(2,1)S(1)} %bitcast.21), channel_id=1, replica_groups={{0,2,4,6,8,10,12,14,16,18,20,22,24,26,28,30,32,34,36,38,40,42,44,46,48,..., dimensions={0} | all-to-all | bytes 1835008 | tf_op jit(solution)/shard_map/all_to_all | solution.py:565
  153.7 0.2 reduce_sum.12
  153.8 0.1 broadcast_in_dim.2
  153.9 19.7 %all_to_all.11 = bf16[64,56,128]{2,1,0:T(8,128)(2,1)S(1)} all-to-all(bf16[64,56,128]{2,1,0:T(8,128)(2,1)S(1)} %broadcast_in_dim.2), channel_id=1, replica_groups={{0,2,4,6,8,10,12,14,16,18,20,22,24,26,28,30,32,34,36,38,40,42,44,46,48,..., dimensions={0} | all-to-all | bytes 1835008 | tf_op jit(solution)/shard_map/all_to_all | solution.py:568
  173.7 4.2 %collective-permute-start.15 = (bf16[64,56,128]{2,1,0:T(8,128)(2,1)S(1)}, bf16[64,56,128]{2,1,0:T(8,128)(2,1)S(1)}, u32[]{:S(2)}, u32[]{:S(2)}) collective-permute-start(bf16[64,56,128]{2,1,0:T(8,128)(2,1)S(1)} %all_to_all.11), channel_id=1, source_target_pairs={{0,1},{1,0},{2,3},{3,2},{4,5},{5,4},{6,7},{7,6},{8,9},{9,8},{10,11... | collective-permute-start | bytes 2752520 | tf_op jit(solution)/shard_map/ppermute | solution.py:569
  177.8 2.1 %collective-permute-done.15 = bf16[64,56,128]{2,1,0:T(8,128)(2,1)S(1)} collective-permute-done((bf16[64,56,128]{2,1,0:T(8,128)(2,1)S(1)}, bf16[64,56,128]{2,1,0:T(8,128)(2,1)S(1)}, u32[]{:S(2)}, u32[]{:S(2)}) %collective-permute-start.15) | collective-permute-done | bytes 917536 | tf_op jit(solution)/shard_map/ppermute | solution.py:569
  179.9 4.6 %shard_map.147 = (f32[2304,256]{1,0:T(8,128)}, f32[2304,128]{1,0:T(8,128)}, f32[36,128]{1,0:T(8,128)}) custom-call(s32[2]{0:T(128)S(1)} %pad_add_fusion.place.refs_0_, bf16[3584,128]{1,0:T(8,128)(2,1)S(1)} %bitcast.13, bf16[3584,128]{1,0:T(8,128)(2,1)S(1)} %bitcast.17), custom_call_target="tpu_custom_call" | custom-call | bytes 5308416 | tf_op jit(solution)/shard_map/pallas_call | solution.py:149
  (26 shorter events, 0.1 us)
Async XLA Ops:
  0.6 16.6 %copy-start = (bf16[2304,256]{1,0:T(8,128)(2,1)S(1)}, bf16[2304,256]{1,0:T(8,128)(2,1)}, u32[]{:S(2)}) copy-start(bf16[2304,256]{1,0:T(8,128)(2,1)} %gate_w.1) | copy-start | bytes 3538948
  0.6 1.0 copy-start.1
  1.7 1.0 copy-start.5
  2.7 1.0 copy-start.7
  3.8 12.4 %copy-start.3 = (bf16[2304,128]{1,0:T(8,128)(2,1)S(1)}, bf16[2304,128]{1,0:T(8,128)(2,1)}, u32[]{:S(2)}) copy-start(bf16[2304,128]{1,0:T(8,128)(2,1)} %cand_w.1) | copy-start | bytes 1769476
  4.8 13.4 %collective-permute-start.3 = (bf16[2,288,256]{2,1,0:T(8,128)(2,1)S(1)}, bf16[2,288,256]{2,1,0:T(8,128)(2,1)}, u32[]{:S(2)}, u32[]{:S(2)}) collective-permute-start(bf16[2,288,256]{2,1,0:T(8,128)(2,1)S(1)} %shard_map.136), channel_id=1, source_target_pairs={{1,2},{2,1},{5,6},{6,5},{9,10},{10,9},{13,14},{14,13},{17,18},{18,... | collective-permute-start | bytes 884744 | tf_op jit(solution)/shard_map/ppermute | solution.py:549
  10.8 7.3 %collective-permute-start.2 = (bf16[2,288,256]{2,1,0:T(8,128)(2,1)S(1)}, bf16[2,288,256]{2,1,0:T(8,128)(2,1)}, u32[]{:S(2)}, u32[]{:S(2)}) collective-permute-start(bf16[2,288,256]{2,1,0:T(8,128)(2,1)S(1)} %shard_map.136), channel_id=1, source_target_pairs={{0,1},{2,3},{1,0},{3,2},{4,5},{6,7},{5,4},{7,6},{8,9},{10,11},{9,8... | collective-permute-start | bytes 884744 | tf_op jit(solution)/shard_map/ppermute | solution.py:549
  10.9 9.1 %collective-permute-start.1 = (bf16[2,512,128]{2,1,0:T(8,128)(2,1)}, bf16[2,512,128]{2,1,0:T(8,128)(2,1)}, u32[]{:S(2)}, u32[]{:S(2)}) collective-permute-start(bf16[2,512,128]{2,1,0:T(8,128)(2,1)} %hidden.1), channel_id=1, source_target_pairs={{4,8},{12,16},{20,24},{28,32},{36,40},{44,48},{52,56},{60,64},{68,... | collective-permute-start | bytes 786440 | tf_op jit(solution)/shard_map/ppermute | solution.py:549
  12.3 10.2 %collective-permute-start = (bf16[2,512,128]{2,1,0:T(8,128)(2,1)}, bf16[2,512,128]{2,1,0:T(8,128)(2,1)}, u32[]{:S(2)}, u32[]{:S(2)}) collective-permute-start(bf16[2,512,128]{2,1,0:T(8,128)(2,1)} %hidden.1), channel_id=1, source_target_pairs={{0,4},{8,12},{16,20},{24,28},{32,36},{40,44},{48,52},{56,60},{64,6... | collective-permute-start | bytes 786440 | tf_op jit(solution)/shard_map/ppermute | solution.py:549
  17.3 0.7 copy-start.11
  17.3 2.7 %copy-start.2 = (bf16[2,512,128]{2,1,0:T(8,128)(2,1)S(1)}, bf16[2,512,128]{2,1,0:T(8,128)(2,1)}, u32[]{:S(2)}) copy-start(bf16[2,512,128]{2,1,0:T(8,128)(2,1)} %grads.1) | copy-start | bytes 786436
  18.0 4.4 %copy-start.6 = (bf16[2,512,256]{2,1,0:T(8,128)(2,1)S(1)}, bf16[2,512,256]{2,1,0:T(8,128)(2,1)}, u32[]{:S(2)}) copy-start(bf16[2,512,256]{2,1,0:T(8,128)(2,1)} %left.5) | copy-start | bytes 1572868
  18.0 4.4 %copy-start.8 = (bf16[2,512,256]{2,1,0:T(8,128)(2,1)S(1)}, bf16[2,512,256]{2,1,0:T(8,128)(2,1)}, u32[]{:S(2)}) copy-start(bf16[2,512,256]{2,1,0:T(8,128)(2,1)} %right.5) | copy-start | bytes 1572868
  18.0 4.4 %copy-start.9 = (s32[2,4]{1,0:T(2,128)S(1)}, s32[2,4]{1,0:T(2,128)}, u32[]{:S(2)}) copy-start(s32[2,4]{1,0:T(2,128)} %offsets.3) | copy-start | bytes 100
  18.0 4.4 %copy-start.10 = (s32[2]{0:T(128)S(1)}, s32[2]{0:T(128)}, u32[]{:S(2)}) copy-start(s32[2]{0:T(128)} %disparity.3) | copy-start | bytes 28
  27.0 3.4 %collective-permute-start.5 = (bf16[2,576,128]{2,1,0:T(8,128)(2,1)S(1)}, bf16[2,576,128]{2,1,0:T(8,128)(2,1)S(1)}, u32[]{:S(2)}, u32[]{:S(2)}) collective-permute-start(bf16[2,576,128]{2,1,0:T(8,128)(2,1)S(1)} %constant_dynamic-update-slice_fusion), channel_id=1, source_target_pairs={{4,8},{12,16},{20,24},{28,32},{36,40},{44,48},{52,56},{60,64},{68,... | collective-permute-start | bytes 884744 | tf_op jit(solution)/shard_map/ppermute | solution.py:549
  27.7 8.3 %collective-permute-start.4 = (bf16[2,576,128]{2,1,0:T(8,128)(2,1)S(1)}, bf16[2,576,128]{2,1,0:T(8,128)(2,1)S(1)}, u32[]{:S(2)}, u32[]{:S(2)}) collective-permute-start(bf16[2,576,128]{2,1,0:T(8,128)(2,1)S(1)} %constant_dynamic-update-slice_fusion), channel_id=1, source_target_pairs={{0,4},{8,12},{16,20},{24,28},{32,36},{40,44},{48,52},{56,60},{64,6... | collective-permute-start | bytes 884744 | tf_op jit(solution)/shard_map/ppermute | solution.py:549
  44.3 7.3 %collective-permute-start.7 = (bf16[2,544,128]{2,1,0:T(8,128)(2,1)S(1)}, bf16[2,544,128]{2,1,0:T(8,128)(2,1)S(1)}, u32[]{:S(2)}, u32[]{:S(2)}) collective-permute-start(bf16[2,544,128]{2,1,0:T(8,128)(2,1)S(1)} %get-tuple-element.72.hidden.refs_5_), channel_id=1, source_target_pairs={{4,8},{12,16},{20,24},{28,32},{36,40},{44,48},{52,56},{60,64},{68,... | collective-permute-start | bytes 835592 | tf_op jit(solution)/shard_map/ppermute | solution.py:549
  45.0 11.2 %collective-permute-start.6 = (bf16[2,544,128]{2,1,0:T(8,128)(2,1)S(1)}, bf16[2,544,128]{2,1,0:T(8,128)(2,1)S(1)}, u32[]{:S(2)}, u32[]{:S(2)}) collective-permute-start(bf16[2,544,128]{2,1,0:T(8,128)(2,1)S(1)} %get-tuple-element.72.hidden.refs_5_), channel_id=1, source_target_pairs={{0,4},{8,12},{16,20},{24,28},{32,36},{40,44},{48,52},{56,60},{64,6... | collective-permute-start | bytes 835592 | tf_op jit(solution)/shard_map/ppermute | solution.py:549
  65.5 8.3 %collective-permute-start.8 = (bf16[3,544,128]{2,1,0:T(8,128)(2,1)S(1)}, bf16[3,544,128]{2,1,0:T(8,128)(2,1)S(1)}, u32[]{:S(2)}, u32[]{:S(2)}) collective-permute-start(bf16[3,544,128]{2,1,0:T(8,128)(2,1)S(1)} %get-tuple-element.75), channel_id=1, source_target_pairs={{0,4},{8,12},{16,20},{24,28},{32,36},{40,44},{48,52},{56,60},{64,6... | collective-permute-start | bytes 1253384 | tf_op jit(solution)/shard_map/ppermute | solution.py:554
  67.0 6.9 %collective-permute-start.9 = (bf16[3,544,128]{2,1,0:T(8,128)(2,1)S(1)}, bf16[3,544,128]{2,1,0:T(8,128)(2,1)S(1)}, u32[]{:S(2)}, u32[]{:S(2)}) collective-permute-start(bf16[3,544,128]{2,1,0:T(8,128)(2,1)S(1)} %get-tuple-element.76), channel_id=1, source_target_pairs={{4,8},{12,16},{20,24},{28,32},{36,40},{44,48},{52,56},{60,64},{68,... | collective-permute-start | bytes 1253384 | tf_op jit(solution)/shard_map/ppermute | solution.py:554
  67.7 6.2 %copy-start.4 = (bf16[3,3,256,128]{2,3,1,0:T(8,128)(2,1)S(1)}, bf16[3,3,256,128]{2,3,1,0:T(8,128)(2,1)}, u32[]{:S(2)}) copy-start(bf16[3,3,256,128]{2,3,1,0:T(8,128)(2,1)} %copy.16) | copy-start | bytes 1769476
  81.9 13.6 %collective-permute-start.10 = (bf16[3,544,128]{2,1,0:T(8,128)(2,1)S(1)}, bf16[3,544,128]{2,1,0:T(8,128)(2,1)S(1)}, u32[]{:S(2)}, u32[]{:S(2)}) collective-permute-start(bf16[3,544,128]{2,1,0:T(8,128)(2,1)S(1)} %get-tuple-element.90), channel_id=1, source_target_pairs={{0,4},{8,12},{16,20},{24,28},{32,36},{40,44},{48,52},{56,60},{64,6... | collective-permute-start | bytes 1253384 | tf_op jit(solution)/shard_map/ppermute | solution.py:554
  88.4 7.1 %collective-permute-start.11 = (bf16[3,544,128]{2,1,0:T(8,128)(2,1)S(1)}, bf16[3,544,128]{2,1,0:T(8,128)(2,1)S(1)}, u32[]{:S(2)}, u32[]{:S(2)}) collective-permute-start(bf16[3,544,128]{2,1,0:T(8,128)(2,1)S(1)} %get-tuple-element.91), channel_id=1, source_target_pairs={{4,8},{12,16},{20,24},{28,32},{36,40},{44,48},{52,56},{60,64},{68,... | collective-permute-start | bytes 1253384 | tf_op jit(solution)/shard_map/ppermute | solution.py:554
  109.0 14.3 %collective-permute-start.12 = (bf16[3584,128]{1,0:T(8,128)(2,1)S(1)}, bf16[3584,128]{1,0:T(8,128)(2,1)S(1)}, u32[]{:S(2)}, u32[]{:S(2)}) collective-permute-start(bf16[3584,128]{1,0:T(8,128)(2,1)S(1)} %get-tuple-element.113), channel_id=1, source_target_pairs={{0,1},{1,0},{2,3},{3,2},{4,5},{5,4},{6,7},{7,6},{8,9},{9,8},{10,11... | collective-permute-start | bytes 2752520 | tf_op jit(solution)/shard_map/ppermute | solution.py:562
  113.4 8.5 %collective-permute-start.14 = (bf16[2,192,256]{2,1,0:T(8,128)(2,1)S(1)}, bf16[2,192,256]{2,1,0:T(8,128)(2,1)S(1)}, u32[]{:S(2)}, u32[]{:S(2)}) collective-permute-start(bf16[2,192,256]{2,1,0:T(8,128)(2,1)S(1)} %get-tuple-element.116), channel_id=1, source_target_pairs={{1,2},{2,1},{5,6},{6,5},{9,10},{10,9},{13,14},{14,13},{17,18},{18,... | collective-permute-start | bytes 589832 | tf_op jit(solution)/shard_map/ppermute | solution.py:549
  116.9 4.9 %collective-permute-start.13 = (bf16[2,192,256]{2,1,0:T(8,128)(2,1)S(1)}, bf16[2,192,256]{2,1,0:T(8,128)(2,1)S(1)}, u32[]{:S(2)}, u32[]{:S(2)}) collective-permute-start(bf16[2,192,256]{2,1,0:T(8,128)(2,1)S(1)} %get-tuple-element.116), channel_id=1, source_target_pairs={{0,1},{2,3},{1,0},{3,2},{4,5},{6,7},{5,4},{7,6},{8,9},{10,11},{9,8... | collective-permute-start | bytes 589832 | tf_op jit(solution)/shard_map/ppermute | solution.py:549
  173.7 6.3 %collective-permute-start.15 = (bf16[64,56,128]{2,1,0:T(8,128)(2,1)S(1)}, bf16[64,56,128]{2,1,0:T(8,128)(2,1)S(1)}, u32[]{:S(2)}, u32[]{:S(2)}) collective-permute-start(bf16[64,56,128]{2,1,0:T(8,128)(2,1)S(1)} %all_to_all.11), channel_id=1, source_target_pairs={{0,1},{1,0},{2,3},{3,2},{4,5},{5,4},{6,7},{7,6},{8,9},{9,8},{10,11... | collective-permute-start | bytes 2752520 | tf_op jit(solution)/shard_map/ppermute | solution.py:569

commit v2 on v1

--- a/solution.py
+++ b/solution.py
@@ -13,6 +13,7 @@
 TAPS = 2 * RADIUS + 1
 HALO = 16
 LANES = 128
+SPLIT = 2
 CHUNK_ROWS = 56
 
 BF16 = jnp.bfloat16
@@ -119,7 +120,7 @@
         in_specs=[pl.BlockSpec(memory_space=pltpu.HBM)] * 4,
         out_specs=VMEM,
         scratch_shapes=[pltpu.SemaphoreType.DMA((8,))],
-        compiler_params=pltpu.CompilerParams(vmem_limit_bytes=4 * 2**20),
+        compiler_params=pltpu.CompilerParams(vmem_limit_bytes=56 * 2**20),
         cost_estimate=pl.CostEstimate(flops=0, bytes_accessed=4 * rows * count * channels, transcendentals=0),
     )(left, right, hidden, grads)
 
@@ -161,7 +162,8 @@
     )(place, half, other)
 
 
-def motion_kernel(place, disparity, offsets, left, right, got_a, got_b, weight, motion, pre, feats, ext, window, flipped):
+def motion_kernel(place, disparity, offsets, left, right, got_a, got_b, weight, hidden, grads,
+                  motion, pre, feats, hidden_ext, grads_ext, ext, window, flipped):
     odd = place[1] % 2 == 1
     cols = left.shape[1]
     wide = cols + 2 * HALO
@@ -176,6 +178,15 @@
     valid = (position >= 0) & (position < DISP)
     for row in range(2):
         from_left, from_right = sides(odd, got_a[row], got_b[row])
+        state, last = tail + 3 * HALO, HALO + cols
+        hidden_ext[row, 0:HALO] = from_left[state : state + HALO, :LANES]
+        hidden_ext[row, HALO:last] = hidden[row]
+        hidden_ext[row, last:] = from_right[state : state + HALO, LANES:]
+        grads_ext[row, 0:HALO] = from_left[state + HALO :, :LANES]
+        grads_ext[row, HALO:last] = grads[row]
+        grads_ext[row, last:] = from_right[state + HALO :, LANES:]
+        motion[row, wide : wide + HALO] = from_left[state : state + HALO, :LANES]
+        motion[row, wide + HALO :] = from_right[state : state + HALO, LANES:]
         ext[0:HALO] = from_left[tail : tail + HALO]
         ext[HALO : HALO + cols] = left[row]
         ext[HALO + cols : wide] = from_right[tail + HALO : tail + 2 * HALO]
@@ -207,20 +218,20 @@
     return (column >= 0) & (column < cols * cols_axis)
 
 
-def fill_rows(store, odd, own, first, second):
-    for row in range(2):
-        above, below = sides(odd, first[row], second[row])
+def fill_rows(store, odd, own, first, second, wide):
+    for row in range(2):
+        above, below = sides(odd, first[row, :wide], second[row, :wide])
         store(row, above.astype(F32))
         store(4 + row, below.astype(F32))
-        store(2 + row, own[row].astype(F32))
+        store(2 + row, own[row, :wide].astype(F32))
 
 
 def gates(fields, resets, gate_w, update, reset, reset_hidden, wide):
-    block = wide // 2
+    block = wide // SPLIT
     deep = gate_w.shape[0] // 3
 
-    def gate_part(step, carry):
-        row, start = step // 2, pl.multiple_of((step % 2) * block, 16)
+    for step in range(4 * SPLIT):
+        row, start = step // SPLIT, (step % SPLIT) * block
         here = pl.ds(start, block)
         total = sum(dot(fields[row + a, here], gate_w[a * deep : (a + 1) * deep]) for a in range(3))
         reset_part = jax.nn.sigmoid(total[:, LANES:])
@@ -228,9 +239,6 @@
         reset[row, here] = reset_part
         hidden = fields[row + 1, here, 2 * LANES : 3 * LANES].astype(F32)
         reset_hidden[row, here] = (reset_part * hidden).astype(BF16)
-        return carry
-
-    lax.fori_loop(0, 8, gate_part, 0)
     for row in range(4):
         store_taps(resets, row, 0, 2 * LANES, reset_hidden[row].astype(F32), True)
         for tap in range(3):
@@ -238,9 +246,9 @@
             resets[row, :, start : start + LANES] = fields[row + 1, :, start : start + LANES]
 
 
-def load_fields(odd, fields, hidden, hidden_a, hidden_b, motion, motion_a, motion_b):
-    fill_rows(lambda r, v: store_taps(fields, r, 0, 2 * LANES, v, True), odd, hidden, hidden_a, hidden_b)
-    fill_rows(lambda r, v: store_taps(fields, r, LANES, 2 * LANES, v, True), odd, motion, motion_a, motion_b)
+def load_field(odd, fields, lane, own, first, second):
+    wide = fields.shape[1]
+    fill_rows(lambda r, v: store_taps(fields, r, lane, 2 * LANES, v, True), odd, own, first, second, wide)
 
 
 def candidate_part(resets, cand_w, row, here):
@@ -249,16 +257,28 @@
     return jnp.tanh(total)
 
 
-def first_kernel(cols_axis, place, hidden, hidden_a, hidden_b, motion, motion_a, motion_b, gate_w, cand_w,
-                 later, update, reset, reset_hidden, candidate, fields, resets):
+def first_kernel(cols_axis, place, hidden, init_a, init_b, motion, motion_a, motion_b, gate_w, cand_w,
+                 later, update, reset, reset_hidden, candidate, hiddens, fields, resets):
     odd = place[0] % 2 == 1
     wide = hidden.shape[1]
-    block = wide // 2
-    load_fields(odd, fields, hidden, hidden_a, hidden_b, motion, motion_a, motion_b)
+    block = wide // SPLIT
+    load_field(odd, fields, LANES, motion, motion_a, motion_b)
+    for row in range(2):
+        got_a, got_b = (
+            jnp.concatenate(
+                [sent[row, wide : wide + HALO], inner[row], sent[row, wide + HALO :]], axis=0
+            )
+            for sent, inner in ((motion_a, init_a), (motion_b, init_b))
+        )
+        above, below = sides(odd, got_a, got_b)
+        for there, value in ((row, above), (2 + row, hidden[row]), (4 + row, below)):
+            store_taps(fields, there, 0, 2 * LANES, value.astype(F32), True)
+            if 0 < there < 5:
+                hiddens[there - 1] = value
     gates(fields, resets, gate_w, update, reset, reset_hidden, wide)
     inside = image_columns(place, wide, wide - 2 * HALO, cols_axis)
     for row in range(2):
-        for start in (0, block):
+        for start in range(0, wide, block):
             here = pl.ds(start, block)
             new = candidate_part(resets, cand_w, row, here)
             candidate[row, here] = new
@@ -268,63 +288,52 @@
             later[row, here] = jnp.where(inside[start : start + block], value, 0.0).astype(BF16)
 
 
-def gradients_out(odd, grad, gate, new, old, row, here, grad_cand, grad_update, send_a, send_b):
+def gradients_out(grad, gate, new, old, row, here, grad_cand, grad_update, send_a, send_b):
     cand_part = (grad * gate * (1.0 - new * new)).astype(BF16)
-    update_part = (grad * (new - old) * gate * (1.0 - gate)).astype(BF16)
     grad_cand[row, here] = cand_part
-    grad_update[row, here] = update_part
     send_a[row, here] = cand_part
     send_b[row, here] = cand_part
-
-    @pl.when(odd == (row == 0))
-    def _():
-        send_a[2, here] = update_part
-
-    @pl.when(odd == (row == 1))
-    def _():
-        send_b[2, here] = update_part
+    grad_update[row, here] = (grad * (new - old) * gate * (1.0 - gate)).astype(BF16)
+
+
+def send_updates(odd, grad_update, send_a, send_b):
+    send_a[2], send_b[2] = sides(odd, grad_update[0], grad_update[1])
 
 
 def second_kernel(place, hidden, hidden_a, hidden_b, motion, motion_a, motion_b, gate_w, cand_w, grad_hidden,
                   update, reset, reset_hidden, grad_cand, grad_update, send_a, send_b, fields, resets):
     odd = place[0] % 2 == 1
     wide = hidden.shape[1]
-    block = wide // 2
-    load_fields(odd, fields, hidden, hidden_a, hidden_b, motion, motion_a, motion_b)
+    block = wide // SPLIT
+    load_field(odd, fields, LANES, motion, motion_a, motion_b)
+    load_field(odd, fields, 0, hidden, hidden_a, hidden_b)
     gates(fields, resets, gate_w, update, reset, reset_hidden, wide)
     for row in range(2):
-        for start in (0, block):
+        for start in range(0, wide, block):
             here = pl.ds(start, block)
             new = candidate_part(resets, cand_w, row, here)
-            gradients_out(odd, grad_hidden[row, here].astype(F32), update[row + 1, here], new,
+            gradients_out(grad_hidden[row, here].astype(F32), update[row + 1, here], new,
                           hidden[row, here].astype(F32), row, here, grad_cand, grad_update, send_a, send_b)
-
-
-def back_step(place, grad_cand, grad_a, grad_b, grad_update, hidden, hidden_a, hidden_b, reset, cand_wt, gate_wt,
+    send_updates(odd, grad_update, send_a, send_b)
+
+
+def back_step(place, grad_cand, grad_a, grad_b, grad_update, hiddens, reset, cand_wt, gate_wt,
               grad_reset, cand_taps, gate_taps, inner, grad_motion, finish):
     odd = place[0] % 2 == 1
-    wide = hidden.shape[1]
-    block = wide // 2
-    fill_rows(lambda r, v: store_taps(cand_taps, r, 0, LANES, v, False), odd, grad_cand, grad_a, grad_b)
+    wide = grad_cand.shape[1]
+    block = wide // SPLIT
+    fill_rows(lambda r, v: store_taps(cand_taps, r, 0, LANES, v, False), odd, grad_cand, grad_a, grad_b, wide)
     deep = cand_wt.shape[0] // 3
     deeper = gate_wt.shape[0] // 3
 
-    def cand_back(step, carry):
-        row, start = step // 2, pl.multiple_of((step % 2) * block, 16)
+    for step in range(4 * SPLIT):
+        row, start = step // SPLIT, (step % SPLIT) * block
         here = pl.ds(start, block)
         total = sum(dot(cand_taps[row + 2 - a, here], cand_wt[a * deep : (a + 1) * deep]) for a in range(3))
         inner[row, here] = total[:, :LANES]
-
-        @pl.when((row == 1) | (row == 2))
-        def _():
+        if row in (1, 2):
             grad_motion[row - 1, here] = total[:, LANES:]
-
-        return carry
-
-    lax.fori_loop(0, 8, cand_back, 0)
-    above_h, below_h = sides(odd, hidden_a[1], hidden_b[1])[0], sides(odd, hidden_a[0], hidden_b[0])[1]
     above_u, below_u = sides(odd, grad_a[2], grad_b[2])
-    hiddens = (above_h, hidden[0], hidden[1], below_h)
     updates = (above_u, grad_update[0], grad_update[1], below_u)
     for row in range(4):
         gate = reset[row]
@@ -334,7 +343,7 @@
         if row in (1, 2):
             grad_reset[row - 1] = value
     for row in range(2):
-        for start in (0, block):
+        for start in range(0, wide, block):
             here = pl.ds(start, block)
             total = sum(
                 dot(gate_taps[row + 2 - a, here], gate_wt[a * deeper : (a + 1) * deeper]) for a in range(3)
@@ -344,12 +353,12 @@
 
 
 def later_back_kernel(cols_axis, place, grad_cand, grad_a, grad_b, grad_update, hidden, hidden_a, hidden_b, reset,
-                      cand_wt, gate_wt, update, grad_hidden, older_hidden, older_update, older_candidate,
+                      cand_wt, gate_wt, update, grad_hidden, older_hiddens, older_update, older_candidate,
                       grad_reset, grad_state, grad_motion, older_cand, older_upd, send_a, send_b,
                       cand_taps, gate_taps, inner):
     odd = place[0] % 2 == 1
     wide = hidden.shape[1]
-    block = wide // 2
+    block = wide // SPLIT
     inside = image_columns(place, wide, wide - 2 * HALO, cols_axis)
 
     def finish(row, start, here, terms):
@@ -357,33 +366,33 @@
         grad = grad_hidden[row, here].astype(F32) * (1.0 - gate) + terms
         grad = jnp.where(inside[start : start + block], grad, 0.0)
         grad_state[row, here] = grad
-        gradients_out(odd, grad, older_update[row + 1, here], older_candidate[row, here],
-                      older_hidden[row, here].astype(F32), row, here, older_cand, older_upd, send_a, send_b)
-
-    back_step(place, grad_cand, grad_a, grad_b, grad_update, hidden, hidden_a, hidden_b, reset, cand_wt, gate_wt,
+        gradients_out(grad, older_update[row + 1, here], older_candidate[row, here],
+                      older_hiddens[row + 1, here].astype(F32), row, here, older_cand, older_upd, send_a, send_b)
+
+    hiddens = hidden_rows(odd, hidden, hidden_a, hidden_b)
+    back_step(place, grad_cand, grad_a, grad_b, grad_update, hiddens, reset, cand_wt, gate_wt,
               grad_reset, cand_taps, gate_taps, inner, grad_motion, finish)
-
-
-def first_back_kernel(place, grad_cand, grad_a, grad_b, grad_update, hidden, hidden_a, hidden_b, reset,
+    send_updates(odd, older_upd, send_a, send_b)
+
+
+def first_back_kernel(place, grad_cand, grad_a, grad_b, grad_update, hiddens, reset,
                       cand_wt, gate_wt, update, grad_state, motion_so_far,
                       grad_reset, grad_first, grad_motion, cand_taps, gate_taps, inner):
     def finish(row, start, here, terms):
         gate = update[row + 1, here]
         grad = grad_state[row, here] * (1.0 - gate) + terms
-        skip = HALO if start == 0 else 0
-        count = grad.shape[0] - HALO
-        grad_first[row, (start + skip) - HALO : (start + skip) - HALO + count] = grad[skip : skip + count].astype(BF16)
+        first, last = max(start, HALO), min(start + grad.shape[0], HALO + grad_first.shape[1])
+        grad_first[row, first - HALO : last - HALO] = grad[first - start : last - start].astype(BF16)
         grad_motion[row, here] += motion_so_far[row, here]
 
-    back_step(place, grad_cand, grad_a, grad_b, grad_update, hidden, hidden_a, hidden_b, reset, cand_wt, gate_wt,
+    back_step(place, grad_cand, grad_a, grad_b, grad_update, hiddens, reset, cand_wt, gate_wt,
               grad_reset, cand_taps, gate_taps, inner, grad_motion, finish)
 
 
 def load_pixels(odd, pixels, hiddens, motion, motion_a, motion_b):
-    wide = motion.shape[1]
-    above, below = sides(odd, motion_a[1], motion_b[1])[0], sides(odd, motion_a[0], motion_b[0])[1]
-    for row, value in enumerate((above, motion[0], motion[1], below)):
-        pixels[row * wide : (row + 1) * wide, LANES:] = value
+    wide = pixels.shape[0] // 4
+    for row, value in enumerate(hidden_rows(odd, motion, motion_a, motion_b)):
+        pixels[row * wide : (row + 1) * wide, LANES:] = value[:wide]
     for row, value in enumerate(hiddens):
         pixels[row * wide : (row + 1) * wide, :LANES] = value
 
@@ -403,14 +412,10 @@
 
 
 def weight_products(pixels, taps, wide, depth, finish):
-    def one_row(a, carry):
-        rows = pixels[pl.ds(pl.multiple_of(a * wide, 16), 2 * wide), :]
-        total = dot_tn(rows, taps[...])
+    for a in range(3):
+        total = dot_tn(pixels[a * wide : (a + 2) * wide], taps[...])
         for b in range(3):
-            finish(pl.multiple_of((3 * a + b) * 2 * LANES, LANES), total[:, b * depth : (b + 1) * depth])
-        return carry
-
-    lax.fori_loop(0, 3, one_row, 0)
+            finish((3 * a + b) * 2 * LANES, total[:, b * depth : (b + 1) * depth])
 
 
 def hidden_rows(odd, hidden, hidden_a, hidden_b):
@@ -426,7 +431,7 @@
 def second_weights_kernel(place, resets, hidden, hidden_a, hidden_b, motion, motion_a, motion_b, cand_grads, update_grads,
                           cand_out, update_out, pixels, taps):
     odd = place[0] % 2 == 1
-    wide = motion.shape[1]
+    wide = taps.shape[0] // 2
     load_pixels(odd, pixels, [resets[row] for row in range(4)], motion, motion_a, motion_b)
     load_grads(taps, cand_grads)
 
@@ -442,11 +447,11 @@
     weight_products(pixels, taps, wide, LANES, update_finish)
 
 
-def first_weights_kernel(place, resets, older, older_a, older_b, hidden, hidden_a, hidden_b, motion, motion_a, motion_b,
+def first_weights_kernel(place, resets, older, hidden, hidden_a, hidden_b, motion, motion_a, motion_b,
                          cand_grads, update_grads, reset_grads, cand_sum, update_sum,
                          cand_out, update_out, reset_out, pixels, taps):
     odd = place[0] % 2 == 1
-    wide = motion.shape[1]
+    wide = taps.shape[0] // 2
     load_pixels(odd, pixels, [resets[row] for row in range(4)], motion, motion_a, motion_b)
     load_grads(taps, cand_grads)
 
@@ -462,7 +467,7 @@
         reset_out[pl.ds(start, 2 * LANES)] = value
 
     weight_products(pixels, taps, wide, LANES, cand_finish)
-    load_hidden(pixels, hidden_rows(odd, older, older_a, older_b), wide)
+    load_hidden(pixels, [older[row] for row in range(4)], wide)
     load_grads(taps, update_grads)
     weight_products(pixels, taps, wide, LANES, update_finish)
     load_hidden(pixels, hidden_rows(odd, hidden, hidden_a, hidden_b), wide)
@@ -470,18 +475,17 @@
     weight_products(pixels, taps, wide, LANES, reset_finish)
 
 
-def last_weights_kernel(place, hidden, hidden_a, hidden_b, motion, motion_a, motion_b, reset_grads, reset_sum,
+def last_weights_kernel(place, hiddens, motion, motion_a, motion_b, reset_grads, reset_sum,
                         update_sum, cand_sum, motion_w, kept, given, pixels, taps, parts):
     odd = place[0] % 2 == 1
-    load_pixels(odd, pixels, hidden_rows(odd, hidden, hidden_a, hidden_b), motion, motion_a, motion_b)
+    load_pixels(odd, pixels, [hiddens[row] for row in range(4)], motion, motion_a, motion_b)
     load_grads(taps, reset_grads)
     rows = cand_sum.shape[0]
 
     def finish(start, value):
-        there = pl.ds(pl.multiple_of(rows + start, LANES), 2 * LANES)
-        parts[there] = (value + reset_sum[pl.ds(start, 2 * LANES)]).astype(BF16)
-
-    weight_products(pixels, taps, motion.shape[1], LANES, finish)
+        parts[rows + start : rows + start + 2 * LANES] = (value + reset_sum[pl.ds(start, 2 * LANES)]).astype(BF16)
+
+    weight_products(pixels, taps, taps.shape[0] // 2, LANES, finish)
     parts[0:rows] = update_sum[...].astype(BF16)
     parts[2 * rows : 3 * rows] = cand_sum[...].astype(BF16)
     parts[3 * rows : 3 * rows + LANES] = motion_w[...].astype(BF16)
@@ -588,50 +592,35 @@
     rows_axis, cols_axis = lax.axis_size("rows"), lax.axis_size("cols")
     rows_index, cols_index = lax.axis_index("rows"), lax.axis_index("cols")
     place = jnp.stack([rows_index, cols_index]).astype(jnp.int32)
-    odd_col = cols_index % 2 == 1
 
     halos = packed(fmap_left, fmap_right, hidden_init, grad_hidden)
     maps_a, maps_b = exchanged(halos, "cols")
     init_a, init_b = exchanged(hidden_init, "rows")
-    base = DISP + 4 * HALO
-    from_left = jnp.where(odd_col, maps_a[:, base:], maps_b[:, base:])
-    from_right = jnp.where(odd_col, maps_b[:, base:], maps_a[:, base:])
-    edges = jnp.concatenate([from_left[:, :HALO, :state], from_right[:, :HALO, state:]], axis=1)
-    hidden = jnp.concatenate([edges[:, :HALO], hidden_init, edges[:, HALO:]], axis=1)
-    grads = jnp.concatenate([from_left[:, HALO:, :state], grad_hidden, from_right[:, HALO:, state:]], axis=1)
-
     motion_w = jnp.pad(motion_weight, ((0, LANES - feats_count), (0, 0)))
     gate_wt = jnp.transpose(gate_weight.reshape(3, 3, 2 * state, 2 * state), (0, 1, 3, 2)).reshape(-1, 2 * state)
     cand_wt = jnp.transpose(cand_weight.reshape(3, 3, 2 * state, state), (0, 1, 3, 2)).reshape(-1, 2 * state)
-    motion_w, gate_wt, cand_wt, init_a, init_b, edges, hidden, grads = lax.optimization_barrier(
-        (motion_w, gate_wt, cand_wt, init_a, init_b, edges, hidden, grads)
+    motion_w, gate_wt, cand_wt, init_a, init_b = lax.optimization_barrier(
+        (motion_w, gate_wt, cand_wt, init_a, init_b)
     )
 
     field = lambda count, dtype: array((count, wide, LANES), dtype)
     band_flops = 2 * rows * wide * 512 * channels
-    motion, motion_pre, feats = kernel_call(
+    motion, motion_pre, feats, hidden, grads = kernel_call(
         motion_kernel,
-        [field(2, BF16), field(2, F32), field(2, BF16)],
-        [place, disp_init, level_offset, fmap_left, fmap_right, maps_a, maps_b, motion_w],
+        [array((2, wide + 2 * HALO, LANES), BF16), field(2, F32), field(2, BF16), field(2, BF16), field(2, BF16)],
+        [place, disp_init, level_offset, fmap_left, fmap_right, maps_a, maps_b, motion_w, hidden_init, grad_hidden],
         3,
         [pltpu.VMEM((wide, channels), BF16), pltpu.VMEM((768, channels), BF16), pltpu.VMEM((832, channels), BF16)],
         2 * band_flops,
     )
-    sent = jnp.concatenate([motion, edges], axis=1)
-    sent_a, sent_b = exchanged(sent, "rows")
-    motion_a, motion_b = sent_a[:, :wide], sent_b[:, :wide]
-    with_edges = lambda inner, got: jnp.concatenate(
-        [got[:, wide : wide + HALO], inner, got[:, wide + HALO :]], axis=1
-    )
-    hidden_a, hidden_b = with_edges(init_a, sent_a), with_edges(init_b, sent_b)
-    motions = (motion, motion_a, motion_b)
+    motions = (motion, *exchanged(motion, "rows"))
     unit = 2 * wide * 9 * 2 * state * state
     fields = [pltpu.VMEM((6, wide, 6 * LANES), BF16), pltpu.VMEM((4, wide, 6 * LANES), BF16)]
 
-    hidden_1, update_0, reset_0, reset_hidden_0, candidate_0 = kernel_call(
+    hidden_1, update_0, reset_0, reset_hidden_0, candidate_0, hiddens_0 = kernel_call(
         lambda *refs: first_kernel(cols_axis, *refs),
-        [field(2, BF16), field(4, F32), field(4, F32), field(4, BF16), field(2, F32)],
-        [place, hidden, hidden_a, hidden_b, *motions, gate_weight, cand_weight],
+        [field(2, BF16), field(4, F32), field(4, F32), field(4, BF16), field(2, F32), field(4, BF16)],
+        [place, hidden, init_a, init_b, *motions, gate_weight, cand_weight],
         1,
         fields,
         10 * unit,
@@ -668,7 +657,7 @@
         [field(2, BF16), field(2, F32), field(2, F32), field(2, BF16), field(2, BF16),
          field(3, BF16), field(3, BF16)],
         [place, grad_cand_1, got_a, got_b, grad_update_1, hidden_1, hidden_1a, hidden_1b, reset_1, cand_wt, gate_wt,
-         update_1, grads, hidden, update_0, candidate_0],
+         update_1, grads, hiddens_0, update_0, candidate_0],
         1,
         back_scratch,
         8 * unit,
@@ -677,7 +666,7 @@
     cand_sum, update_sum, reset_sum = kernel_call(
         first_weights_kernel,
         [weights, weights, weights],
-        [place, reset_hidden_0, hidden, hidden_a, hidden_b, hidden_1, hidden_1a, hidden_1b, *motions,
+        [place, reset_hidden_0, hiddens_0, hidden_1, hidden_1a, hidden_1b, *motions,
          grad_cand_0, grad_update_0, grad_reset_1, cand_sum, update_sum],
         1,
         [pixels, taps],
@@ -689,7 +678,7 @@
     grad_reset_0, grad_first, grad_motion = kernel_call(
         first_back_kernel,
         [field(2, BF16), array((2, cols, LANES), BF16), field(2, F32)],
-        [place, grad_cand_0, got_a, got_b, grad_update_0, hidden, hidden_a, hidden_b, reset_0, cand_wt, gate_wt,
+        [place, grad_cand_0, got_a, got_b, grad_update_0, hiddens_0, reset_0, cand_wt, gate_wt,
          update_0, grad_state, grad_motion_1],
         1,
         back_scratch,
@@ -710,7 +699,7 @@
     kept, given = kernel_call(
         last_weights_kernel,
         [array((total // 2, LANES), BF16), array((total // 2, LANES), BF16)],
-        [place, hidden, hidden_a, hidden_b, *motions, grad_reset_0, reset_sum, update_sum, cand_sum, motion_sum],
+        [place, hiddens_0, *motions, grad_reset_0, reset_sum, update_sum, cand_sum, motion_sum],
         1,
         [pixels, taps, pltpu.VMEM((total, LANES), BF16)],
         2 * unit,

time: 185 us -> 169 us (0.914)
  Pallas kernels: 60.1 us -> 45.4 us
  waiting for transfers between devices: 20.4 us -> 24.5 us
  other arithmetic: 4.27 us -> 0.48 us
  local copies, waits for them, and re-layouts: 5.16 us -> 2.91 us
    pallas_call x10, Pallas kernels: 54.6 us -> 39 us  [kernel_call(): pl.pallas_call(body, out_shape=outs, in_specs=[SMEM] * scalars + [VMEM] *...]
    concatenate x5 -> x0, other arithmetic: 2.94 us -> none  [the longest x2 1.94 us: on_device(): jnp.concatenate([got[:, wide:wide + HALO], inner, got[:, wide + HALO:]],...]
    unnamed x25 -> x20, local copies, waits for them, and re-layouts: 3.19 us -> 0.99 us
    ppermute x10, waiting for transfers between devices: 16.4 us -> 18.5 us  [exchanged(): return (lax.ppermute(value, axis, first), lax.ppermute(value, axis, second))]
    ppermute x2, starting transfers between devices: 7.89 us -> 5.87 us  [exchanged_pair(): lax.ppermute(value_a, axis, first)]
    ppermute x2, waiting for transfers between devices: 1.83 us -> 3.8 us  [exchanged_pair(): lax.ppermute(value_a, axis, first)]
  transfers between devices with their start and end apart: 16 -> 16, of which waited for: 6 -> 7; matrix products, arithmetic and copies ran while one was open for 3% -> 1% of each run, Pallas kernels for 6% -> 5%
where the time goes in v2:
time: 169 us
  blocking collectives  51.1 us (30%)
  Pallas kernels  45.4 us (27%)
  starting transfers between devices  43.4 us (26%)
  waiting for transfers between devices  24.5 us (14%)
  local copies, waits for them, and re-layouts  2.91 us (2%)
    pallas_call x10, Pallas kernels, kernel_call(): pl.pallas_call(body, out_shape=outs, in_specs=[SMEM] * scalars + [VMEM] *...  39 us
    all_to_all x1, blocking collectives, summed_everywhere(): lax.all_to_all(half, axes, 0, 0, tiled=True, axis_index_groups=groups)  31.7 us
    ppermute x10, starting transfers between devices, exchanged(): return (lax.ppermute(value, axis, first), lax.ppermute(value, axis, second))  26.5 us
    all_to_all x1, blocking collectives, summed_everywhere(): lax.all_to_all(spread, axes, 0, 0, tiled=True, axis_index_groups=groups)  19.3 us
    ppermute x10, waiting for transfers between devices, exchanged(): return (lax.ppermute(value, axis, first), lax.ppermute(value, axis, second))  18.5 us
    ppermute x2, starting transfers between devices, exchanged_pair(): lax.ppermute(value_a, axis, first)  5.87 us
    ppermute x1, starting transfers between devices, summed_everywhere(): got = lax.ppermute(given, 'cols', swap)  5.24 us
    pallas_call x1, Pallas kernels, unpacked(): pl.pallas_call(lambda *refs: unpack_kernel(count, scale, *refs), grid=(co...  4.56 us
  transfers between devices with their start and end apart: 16, of which 7 were waited for; matrix products, arithmetic and copies ran while one was open for 1% of the time, Pallas kernels for 5%

profile of v2, /device:TPU:1, one launch (start us, length us, event | category | flops | bytes accessed | tf_op | source)
XLA Modules:
  0.0 168.6 jit_solution(14374122464325953190)
XLA Ops:
  0.6 0.0 copy-start.4
  0.7 1.9 %shard_map.136 = bf16[2,288,256]{2,1,0:T(8,128)(2,1)} custom-call(bf16[2,512,256]{2,1,0:T(8,128)(2,1)} %left.5, bf16[2,512,256]{2,1,0:T(8,128)(2,1)} %right.5, bf16[2,512,128]{2,1,0:T(8,128)(2,1)} %hidden.3, bf16[2,512,128]{2,1,0:T(8,128)(2,1)} %grads.3), custom_call_target="tpu_custom_call" | custom-call | bytes 589824 | tf_op jit(solution)/shard_map/pallas_call | solution.py:117
  2.5 6.0 %collective-permute-start.1 = (bf16[2,288,256]{2,1,0:T(8,128)(2,1)}, bf16[2,288,256]{2,1,0:T(8,128)(2,1)}, u32[]{:S(2)}, u32[]{:S(2)}) collective-permute-start(bf16[2,288,256]{2,1,0:T(8,128)(2,1)} %shard_map.136), channel_id=1, source_target_pairs={{1,2},{2,1},{5,6},{6,5},{9,10},{10,9},{13,14},{14,13},{17,18},{18,... | collective-permute-start | bytes 884744 | tf_op jit(solution)/shard_map/ppermute | solution.py:553
  8.6 0.1 collective-permute-start
  8.7 1.7 %collective-permute-start.2 = (bf16[2,512,128]{2,1,0:T(8,128)(2,1)}, bf16[2,512,128]{2,1,0:T(8,128)(2,1)}, u32[]{:S(2)}, u32[]{:S(2)}) collective-permute-start(bf16[2,512,128]{2,1,0:T(8,128)(2,1)} %hidden.3), channel_id=1, source_target_pairs={{0,4},{8,12},{16,20},{24,28},{32,36},{40,44},{48,52},{56,60},{64,6... | collective-permute-start | bytes 786440 | tf_op jit(solution)/shard_map/ppermute | solution.py:553
  10.4 1.4 collective-permute-start.3
  11.7 1.1 copy.16
  12.8 0.0 copy-start.7
  12.8 0.0 copy-start.8
  12.8 0.7 copy.15
  13.6 0.0 copy-done.9
  13.6 0.1 pad_add_fusion.place.refs_0_
  13.7 3.2 %collective-permute-done.2.refs_2_ = bf16[2,512,128]{2,1,0:T(8,128)(2,1)} collective-permute-done((bf16[2,512,128]{2,1,0:T(8,128)(2,1)}, bf16[2,512,128]{2,1,0:T(8,128)(2,1)}, u32[]{:S(2)}, u32[]{:S(2)}) %collective-permute-start.2) | collective-permute-done | bytes 262176 | tf_op jit(solution)/shard_map/ppermute | solution.py:553
  16.9 0.0 collective-permute-done.3.refs_3_
  16.9 0.0 collective-permute-done.1.got_b
  16.9 0.0 collective-permute-done.got_a
  16.9 0.0 copy-done
  16.9 0.0 copy-done.1
  16.9 0.0 copy-done.7
  17.0 0.0 copy-done.8
  17.0 0.0 copy-start.3
  17.0 0.9 copy-done.3
  17.9 4.7 %shard_map.137 = (bf16[2,576,128]{2,1,0:T(8,128)(2,1)S(1)}, f32[2,544,128]{2,1,0:T(8,128)S(1)}, bf16[2,544,128]{2,1,0:T(8,128)(2,1)S(1)}, bf16[2,544,128]{2,1,0:T(8,128)(2,1)S(1)}, bf16[2,544,128]{2,1,0:T(8,128)(2,1)S(1)}) custom-call(s32[2]{0:T(128)S(1)} %pad_add_fusion.place.refs_0_, s32[2]{0:T(128)S(1)} %copy-done.8, s32[2,4]{1,0:T(2,128)S(1)} %copy-done.7, ...), custom_call_target="tpu_custom_call" | custom-call | flops 570425344 | bytes 3883056 | tf_op jit(solution)/shard_map/pallas_call | solution.py:46
  22.6 0.7 collective-permute-start.5
  23.3 7.1 %collective-permute-start.4 = (bf16[2,576,128]{2,1,0:T(8,128)(2,1)S(1)}, bf16[2,576,128]{2,1,0:T(8,128)(2,1)S(1)}, u32[]{:S(2)}, u32[]{:S(2)}) collective-permute-start(bf16[2,576,128]{2,1,0:T(8,128)(2,1)S(1)} %get-tuple-element.70.refs_4_.motion), channel_id=1, source_target_pairs={{0,4},{8,12},{16,20},{24,28},{32,36},{40,44},{48,52},{56,60},{64,6... | collective-permute-start | bytes 884744 | tf_op jit(solution)/shard_map/ppermute | solution.py:553
  30.4 0.0 collective-permute-done.5.refs_6_.motion_b
  30.4 5.5 %collective-permute-done.4.refs_5_.motion_a = bf16[2,576,128]{2,1,0:T(8,128)(2,1)S(1)} collective-permute-done((bf16[2,576,128]{2,1,0:T(8,128)(2,1)S(1)}, bf16[2,576,128]{2,1,0:T(8,128)(2,1)S(1)}, u32[]{:S(2)}, u32[]{:S(2)}) %collective-permute-start.4) | collective-permute-done | bytes 294944 | tf_op jit(solution)/shard_map/ppermute | solution.py:553
  35.8 5.5 %shard_map.138 = (bf16[2,544,128]{2,1,0:T(8,128)(2,1)S(1)}, f32[4,544,128]{2,1,0:T(8,128)S(1)}, f32[4,544,128]{2,1,0:T(8,128)S(1)}, bf16[4,544,128]{2,1,0:T(8,12...) custom-call(s32[2]{0:T(128)S(1)} %pad_add_fusion.place.refs_0_, ...), custom_call_target="tpu_custom_call" | custom-call | flops 3208642560 | bytes 7634952 | tf_op jit(solution)/shard_map/pallas_call | solution.py:46
  41.3 0.7 collective-permute-start.7
  42.0 5.6 %collective-permute-start.6 = (bf16[2,544,128]{2,1,0:T(8,128)(2,1)S(1)}, bf16[2,544,128]{2,1,0:T(8,128)(2,1)S(1)}, u32[]{:S(2)}, u32[]{:S(2)}) collective-permute-start(bf16[2,544,128]{2,1,0:T(8,128)(2,1)S(1)} %get-tuple-element.72.hidden.refs_5_), channel_id=1, source_target_pairs={{0,4},{8,12},{16,20},{24,28},{32,36},{40,44},{48,52},{56,60},{64,6... | collective-permute-start | bytes 835592 | tf_op jit(solution)/shard_map/ppermute | solution.py:553
  47.6 0.0 collective-permute-done.7.hidden_b.refs_7_
  47.6 4.6 %collective-permute-done.6.hidden_a.refs_6_ = bf16[2,544,128]{2,1,0:T(8,128)(2,1)S(1)} collective-permute-done((bf16[2,544,128]{2,1,0:T(8,128)(2,1)S(1)}, bf16[2,544,128]{2,1,0:T(8,128)(2,1)S(1)}, u32[]{:S(2)}, u32[]{:S(2)}) %collective-permute-start.6) | collective-permute-done | bytes 278560 | tf_op jit(solution)/shard_map/ppermute | solution.py:553
  52.2 5.1 %shard_map.139 = (f32[4,544,128]{2,1,0:T(8,128)S(1)}, f32[4,544,128]{2,1,0:T(8,128)S(1)}, bf16[4,544,128]{2,1,0:T(8,128)(2,1)S(1)}, bf16[2,544,128]{2,1,0:T(8,12...) custom-call(s32[2]{0:T(128)S(1)} %pad_add_fusion.place.refs_0_, ...), custom_call_target="tpu_custom_call" | custom-call | flops 3208642560 | bytes 7946248 | tf_op jit(solution)/shard_map/pallas_call | solution.py:46
  57.3 1.3 collective-permute-start.8
  58.6 0.7 collective-permute-start.9
  59.3 0.0 copy-start.6
  59.3 3.0 %shard_map.140 = (f32[2304,128]{1,0:T(8,128)S(1)}, f32[2304,128]{1,0:T(8,128)S(1)}) custom-call(s32[2]{0:T(128)S(1)} %pad_add_fusion.place.refs_0_, bf16[4,544,128]{2,1,0:T(8,128)(2,1)S(1)} %get-tuple-element.77.resets, bf16[2,544,128]{2,1,0:T(8,128)(2,1)S(1)} %get-tuple-element.72.hidden.refs_5_, ...), custom_call_target="tpu_custom_call" | custom-call | flops 1283457024 | bytes 5193736 | tf_op jit(solution)/shard_map/pallas_call | solution.py:46
  62.3 3.3 %collective-permute-done.8.refs_2_ = bf16[3,544,128]{2,1,0:T(8,128)(2,1)S(1)} collective-permute-done((bf16[3,544,128]{2,1,0:T(8,128)(2,1)S(1)}, bf16[3,544,128]{2,1,0:T(8,128)(2,1)S(1)}, u32[]{:S(2)}, u32[]{:S(2)}) %collective-permute-start.8) | collective-permute-done | bytes 417824 | tf_op jit(solution)/shard_map/ppermute | solution.py:558
  65.6 0.0 collective-permute-done.9.refs_3_
  65.6 0.0 copy-done.6
  65.6 4.2 %shard_map.141 = (bf16[2,544,128]{2,1,0:T(8,128)(2,1)S(1)}, f32[2,544,128]{2,1,0:T(8,128)S(1)}, f32[2,544,128]{2,1,0:T(8,128)S(1)}, bf16[2,544,128]{2,1,0:T(8,12...) custom-call(s32[2]{0:T(128)S(1)} %pad_add_fusion.place.refs_0_, ...), custom_call_target="tpu_custom_call" | custom-call | flops 2566914048 | bytes 11517960 | tf_op jit(solution)/shard_map/pallas_call | solution.py:46
  69.8 4.6 %collective-permute-start.10 = (bf16[3,544,128]{2,1,0:T(8,128)(2,1)S(1)}, bf16[3,544,128]{2,1,0:T(8,128)(2,1)S(1)}, u32[]{:S(2)}, u32[]{:S(2)}) collective-permute-start(bf16[3,544,128]{2,1,0:T(8,128)(2,1)S(1)} %get-tuple-element.90), channel_id=1, source_target_pairs={{0,4},{8,12},{16,20},{24,28},{32,36},{40,44},{48,52},{56,60},{64,6... | collective-permute-start | bytes 1253384 | tf_op jit(solution)/shard_map/ppermute | solution.py:558
  74.4 0.9 collective-permute-start.11
  75.3 4.0 %shard_map.142 = (f32[2304,128]{1,0:T(8,128)S(1)}, f32[2304,128]{1,0:T(8,128)S(1)}, f32[2304,128]{1,0:T(8,128)S(1)}) custom-call(s32[2]{0:T(128)S(1)} %pad_add_fusion.place.refs_0_, bf16[4,544,128]{2,1,0:T(8,128)(2,1)S(1)} %get-tuple-element.92.resets, bf16[4,544,128]{2,1,0:T(8,128)(2,1)S(1)} %get-tuple-element.71.refs_13_.older.hiddens, ...), custom_call_target="tpu_custom_call" | custom-call | flops 1925185536 | bytes 9568264 | tf_op jit(solution)/shard_map/pallas_call | solution.py:46
  79.4 0.5 collective-permute-done.10.grad_a
  79.9 0.0 collective-permute-done.11.grad_b
  79.9 4.8 %shard_map.143 = (bf16[2,544,128]{2,1,0:T(8,128)(2,1)S(1)}, bf16[2,512,128]{2,1,0:T(8,128)(2,1)}, f32[2,544,128]{2,1,0:T(8,128)S(1)}) custom-call(s32[2]{0:T(128)S(1)} %pad_add_fusion.place.refs_0_, bf16[2,544,128]{2,1,0:T(8,128)(2,1)S(1)} %get-tuple-element.89.cand_grads.grad_cand, bf16[3,544,128]{2,1,0:T(8,128)(2,1)S(1)} %collective-permute-done.10.grad_a, ...), custom_call_target="tpu_custom_call" | custom-call | flops 2566914048 | bytes 8159240 | tf_op jit(solution)/shard_map/pallas_call | solution.py:46
  84.6 4.0 %shard_map.144 = (bf16[2,512,256]{2,1,0:T(8,128)(2,1)}, bf16[2,192,256]{2,1,0:T(8,128)(2,1)S(1)}, f32[2,512,256]{2,1,0:T(8,128)S(1)}, f32[128,128]{1,0:T(8,128)S(1)}) custom-call(s32[2]{0:T(128)S(1)} %pad_add_fusion.place.refs_0_, s32[2]{0:T(128)S(1)} %copy-done.8, s32[2,4]{1,0:T(2,128)S(1)} %copy-done.7, bf16[2,512,256]{2,1,0:T(8,128)(2,1)S(1)} %copy-done, ...), custom_call_target="tpu_custom_call" | custom-call | flops 855638016 | bytes 4898864 | tf_op jit(solution)/shard_map/pallas_call | solution.py:46
  88.7 2.3 %shard_map.145 = (bf16[3584,128]{1,0:T(8,128)(2,1)S(1)}, bf16[3584,128]{1,0:T(8,128)(2,1)S(1)}) custom-call(s32[2]{0:T(128)S(1)} %pad_add_fusion.place.refs_0_, bf16[4,544,128]{2,1,0:T(8,128)(2,1)S(1)} %get-tuple-element.71.refs_13_.older.hiddens, bf16[2,576,128]{2,1,0:T(8,128)(2,1)S(1)} %get-tuple-element.70.refs_4_.motion, ...), custom_call_target="tpu_custom_call" | custom-call | flops 641728512 | bytes 7159816 | tf_op jit(solution)/shard_map/pallas_call | solution.py:46
  90.9 5.2 %collective-permute-start.12 = (bf16[3584,128]{1,0:T(8,128)(2,1)S(1)}, bf16[3584,128]{1,0:T(8,128)(2,1)S(1)}, u32[]{:S(2)}, u32[]{:S(2)}) collective-permute-start(bf16[3584,128]{1,0:T(8,128)(2,1)S(1)} %get-tuple-element.113), channel_id=1, source_target_pairs={{0,1},{1,0},{2,3},{3,2},{4,5},{5,4},{6,7},{7,6},{8,9},{9,8},{10,11... | collective-permute-start | bytes 2752520 | tf_op jit(solution)/shard_map/ppermute | solution.py:566
  96.2 3.2 %collective-permute-start.14 = (bf16[2,192,256]{2,1,0:T(8,128)(2,1)S(1)}, bf16[2,192,256]{2,1,0:T(8,128)(2,1)S(1)}, u32[]{:S(2)}, u32[]{:S(2)}) collective-permute-start(bf16[2,192,256]{2,1,0:T(8,128)(2,1)S(1)} %get-tuple-element.116), channel_id=1, source_target_pairs={{1,2},{2,1},{5,6},{6,5},{9,10},{10,9},{13,14},{14,13},{17,18},{18,... | collective-permute-start | bytes 589832 | tf_op jit(solution)/shard_map/ppermute | solution.py:553
  99.4 0.1 collective-permute-start.13
  99.5 5.2 %collective-permute-done.14.back_b = bf16[2,192,256]{2,1,0:T(8,128)(2,1)S(1)} collective-permute-done((bf16[2,192,256]{2,1,0:T(8,128)(2,1)S(1)}, bf16[2,192,256]{2,1,0:T(8,128)(2,1)S(1)}, u32[]{:S(2)}, u32[]{:S(2)}) %collective-permute-start.14) | collective-permute-done | bytes 196640 | tf_op jit(solution)/shard_map/ppermute | solution.py:553
  104.7 0.0 collective-permute-done.13.back_a
  104.7 1.4 shard_map.146
  106.1 0.0 collective-permute-done.12
  106.1 0.2 add_convert_fusion
  106.3 31.7 %all_to_all.10 = bf16[64,56,128]{2,1,0:T(8,128)(2,1)S(1)} all-to-all(bf16[64,56,128]{2,1,0:T(8,128)(2,1)S(1)} %bitcast.21), channel_id=1, replica_groups={{0,2,4,6,8,10,12,14,16,18,20,22,24,26,28,30,32,34,36,38,40,42,44,46,48,..., dimensions={0} | all-to-all | bytes 1835008 | tf_op jit(solution)/shard_map/all_to_all | solution.py:569
  138.1 0.2 reduce_sum.12
  138.2 0.1 broadcast_in_dim.2
  138.4 19.3 %all_to_all.11 = bf16[64,56,128]{2,1,0:T(8,128)(2,1)S(1)} all-to-all(bf16[64,56,128]{2,1,0:T(8,128)(2,1)S(1)} %broadcast_in_dim.2), channel_id=1, replica_groups={{0,2,4,6,8,10,12,14,16,18,20,22,24,26,28,30,32,34,36,38,40,42,44,46,48,..., dimensions={0} | all-to-all | bytes 1835008 | tf_op jit(solution)/shard_map/all_to_all | solution.py:572
  157.7 4.2 %collective-permute-start.15 = (bf16[64,56,128]{2,1,0:T(8,128)(2,1)S(1)}, bf16[64,56,128]{2,1,0:T(8,128)(2,1)S(1)}, u32[]{:S(2)}, u32[]{:S(2)}) collective-permute-start(bf16[64,56,128]{2,1,0:T(8,128)(2,1)S(1)} %all_to_all.11), channel_id=1, source_target_pairs={{0,1},{1,0},{2,3},{3,2},{4,5},{5,4},{6,7},{7,6},{8,9},{9,8},{10,11... | collective-permute-start | bytes 2752520 | tf_op jit(solution)/shard_map/ppermute | solution.py:573
  161.9 2.1 %collective-permute-done.15 = bf16[64,56,128]{2,1,0:T(8,128)(2,1)S(1)} collective-permute-done((bf16[64,56,128]{2,1,0:T(8,128)(2,1)S(1)}, bf16[64,56,128]{2,1,0:T(8,128)(2,1)S(1)}, u32[]{:S(2)}, u32[]{:S(2)}) %collective-permute-start.15) | collective-permute-done | bytes 917536 | tf_op jit(solution)/shard_map/ppermute | solution.py:573
  164.0 4.6 %shard_map.147 = (f32[2304,256]{1,0:T(8,128)}, f32[2304,128]{1,0:T(8,128)}, f32[36,128]{1,0:T(8,128)}) custom-call(s32[2]{0:T(128)S(1)} %pad_add_fusion.place.refs_0_, bf16[3584,128]{1,0:T(8,128)(2,1)S(1)} %bitcast.13, bf16[3584,128]{1,0:T(8,128)(2,1)S(1)} %bitcast.17), custom_call_target="tpu_custom_call" | custom-call | bytes 5308416 | tf_op jit(solution)/shard_map/pallas_call | solution.py:150
  (9 shorter events, 0.0 us)
Async XLA Ops:
  0.6 11.1 %copy-start.4 = (bf16[2304,128]{1,0:T(8,128)(2,1)S(1)}, bf16[2304,128]{1,0:T(8,128)(2,1)}, u32[]{:S(2)}) copy-start(bf16[2304,128]{1,0:T(8,128)(2,1)} %cand_w.1) | copy-start | bytes 1769476
  0.6 12.2 %copy-start.2 = (bf16[2304,256]{1,0:T(8,128)(2,1)S(1)}, bf16[2304,256]{1,0:T(8,128)(2,1)}, u32[]{:S(2)}) copy-start(bf16[2304,256]{1,0:T(8,128)(2,1)} %gate_w.1) | copy-start | bytes 3538948
  2.5 14.4 %collective-permute-start.1 = (bf16[2,288,256]{2,1,0:T(8,128)(2,1)}, bf16[2,288,256]{2,1,0:T(8,128)(2,1)}, u32[]{:S(2)}, u32[]{:S(2)}) collective-permute-start(bf16[2,288,256]{2,1,0:T(8,128)(2,1)} %shard_map.136), channel_id=1, source_target_pairs={{1,2},{2,1},{5,6},{6,5},{9,10},{10,9},{13,14},{14,13},{17,18},{18,... | collective-permute-start | bytes 884744 | tf_op jit(solution)/shard_map/ppermute | solution.py:553
  8.6 8.4 %collective-permute-start = (bf16[2,288,256]{2,1,0:T(8,128)(2,1)}, bf16[2,288,256]{2,1,0:T(8,128)(2,1)}, u32[]{:S(2)}, u32[]{:S(2)}) collective-permute-start(bf16[2,288,256]{2,1,0:T(8,128)(2,1)} %shard_map.136), channel_id=1, source_target_pairs={{0,1},{2,3},{1,0},{3,2},{4,5},{6,7},{5,4},{7,6},{8,9},{10,11},{9,8... | collective-permute-start | bytes 884744 | tf_op jit(solution)/shard_map/ppermute | solution.py:553
  8.7 8.2 %collective-permute-start.2 = (bf16[2,512,128]{2,1,0:T(8,128)(2,1)}, bf16[2,512,128]{2,1,0:T(8,128)(2,1)}, u32[]{:S(2)}, u32[]{:S(2)}) collective-permute-start(bf16[2,512,128]{2,1,0:T(8,128)(2,1)} %hidden.3), channel_id=1, source_target_pairs={{0,4},{8,12},{16,20},{24,28},{32,36},{40,44},{48,52},{56,60},{64,6... | collective-permute-start | bytes 786440 | tf_op jit(solution)/shard_map/ppermute | solution.py:553
  10.4 6.5 %collective-permute-start.3 = (bf16[2,512,128]{2,1,0:T(8,128)(2,1)}, bf16[2,512,128]{2,1,0:T(8,128)(2,1)}, u32[]{:S(2)}, u32[]{:S(2)}) collective-permute-start(bf16[2,512,128]{2,1,0:T(8,128)(2,1)} %hidden.3), channel_id=1, source_target_pairs={{4,8},{12,16},{20,24},{28,32},{36,40},{44,48},{52,56},{60,64},{68,... | collective-permute-start | bytes 786440 | tf_op jit(solution)/shard_map/ppermute | solution.py:553
  12.8 0.8 copy-start.9
  12.8 4.1 %copy-start = (bf16[2,512,256]{2,1,0:T(8,128)(2,1)S(1)}, bf16[2,512,256]{2,1,0:T(8,128)(2,1)}, u32[]{:S(2)}) copy-start(bf16[2,512,256]{2,1,0:T(8,128)(2,1)} %left.5) | copy-start | bytes 1572868
  12.8 4.1 %copy-start.1 = (bf16[2,512,256]{2,1,0:T(8,128)(2,1)S(1)}, bf16[2,512,256]{2,1,0:T(8,128)(2,1)}, u32[]{:S(2)}) copy-start(bf16[2,512,256]{2,1,0:T(8,128)(2,1)} %right.5) | copy-start | bytes 1572868
  12.8 4.1 %copy-start.7 = (s32[2,4]{1,0:T(2,128)S(1)}, s32[2,4]{1,0:T(2,128)}, u32[]{:S(2)}) copy-start(s32[2,4]{1,0:T(2,128)} %offsets.3) | copy-start | bytes 100
  12.8 4.1 %copy-start.8 = (s32[2]{0:T(128)S(1)}, s32[2]{0:T(128)}, u32[]{:S(2)}) copy-start(s32[2]{0:T(128)} %disparity.3) | copy-start | bytes 28
  17.0 1.0 copy-start.3
  17.9 17.9 %copy-start.5 = (bf16[2304,128]{1,0:T(8,128)(2,1)S(1)}, bf16[2304,128]{1,0:T(8,128)(2,1)}, u32[]{:S(2)}) copy-start(bf16[2304,128]{1,0:T(8,128)(2,1)} %cand_w.1) | copy-start | bytes 1769476
  22.6 7.8 %collective-permute-start.5 = (bf16[2,576,128]{2,1,0:T(8,128)(2,1)S(1)}, bf16[2,576,128]{2,1,0:T(8,128)(2,1)S(1)}, u32[]{:S(2)}, u32[]{:S(2)}) collective-permute-start(bf16[2,576,128]{2,1,0:T(8,128)(2,1)S(1)} %get-tuple-element.70.refs_4_.motion), channel_id=1, source_target_pairs={{4,8},{12,16},{20,24},{28,32},{36,40},{44,48},{52,56},{60,64},{68,... | collective-permute-start | bytes 884744 | tf_op jit(solution)/shard_map/ppermute | solution.py:553
  23.3 12.6 %collective-permute-start.4 = (bf16[2,576,128]{2,1,0:T(8,128)(2,1)S(1)}, bf16[2,576,128]{2,1,0:T(8,128)(2,1)S(1)}, u32[]{:S(2)}, u32[]{:S(2)}) collective-permute-start(bf16[2,576,128]{2,1,0:T(8,128)(2,1)S(1)} %get-tuple-element.70.refs_4_.motion), channel_id=1, source_target_pairs={{0,4},{8,12},{16,20},{24,28},{32,36},{40,44},{48,52},{56,60},{64,6... | collective-permute-start | bytes 884744 | tf_op jit(solution)/shard_map/ppermute | solution.py:553
  41.3 6.3 %collective-permute-start.7 = (bf16[2,544,128]{2,1,0:T(8,128)(2,1)S(1)}, bf16[2,544,128]{2,1,0:T(8,128)(2,1)S(1)}, u32[]{:S(2)}, u32[]{:S(2)}) collective-permute-start(bf16[2,544,128]{2,1,0:T(8,128)(2,1)S(1)} %get-tuple-element.72.hidden.refs_5_), channel_id=1, source_target_pairs={{4,8},{12,16},{20,24},{28,32},{36,40},{44,48},{52,56},{60,64},{68,... | collective-permute-start | bytes 835592 | tf_op jit(solution)/shard_map/ppermute | solution.py:553
  42.0 10.2 %collective-permute-start.6 = (bf16[2,544,128]{2,1,0:T(8,128)(2,1)S(1)}, bf16[2,544,128]{2,1,0:T(8,128)(2,1)S(1)}, u32[]{:S(2)}, u32[]{:S(2)}) collective-permute-start(bf16[2,544,128]{2,1,0:T(8,128)(2,1)S(1)} %get-tuple-element.72.hidden.refs_5_), channel_id=1, source_target_pairs={{0,4},{8,12},{16,20},{24,28},{32,36},{40,44},{48,52},{56,60},{64,6... | collective-permute-start | bytes 835592 | tf_op jit(solution)/shard_map/ppermute | solution.py:553
  57.3 8.2 %collective-permute-start.8 = (bf16[3,544,128]{2,1,0:T(8,128)(2,1)S(1)}, bf16[3,544,128]{2,1,0:T(8,128)(2,1)S(1)}, u32[]{:S(2)}, u32[]{:S(2)}) collective-permute-start(bf16[3,544,128]{2,1,0:T(8,128)(2,1)S(1)} %get-tuple-element.75), channel_id=1, source_target_pairs={{0,4},{8,12},{16,20},{24,28},{32,36},{40,44},{48,52},{56,60},{64,6... | collective-permute-start | bytes 1253384 | tf_op jit(solution)/shard_map/ppermute | solution.py:558
  58.6 7.0 %collective-permute-start.9 = (bf16[3,544,128]{2,1,0:T(8,128)(2,1)S(1)}, bf16[3,544,128]{2,1,0:T(8,128)(2,1)S(1)}, u32[]{:S(2)}, u32[]{:S(2)}) collective-permute-start(bf16[3,544,128]{2,1,0:T(8,128)(2,1)S(1)} %get-tuple-element.76), channel_id=1, source_target_pairs={{4,8},{12,16},{20,24},{28,32},{36,40},{44,48},{52,56},{60,64},{68,... | collective-permute-start | bytes 1253384 | tf_op jit(solution)/shard_map/ppermute | solution.py:558
  59.3 6.3 %copy-start.6 = (bf16[3,3,256,128]{2,3,1,0:T(8,128)(2,1)S(1)}, bf16[3,3,256,128]{2,3,1,0:T(8,128)(2,1)}, u32[]{:S(2)}) copy-start(bf16[3,3,256,128]{2,3,1,0:T(8,128)(2,1)} %copy.16) | copy-start | bytes 1769476
  69.8 10.0 %collective-permute-start.10 = (bf16[3,544,128]{2,1,0:T(8,128)(2,1)S(1)}, bf16[3,544,128]{2,1,0:T(8,128)(2,1)S(1)}, u32[]{:S(2)}, u32[]{:S(2)}) collective-permute-start(bf16[3,544,128]{2,1,0:T(8,128)(2,1)S(1)} %get-tuple-element.90), channel_id=1, source_target_pairs={{0,4},{8,12},{16,20},{24,28},{32,36},{40,44},{48,52},{56,60},{64,6... | collective-permute-start | bytes 1253384 | tf_op jit(solution)/shard_map/ppermute | solution.py:558
  74.4 5.4 %collective-permute-start.11 = (bf16[3,544,128]{2,1,0:T(8,128)(2,1)S(1)}, bf16[3,544,128]{2,1,0:T(8,128)(2,1)S(1)}, u32[]{:S(2)}, u32[]{:S(2)}) collective-permute-start(bf16[3,544,128]{2,1,0:T(8,128)(2,1)S(1)} %get-tuple-element.91), channel_id=1, source_target_pairs={{4,8},{12,16},{20,24},{28,32},{36,40},{44,48},{52,56},{60,64},{68,... | collective-permute-start | bytes 1253384 | tf_op jit(solution)/shard_map/ppermute | solution.py:558
  90.9 15.2 %collective-permute-start.12 = (bf16[3584,128]{1,0:T(8,128)(2,1)S(1)}, bf16[3584,128]{1,0:T(8,128)(2,1)S(1)}, u32[]{:S(2)}, u32[]{:S(2)}) collective-permute-start(bf16[3584,128]{1,0:T(8,128)(2,1)S(1)} %get-tuple-element.113), channel_id=1, source_target_pairs={{0,1},{1,0},{2,3},{3,2},{4,5},{5,4},{6,7},{7,6},{8,9},{9,8},{10,11... | collective-permute-start | bytes 2752520 | tf_op jit(solution)/shard_map/ppermute | solution.py:566
  96.2 8.5 %collective-permute-start.14 = (bf16[2,192,256]{2,1,0:T(8,128)(2,1)S(1)}, bf16[2,192,256]{2,1,0:T(8,128)(2,1)S(1)}, u32[]{:S(2)}, u32[]{:S(2)}) collective-permute-start(bf16[2,192,256]{2,1,0:T(8,128)(2,1)S(1)} %get-tuple-element.116), channel_id=1, source_target_pairs={{1,2},{2,1},{5,6},{6,5},{9,10},{10,9},{13,14},{14,13},{17,18},{18,... | collective-permute-start | bytes 589832 | tf_op jit(solution)/shard_map/ppermute | solution.py:553
  99.4 5.3 %collective-permute-start.13 = (bf16[2,192,256]{2,1,0:T(8,128)(2,1)S(1)}, bf16[2,192,256]{2,1,0:T(8,128)(2,1)S(1)}, u32[]{:S(2)}, u32[]{:S(2)}) collective-permute-start(bf16[2,192,256]{2,1,0:T(8,128)(2,1)S(1)} %get-tuple-element.116), channel_id=1, source_target_pairs={{0,1},{2,3},{1,0},{3,2},{4,5},{6,7},{5,4},{7,6},{8,9},{10,11},{9,8... | collective-permute-start | bytes 589832 | tf_op jit(solution)/shard_map/ppermute | solution.py:553
  157.7 6.3 %collective-permute-start.15 = (bf16[64,56,128]{2,1,0:T(8,128)(2,1)S(1)}, bf16[64,56,128]{2,1,0:T(8,128)(2,1)S(1)}, u32[]{:S(2)}, u32[]{:S(2)}) collective-permute-start(bf16[64,56,128]{2,1,0:T(8,128)(2,1)S(1)} %all_to_all.11), channel_id=1, source_target_pairs={{0,1},{1,0},{2,3},{3,2},{4,5},{5,4},{6,7},{7,6},{8,9},{9,8},{10,11... | collective-permute-start | bytes 2752520 | tf_op jit(solution)/shard_map/ppermute | solution.py:573

commit v3 on v2

--- a/solution.py
+++ b/solution.py
@@ -125,41 +125,51 @@
     )(left, right, hidden, grads)
 
 
-def unpack_kernel(count, scale, place, half, other, gate, cand, motion):
+def spread_half(core, half, scale, gate, cand, gate_part, cand_part, sems):
+    depth = gate_part.shape[0]
+    count = cand_part.shape[0]
+    block = depth // 4
+    lanes = pl.ds(pl.multiple_of(core * LANES, LANES), LANES)
+    copies = []
+    for number in range(4):
+        here = pl.ds(number * block, block)
+        gate_part[here] = half[here].astype(F32) * scale
+        copies.append(pltpu.make_async_copy(gate_part.at[here], gate.at[here, lanes], sems.at[number]))
+        copies[-1].start()
+    cand_part[...] = half[depth : depth + count].astype(F32) * scale
+    there = pl.ds(pl.multiple_of(core * count, LANES), count)
+    copies.append(pltpu.make_async_copy(cand_part, cand.at[there], sems.at[4]))
+    copies[-1].start()
+    for copy in copies:
+        copy.wait()
+
+
+def own_half_kernel(scale, place, half, gate, cand, gate_part, cand_part, sems):
+    spread_half(place[1] % 2, half, scale, gate, cand, gate_part, cand_part, sems)
+
+
+def other_half_kernel(scale, place, half, other, gate_in, cand_in, motion, gate, cand, gate_part, cand_part, sems):
     core = place[1] % 2
-    block = gate.shape[0]
-    per_half = half.shape[0] // block
-    step = pl.program_id(0)
-
-    def part(number):
-        start = pl.multiple_of((number % per_half) * block, block)
-        mine = half[pl.ds(start, block)]
-        theirs = other[pl.ds(start, block)]
-        return jnp.where(number // per_half == core, mine, theirs).astype(F32) * scale
-
-    gate[:, :LANES] = part(step)
-    gate[:, LANES:] = part(step + count)
-    cand[...] = part(step + 2 * count)
-    motion[...] = part(3 * count)[: motion.shape[0]]
-
-
-def unpacked(place, half, other, depth, feats_count, scale):
-    block = 256
-    count = depth // block
-    whole = lambda i: (0, 0)
+    start = gate_part.shape[0] + cand_part.shape[0]
+    rows = pl.ds(start, motion.shape[0])
+    motion[...] = jnp.where(core == 0, half[rows], other[rows]).astype(F32) * scale
+    spread_half(1 - core, other, scale, gate, cand, gate_part, cand_part, sems)
+
+
+def half_call(body, place, arrays, outs, depth, aliases):
+    anywhere = pl.BlockSpec(memory_space=pltpu.HBM)
     return pl.pallas_call(
-        lambda *refs: unpack_kernel(count, scale, *refs),
-        grid=(count,),
-        out_shape=[array((depth, 2 * LANES), F32), array((depth, LANES), F32), array((feats_count, LANES), F32)],
-        in_specs=[SMEM, pl.BlockSpec(half.shape, whole), pl.BlockSpec(half.shape, whole)],
-        out_specs=[
-            pl.BlockSpec((block, 2 * LANES), lambda i: (i, 0)),
-            pl.BlockSpec((block, LANES), lambda i: (i, 0)),
-            pl.BlockSpec((feats_count, LANES), whole),
+        body,
+        out_shape=outs,
+        in_specs=[SMEM] + [VMEM] * (len(arrays) - len(aliases)) + [anywhere] * len(aliases),
+        out_specs=[VMEM] * (len(outs) - 2) + [anywhere] * 2,
+        scratch_shapes=[
+            pltpu.VMEM((depth, LANES), F32), pltpu.VMEM((depth // 2, LANES), F32), pltpu.SemaphoreType.DMA((5,))
         ],
+        input_output_aliases=aliases,
         compiler_params=pltpu.CompilerParams(vmem_limit_bytes=12 * 2**20),
-        cost_estimate=pl.CostEstimate(flops=0, bytes_accessed=6 * depth * 384, transcendentals=0),
-    )(place, half, other)
+        cost_estimate=pl.CostEstimate(flops=0, bytes_accessed=6 * depth * LANES, transcendentals=0),
+    )(place, *arrays)
 
 
 def motion_kernel(place, disparity, offsets, left, right, got_a, got_b, weight, hidden, grads,
@@ -376,8 +386,8 @@
 
 
 def first_back_kernel(place, grad_cand, grad_a, grad_b, grad_update, hiddens, reset,
-                      cand_wt, gate_wt, update, grad_state, motion_so_far,
-                      grad_reset, grad_first, grad_motion, cand_taps, gate_taps, inner):
+                      cand_wt, gate_wt, update, grad_state, motion_so_far, pre, feats, weight,
+                      grad_reset, grad_first, grad_feats, motion_w, cand_taps, gate_taps, inner, grad_motion):
     def finish(row, start, here, terms):
         gate = update[row + 1, here]
         grad = grad_state[row, here] * (1.0 - gate) + terms
@@ -387,6 +397,16 @@
 
     back_step(place, grad_cand, grad_a, grad_b, grad_update, hiddens, reset, cand_wt, gate_wt,
               grad_reset, cand_taps, gate_taps, inner, grad_motion, finish)
+    inner_cols = slice(HALO, HALO + grad_feats.shape[1])
+    total = jnp.zeros((LANES, LANES), F32)
+    for row in range(2):
+        value = pre[row, inner_cols]
+        gate = jax.nn.sigmoid(value)
+        slope = gate * (1.0 + value * (1.0 - gate))
+        grad_pre = (grad_motion[row, inner_cols] * slope).astype(BF16)
+        total = total + dot_tn(feats[row, inner_cols], grad_pre)
+        grad_feats[row] = dot_nt(grad_pre, weight[...])
+    motion_w[...] = total
 
 
 def load_pixels(odd, pixels, hiddens, motion, motion_a, motion_b):
@@ -481,19 +501,21 @@
     load_pixels(odd, pixels, [hiddens[row] for row in range(4)], motion, motion_a, motion_b)
     load_grads(taps, reset_grads)
     rows = cand_sum.shape[0]
+    split = rows // 2
+    last = rows + split
 
     def finish(start, value):
-        parts[rows + start : rows + start + 2 * LANES] = (value + reset_sum[pl.ds(start, 2 * LANES)]).astype(BF16)
+        parts[1, start : start + 2 * LANES] = (value + reset_sum[pl.ds(start, 2 * LANES)]).astype(BF16)
 
     weight_products(pixels, taps, taps.shape[0] // 2, LANES, finish)
-    parts[0:rows] = update_sum[...].astype(BF16)
-    parts[2 * rows : 3 * rows] = cand_sum[...].astype(BF16)
-    parts[3 * rows : 3 * rows + LANES] = motion_w[...].astype(BF16)
-    parts[3 * rows + LANES :] = jnp.zeros((parts.shape[0] - 3 * rows - LANES, LANES), BF16)
-    half = parts.shape[0] // 2
+    parts[0, 0:rows] = update_sum[...].astype(BF16)
+    for half in range(2):
+        parts[half, rows:last] = cand_sum[half * split : (half + 1) * split].astype(BF16)
+    parts[0, last:] = motion_w[...].astype(BF16)
+    parts[1, last:] = jnp.zeros((parts.shape[1] - last, LANES), BF16)
     core = place[1] % 2
-    kept[...] = parts[pl.ds(pl.multiple_of(core * half, LANES), half)]
-    given[...] = parts[pl.ds(pl.multiple_of((1 - core) * half, LANES), half)]
+    kept[...] = parts[core]
+    given[...] = parts[1 - core]
 
 
 def right_kernel(place, own, back_a, back_b, grad_right):
@@ -505,8 +527,8 @@
         grad_right[row, split:] = (own[row, split:] + returned).astype(BF16)
 
 
-def band_back_kernel(place, disparity, offsets, left, right, got_a, got_b, weight, grad_motion, pre, feats,
-                     grad_left, back, own, motion_w, window, grad_window):
+def band_back_kernel(place, disparity, offsets, left, right, got_a, got_b, grad_feats,
+                     grad_left, back, own, window, grad_window):
     odd = place[1] % 2 == 1
     cols = left.shape[1]
     block = cols // 2
@@ -514,31 +536,22 @@
     scaling = 1.0 / math.sqrt(left.shape[2])
     position = DISP - lax.broadcasted_iota(jnp.int32, (span, LANES), 0)
     valid = (position >= 0) & (position < DISP)
-    inner = slice(HALO, HALO + cols)
-    total_w = jnp.zeros((LANES, LANES), F32)
     for row in range(2):
         from_left = sides(odd, got_a[row], got_b[row])[0]
         window[0:DISP] = from_left[HALO : HALO + DISP]
         window[DISP : DISP + cols] = right[row]
         window[DISP + cols :] = jnp.zeros((window.shape[0] - DISP - cols, window.shape[1]), BF16)
         grad_window[...] = jnp.zeros(grad_window.shape, F32)
-        value = pre[row, inner]
-        gate = jax.nn.sigmoid(value)
-        slope = gate * (1.0 + value * (1.0 - gate))
-        grad_pre = (grad_motion[row, inner] * slope).astype(BF16)
-        total_w = total_w + dot_tn(feats[row, inner], grad_pre)
-        grad_feats = dot_nt(grad_pre, weight[...])
         table = lookup_rows(position, valid, disparity, offsets, row)
         for part in range(2):
             here = slice(part * block, (part + 1) * block)
             there = slice(part * block, part * block + span)
-            band = split_dot(grad_feats[here], table, dot_nt)
+            band = split_dot(grad_feats[row, here], table, dot_nt)
             scores = (pltpu.roll(band, 0, 1, stride=1, stride_axis=0) * scaling).astype(BF16)
             grad_left[row, here] = dot(scores, window[there]).astype(BF16)
             grad_window[there] += dot_tn(scores, left[row, here])
         back[row] = grad_window[0:DISP].astype(BF16)
         own[row] = grad_window[DISP : DISP + cols]
-    motion_w[...] = total_w
 
 
 def pairings(count):
@@ -558,20 +571,27 @@
     return lax.ppermute(value_a, axis, first), lax.ppermute(value_b, axis, second)
 
 
-def summed_everywhere(kept, given, axes, meanwhile):
-    cols_count = lax.axis_size("cols")
-    devices = lax.axis_size("rows") * cols_count
-    swap = [(i, i ^ 1) for i in range(cols_count)]
-    groups = [[i for i in range(devices) if i % 2 == c] for c in range(2)]
-    got = lax.ppermute(given, "cols", swap)
-    got, meanwhile = lax.optimization_barrier((got, meanwhile))
-    half = (kept.astype(F32) + got.astype(F32)).astype(BF16).reshape(devices // 2, -1, LANES)
-    pieces = lax.all_to_all(half, axes, 0, 0, tiled=True, axis_index_groups=groups)
+def core_groups():
+    devices = lax.axis_size("rows") * lax.axis_size("cols")
+    return [[i for i in range(devices) if i % 2 == c] for c in range(2)]
+
+
+def shared_out(kept, given, axes):
+    got = swapped(given)
+    half = (kept.astype(F32) + got.astype(F32)).astype(BF16)
+    half = half.reshape(len(core_groups()[0]), -1, LANES)
+    return lax.all_to_all(half, axes, 0, 0, tiled=True, axis_index_groups=core_groups())
+
+
+def gathered(pieces, axes):
     piece = jnp.sum(pieces.astype(F32), axis=0).astype(BF16)
     spread = jnp.broadcast_to(piece[None], pieces.shape)
-    half = lax.all_to_all(spread, axes, 0, 0, tiled=True, axis_index_groups=groups)
-    other = lax.ppermute(half, "cols", swap)
-    return half.reshape(-1, LANES), other.reshape(-1, LANES), meanwhile
+    half = lax.all_to_all(spread, axes, 0, 0, tiled=True, axis_index_groups=core_groups())
+    return half.reshape(-1, LANES)
+
+
+def swapped(value):
+    return lax.ppermute(value, "cols", [(i, i ^ 1) for i in range(lax.axis_size("cols"))])
 
 
 def on_device(
@@ -599,9 +619,7 @@
     motion_w = jnp.pad(motion_weight, ((0, LANES - feats_count), (0, 0)))
     gate_wt = jnp.transpose(gate_weight.reshape(3, 3, 2 * state, 2 * state), (0, 1, 3, 2)).reshape(-1, 2 * state)
     cand_wt = jnp.transpose(cand_weight.reshape(3, 3, 2 * state, state), (0, 1, 3, 2)).reshape(-1, 2 * state)
-    motion_w, gate_wt, cand_wt, init_a, init_b = lax.optimization_barrier(
-        (motion_w, gate_wt, cand_wt, init_a, init_b)
-    )
+    motion_w, gate_wt, cand_wt = lax.optimization_barrier((motion_w, gate_wt, cand_wt))
 
     field = lambda count, dtype: array((count, wide, LANES), dtype)
     band_flops = 2 * rows * wide * 512 * channels
@@ -613,6 +631,7 @@
         [pltpu.VMEM((wide, channels), BF16), pltpu.VMEM((768, channels), BF16), pltpu.VMEM((832, channels), BF16)],
         2 * band_flops,
     )
+    motion, init_a, init_b = lax.optimization_barrier((motion, init_a, init_b))
     motions = (motion, *exchanged(motion, "rows"))
     unit = 2 * wide * 9 * 2 * state * state
     fields = [pltpu.VMEM((6, wide, 6 * LANES), BF16), pltpu.VMEM((4, wide, 6 * LANES), BF16)]
@@ -675,44 +694,51 @@
     got_a, got_b, cand_sum, update_sum, reset_sum = lax.optimization_barrier(
         (got_a, got_b, cand_sum, update_sum, reset_sum)
     )
-    grad_reset_0, grad_first, grad_motion = kernel_call(
+    grad_reset_0, grad_first, grad_feats, motion_sum = kernel_call(
         first_back_kernel,
-        [field(2, BF16), array((2, cols, LANES), BF16), field(2, F32)],
+        [field(2, BF16), array((2, cols, LANES), BF16), array((2, cols, LANES), F32), array((LANES, LANES), F32)],
         [place, grad_cand_0, got_a, got_b, grad_update_0, hiddens_0, reset_0, cand_wt, gate_wt,
-         update_0, grad_state, grad_motion_1],
+         update_0, grad_state, grad_motion_1, motion_pre, feats, motion_w],
         1,
-        back_scratch,
+        back_scratch + [pltpu.VMEM((2, wide, LANES), F32)],
         8 * unit,
     )
-    grad_left, back, own, motion_sum = kernel_call(
-        band_back_kernel,
-        [array((2, cols, channels), BF16), array((2, DISP, channels), BF16), array((2, cols, channels), F32),
-         array((LANES, LANES), F32)],
-        [place, disp_init, level_offset, fmap_left, fmap_right, maps_a, maps_b, motion_w, grad_motion, motion_pre, feats],
-        3,
-        [pltpu.VMEM((768, channels), BF16), pltpu.VMEM((768, channels), F32)],
-        3 * band_flops,
-    )
-    back_a, back_b = exchanged(back, "cols")
-    devices = rows_axis * cols_axis
-    total = devices * CHUNK_ROWS
+    total = rows_axis * cols_axis * CHUNK_ROWS
     kept, given = kernel_call(
         last_weights_kernel,
         [array((total // 2, LANES), BF16), array((total // 2, LANES), BF16)],
         [place, hiddens_0, *motions, grad_reset_0, reset_sum, update_sum, cand_sum, motion_sum],
         1,
-        [pixels, taps, pltpu.VMEM((total, LANES), BF16)],
+        [pixels, taps, pltpu.VMEM((2, total // 2, LANES), BF16)],
         2 * unit,
     )
+    grad_left, back, own = kernel_call(
+        band_back_kernel,
+        [array((2, cols, channels), BF16), array((2, DISP, channels), BF16), array((2, cols, channels), F32)],
+        [place, disp_init, level_offset, fmap_left, fmap_right, maps_a, maps_b, grad_feats],
+        3,
+        [pltpu.VMEM((768, channels), BF16), pltpu.VMEM((768, channels), F32)],
+        3 * band_flops,
+    )
+    pieces = shared_out(kept, given, ("rows", "cols"))
+    pieces, grad_left, back, own = lax.optimization_barrier((pieces, grad_left, back, own))
+    back_a, back_b = exchanged(back, "cols")
     (grad_right,) = kernel_call(
         right_kernel, [array((2, cols, channels), BF16)], [place, own, back_a, back_b], 1, [], 0
     )
-    half, other, (grad_left, grad_right, grad_first) = summed_everywhere(
-        kept, given, ("rows", "cols"), (grad_left, grad_right, grad_first)
-    )
+    half = gathered(pieces, ("rows", "cols"))
+    half, grad_right = lax.optimization_barrier((half, grad_right))
     normaliser = 1.0 / math.sqrt(rows * rows_axis * cols * cols_axis)
-    grad_gate_w, grad_cand_w, grad_motion_w = unpacked(
-        place, half, other, cand_weight.shape[0], feats_count, normaliser
+    other = swapped(half)
+    depth = cand_weight.shape[0]
+    results = [array(gate_weight.shape, F32), array(cand_weight.shape, F32)]
+    own_parts = half_call(
+        lambda *refs: own_half_kernel(normaliser, *refs), place, [half], results, depth, {}
+    )
+    other, *own_parts = lax.optimization_barrier((other, *own_parts))
+    grad_motion_w, grad_gate_w, grad_cand_w = half_call(
+        lambda *refs: other_half_kernel(normaliser, *refs), place, [half, other, *own_parts],
+        [array((feats_count, LANES), F32)] + results, depth, {3: 1, 4: 2},
     )
     return (grad_left, grad_right, grad_first, grad_motion_w, grad_gate_w, grad_cand_w)
 

time: 169 us -> 159 us (0.941)
  blocking collectives: 51.1 us -> 0 us
  starting transfers between devices: 43.4 us -> 67.1 us
  waiting for transfers between devices: 24.5 us -> 37.9 us
  other arithmetic: 0.48 us -> 2.58 us
    all_to_all x2 -> x0, blocking collectives: 51.1 us -> none  [the longest x1 31.7 us: summed_everywhere(): lax.all_to_all(half, axes, 0, 0, tiled=True, axis_index_groups=groups)]
    all_to_all x0 -> x2, starting transfers between devices: none -> 25.8 us  [the longest x1 20.3 us: shared_out(): lax.all_to_all(half, axes, 0, 0, tiled=True, axis_index_groups=core_group...]
    all_to_all x0 -> x2, waiting for transfers between devices: none -> 11.9 us  [the longest x1 11.9 us: shared_out(): lax.all_to_all(half, axes, 0, 0, tiled=True, axis_index_groups=core_group...]
    ppermute x2, starting transfers between devices: 9.47 us -> 6.55 us  [swapped(): lax.ppermute(value, 'cols', [(i, i ^ 1) for i in range(lax.axis_size('col...]
    pallas_call x1 -> x2, Pallas kernels: 4.56 us -> 4.22 us  [half_call(): pl.pallas_call(body, out_shape=outs, in_specs=[SMEM] + [VMEM] * (len(arra...]
  transfers between devices with their start and end apart: 16 -> 18, of which waited for: 7 -> 8; matrix products, arithmetic and copies ran while one was open for 1% -> 1% of each run, Pallas kernels for 5% -> 12%
where the time goes in v3:
time: 159 us; the launch traced here: 158 us
  starting transfers between devices  67.1 us (42%)
  Pallas kernels  45.3 us (28%)
  waiting for transfers between devices  37.9 us (24%)
  local copies, waits for them, and re-layouts  4.18 us (3%)
  other arithmetic  2.58 us (2%)
    pallas_call x10, Pallas kernels, kernel_call(): pl.pallas_call(body, out_shape=outs, in_specs=[SMEM] * scalars + [VMEM] *...  39.2 us
    ppermute x10, starting transfers between devices, exchanged(): return (lax.ppermute(value, axis, first), lax.ppermute(value, axis, second))  27.1 us
    all_to_all x1, starting transfers between devices, shared_out(): lax.all_to_all(half, axes, 0, 0, tiled=True, axis_index_groups=core_group...  20.3 us
    ppermute x10, waiting for transfers between devices, exchanged(): return (lax.ppermute(value, axis, first), lax.ppermute(value, axis, second))  19.6 us
    all_to_all x1, waiting for transfers between devices, shared_out(): lax.all_to_all(half, axes, 0, 0, tiled=True, axis_index_groups=core_group...  11.9 us
    ppermute x2, starting transfers between devices, swapped(): lax.ppermute(value, 'cols', [(i, i ^ 1) for i in range(lax.axis_size('col...  6.55 us
    ppermute x2, starting transfers between devices, exchanged_pair(): lax.ppermute(value_a, axis, first)  6.14 us
    all_to_all x1, starting transfers between devices, gathered(): lax.all_to_all(spread, axes, 0, 0, tiled=True, axis_index_groups=core_gro...  5.43 us
  transfers between devices with their start and end apart: 18, of which 8 were waited for; matrix products, arithmetic and copies ran while one was open for 1% of the time, Pallas kernels for 12%

profile of v3, /device:TPU:1, one launch (start us, length us, event | category | flops | bytes accessed | tf_op | source)
XLA Modules:
  0.0 158.2 jit_solution(7256264236758472193)
XLA Ops:
  0.6 0.0 copy-start.4
  0.6 0.0 copy-start.2
  0.7 1.9 %shard_map.136 = bf16[2,288,256]{2,1,0:T(8,128)(2,1)} custom-call(bf16[2,512,256]{2,1,0:T(8,128)(2,1)} %left.5, bf16[2,512,256]{2,1,0:T(8,128)(2,1)} %right.5, bf16[2,512,128]{2,1,0:T(8,128)(2,1)} %hidden.3, bf16[2,512,128]{2,1,0:T(8,128)(2,1)} %grads.3), custom_call_target="tpu_custom_call" | custom-call | bytes 589824 | tf_op jit(solution)/shard_map/pallas_call | solution.py:117
  2.5 6.0 %collective-permute-start.1 = (bf16[2,288,256]{2,1,0:T(8,128)(2,1)}, bf16[2,288,256]{2,1,0:T(8,128)(2,1)}, u32[]{:S(2)}, u32[]{:S(2)}) collective-permute-start(bf16[2,288,256]{2,1,0:T(8,128)(2,1)} %shard_map.136), channel_id=1, source_target_pairs={{1,2},{2,1},{5,6},{6,5},{9,10},{10,9},{13,14},{14,13},{17,18},{18,... | collective-permute-start | bytes 884744 | tf_op jit(solution)/shard_map/ppermute | solution.py:566
  8.6 0.1 collective-permute-start
  8.7 1.4 collective-permute-start.3
  10.0 3.9 %collective-permute-start.2 = (bf16[2,512,128]{2,1,0:T(8,128)(2,1)}, bf16[2,512,128]{2,1,0:T(8,128)(2,1)}, u32[]{:S(2)}, u32[]{:S(2)}) collective-permute-start(bf16[2,512,128]{2,1,0:T(8,128)(2,1)} %hidden.3), channel_id=1, source_target_pairs={{0,4},{8,12},{16,20},{24,28},{32,36},{40,44},{48,52},{56,60},{64,6... | collective-permute-start | bytes 786440 | tf_op jit(solution)/shard_map/ppermute | solution.py:566
  13.9 1.1 copy.18
  15.0 0.0 copy-start.7
  15.0 0.0 copy-start.8
  15.0 0.7 copy.17
  15.8 0.1 pad_add_fusion.place.refs_0_
  15.9 0.0 collective-permute-done.1.got_b
  15.9 0.0 collective-permute-done.got_a
  15.9 0.2 copy-done
  16.1 0.2 copy-done.1
  16.2 0.9 copy-done.3
  17.2 4.7 %shard_map.137 = (bf16[2,576,128]{2,1,0:T(8,128)(2,1)S(1)}, f32[2,544,128]{2,1,0:T(8,128)S(1)}, bf16[2,544,128]{2,1,0:T(8,128)(2,1)S(1)}, bf16[2,544,128]{2,1,0:T(8,128)(2,1)S(1)}, bf16[2,544,128]{2,1,0:T(8,128)(2,1)S(1)}) custom-call(s32[2]{0:T(128)S(1)} %pad_add_fusion.place.refs_0_, s32[2]{0:T(128)S(1)} %copy-done.8, s32[2,4]{1,0:T(2,128)S(1)} %copy-done.7, ...), custom_call_target="tpu_custom_call" | custom-call | flops 570425344 | bytes 3883056 | tf_op jit(solution)/shard_map/pallas_call | solution.py:46
  21.9 0.0 collective-permute-done.3.refs_3_
  21.9 0.0 collective-permute-done.2.refs_2_
  21.9 0.7 collective-permute-start.5
  22.6 2.7 %collective-permute-start.4 = (bf16[2,576,128]{2,1,0:T(8,128)(2,1)S(1)}, bf16[2,576,128]{2,1,0:T(8,128)(2,1)S(1)}, u32[]{:S(2)}, u32[]{:S(2)}) collective-permute-start(bf16[2,576,128]{2,1,0:T(8,128)(2,1)S(1)} %get-tuple-element.79.refs_4_.motion), channel_id=1, source_target_pairs={{0,4},{8,12},{16,20},{24,28},{32,36},{40,44},{48,52},{56,60},{64,6... | collective-permute-start | bytes 884744 | tf_op jit(solution)/shard_map/ppermute | solution.py:566
  25.2 0.0 collective-permute-done.5.refs_6_.motion_b
  25.2 6.3 %collective-permute-done.4.refs_5_.motion_a = bf16[2,576,128]{2,1,0:T(8,128)(2,1)S(1)} collective-permute-done((bf16[2,576,128]{2,1,0:T(8,128)(2,1)S(1)}, bf16[2,576,128]{2,1,0:T(8,128)(2,1)S(1)}, u32[]{:S(2)}, u32[]{:S(2)}) %collective-permute-start.4) | collective-permute-done | bytes 294944 | tf_op jit(solution)/shard_map/ppermute | solution.py:566
  31.5 5.5 %shard_map.138 = (bf16[2,544,128]{2,1,0:T(8,128)(2,1)S(1)}, f32[4,544,128]{2,1,0:T(8,128)S(1)}, f32[4,544,128]{2,1,0:T(8,128)S(1)}, bf16[4,544,128]{2,1,0:T(8,12...) custom-call(s32[2]{0:T(128)S(1)} %pad_add_fusion.place.refs_0_, ...), custom_call_target="tpu_custom_call" | custom-call | flops 3208642560 | bytes 7634952 | tf_op jit(solution)/shard_map/pallas_call | solution.py:46
  37.1 0.7 collective-permute-start.7
  37.7 4.7 %collective-permute-start.6 = (bf16[2,544,128]{2,1,0:T(8,128)(2,1)S(1)}, bf16[2,544,128]{2,1,0:T(8,128)(2,1)S(1)}, u32[]{:S(2)}, u32[]{:S(2)}) collective-permute-start(bf16[2,544,128]{2,1,0:T(8,128)(2,1)S(1)} %get-tuple-element.81.hidden.refs_5_), channel_id=1, source_target_pairs={{0,4},{8,12},{16,20},{24,28},{32,36},{40,44},{48,52},{56,60},{64,6... | collective-permute-start | bytes 835592 | tf_op jit(solution)/shard_map/ppermute | solution.py:566
  42.5 0.0 collective-permute-done.7.hidden_b.refs_7_
  42.5 4.7 %collective-permute-done.6.hidden_a.refs_6_ = bf16[2,544,128]{2,1,0:T(8,128)(2,1)S(1)} collective-permute-done((bf16[2,544,128]{2,1,0:T(8,128)(2,1)S(1)}, bf16[2,544,128]{2,1,0:T(8,128)(2,1)S(1)}, u32[]{:S(2)}, u32[]{:S(2)}) %collective-permute-start.6) | collective-permute-done | bytes 278560 | tf_op jit(solution)/shard_map/ppermute | solution.py:566
  47.2 5.1 %shard_map.139 = (f32[4,544,128]{2,1,0:T(8,128)S(1)}, f32[4,544,128]{2,1,0:T(8,128)S(1)}, bf16[4,544,128]{2,1,0:T(8,128)(2,1)S(1)}, bf16[2,544,128]{2,1,0:T(8,12...) custom-call(s32[2]{0:T(128)S(1)} %pad_add_fusion.place.refs_0_, ...), custom_call_target="tpu_custom_call" | custom-call | flops 3208642560 | bytes 7946248 | tf_op jit(solution)/shard_map/pallas_call | solution.py:46
  52.3 1.3 collective-permute-start.8
  53.6 0.7 collective-permute-start.9
  54.2 0.0 copy-start.6
  54.3 3.0 %shard_map.140 = (f32[2304,128]{1,0:T(8,128)S(1)}, f32[2304,128]{1,0:T(8,128)S(1)}) custom-call(s32[2]{0:T(128)S(1)} %pad_add_fusion.place.refs_0_, bf16[4,544,128]{2,1,0:T(8,128)(2,1)S(1)} %get-tuple-element.86.resets, bf16[2,544,128]{2,1,0:T(8,128)(2,1)S(1)} %get-tuple-element.81.hidden.refs_5_, ...), custom_call_target="tpu_custom_call" | custom-call | flops 1283457024 | bytes 5193736 | tf_op jit(solution)/shard_map/pallas_call | solution.py:46
  57.3 3.3 %collective-permute-done.8.refs_2_ = bf16[3,544,128]{2,1,0:T(8,128)(2,1)S(1)} collective-permute-done((bf16[3,544,128]{2,1,0:T(8,128)(2,1)S(1)}, bf16[3,544,128]{2,1,0:T(8,128)(2,1)S(1)}, u32[]{:S(2)}, u32[]{:S(2)}) %collective-permute-start.8) | collective-permute-done | bytes 417824 | tf_op jit(solution)/shard_map/ppermute | solution.py:571
  60.6 0.0 collective-permute-done.9.refs_3_
  60.6 4.4 %shard_map.141 = (bf16[2,544,128]{2,1,0:T(8,128)(2,1)S(1)}, f32[2,544,128]{2,1,0:T(8,128)S(1)}, f32[2,544,128]{2,1,0:T(8,128)S(1)}, bf16[2,544,128]{2,1,0:T(8,12...) custom-call(s32[2]{0:T(128)S(1)} %pad_add_fusion.place.refs_0_, ...), custom_call_target="tpu_custom_call" | custom-call | flops 2566914048 | bytes 11517960 | tf_op jit(solution)/shard_map/pallas_call | solution.py:46
  65.0 4.9 %collective-permute-start.10 = (bf16[3,544,128]{2,1,0:T(8,128)(2,1)S(1)}, bf16[3,544,128]{2,1,0:T(8,128)(2,1)S(1)}, u32[]{:S(2)}, u32[]{:S(2)}) collective-permute-start(bf16[3,544,128]{2,1,0:T(8,128)(2,1)S(1)} %get-tuple-element.99), channel_id=1, source_target_pairs={{0,4},{8,12},{16,20},{24,28},{32,36},{40,44},{48,52},{56,60},{64,6... | collective-permute-start | bytes 1253384 | tf_op jit(solution)/shard_map/ppermute | solution.py:571
  69.9 0.9 collective-permute-start.11
  70.8 4.2 %shard_map.142 = (f32[2304,128]{1,0:T(8,128)S(1)}, f32[2304,128]{1,0:T(8,128)S(1)}, f32[2304,128]{1,0:T(8,128)S(1)}) custom-call(s32[2]{0:T(128)S(1)} %pad_add_fusion.place.refs_0_, bf16[4,544,128]{2,1,0:T(8,128)(2,1)S(1)} %get-tuple-element.101.resets, bf16[4,544,128]{2,1,0:T(8,128)(2,1)S(1)} %get-tuple-element.80.refs_13_.older.hiddens, ...), custom_call_target="tpu_custom_call" | custom-call | flops 1925185536 | bytes 9568264 | tf_op jit(solution)/shard_map/pallas_call | solution.py:46
  75.0 0.7 collective-permute-done.10.grad_a
  75.7 0.0 collective-permute-done.11.grad_b
  75.7 4.9 %shard_map.143 = (bf16[2,544,128]{2,1,0:T(8,128)(2,1)S(1)}, bf16[2,512,128]{2,1,0:T(8,128)(2,1)}, f32[2,512,128]{2,1,0:T(8,128)S(1)}, f32[128,128]{1,0:T(8,128)S(1)}) custom-call(s32[2]{0:T(128)S(1)} %pad_add_fusion.place.refs_0_, bf16[2,544,128]{2,1,0:T(8,128)(2,1)S(1)} %get-tuple-element.98.cand_grads.grad_cand, ...), custom_call_target="tpu_custom_call" | custom-call | flops 2566914048 | bytes 9060360 | tf_op jit(solution)/shard_map/pallas_call | solution.py:46
  80.6 2.3 %shard_map.144 = (bf16[3584,128]{1,0:T(8,128)(2,1)S(1)}, bf16[3584,128]{1,0:T(8,128)(2,1)S(1)}) custom-call(s32[2]{0:T(128)S(1)} %pad_add_fusion.place.refs_0_, bf16[4,544,128]{2,1,0:T(8,128)(2,1)S(1)} %get-tuple-element.80.refs_13_.older.hiddens, bf16[2,576,128]{2,1,0:T(8,128)(2,1)S(1)} %get-tuple-element.79.refs_4_.motion, ...), custom_call_target="tpu_custom_call" | custom-call | flops 641728512 | bytes 7159816 | tf_op jit(solution)/shard_map/pallas_call | solution.py:46
  82.9 0.0 copy-done.9
  82.9 4.9 %collective-permute-start.12 = (bf16[3584,128]{1,0:T(8,128)(2,1)S(1)}, bf16[3584,128]{1,0:T(8,128)(2,1)S(1)}, u32[]{:S(2)}, u32[]{:S(2)}) collective-permute-start(bf16[3584,128]{1,0:T(8,128)(2,1)S(1)} %get-tuple-element.122), channel_id=1, source_target_pairs={{0,1},{1,0},{2,3},{3,2},{4,5},{5,4},{6,7},{7,6},{8,9},{9,8},{10,11... | collective-permute-start | bytes 2752520 | tf_op jit(solution)/shard_map/ppermute | solution.py:594
  87.7 2.1 %collective-permute-done.12 = bf16[3584,128]{1,0:T(8,128)(2,1)S(1)} collective-permute-done((bf16[3584,128]{1,0:T(8,128)(2,1)S(1)}, bf16[3584,128]{1,0:T(8,128)(2,1)S(1)}, u32[]{:S(2)}, u32[]{:S(2)}) %collective-permute-start.12) | collective-permute-done | bytes 917536 | tf_op jit(solution)/shard_map/ppermute | solution.py:594
  89.8 1.2 add_convert_fusion
  91.0 20.3 %all-to-all-start = ((bf16[64,56,128]{2,1,0:T(8,128)(2,1)}), bf16[64,56,128]{2,1,0:T(8,128)(2,1)}, u32[]{:S(2)}, u32[]{:S(2)}) async-start(bf16[64,56,128]{2,1,0:T(8,128)(2,1)} %bitcast.8), calls=%async_computation | async-start | bytes 1835008 | tf_op jit(solution)/shard_map/all_to_all | solution.py:583
  111.3 3.7 %shard_map.145 = (bf16[2,512,256]{2,1,0:T(8,128)(2,1)}, bf16[2,192,256]{2,1,0:T(8,128)(2,1)S(1)}, f32[2,512,256]{2,1,0:T(8,128)S(1)}) custom-call(s32[2]{0:T(128)S(1)} %pad_add_fusion.place.refs_0_, s32[2]{0:T(128)S(1)} %copy-done.8, s32[2,4]{1,0:T(2,128)S(1)} %copy-done.7, bf16[2,512,256]{2,1,0:T(8,128)(2,1)S(1)} %copy-done, ...), custom_call_target="tpu_custom_call" | custom-call | flops 855638016 | bytes 3932208 | tf_op jit(solution)/shard_map/pallas_call | solution.py:46
  115.1 11.9 %all-to-all-done = bf16[64,56,128]{2,1,0:T(8,128)(2,1)} async-done(((bf16[64,56,128]{2,1,0:T(8,128)(2,1)}), bf16[64,56,128]{2,1,0:T(8,128)(2,1)}, u32[]{:S(2)}, u32[]{:S(2)}) %all-to-all-start) | async-done | bytes 917536 | tf_op jit(solution)/shard_map/all_to_all | solution.py:583
  127.0 1.3 reduce_sum.12
  128.3 1.0 broadcast_in_dim.2
  129.3 5.4 %all-to-all-start.1 = ((bf16[64,56,128]{2,1,0:T(8,128)(2,1)}), bf16[64,56,128]{2,1,0:T(8,128)(2,1)S(1)}, u32[]{:S(2)}, u32[]{:S(2)}) async-start(bf16[64,56,128]{2,1,0:T(8,128)(2,1)} %broadcast_in_dim.2), calls=%async_computation.1 | async-start | bytes 1835008 | tf_op jit(solution)/shard_map/all_to_all | solution.py:589
  134.8 6.8 %collective-permute-start.14 = (bf16[2,192,256]{2,1,0:T(8,128)(2,1)S(1)}, bf16[2,192,256]{2,1,0:T(8,128)(2,1)S(1)}, u32[]{:S(2)}, u32[]{:S(2)}) collective-permute-start(bf16[2,192,256]{2,1,0:T(8,128)(2,1)S(1)} %get-tuple-element.130), channel_id=1, source_target_pairs={{1,2},{2,1},{5,6},{6,5},{9,10},{10,9},{13,14},{14,13},{17,18},{18,... | collective-permute-start | bytes 589832 | tf_op jit(solution)/shard_map/ppermute | solution.py:566
  141.6 0.1 collective-permute-start.13
  141.7 8.6 %collective-permute-done.14.back_b = bf16[2,192,256]{2,1,0:T(8,128)(2,1)S(1)} collective-permute-done((bf16[2,192,256]{2,1,0:T(8,128)(2,1)S(1)}, bf16[2,192,256]{2,1,0:T(8,128)(2,1)S(1)}, u32[]{:S(2)}, u32[]{:S(2)}) %collective-permute-start.14) | collective-permute-done | bytes 196640 | tf_op jit(solution)/shard_map/ppermute | solution.py:566
  150.3 0.0 collective-permute-done.13.back_a
  150.3 1.4 shard_map.146
  151.8 0.0 all-to-all-done.1
  151.8 1.7 %collective-permute-start.15 = (bf16[3584,128]{1,0:T(8,128)(2,1)S(1)}, bf16[3584,128]{1,0:T(8,128)(2,1)S(1)}, u32[]{:S(2)}, u32[]{:S(2)}) collective-permute-start(bf16[3584,128]{1,0:T(8,128)(2,1)S(1)} %bitcast.12), channel_id=1, source_target_pairs={{0,1},{1,0},{2,3},{3,2},{4,5},{5,4},{6,7},{7,6},{8,9},{9,8},{10,11... | collective-permute-start | bytes 2752520 | tf_op jit(solution)/shard_map/ppermute | solution.py:594
  153.5 1.8 %shard_map.147 = (f32[2304,256]{1,0:T(8,128)}, f32[2304,128]{1,0:T(8,128)}) custom-call(s32[2]{0:T(128)S(1)} %pad_add_fusion.place.refs_0_, bf16[3584,128]{1,0:T(8,128)(2,1)S(1)} %bitcast.13), custom_call_target="tpu_custom_call" | custom-call | bytes 1769472 | tf_op jit(solution)/shard_map/pallas_call | solution.py:161
  155.3 0.3 collective-permute-done.15.refs_2_
  155.6 2.4 %shard_map.148 = (f32[36,128]{1,0:T(8,128)}, f32[2304,256]{1,0:T(8,128)}, f32[2304,128]{1,0:T(8,128)}) custom-call(s32[2]{0:T(128)S(1)} %pad_add_fusion.place.refs_0_, bf16[3584,128]{1,0:T(8,128)(2,1)S(1)} %bitcast.14, bf16[3584,128]{1,0:T(8,128)(2,1)S(1)} %collective-permute-done.15.refs_2_, ...), custom_call_target="tpu_custom_call", output_to_operand_aliasing={{1}: (3, {}), {2}: (4, {})} | custom-call | bytes 1769472 | tf_op jit(solution)/shard_map/pallas_call | solution.py:161
  (16 shorter events, 0.0 us)
Async XLA Ops:
  0.6 13.3 %copy-start.4 = (bf16[2304,128]{1,0:T(8,128)(2,1)S(1)}, bf16[2304,128]{1,0:T(8,128)(2,1)}, u32[]{:S(2)}) copy-start(bf16[2304,128]{1,0:T(8,128)(2,1)} %cand_w.1) | copy-start | bytes 1769476
  0.6 14.4 %copy-start.2 = (bf16[2304,256]{1,0:T(8,128)(2,1)S(1)}, bf16[2304,256]{1,0:T(8,128)(2,1)}, u32[]{:S(2)}) copy-start(bf16[2304,256]{1,0:T(8,128)(2,1)} %gate_w.1) | copy-start | bytes 3538948
  2.5 13.4 %collective-permute-start.1 = (bf16[2,288,256]{2,1,0:T(8,128)(2,1)}, bf16[2,288,256]{2,1,0:T(8,128)(2,1)}, u32[]{:S(2)}, u32[]{:S(2)}) collective-permute-start(bf16[2,288,256]{2,1,0:T(8,128)(2,1)} %shard_map.136), channel_id=1, source_target_pairs={{1,2},{2,1},{5,6},{6,5},{9,10},{10,9},{13,14},{14,13},{17,18},{18,... | collective-permute-start | bytes 884744 | tf_op jit(solution)/shard_map/ppermute | solution.py:566
  8.6 7.3 %collective-permute-start = (bf16[2,288,256]{2,1,0:T(8,128)(2,1)}, bf16[2,288,256]{2,1,0:T(8,128)(2,1)}, u32[]{:S(2)}, u32[]{:S(2)}) collective-permute-start(bf16[2,288,256]{2,1,0:T(8,128)(2,1)} %shard_map.136), channel_id=1, source_target_pairs={{0,1},{2,3},{1,0},{3,2},{4,5},{6,7},{5,4},{7,6},{8,9},{10,11},{9,8... | collective-permute-start | bytes 884744 | tf_op jit(solution)/shard_map/ppermute | solution.py:566
  8.7 13.2 %collective-permute-start.3 = (bf16[2,512,128]{2,1,0:T(8,128)(2,1)}, bf16[2,512,128]{2,1,0:T(8,128)(2,1)}, u32[]{:S(2)}, u32[]{:S(2)}) collective-permute-start(bf16[2,512,128]{2,1,0:T(8,128)(2,1)} %hidden.3), channel_id=1, source_target_pairs={{4,8},{12,16},{20,24},{28,32},{36,40},{44,48},{52,56},{60,64},{68,... | collective-permute-start | bytes 786440 | tf_op jit(solution)/shard_map/ppermute | solution.py:566
  10.0 11.8 %collective-permute-start.2 = (bf16[2,512,128]{2,1,0:T(8,128)(2,1)}, bf16[2,512,128]{2,1,0:T(8,128)(2,1)}, u32[]{:S(2)}, u32[]{:S(2)}) collective-permute-start(bf16[2,512,128]{2,1,0:T(8,128)(2,1)} %hidden.3), channel_id=1, source_target_pairs={{0,4},{8,12},{16,20},{24,28},{32,36},{40,44},{48,52},{56,60},{64,6... | collective-permute-start | bytes 786440 | tf_op jit(solution)/shard_map/ppermute | solution.py:566
  15.0 0.8 copy-start.11
  15.0 1.1 copy-start
  15.0 1.2 copy-start.1
  15.0 1.2 copy-start.7
  15.0 1.2 copy-start.8
  16.2 1.0 copy-start.3
  17.2 14.4 %copy-start.5 = (bf16[2304,128]{1,0:T(8,128)(2,1)S(1)}, bf16[2304,128]{1,0:T(8,128)(2,1)}, u32[]{:S(2)}) copy-start(bf16[2304,128]{1,0:T(8,128)(2,1)} %cand_w.1) | copy-start | bytes 1769476
  21.9 3.4 %collective-permute-start.5 = (bf16[2,576,128]{2,1,0:T(8,128)(2,1)S(1)}, bf16[2,576,128]{2,1,0:T(8,128)(2,1)S(1)}, u32[]{:S(2)}, u32[]{:S(2)}) collective-permute-start(bf16[2,576,128]{2,1,0:T(8,128)(2,1)S(1)} %get-tuple-element.79.refs_4_.motion), channel_id=1, source_target_pairs={{4,8},{12,16},{20,24},{28,32},{36,40},{44,48},{52,56},{60,64},{68,... | collective-permute-start | bytes 884744 | tf_op jit(solution)/shard_map/ppermute | solution.py:566
  22.6 9.0 %collective-permute-start.4 = (bf16[2,576,128]{2,1,0:T(8,128)(2,1)S(1)}, bf16[2,576,128]{2,1,0:T(8,128)(2,1)S(1)}, u32[]{:S(2)}, u32[]{:S(2)}) collective-permute-start(bf16[2,576,128]{2,1,0:T(8,128)(2,1)S(1)} %get-tuple-element.79.refs_4_.motion), channel_id=1, source_target_pairs={{0,4},{8,12},{16,20},{24,28},{32,36},{40,44},{48,52},{56,60},{64,6... | collective-permute-start | bytes 884744 | tf_op jit(solution)/shard_map/ppermute | solution.py:566
  37.1 5.4 %collective-permute-start.7 = (bf16[2,544,128]{2,1,0:T(8,128)(2,1)S(1)}, bf16[2,544,128]{2,1,0:T(8,128)(2,1)S(1)}, u32[]{:S(2)}, u32[]{:S(2)}) collective-permute-start(bf16[2,544,128]{2,1,0:T(8,128)(2,1)S(1)} %get-tuple-element.81.hidden.refs_5_), channel_id=1, source_target_pairs={{4,8},{12,16},{20,24},{28,32},{36,40},{44,48},{52,56},{60,64},{68,... | collective-permute-start | bytes 835592 | tf_op jit(solution)/shard_map/ppermute | solution.py:566
  37.7 9.4 %collective-permute-start.6 = (bf16[2,544,128]{2,1,0:T(8,128)(2,1)S(1)}, bf16[2,544,128]{2,1,0:T(8,128)(2,1)S(1)}, u32[]{:S(2)}, u32[]{:S(2)}) collective-permute-start(bf16[2,544,128]{2,1,0:T(8,128)(2,1)S(1)} %get-tuple-element.81.hidden.refs_5_), channel_id=1, source_target_pairs={{0,4},{8,12},{16,20},{24,28},{32,36},{40,44},{48,52},{56,60},{64,6... | collective-permute-start | bytes 835592 | tf_op jit(solution)/shard_map/ppermute | solution.py:566
  52.3 8.3 %collective-permute-start.8 = (bf16[3,544,128]{2,1,0:T(8,128)(2,1)S(1)}, bf16[3,544,128]{2,1,0:T(8,128)(2,1)S(1)}, u32[]{:S(2)}, u32[]{:S(2)}) collective-permute-start(bf16[3,544,128]{2,1,0:T(8,128)(2,1)S(1)} %get-tuple-element.84), channel_id=1, source_target_pairs={{0,4},{8,12},{16,20},{24,28},{32,36},{40,44},{48,52},{56,60},{64,6... | collective-permute-start | bytes 1253384 | tf_op jit(solution)/shard_map/ppermute | solution.py:571
  53.6 7.0 %collective-permute-start.9 = (bf16[3,544,128]{2,1,0:T(8,128)(2,1)S(1)}, bf16[3,544,128]{2,1,0:T(8,128)(2,1)S(1)}, u32[]{:S(2)}, u32[]{:S(2)}) collective-permute-start(bf16[3,544,128]{2,1,0:T(8,128)(2,1)S(1)} %get-tuple-element.85), channel_id=1, source_target_pairs={{4,8},{12,16},{20,24},{28,32},{36,40},{44,48},{52,56},{60,64},{68,... | collective-permute-start | bytes 1253384 | tf_op jit(solution)/shard_map/ppermute | solution.py:571
  54.2 6.4 %copy-start.6 = (bf16[3,3,256,128]{2,3,1,0:T(8,128)(2,1)S(1)}, bf16[3,3,256,128]{2,3,1,0:T(8,128)(2,1)}, u32[]{:S(2)}) copy-start(bf16[3,3,256,128]{2,3,1,0:T(8,128)(2,1)} %copy.18) | copy-start | bytes 1769476
  65.0 10.7 %collective-permute-start.10 = (bf16[3,544,128]{2,1,0:T(8,128)(2,1)S(1)}, bf16[3,544,128]{2,1,0:T(8,128)(2,1)S(1)}, u32[]{:S(2)}, u32[]{:S(2)}) collective-permute-start(bf16[3,544,128]{2,1,0:T(8,128)(2,1)S(1)} %get-tuple-element.99), channel_id=1, source_target_pairs={{0,4},{8,12},{16,20},{24,28},{32,36},{40,44},{48,52},{56,60},{64,6... | collective-permute-start | bytes 1253384 | tf_op jit(solution)/shard_map/ppermute | solution.py:571
  69.9 5.8 %collective-permute-start.11 = (bf16[3,544,128]{2,1,0:T(8,128)(2,1)S(1)}, bf16[3,544,128]{2,1,0:T(8,128)(2,1)S(1)}, u32[]{:S(2)}, u32[]{:S(2)}) collective-permute-start(bf16[3,544,128]{2,1,0:T(8,128)(2,1)S(1)} %get-tuple-element.100), channel_id=1, source_target_pairs={{4,8},{12,16},{20,24},{28,32},{36,40},{44,48},{52,56},{60,64},{68,... | collective-permute-start | bytes 1253384 | tf_op jit(solution)/shard_map/ppermute | solution.py:571
  80.6 2.3 %copy-start.9 = (f32[2,512,128]{2,1,0:T(8,128)}, f32[2,512,128]{2,1,0:T(8,128)S(1)}, u32[]{:S(2)}) copy-start(f32[2,512,128]{2,1,0:T(8,128)S(1)} %get-tuple-element.123.grad_feats) | copy-start | bytes 1572868
  82.9 7.0 %collective-permute-start.12 = (bf16[3584,128]{1,0:T(8,128)(2,1)S(1)}, bf16[3584,128]{1,0:T(8,128)(2,1)S(1)}, u32[]{:S(2)}, u32[]{:S(2)}) collective-permute-start(bf16[3584,128]{1,0:T(8,128)(2,1)S(1)} %get-tuple-element.122), channel_id=1, source_target_pairs={{0,1},{1,0},{2,3},{3,2},{4,5},{5,4},{6,7},{7,6},{8,9},{9,8},{10,11... | collective-permute-start | bytes 2752520 | tf_op jit(solution)/shard_map/ppermute | solution.py:594
  91.0 20.4 %copy-start.10 = (f32[2,512,128]{2,1,0:T(8,128)S(1)}, f32[2,512,128]{2,1,0:T(8,128)}, u32[]{:S(2)}) copy-start(f32[2,512,128]{2,1,0:T(8,128)} %copy-done.9) | copy-start | bytes 1572868
  91.0 36.0 %all-to-all-start = ((bf16[64,56,128]{2,1,0:T(8,128)(2,1)}), bf16[64,56,128]{2,1,0:T(8,128)(2,1)}, u32[]{:S(2)}, u32[]{:S(2)}) async-start(bf16[64,56,128]{2,1,0:T(8,128)(2,1)} %bitcast.8), calls=%async_computation | async-start | bytes 1835008 | tf_op jit(solution)/shard_map/all_to_all | solution.py:583
  129.3 22.4 %all-to-all-start.1 = ((bf16[64,56,128]{2,1,0:T(8,128)(2,1)}), bf16[64,56,128]{2,1,0:T(8,128)(2,1)S(1)}, u32[]{:S(2)}, u32[]{:S(2)}) async-start(bf16[64,56,128]{2,1,0:T(8,128)(2,1)} %broadcast_in_dim.2), calls=%async_computation.1 | async-start | bytes 1835008 | tf_op jit(solution)/shard_map/all_to_all | solution.py:589
  134.8 15.5 %collective-permute-start.14 = (bf16[2,192,256]{2,1,0:T(8,128)(2,1)S(1)}, bf16[2,192,256]{2,1,0:T(8,128)(2,1)S(1)}, u32[]{:S(2)}, u32[]{:S(2)}) collective-permute-start(bf16[2,192,256]{2,1,0:T(8,128)(2,1)S(1)} %get-tuple-element.130), channel_id=1, source_target_pairs={{1,2},{2,1},{5,6},{6,5},{9,10},{10,9},{13,14},{14,13},{17,18},{18,... | collective-permute-start | bytes 589832 | tf_op jit(solution)/shard_map/ppermute | solution.py:566
  141.6 8.7 %collective-permute-start.13 = (bf16[2,192,256]{2,1,0:T(8,128)(2,1)S(1)}, bf16[2,192,256]{2,1,0:T(8,128)(2,1)S(1)}, u32[]{:S(2)}, u32[]{:S(2)}) collective-permute-start(bf16[2,192,256]{2,1,0:T(8,128)(2,1)S(1)} %get-tuple-element.130), channel_id=1, source_target_pairs={{0,1},{2,3},{1,0},{3,2},{4,5},{6,7},{5,4},{7,6},{8,9},{10,11},{9,8... | collective-permute-start | bytes 589832 | tf_op jit(solution)/shard_map/ppermute | solution.py:566
  151.8 3.8 %collective-permute-start.15 = (bf16[3584,128]{1,0:T(8,128)(2,1)S(1)}, bf16[3584,128]{1,0:T(8,128)(2,1)S(1)}, u32[]{:S(2)}, u32[]{:S(2)}) collective-permute-start(bf16[3584,128]{1,0:T(8,128)(2,1)S(1)} %bitcast.12), channel_id=1, source_target_pairs={{0,1},{1,0},{2,3},{3,2},{4,5},{5,4},{6,7},{7,6},{8,9},{9,8},{10,11... | collective-permute-start | bytes 2752520 | tf_op jit(solution)/shard_map/ppermute | solution.py:594

commit v4 on v3

--- a/solution.py
+++ b/solution.py
@@ -228,37 +228,67 @@
     return (column >= 0) & (column < cols * cols_axis)
 
 
-def fill_rows(store, odd, own, first, second, wide):
+def fill_neighbours(store, odd, first, second, wide):
     for row in range(2):
         above, below = sides(odd, first[row, :wide], second[row, :wide])
         store(row, above.astype(F32))
         store(4 + row, below.astype(F32))
-        store(2 + row, own[row, :wide].astype(F32))
-
-
-def gates(fields, resets, gate_w, update, reset, reset_hidden, wide):
-    block = wide // SPLIT
-    deep = gate_w.shape[0] // 3
-
+
+
+def own_products(partial, taps, weights, source):
+    deep = weights.shape[0] // 3
+    block = partial.shape[1] // SPLIT
     for step in range(4 * SPLIT):
         row, start = step // SPLIT, (step % SPLIT) * block
         here = pl.ds(start, block)
-        total = sum(dot(fields[row + a, here], gate_w[a * deep : (a + 1) * deep]) for a in range(3))
+        partial[row, here] = sum(
+            dot(taps[source(row, a), here], weights[a * deep : (a + 1) * deep])
+            for a in range(3)
+            if source(row, a) in (0, 1)
+        )
+
+
+def own_gates_kernel(hidden, motion, gate_w, taps, partial):
+    wide = hidden.shape[1]
+    for row in range(2):
+        store_taps(taps, row, 0, 2 * LANES, hidden[row].astype(F32), True)
+        store_taps(taps, row, LANES, 2 * LANES, motion[row, :wide].astype(F32), True)
+    own_products(partial, taps, gate_w, lambda row, a: row + a - 2)
+
+
+def own_cand_kernel(grad_cand, cand_wt, partial, taps):
+    for row in range(2):
+        store_taps(taps, row, 0, LANES, grad_cand[row].astype(F32), False)
+    own_products(partial, taps, cand_wt, lambda row, a: row - a)
+
+
+def gates(fields, own, partial, resets, gate_w, update, reset, reset_hidden, wide):
+    block = wide // SPLIT
+    deep = gate_w.shape[0] // 3
+    six = [fields.at[0], fields.at[1], own.at[0], own.at[1], fields.at[4], fields.at[5]]
+    for step in range(4 * SPLIT):
+        row, start = step // SPLIT, (step % SPLIT) * block
+        here = pl.ds(start, block)
+        total = partial[row, here] + sum(
+            dot(six[row + a][here], gate_w[a * deep : (a + 1) * deep])
+            for a in range(3)
+            if row + a not in (2, 3)
+        )
         reset_part = jax.nn.sigmoid(total[:, LANES:])
         update[row, here] = jax.nn.sigmoid(total[:, :LANES])
         reset[row, here] = reset_part
-        hidden = fields[row + 1, here, 2 * LANES : 3 * LANES].astype(F32)
+        hidden = six[row + 1][here, 2 * LANES : 3 * LANES].astype(F32)
         reset_hidden[row, here] = (reset_part * hidden).astype(BF16)
     for row in range(4):
         store_taps(resets, row, 0, 2 * LANES, reset_hidden[row].astype(F32), True)
         for tap in range(3):
             start = (2 * tap + 1) * LANES
-            resets[row, :, start : start + LANES] = fields[row + 1, :, start : start + LANES]
-
-
-def load_field(odd, fields, lane, own, first, second):
+            resets[row, :, start : start + LANES] = six[row + 1][:, start : start + LANES]
+
+
+def load_field(odd, fields, lane, first, second):
     wide = fields.shape[1]
-    fill_rows(lambda r, v: store_taps(fields, r, lane, 2 * LANES, v, True), odd, own, first, second, wide)
+    fill_neighbours(lambda r, v: store_taps(fields, r, lane, 2 * LANES, v, True), odd, first, second, wide)
 
 
 def candidate_part(resets, cand_w, row, here):
@@ -267,12 +297,12 @@
     return jnp.tanh(total)
 
 
-def first_kernel(cols_axis, place, hidden, init_a, init_b, motion, motion_a, motion_b, gate_w, cand_w,
+def first_kernel(cols_axis, place, hidden, init_a, init_b, motion_a, motion_b, gate_w, cand_w, own, partial,
                  later, update, reset, reset_hidden, candidate, hiddens, fields, resets):
     odd = place[0] % 2 == 1
     wide = hidden.shape[1]
     block = wide // SPLIT
-    load_field(odd, fields, LANES, motion, motion_a, motion_b)
+    load_field(odd, fields, LANES, motion_a, motion_b)
     for row in range(2):
         got_a, got_b = (
             jnp.concatenate(
@@ -281,11 +311,12 @@
             for sent, inner in ((motion_a, init_a), (motion_b, init_b))
         )
         above, below = sides(odd, got_a, got_b)
-        for there, value in ((row, above), (2 + row, hidden[row]), (4 + row, below)):
+        for there, value in ((row, above), (4 + row, below)):
             store_taps(fields, there, 0, 2 * LANES, value.astype(F32), True)
             if 0 < there < 5:
                 hiddens[there - 1] = value
-    gates(fields, resets, gate_w, update, reset, reset_hidden, wide)
+        hiddens[1 + row] = hidden[row]
+    gates(fields, own, partial, resets, gate_w, update, reset, reset_hidden, wide)
     inside = image_columns(place, wide, wide - 2 * HALO, cols_axis)
     for row in range(2):
         for start in range(0, wide, block):
@@ -310,14 +341,14 @@
     send_a[2], send_b[2] = sides(odd, grad_update[0], grad_update[1])
 
 
-def second_kernel(place, hidden, hidden_a, hidden_b, motion, motion_a, motion_b, gate_w, cand_w, grad_hidden,
+def second_kernel(place, hidden, hidden_a, hidden_b, motion_a, motion_b, gate_w, cand_w, own, partial, grad_hidden,
                   update, reset, reset_hidden, grad_cand, grad_update, send_a, send_b, fields, resets):
     odd = place[0] % 2 == 1
     wide = hidden.shape[1]
     block = wide // SPLIT
-    load_field(odd, fields, LANES, motion, motion_a, motion_b)
-    load_field(odd, fields, 0, hidden, hidden_a, hidden_b)
-    gates(fields, resets, gate_w, update, reset, reset_hidden, wide)
+    load_field(odd, fields, LANES, motion_a, motion_b)
+    load_field(odd, fields, 0, hidden_a, hidden_b)
+    gates(fields, own, partial, resets, gate_w, update, reset, reset_hidden, wide)
     for row in range(2):
         for start in range(0, wide, block):
             here = pl.ds(start, block)
@@ -327,19 +358,23 @@
     send_updates(odd, grad_update, send_a, send_b)
 
 
-def back_step(place, grad_cand, grad_a, grad_b, grad_update, hiddens, reset, cand_wt, gate_wt,
+def back_step(place, partial, grad_a, grad_b, grad_update, hiddens, reset, cand_wt, gate_wt,
               grad_reset, cand_taps, gate_taps, inner, grad_motion, finish):
     odd = place[0] % 2 == 1
-    wide = grad_cand.shape[1]
+    wide = partial.shape[1]
     block = wide // SPLIT
-    fill_rows(lambda r, v: store_taps(cand_taps, r, 0, LANES, v, False), odd, grad_cand, grad_a, grad_b, wide)
+    fill_neighbours(lambda r, v: store_taps(cand_taps, r, 0, LANES, v, False), odd, grad_a, grad_b, wide)
     deep = cand_wt.shape[0] // 3
     deeper = gate_wt.shape[0] // 3
 
     for step in range(4 * SPLIT):
         row, start = step // SPLIT, (step % SPLIT) * block
         here = pl.ds(start, block)
-        total = sum(dot(cand_taps[row + 2 - a, here], cand_wt[a * deep : (a + 1) * deep]) for a in range(3))
+        total = partial[row, here] + sum(
+            dot(cand_taps[row + 2 - a, here], cand_wt[a * deep : (a + 1) * deep])
+            for a in range(3)
+            if row - a not in (0, 1)
+        )
         inner[row, here] = total[:, :LANES]
         if row in (1, 2):
             grad_motion[row - 1, here] = total[:, LANES:]
@@ -362,7 +397,7 @@
             finish(row, start, here, inner[row + 1, here] * reset[row + 1, here] + total[:, :LANES])
 
 
-def later_back_kernel(cols_axis, place, grad_cand, grad_a, grad_b, grad_update, hidden, hidden_a, hidden_b, reset,
+def later_back_kernel(cols_axis, place, partial, grad_a, grad_b, grad_update, hidden, hidden_a, hidden_b, reset,
                       cand_wt, gate_wt, update, grad_hidden, older_hiddens, older_update, older_candidate,
                       grad_reset, grad_state, grad_motion, older_cand, older_upd, send_a, send_b,
                       cand_taps, gate_taps, inner):
@@ -380,12 +415,12 @@
                       older_hiddens[row + 1, here].astype(F32), row, here, older_cand, older_upd, send_a, send_b)
 
     hiddens = hidden_rows(odd, hidden, hidden_a, hidden_b)
-    back_step(place, grad_cand, grad_a, grad_b, grad_update, hiddens, reset, cand_wt, gate_wt,
+    back_step(place, partial, grad_a, grad_b, grad_update, hiddens, reset, cand_wt, gate_wt,
               grad_reset, cand_taps, gate_taps, inner, grad_motion, finish)
     send_updates(odd, older_upd, send_a, send_b)
 
 
-def first_back_kernel(place, grad_cand, grad_a, grad_b, grad_update, hiddens, reset,
+def first_back_kernel(place, partial, grad_a, grad_b, grad_update, hiddens, reset,
                       cand_wt, gate_wt, update, grad_state, motion_so_far, pre, feats, weight,
                       grad_reset, grad_first, grad_feats, motion_w, cand_taps, gate_taps, inner, grad_motion):
     def finish(row, start, here, terms):
@@ -395,7 +430,7 @@
         grad_first[row, first - HALO : last - HALO] = grad[first - start : last - start].astype(BF16)
         grad_motion[row, here] += motion_so_far[row, here]
 
-    back_step(place, grad_cand, grad_a, grad_b, grad_update, hiddens, reset, cand_wt, gate_wt,
+    back_step(place, partial, grad_a, grad_b, grad_update, hiddens, reset, cand_wt, gate_wt,
               grad_reset, cand_taps, gate_taps, inner, grad_motion, finish)
     inner_cols = slice(HALO, HALO + grad_feats.shape[1])
     total = jnp.zeros((LANES, LANES), F32)
@@ -583,9 +618,12 @@
     return lax.all_to_all(half, axes, 0, 0, tiled=True, axis_index_groups=core_groups())
 
 
+def spread_kernel(pieces, out):
+    out[...] = jnp.broadcast_to(jnp.sum(pieces[...].astype(F32), axis=0).astype(BF16)[None], out.shape)
+
+
 def gathered(pieces, axes):
-    piece = jnp.sum(pieces.astype(F32), axis=0).astype(BF16)
-    spread = jnp.broadcast_to(piece[None], pieces.shape)
+    (spread,) = kernel_call(spread_kernel, [array(pieces.shape, BF16)], [pieces], 0, [], 0)
     half = lax.all_to_all(spread, axes, 0, 0, tiled=True, axis_index_groups=core_groups())
     return half.reshape(-1, LANES)
 
@@ -636,19 +674,27 @@
     unit = 2 * wide * 9 * 2 * state * state
     fields = [pltpu.VMEM((6, wide, 6 * LANES), BF16), pltpu.VMEM((4, wide, 6 * LANES), BF16)]
 
+    field_taps = array((2, wide, 6 * LANES), BF16)
+    partials = array((4, wide, 2 * LANES), F32)
+    own_taps, partial = kernel_call(
+        own_gates_kernel, [field_taps, partials], [hidden, motion, gate_weight], 0, [], 4 * unit
+    )
     hidden_1, update_0, reset_0, reset_hidden_0, candidate_0, hiddens_0 = kernel_call(
         lambda *refs: first_kernel(cols_axis, *refs),
         [field(2, BF16), field(4, F32), field(4, F32), field(4, BF16), field(2, F32), field(4, BF16)],
-        [place, hidden, init_a, init_b, *motions, gate_weight, cand_weight],
+        [place, hidden, init_a, init_b, *motions[1:], gate_weight, cand_weight, own_taps, partial],
         1,
         fields,
         10 * unit,
     )
     hidden_1a, hidden_1b = exchanged(hidden_1, "rows")
+    own_taps, partial = kernel_call(
+        own_gates_kernel, [field_taps, partials], [hidden_1, motion, gate_weight], 0, [], 4 * unit
+    )
     update_1, reset_1, reset_hidden_1, grad_cand_1, grad_update_1, send_a, send_b = kernel_call(
         second_kernel,
         [field(4, F32), field(4, F32), field(4, BF16), field(2, BF16), field(2, BF16), field(3, BF16), field(3, BF16)],
-        [place, hidden_1, hidden_1a, hidden_1b, *motions, gate_weight, cand_weight, grads],
+        [place, hidden_1, hidden_1a, hidden_1b, *motions[1:], gate_weight, cand_weight, own_taps, partial, grads],
         1,
         fields,
         10 * unit,
@@ -665,6 +711,9 @@
         [pixels, taps],
         4 * unit,
     )
+    (partial,) = kernel_call(
+        own_cand_kernel, [partials], [grad_cand_1, cand_wt], 0, [pltpu.VMEM((2, wide, 3 * LANES), BF16)], 2 * unit
+    )
     got_a, got_b, cand_sum, update_sum = lax.optimization_barrier((got_a, got_b, cand_sum, update_sum))
     back_scratch = [
         pltpu.VMEM((6, wide, 3 * LANES), BF16),
@@ -675,7 +724,7 @@
         lambda *refs: later_back_kernel(cols_axis, *refs),
         [field(2, BF16), field(2, F32), field(2, F32), field(2, BF16), field(2, BF16),
          field(3, BF16), field(3, BF16)],
-        [place, grad_cand_1, got_a, got_b, grad_update_1, hidden_1, hidden_1a, hidden_1b, reset_1, cand_wt, gate_wt,
+        [place, partial, got_a, got_b, grad_update_1, hidden_1, hidden_1a, hidden_1b, reset_1, cand_wt, gate_wt,
          update_1, grads, hiddens_0, update_0, candidate_0],
         1,
         back_scratch,
@@ -691,13 +740,16 @@
         [pixels, taps],
         6 * unit,
     )
+    (partial,) = kernel_call(
+        own_cand_kernel, [partials], [grad_cand_0, cand_wt], 0, [pltpu.VMEM((2, wide, 3 * LANES), BF16)], 2 * unit
+    )
     got_a, got_b, cand_sum, update_sum, reset_sum = lax.optimization_barrier(
         (got_a, got_b, cand_sum, update_sum, reset_sum)
     )
     grad_reset_0, grad_first, grad_feats, motion_sum = kernel_call(
         first_back_kernel,
         [field(2, BF16), array((2, cols, LANES), BF16), array((2, cols, LANES), F32), array((LANES, LANES), F32)],
-        [place, grad_cand_0, got_a, got_b, grad_update_0, hiddens_0, reset_0, cand_wt, gate_wt,
+        [place, partial, got_a, got_b, grad_update_0, hiddens_0, reset_0, cand_wt, gate_wt,
          update_0, grad_state, grad_motion_1, motion_pre, feats, motion_w],
         1,
         back_scratch + [pltpu.VMEM((2, wide, LANES), F32)],

time: 159 us -> 153 us (0.962)
  waiting for transfers between devices: 37.9 us -> 32.5 us
  Pallas kernels: 45.3 us -> 47.9 us
    ppermute x10, waiting for transfers between devices: 19.6 us -> 16.6 us  [exchanged(): return (lax.ppermute(value, axis, first), lax.ppermute(value, axis, second))]
    pallas_call x10 -> x15, Pallas kernels: 39.2 us -> 41.8 us  [kernel_call(): pl.pallas_call(body, out_shape=outs, in_specs=[SMEM] * scalars + [VMEM] *...]
  transfers between devices with their start and end apart: 18 -> 18, of which waited for: 8 -> 7; matrix products, arithmetic and copies ran while one was open for 1% -> 1% of each run, Pallas kernels for 12% -> 16%
where the time goes in v4:
time: 153 us
  starting transfers between devices  67 us (44%)
  Pallas kernels  47.9 us (31%)
  waiting for transfers between devices  32.5 us (21%)
  local copies, waits for them, and re-layouts  2.95 us (2%)
    pallas_call x15, Pallas kernels, kernel_call(): pl.pallas_call(body, out_shape=outs, in_specs=[SMEM] * scalars + [VMEM] *...  41.8 us
    ppermute x10, starting transfers between devices, exchanged(): return (lax.ppermute(value, axis, first), lax.ppermute(value, axis, second))  28.4 us
    all_to_all x1, starting transfers between devices, shared_out(): lax.all_to_all(half, axes, 0, 0, tiled=True, axis_index_groups=core_group...  19.2 us
    ppermute x10, waiting for transfers between devices, exchanged(): return (lax.ppermute(value, axis, first), lax.ppermute(value, axis, second))  16.6 us
    all_to_all x1, waiting for transfers between devices, shared_out(): lax.all_to_all(half, axes, 0, 0, tiled=True, axis_index_groups=core_group...  11.1 us
    ppermute x2, starting transfers between devices, swapped(): lax.ppermute(value, 'cols', [(i, i ^ 1) for i in range(lax.axis_size('col...  6.2 us
    ppermute x2, starting transfers between devices, exchanged_pair(): lax.ppermute(value_a, axis, first)  6.13 us
    all_to_all x1, starting transfers between devices, gathered(): lax.all_to_all(spread, axes, 0, 0, tiled=True, axis_index_groups=core_gro...  5.56 us
  transfers between devices with their start and end apart: 18, of which 7 were waited for; matrix products, arithmetic and copies ran while one was open for 1% of the time, Pallas kernels for 16%

profile of v4, /device:TPU:1, one launch (start us, length us, event | category | flops | bytes accessed | tf_op | source)
XLA Modules:
  0.0 152.8 jit_solution(3712038639815415961)
XLA Ops:
  0.6 0.0 copy-start.7
  0.7 1.8 %shard_map.136 = bf16[2,288,256]{2,1,0:T(8,128)(2,1)} custom-call(bf16[2,512,256]{2,1,0:T(8,128)(2,1)} %left.5, bf16[2,512,256]{2,1,0:T(8,128)(2,1)} %right.5, bf16[2,512,128]{2,1,0:T(8,128)(2,1)} %hidden.3, bf16[2,512,128]{2,1,0:T(8,128)(2,1)} %grads.3), custom_call_target="tpu_custom_call" | custom-call | bytes 589824 | tf_op jit(solution)/shard_map/pallas_call | solution.py:117
  2.5 6.0 %collective-permute-start.1 = (bf16[2,288,256]{2,1,0:T(8,128)(2,1)}, bf16[2,288,256]{2,1,0:T(8,128)(2,1)}, u32[]{:S(2)}, u32[]{:S(2)}) collective-permute-start(bf16[2,288,256]{2,1,0:T(8,128)(2,1)} %shard_map.136), channel_id=1, source_target_pairs={{1,2},{2,1},{5,6},{6,5},{9,10},{10,9},{13,14},{14,13},{17,18},{18,... | collective-permute-start | bytes 884744 | tf_op jit(solution)/shard_map/ppermute | solution.py:601
  8.5 0.1 collective-permute-start
  8.6 1.4 collective-permute-start.3
  10.0 3.9 %collective-permute-start.2 = (bf16[2,512,128]{2,1,0:T(8,128)(2,1)S(1)}, bf16[2,512,128]{2,1,0:T(8,128)(2,1)}, u32[]{:S(2)}, u32[]{:S(2)}) collective-permute-start(bf16[2,512,128]{2,1,0:T(8,128)(2,1)S(1)} %copy-done.4), channel_id=1, source_target_pairs={{0,4},{8,12},{16,20},{24,28},{32,36},{40,44},{48,52},{56,60},{64,6... | collective-permute-start | bytes 786440 | tf_op jit(solution)/shard_map/ppermute | solution.py:601
  13.9 0.2 copy.18
  14.1 0.0 copy-start.11
  14.2 0.0 copy-start
  14.2 0.0 copy-start.1
  14.2 0.0 copy-start.3
  14.2 0.0 copy-start.9
  14.2 0.0 copy-start.10
  14.2 1.7 %copy.17 = bf16[3,3,256,256]{2,3,1,0:T(8,128)(2,1)S(1)} copy(bf16[3,3,256,256]{3,2,1,0:T(8,128)(2,1)} %bitcast.21) | data formatting | bytes 2359296 | tf_op jit(solution)/shard_map/reshape | solution.py:658
  15.9 0.0 copy-start.2
  15.9 0.1 pad_add_fusion.place.refs_0_
  16.0 0.0 collective-permute-done.1.got_b
  16.0 0.0 collective-permute-done.got_a
  16.1 4.6 %shard_map.137 = (bf16[2,576,128]{2,1,0:T(8,128)(2,1)S(1)}, f32[2,544,128]{2,1,0:T(8,128)S(1)}, bf16[2,544,128]{2,1,0:T(8,128)(2,1)S(1)}, bf16[2,544,128]{2,1,0:T(8,128)(2,1)S(1)}, bf16[2,544,128]{2,1,0:T(8,128)(2,1)S(1)}) custom-call(s32[2]{0:T(128)S(1)} %pad_add_fusion.place.refs_0_, s32[2]{0:T(128)S(1)} %copy-done.10, s32[2,4]{1,0:T(2,128)S(1)} %copy-done.9, ...), custom_call_target="tpu_custom_call" | custom-call | flops 570425344 | bytes 3883056 | tf_op jit(solution)/shard_map/pallas_call | solution.py:46
  20.7 0.0 collective-permute-done.3.refs_3_
  20.7 0.0 collective-permute-done.2.refs_2_
  20.7 0.7 collective-permute-start.5
  21.4 2.7 %collective-permute-start.4 = (bf16[2,576,128]{2,1,0:T(8,128)(2,1)S(1)}, bf16[2,576,128]{2,1,0:T(8,128)(2,1)S(1)}, u32[]{:S(2)}, u32[]{:S(2)}) collective-permute-start(bf16[2,576,128]{2,1,0:T(8,128)(2,1)S(1)} %get-tuple-element.83.motion), channel_id=1, source_target_pairs={{0,4},{8,12},{16,20},{24,28},{32,36},{40,44},{48,52},{56,60},{64,6... | collective-permute-start | bytes 884744 | tf_op jit(solution)/shard_map/ppermute | solution.py:601
  24.0 1.6 %shard_map.138 = (bf16[2,544,768]{2,1,0:T(8,128)(2,1)S(1)}, f32[4,544,256]{2,1,0:T(8,128)S(1)}) custom-call(bf16[2,544,128]{2,1,0:T(8,128)(2,1)S(1)} %get-tuple-element.79.hidden.refs_1_, bf16[2,576,128]{2,1,0:T(8,128)(2,1)S(1)} %get-tuple-element.83.motion, bf16[2304,256]{1,0:T(8,128)(2,1)S(1)} %copy-done.2), custom_call_target="tpu_custom_call" | custom-call | flops 1283457024 | bytes 5652480 | tf_op jit(solution)/shard_map/pallas_call | solution.py:46
  25.6 0.0 collective-permute-done.5.refs_5_.motion_b
  25.6 4.7 %collective-permute-done.4.refs_4_.motion_a = bf16[2,576,128]{2,1,0:T(8,128)(2,1)S(1)} collective-permute-done((bf16[2,576,128]{2,1,0:T(8,128)(2,1)S(1)}, bf16[2,576,128]{2,1,0:T(8,128)(2,1)S(1)}, u32[]{:S(2)}, u32[]{:S(2)}) %collective-permute-start.4) | collective-permute-done | bytes 294944 | tf_op jit(solution)/shard_map/ppermute | solution.py:601
  30.4 4.4 %shard_map.139 = (bf16[2,544,128]{2,1,0:T(8,128)(2,1)S(1)}, f32[4,544,128]{2,1,0:T(8,128)S(1)}, f32[4,544,128]{2,1,0:T(8,128)S(1)}, bf16[4,544,128]{2,1,0:T(8,12...) custom-call(s32[2]{0:T(128)S(1)} %pad_add_fusion.place.refs_0_, ...), custom_call_target="tpu_custom_call" | custom-call | flops 3208642560 | bytes 11239432 | tf_op jit(solution)/shard_map/pallas_call | solution.py:46
  34.8 0.7 collective-permute-start.7
  35.5 6.0 %collective-permute-start.6 = (bf16[2,544,128]{2,1,0:T(8,128)(2,1)S(1)}, bf16[2,544,128]{2,1,0:T(8,128)(2,1)S(1)}, u32[]{:S(2)}, u32[]{:S(2)}) collective-permute-start(bf16[2,544,128]{2,1,0:T(8,128)(2,1)S(1)} %get-tuple-element.87.hidden.refs_5_), channel_id=1, source_target_pairs={{0,4},{8,12},{16,20},{24,28},{32,36},{40,44},{48,52},{56,60},{64,6... | collective-permute-start | bytes 835592 | tf_op jit(solution)/shard_map/ppermute | solution.py:601
  41.5 1.6 %shard_map.140 = (bf16[2,544,768]{2,1,0:T(8,128)(2,1)S(1)}, f32[4,544,256]{2,1,0:T(8,128)S(1)}) custom-call(bf16[2,544,128]{2,1,0:T(8,128)(2,1)S(1)} %get-tuple-element.87.hidden.refs_5_, bf16[2,576,128]{2,1,0:T(8,128)(2,1)S(1)} %get-tuple-element.83.motion, bf16[2304,256]{1,0:T(8,128)(2,1)S(1)} %copy-done.2), custom_call_target="tpu_custom_call" | custom-call | flops 1283457024 | bytes 5652480 | tf_op jit(solution)/shard_map/pallas_call | solution.py:46
  43.1 3.3 %collective-permute-done.6.hidden_a.refs_6_ = bf16[2,544,128]{2,1,0:T(8,128)(2,1)S(1)} collective-permute-done((bf16[2,544,128]{2,1,0:T(8,128)(2,1)S(1)}, bf16[2,544,128]{2,1,0:T(8,128)(2,1)S(1)}, u32[]{:S(2)}, u32[]{:S(2)}) %collective-permute-start.6) | collective-permute-done | bytes 278560 | tf_op jit(solution)/shard_map/ppermute | solution.py:601
  46.3 4.0 %shard_map.141 = (f32[4,544,128]{2,1,0:T(8,128)S(1)}, f32[4,544,128]{2,1,0:T(8,128)S(1)}, bf16[4,544,128]{2,1,0:T(8,128)(2,1)S(1)}, bf16[2,544,128]{2,1,0:T(8,12...) custom-call(s32[2]{0:T(128)S(1)} %pad_add_fusion.place.refs_0_, ...), custom_call_target="tpu_custom_call" | custom-call | flops 3208642560 | bytes 11550728 | tf_op jit(solution)/shard_map/pallas_call | solution.py:46
  50.3 1.3 collective-permute-start.8
  51.6 0.7 collective-permute-start.9
  52.3 1.0 shard_map.142.refs_1_
  53.3 3.0 %shard_map.143 = (f32[2304,128]{1,0:T(8,128)S(1)}, f32[2304,128]{1,0:T(8,128)S(1)}) custom-call(s32[2]{0:T(128)S(1)} %pad_add_fusion.place.refs_0_, bf16[4,544,128]{2,1,0:T(8,128)(2,1)S(1)} %get-tuple-element.95.resets, bf16[2,544,128]{2,1,0:T(8,128)(2,1)S(1)} %get-tuple-element.87.hidden.refs_5_, ...), custom_call_target="tpu_custom_call" | custom-call | flops 1283457024 | bytes 5193736 | tf_op jit(solution)/shard_map/pallas_call | solution.py:46
  56.4 2.4 %collective-permute-done.8.refs_2_ = bf16[3,544,128]{2,1,0:T(8,128)(2,1)S(1)} collective-permute-done((bf16[3,544,128]{2,1,0:T(8,128)(2,1)S(1)}, bf16[3,544,128]{2,1,0:T(8,128)(2,1)S(1)}, u32[]{:S(2)}, u32[]{:S(2)}) %collective-permute-start.8) | collective-permute-done | bytes 417824 | tf_op jit(solution)/shard_map/ppermute | solution.py:606
  58.8 3.6 %shard_map.144 = (bf16[2,544,128]{2,1,0:T(8,128)(2,1)S(1)}, f32[2,544,128]{2,1,0:T(8,128)S(1)}, f32[2,544,128]{2,1,0:T(8,128)S(1)}, bf16[2,544,128]{2,1,0:T(8,12...) custom-call(s32[2]{0:T(128)S(1)} %pad_add_fusion.place.refs_0_, ...), custom_call_target="tpu_custom_call" | custom-call | flops 2566914048 | bytes 13467656 | tf_op jit(solution)/shard_map/pallas_call | solution.py:46
  62.5 4.9 %collective-permute-start.10 = (bf16[3,544,128]{2,1,0:T(8,128)(2,1)S(1)}, bf16[3,544,128]{2,1,0:T(8,128)(2,1)S(1)}, u32[]{:S(2)}, u32[]{:S(2)}) collective-permute-start(bf16[3,544,128]{2,1,0:T(8,128)(2,1)S(1)} %get-tuple-element.107), channel_id=1, source_target_pairs={{0,4},{8,12},{16,20},{24,28},{32,36},{40,44},{48,52},{56,60},{64,6... | collective-permute-start | bytes 1253384 | tf_op jit(solution)/shard_map/ppermute | solution.py:606
  67.4 0.9 collective-permute-start.11
  68.3 1.0 shard_map.145.partial
  69.3 4.2 %shard_map.146 = (f32[2304,128]{1,0:T(8,128)S(1)}, f32[2304,128]{1,0:T(8,128)S(1)}, f32[2304,128]{1,0:T(8,128)S(1)}) custom-call(s32[2]{0:T(128)S(1)} %pad_add_fusion.place.refs_0_, bf16[4,544,128]{2,1,0:T(8,128)(2,1)S(1)} %get-tuple-element.109.resets, bf16[4,544,128]{2,1,0:T(8,128)(2,1)S(1)} %get-tuple-element.86.refs_13_.older.hiddens, ...), custom_call_target="tpu_custom_call" | custom-call | flops 1925185536 | bytes 9568264 | tf_op jit(solution)/shard_map/pallas_call | solution.py:46
  73.5 0.0 collective-permute-done.10.grad_a
  73.5 0.0 collective-permute-done.11.grad_b
  73.5 4.2 %shard_map.147 = (bf16[2,544,128]{2,1,0:T(8,128)(2,1)S(1)}, bf16[2,512,128]{2,1,0:T(8,128)(2,1)}, f32[2,512,128]{2,1,0:T(8,128)S(1)}, f32[128,128]{1,0:T(8,128)S(1)}) custom-call(s32[2]{0:T(128)S(1)} %pad_add_fusion.place.refs_0_, f32[4,544,256]{2,1,0:T(8,128)S(1)} %shard_map.145.partial, bf16[3,544,128]{2,1,0:T(8,128)(2,1)S(1)} %collective-permute-done.10.grad_a, ...), custom_call_target="tpu_custom_call" | custom-call | flops 2566914048 | bytes 11010056 | tf_op jit(solution)/shard_map/pallas_call | solution.py:46
  77.7 2.3 %shard_map.148 = (bf16[3584,128]{1,0:T(8,128)(2,1)S(1)}, bf16[3584,128]{1,0:T(8,128)(2,1)S(1)}) custom-call(s32[2]{0:T(128)S(1)} %pad_add_fusion.place.refs_0_, bf16[4,544,128]{2,1,0:T(8,128)(2,1)S(1)} %get-tuple-element.86.refs_13_.older.hiddens, bf16[2,576,128]{2,1,0:T(8,128)(2,1)S(1)} %get-tuple-element.83.motion, ...), custom_call_target="tpu_custom_call" | custom-call | flops 641728512 | bytes 7159816 | tf_op jit(solution)/shard_map/pallas_call | solution.py:46
  80.0 4.5 %collective-permute-start.12 = (bf16[3584,128]{1,0:T(8,128)(2,1)S(1)}, bf16[3584,128]{1,0:T(8,128)(2,1)S(1)}, u32[]{:S(2)}, u32[]{:S(2)}) collective-permute-start(bf16[3584,128]{1,0:T(8,128)(2,1)S(1)} %get-tuple-element.130), channel_id=1, source_target_pairs={{0,1},{1,0},{2,3},{3,2},{4,5},{5,4},{6,7},{7,6},{8,9},{9,8},{10,11... | collective-permute-start | bytes 2752520 | tf_op jit(solution)/shard_map/ppermute | solution.py:632
  84.5 2.1 %collective-permute-done.12 = bf16[3584,128]{1,0:T(8,128)(2,1)S(1)} collective-permute-done((bf16[3584,128]{1,0:T(8,128)(2,1)S(1)}, bf16[3584,128]{1,0:T(8,128)(2,1)S(1)}, u32[]{:S(2)}, u32[]{:S(2)}) %collective-permute-start.12) | collective-permute-done | bytes 917536 | tf_op jit(solution)/shard_map/ppermute | solution.py:632
  86.6 1.2 add_convert_fusion
  87.7 19.2 %all-to-all-start = ((bf16[64,56,128]{2,1,0:T(8,128)(2,1)}), bf16[64,56,128]{2,1,0:T(8,128)(2,1)S(1)}, u32[]{:S(2)}, u32[]{:S(2)}) async-start(bf16[64,56,128]{2,1,0:T(8,128)(2,1)} %bitcast.23), calls=%async_computation | async-start | bytes 1835008 | tf_op jit(solution)/shard_map/all_to_all | solution.py:618
  106.9 3.7 %shard_map.149 = (bf16[2,512,256]{2,1,0:T(8,128)(2,1)}, bf16[2,192,256]{2,1,0:T(8,128)(2,1)S(1)}, f32[2,512,256]{2,1,0:T(8,128)S(1)}) custom-call(s32[2]{0:T(128)S(1)} %pad_add_fusion.place.refs_0_, s32[2]{0:T(128)S(1)} %copy-done.10, s32[2,4]{1,0:T(2,128)S(1)} %copy-done.9, bf16[2,512,256]{2,1,0:T(8,128)(2,1)S(1)} %copy-done, ...), custom_call_target="tpu_custom_call" | custom-call | flops 855638016 | bytes 3932208 | tf_op jit(solution)/shard_map/pallas_call | solution.py:46
  110.7 1.0 copy-done.5
  111.6 11.1 %all-to-all-done.pieces = bf16[64,56,128]{2,1,0:T(8,128)(2,1)S(1)} async-done(((bf16[64,56,128]{2,1,0:T(8,128)(2,1)}), bf16[64,56,128]{2,1,0:T(8,128)(2,1)S(1)}, u32[]{:S(2)}, u32[]{:S(2)}) %all-to-all-start) | async-done | bytes 917536 | tf_op jit(solution)/shard_map/all_to_all | solution.py:618
  122.7 1.1 shard_map.150
  123.8 5.6 %all-to-all-start.1 = ((bf16[64,56,128]{2,1,0:T(8,128)(2,1)}), bf16[64,56,128]{2,1,0:T(8,128)(2,1)S(1)}, u32[]{:S(2)}, u32[]{:S(2)}) async-start(bf16[64,56,128]{2,1,0:T(8,128)(2,1)} %shard_map.150), calls=%async_computation.1 | async-start | bytes 1835008 | tf_op jit(solution)/shard_map/all_to_all | solution.py:627
  129.4 6.8 %collective-permute-start.14 = (bf16[2,192,256]{2,1,0:T(8,128)(2,1)S(1)}, bf16[2,192,256]{2,1,0:T(8,128)(2,1)S(1)}, u32[]{:S(2)}, u32[]{:S(2)}) collective-permute-start(bf16[2,192,256]{2,1,0:T(8,128)(2,1)S(1)} %get-tuple-element.138), channel_id=1, source_target_pairs={{1,2},{2,1},{5,6},{6,5},{9,10},{10,9},{13,14},{14,13},{17,18},{18,... | collective-permute-start | bytes 589832 | tf_op jit(solution)/shard_map/ppermute | solution.py:601
  136.2 0.1 collective-permute-start.13
  136.3 8.6 %collective-permute-done.14.back_b = bf16[2,192,256]{2,1,0:T(8,128)(2,1)S(1)} collective-permute-done((bf16[2,192,256]{2,1,0:T(8,128)(2,1)S(1)}, bf16[2,192,256]{2,1,0:T(8,128)(2,1)S(1)}, u32[]{:S(2)}, u32[]{:S(2)}) %collective-permute-start.14) | collective-permute-done | bytes 196640 | tf_op jit(solution)/shard_map/ppermute | solution.py:601
  144.9 0.0 collective-permute-done.13.back_a
  144.9 1.4 shard_map.151
  146.4 1.7 %collective-permute-start.15 = (bf16[3584,128]{1,0:T(8,128)(2,1)S(1)}, bf16[3584,128]{1,0:T(8,128)(2,1)S(1)}, u32[]{:S(2)}, u32[]{:S(2)}) collective-permute-start(bf16[3584,128]{1,0:T(8,128)(2,1)S(1)} %bitcast.18), channel_id=1, source_target_pairs={{0,1},{1,0},{2,3},{3,2},{4,5},{5,4},{6,7},{7,6},{8,9},{9,8},{10,11... | collective-permute-start | bytes 2752520 | tf_op jit(solution)/shard_map/ppermute | solution.py:632
  148.1 1.8 %shard_map.152 = (f32[2304,256]{1,0:T(8,128)}, f32[2304,128]{1,0:T(8,128)}) custom-call(s32[2]{0:T(128)S(1)} %pad_add_fusion.place.refs_0_, bf16[3584,128]{1,0:T(8,128)(2,1)S(1)} %bitcast.19), custom_call_target="tpu_custom_call" | custom-call | bytes 1769472 | tf_op jit(solution)/shard_map/pallas_call | solution.py:161
  149.9 0.3 collective-permute-done.15.refs_2_
  150.2 2.4 %shard_map.153 = (f32[36,128]{1,0:T(8,128)}, f32[2304,256]{1,0:T(8,128)}, f32[2304,128]{1,0:T(8,128)}) custom-call(s32[2]{0:T(128)S(1)} %pad_add_fusion.place.refs_0_, bf16[3584,128]{1,0:T(8,128)(2,1)S(1)} %bitcast.20, bf16[3584,128]{1,0:T(8,128)(2,1)S(1)} %collective-permute-done.15.refs_2_, ...), custom_call_target="tpu_custom_call", output_to_operand_aliasing={{1}: (3, {}), {2}: (4, {})} | custom-call | bytes 1769472 | tf_op jit(solution)/shard_map/pallas_call | solution.py:161
  (19 shorter events, 0.0 us)
Async XLA Ops:
  0.6 8.0 %copy-start.4 = (bf16[2,512,128]{2,1,0:T(8,128)(2,1)S(1)}, bf16[2,512,128]{2,1,0:T(8,128)(2,1)}, u32[]{:S(2)}) copy-start(bf16[2,512,128]{2,1,0:T(8,128)(2,1)} %hidden.3) | copy-start | bytes 786436
  0.6 13.3 %copy-start.7 = (bf16[2304,128]{1,0:T(8,128)(2,1)S(1)}, bf16[2304,128]{1,0:T(8,128)(2,1)}, u32[]{:S(2)}) copy-start(bf16[2304,128]{1,0:T(8,128)(2,1)} %cand_w.1) | copy-start | bytes 1769476
  2.5 13.5 %collective-permute-start.1 = (bf16[2,288,256]{2,1,0:T(8,128)(2,1)}, bf16[2,288,256]{2,1,0:T(8,128)(2,1)}, u32[]{:S(2)}, u32[]{:S(2)}) collective-permute-start(bf16[2,288,256]{2,1,0:T(8,128)(2,1)} %shard_map.136), channel_id=1, source_target_pairs={{1,2},{2,1},{5,6},{6,5},{9,10},{10,9},{13,14},{14,13},{17,18},{18,... | collective-permute-start | bytes 884744 | tf_op jit(solution)/shard_map/ppermute | solution.py:601
  8.5 7.5 %collective-permute-start = (bf16[2,288,256]{2,1,0:T(8,128)(2,1)}, bf16[2,288,256]{2,1,0:T(8,128)(2,1)}, u32[]{:S(2)}, u32[]{:S(2)}) collective-permute-start(bf16[2,288,256]{2,1,0:T(8,128)(2,1)} %shard_map.136), channel_id=1, source_target_pairs={{0,1},{2,3},{1,0},{3,2},{4,5},{6,7},{5,4},{7,6},{8,9},{10,11},{9,8... | collective-permute-start | bytes 884744 | tf_op jit(solution)/shard_map/ppermute | solution.py:601
  8.6 12.0 %collective-permute-start.3 = (bf16[2,512,128]{2,1,0:T(8,128)(2,1)S(1)}, bf16[2,512,128]{2,1,0:T(8,128)(2,1)}, u32[]{:S(2)}, u32[]{:S(2)}) collective-permute-start(bf16[2,512,128]{2,1,0:T(8,128)(2,1)S(1)} %copy-done.4), channel_id=1, source_target_pairs={{4,8},{12,16},{20,24},{28,32},{36,40},{44,48},{52,56},{60,64},{68,... | collective-permute-start | bytes 786440 | tf_op jit(solution)/shard_map/ppermute | solution.py:601
  10.0 10.7 %collective-permute-start.2 = (bf16[2,512,128]{2,1,0:T(8,128)(2,1)S(1)}, bf16[2,512,128]{2,1,0:T(8,128)(2,1)}, u32[]{:S(2)}, u32[]{:S(2)}) collective-permute-start(bf16[2,512,128]{2,1,0:T(8,128)(2,1)S(1)} %copy-done.4), channel_id=1, source_target_pairs={{0,4},{8,12},{16,20},{24,28},{32,36},{40,44},{48,52},{56,60},{64,6... | collective-permute-start | bytes 786440 | tf_op jit(solution)/shard_map/ppermute | solution.py:601
  14.1 1.7 %copy-start.11 = (bf16[36,128]{1,0:T(8,128)(2,1)S(1)}, bf16[36,128]{1,0:T(8,128)(2,1)}, u32[]{:S(2)}) copy-start(bf16[36,128]{1,0:T(8,128)(2,1)} %param.14) | copy-start | bytes 27652
  14.2 1.9 %copy-start = (bf16[2,512,256]{2,1,0:T(8,128)(2,1)S(1)}, bf16[2,512,256]{2,1,0:T(8,128)(2,1)}, u32[]{:S(2)}) copy-start(bf16[2,512,256]{2,1,0:T(8,128)(2,1)} %left.5) | copy-start | bytes 1572868
  14.2 1.9 %copy-start.1 = (bf16[2,512,256]{2,1,0:T(8,128)(2,1)S(1)}, bf16[2,512,256]{2,1,0:T(8,128)(2,1)}, u32[]{:S(2)}) copy-start(bf16[2,512,256]{2,1,0:T(8,128)(2,1)} %right.5) | copy-start | bytes 1572868
  14.2 1.8 %copy-start.3 = (bf16[2,512,128]{2,1,0:T(8,128)(2,1)S(1)}, bf16[2,512,128]{2,1,0:T(8,128)(2,1)}, u32[]{:S(2)}) copy-start(bf16[2,512,128]{2,1,0:T(8,128)(2,1)} %grads.3) | copy-start | bytes 786436
  14.2 1.8 %copy-start.9 = (s32[2,4]{1,0:T(2,128)S(1)}, s32[2,4]{1,0:T(2,128)}, u32[]{:S(2)}) copy-start(s32[2,4]{1,0:T(2,128)} %offsets.3) | copy-start | bytes 100
  14.2 1.8 %copy-start.10 = (s32[2]{0:T(128)S(1)}, s32[2]{0:T(128)}, u32[]{:S(2)}) copy-start(s32[2]{0:T(128)} %disparity.3) | copy-start | bytes 28
  15.9 8.1 %copy-start.2 = (bf16[2304,256]{1,0:T(8,128)(2,1)S(1)}, bf16[2304,256]{1,0:T(8,128)(2,1)}, u32[]{:S(2)}) copy-start(bf16[2304,256]{1,0:T(8,128)(2,1)} %gate_w.5) | copy-start | bytes 3538948
  20.7 4.9 %collective-permute-start.5 = (bf16[2,576,128]{2,1,0:T(8,128)(2,1)S(1)}, bf16[2,576,128]{2,1,0:T(8,128)(2,1)S(1)}, u32[]{:S(2)}, u32[]{:S(2)}) collective-permute-start(bf16[2,576,128]{2,1,0:T(8,128)(2,1)S(1)} %get-tuple-element.83.motion), channel_id=1, source_target_pairs={{4,8},{12,16},{20,24},{28,32},{36,40},{44,48},{52,56},{60,64},{68,... | collective-permute-start | bytes 884744 | tf_op jit(solution)/shard_map/ppermute | solution.py:601
  21.4 9.0 %collective-permute-start.4 = (bf16[2,576,128]{2,1,0:T(8,128)(2,1)S(1)}, bf16[2,576,128]{2,1,0:T(8,128)(2,1)S(1)}, u32[]{:S(2)}, u32[]{:S(2)}) collective-permute-start(bf16[2,576,128]{2,1,0:T(8,128)(2,1)S(1)} %get-tuple-element.83.motion), channel_id=1, source_target_pairs={{0,4},{8,12},{16,20},{24,28},{32,36},{40,44},{48,52},{56,60},{64,6... | collective-permute-start | bytes 884744 | tf_op jit(solution)/shard_map/ppermute | solution.py:601
  24.0 6.3 %copy-start.8 = (bf16[2304,128]{1,0:T(8,128)(2,1)S(1)}, bf16[2304,128]{1,0:T(8,128)(2,1)}, u32[]{:S(2)}) copy-start(bf16[2304,128]{1,0:T(8,128)(2,1)} %cand_w.1) | copy-start | bytes 1769476
  34.8 8.3 %collective-permute-start.7 = (bf16[2,544,128]{2,1,0:T(8,128)(2,1)S(1)}, bf16[2,544,128]{2,1,0:T(8,128)(2,1)S(1)}, u32[]{:S(2)}, u32[]{:S(2)}) collective-permute-start(bf16[2,544,128]{2,1,0:T(8,128)(2,1)S(1)} %get-tuple-element.87.hidden.refs_5_), channel_id=1, source_target_pairs={{4,8},{12,16},{20,24},{28,32},{36,40},{44,48},{52,56},{60,64},{68,... | collective-permute-start | bytes 835592 | tf_op jit(solution)/shard_map/ppermute | solution.py:601
  35.5 10.9 %collective-permute-start.6 = (bf16[2,544,128]{2,1,0:T(8,128)(2,1)S(1)}, bf16[2,544,128]{2,1,0:T(8,128)(2,1)S(1)}, u32[]{:S(2)}, u32[]{:S(2)}) collective-permute-start(bf16[2,544,128]{2,1,0:T(8,128)(2,1)S(1)} %get-tuple-element.87.hidden.refs_5_), channel_id=1, source_target_pairs={{0,4},{8,12},{16,20},{24,28},{32,36},{40,44},{48,52},{56,60},{64,6... | collective-permute-start | bytes 835592 | tf_op jit(solution)/shard_map/ppermute | solution.py:601
  50.3 8.5 %collective-permute-start.8 = (bf16[3,544,128]{2,1,0:T(8,128)(2,1)S(1)}, bf16[3,544,128]{2,1,0:T(8,128)(2,1)S(1)}, u32[]{:S(2)}, u32[]{:S(2)}) collective-permute-start(bf16[3,544,128]{2,1,0:T(8,128)(2,1)S(1)} %get-tuple-element.93), channel_id=1, source_target_pairs={{0,4},{8,12},{16,20},{24,28},{32,36},{40,44},{48,52},{56,60},{64,6... | collective-permute-start | bytes 1253384 | tf_op jit(solution)/shard_map/ppermute | solution.py:606
  51.6 7.2 %collective-permute-start.9 = (bf16[3,544,128]{2,1,0:T(8,128)(2,1)S(1)}, bf16[3,544,128]{2,1,0:T(8,128)(2,1)S(1)}, u32[]{:S(2)}, u32[]{:S(2)}) collective-permute-start(bf16[3,544,128]{2,1,0:T(8,128)(2,1)S(1)} %get-tuple-element.94), channel_id=1, source_target_pairs={{4,8},{12,16},{20,24},{28,32},{36,40},{44,48},{52,56},{60,64},{68,... | collective-permute-start | bytes 1253384 | tf_op jit(solution)/shard_map/ppermute | solution.py:606
  62.5 11.0 %collective-permute-start.10 = (bf16[3,544,128]{2,1,0:T(8,128)(2,1)S(1)}, bf16[3,544,128]{2,1,0:T(8,128)(2,1)S(1)}, u32[]{:S(2)}, u32[]{:S(2)}) collective-permute-start(bf16[3,544,128]{2,1,0:T(8,128)(2,1)S(1)} %get-tuple-element.107), channel_id=1, source_target_pairs={{0,4},{8,12},{16,20},{24,28},{32,36},{40,44},{48,52},{56,60},{64,6... | collective-permute-start | bytes 1253384 | tf_op jit(solution)/shard_map/ppermute | solution.py:606
  67.4 6.2 %collective-permute-start.11 = (bf16[3,544,128]{2,1,0:T(8,128)(2,1)S(1)}, bf16[3,544,128]{2,1,0:T(8,128)(2,1)S(1)}, u32[]{:S(2)}, u32[]{:S(2)}) collective-permute-start(bf16[3,544,128]{2,1,0:T(8,128)(2,1)S(1)} %get-tuple-element.108), channel_id=1, source_target_pairs={{4,8},{12,16},{20,24},{28,32},{36,40},{44,48},{52,56},{60,64},{68,... | collective-permute-start | bytes 1253384 | tf_op jit(solution)/shard_map/ppermute | solution.py:606
  80.0 6.6 %collective-permute-start.12 = (bf16[3584,128]{1,0:T(8,128)(2,1)S(1)}, bf16[3584,128]{1,0:T(8,128)(2,1)S(1)}, u32[]{:S(2)}, u32[]{:S(2)}) collective-permute-start(bf16[3584,128]{1,0:T(8,128)(2,1)S(1)} %get-tuple-element.130), channel_id=1, source_target_pairs={{0,1},{1,0},{2,3},{3,2},{4,5},{5,4},{6,7},{7,6},{8,9},{9,8},{10,11... | collective-permute-start | bytes 2752520 | tf_op jit(solution)/shard_map/ppermute | solution.py:632
  87.7 35.0 %all-to-all-start = ((bf16[64,56,128]{2,1,0:T(8,128)(2,1)}), bf16[64,56,128]{2,1,0:T(8,128)(2,1)S(1)}, u32[]{:S(2)}, u32[]{:S(2)}) async-start(bf16[64,56,128]{2,1,0:T(8,128)(2,1)} %bitcast.23), calls=%async_computation | async-start | bytes 1835008 | tf_op jit(solution)/shard_map/all_to_all | solution.py:618
  110.7 1.0 copy-start.5
  123.8 21.1 %copy-start.6 = (f32[2,512,256]{2,1,0:T(8,128)S(1)}, f32[2,512,256]{2,1,0:T(8,128)}, u32[]{:S(2)}) copy-start(f32[2,512,256]{2,1,0:T(8,128)} %copy-done.5) | copy-start | bytes 3145732
  123.8 22.5 %all-to-all-start.1 = ((bf16[64,56,128]{2,1,0:T(8,128)(2,1)}), bf16[64,56,128]{2,1,0:T(8,128)(2,1)S(1)}, u32[]{:S(2)}, u32[]{:S(2)}) async-start(bf16[64,56,128]{2,1,0:T(8,128)(2,1)} %shard_map.150), calls=%async_computation.1 | async-start | bytes 1835008 | tf_op jit(solution)/shard_map/all_to_all | solution.py:627
  129.4 15.5 %collective-permute-start.14 = (bf16[2,192,256]{2,1,0:T(8,128)(2,1)S(1)}, bf16[2,192,256]{2,1,0:T(8,128)(2,1)S(1)}, u32[]{:S(2)}, u32[]{:S(2)}) collective-permute-start(bf16[2,192,256]{2,1,0:T(8,128)(2,1)S(1)} %get-tuple-element.138), channel_id=1, source_target_pairs={{1,2},{2,1},{5,6},{6,5},{9,10},{10,9},{13,14},{14,13},{17,18},{18,... | collective-permute-start | bytes 589832 | tf_op jit(solution)/shard_map/ppermute | solution.py:601
  136.2 8.7 %collective-permute-start.13 = (bf16[2,192,256]{2,1,0:T(8,128)(2,1)S(1)}, bf16[2,192,256]{2,1,0:T(8,128)(2,1)S(1)}, u32[]{:S(2)}, u32[]{:S(2)}) collective-permute-start(bf16[2,192,256]{2,1,0:T(8,128)(2,1)S(1)} %get-tuple-element.138), channel_id=1, source_target_pairs={{0,1},{2,3},{1,0},{3,2},{4,5},{6,7},{5,4},{7,6},{8,9},{10,11},{9,8... | collective-permute-start | bytes 589832 | tf_op jit(solution)/shard_map/ppermute | solution.py:601
  146.4 3.8 %collective-permute-start.15 = (bf16[3584,128]{1,0:T(8,128)(2,1)S(1)}, bf16[3584,128]{1,0:T(8,128)(2,1)S(1)}, u32[]{:S(2)}, u32[]{:S(2)}) collective-permute-start(bf16[3584,128]{1,0:T(8,128)(2,1)S(1)} %bitcast.18), channel_id=1, source_target_pairs={{0,1},{1,0},{2,3},{3,2},{4,5},{5,4},{6,7},{7,6},{8,9},{9,8},{10,11... | collective-permute-start | bytes 2752520 | tf_op jit(solution)/shard_map/ppermute | solution.py:632

commit v5 on v4

--- a/solution.py
+++ b/solution.py
@@ -125,35 +125,37 @@
     )(left, right, hidden, grads)
 
 
-def spread_half(core, half, scale, gate, cand, gate_part, cand_part, sems):
-    depth = gate_part.shape[0]
-    count = cand_part.shape[0]
-    block = depth // 4
-    lanes = pl.ds(pl.multiple_of(core * LANES, LANES), LANES)
+def turn_kernel(gate_w, cand_w, gate_wt, cand_wt):
+    for tap in range(9):
+        here = slice(tap * 2 * LANES, (tap + 1) * 2 * LANES)
+        gate_wt[here] = gate_w[here].T
+        cand_wt[tap * LANES : (tap + 1) * LANES] = cand_w[here].T
+
+
+def spread_half(core, half, scale, gate, cand, parts, sems):
+    count = parts.shape[1]
+    there = pl.ds(pl.multiple_of(core * count, LANES), count)
+    targets = (gate.at[there, pl.ds(0, LANES)], cand.at[there], gate.at[there, pl.ds(LANES, LANES)])
     copies = []
-    for number in range(4):
-        here = pl.ds(number * block, block)
-        gate_part[here] = half[here].astype(F32) * scale
-        copies.append(pltpu.make_async_copy(gate_part.at[here], gate.at[here, lanes], sems.at[number]))
+    for number, target in enumerate(targets):
+        parts[number] = half[number * count : (number + 1) * count].astype(F32) * scale
+        copies.append(pltpu.make_async_copy(parts.at[number], target, sems.at[number]))
         copies[-1].start()
-    cand_part[...] = half[depth : depth + count].astype(F32) * scale
-    there = pl.ds(pl.multiple_of(core * count, LANES), count)
-    copies.append(pltpu.make_async_copy(cand_part, cand.at[there], sems.at[4]))
-    copies[-1].start()
     for copy in copies:
         copy.wait()
 
 
-def own_half_kernel(scale, place, half, gate, cand, gate_part, cand_part, sems):
-    spread_half(place[1] % 2, half, scale, gate, cand, gate_part, cand_part, sems)
-
-
-def other_half_kernel(scale, place, half, other, gate_in, cand_in, motion, gate, cand, gate_part, cand_part, sems):
+def own_half_kernel(scale, place, half, gate, cand, parts, sems):
+    spread_half(place[1] % 2, half, scale, gate, cand, parts, sems)
+
+
+def other_half_kernel(scale, place, half, other, gate_in, cand_in, motion, gate, cand, parts, sems):
     core = place[1] % 2
-    start = gate_part.shape[0] + cand_part.shape[0]
-    rows = pl.ds(start, motion.shape[0])
-    motion[...] = jnp.where(core == 0, half[rows], other[rows]).astype(F32) * scale
-    spread_half(1 - core, other, scale, gate, cand, gate_part, cand_part, sems)
+    start = 3 * parts.shape[1]
+    count = motion.shape[0]
+    rows = slice(start, start + LANES)
+    motion[...] = jnp.where(core == 0, half[rows], other[rows]).astype(F32)[:count] * scale
+    spread_half(1 - core, other, scale, gate, cand, parts, sems)
 
 
 def half_call(body, place, arrays, outs, depth, aliases):
@@ -164,7 +166,7 @@
         in_specs=[SMEM] + [VMEM] * (len(arrays) - len(aliases)) + [anywhere] * len(aliases),
         out_specs=[VMEM] * (len(outs) - 2) + [anywhere] * 2,
         scratch_shapes=[
-            pltpu.VMEM((depth, LANES), F32), pltpu.VMEM((depth // 2, LANES), F32), pltpu.SemaphoreType.DMA((5,))
+            pltpu.VMEM((3, depth // 2, LANES), F32), pltpu.SemaphoreType.DMA((3,))
         ],
         input_output_aliases=aliases,
         compiler_params=pltpu.CompilerParams(vmem_limit_bytes=12 * 2**20),
@@ -502,21 +504,33 @@
     weight_products(pixels, taps, wide, LANES, update_finish)
 
 
+def store_halves(parts, offset, rows, start, value):
+    for piece in range(0, 2 * LANES, LANES):
+        half, row = divmod(start + piece, rows // 2)
+        there = offset + row
+        parts[half, there : there + LANES] = value[piece : piece + LANES].astype(BF16)
+
+
+def share_cores(place, parts, kept, given):
+    core = place[1] % 2
+    kept[...] = parts[core]
+    given[...] = parts[1 - core]
+
+
 def first_weights_kernel(place, resets, older, hidden, hidden_a, hidden_b, motion, motion_a, motion_b,
                          cand_grads, update_grads, reset_grads, cand_sum, update_sum,
-                         cand_out, update_out, reset_out, pixels, taps):
+                         kept, given, reset_out, pixels, taps, parts):
     odd = place[0] % 2 == 1
     wide = taps.shape[0] // 2
+    rows = cand_sum.shape[0]
     load_pixels(odd, pixels, [resets[row] for row in range(4)], motion, motion_a, motion_b)
     load_grads(taps, cand_grads)
 
     def cand_finish(start, value):
-        here = pl.ds(start, 2 * LANES)
-        cand_out[here] = cand_sum[here] + value
+        store_halves(parts, rows // 2, rows, start, cand_sum[pl.ds(start, 2 * LANES)] + value)
 
     def update_finish(start, value):
-        here = pl.ds(start, 2 * LANES)
-        update_out[here] = update_sum[here] + value
+        store_halves(parts, 0, rows, start, update_sum[pl.ds(start, 2 * LANES)] + value)
 
     def reset_finish(start, value):
         reset_out[pl.ds(start, 2 * LANES)] = value
@@ -525,32 +539,32 @@
     load_hidden(pixels, [older[row] for row in range(4)], wide)
     load_grads(taps, update_grads)
     weight_products(pixels, taps, wide, LANES, update_finish)
+    share_cores(place, parts, kept, given)
     load_hidden(pixels, hidden_rows(odd, hidden, hidden_a, hidden_b), wide)
     load_grads(taps, reset_grads)
     weight_products(pixels, taps, wide, LANES, reset_finish)
 
 
-def last_weights_kernel(place, hiddens, motion, motion_a, motion_b, reset_grads, reset_sum,
-                        update_sum, cand_sum, motion_w, kept, given, pixels, taps, parts):
+def last_weights_kernel(place, hiddens, motion, motion_a, motion_b, reset_grads, reset_sum, motion_w,
+                        kept, given, pixels, taps, parts):
     odd = place[0] % 2 == 1
     load_pixels(odd, pixels, [hiddens[row] for row in range(4)], motion, motion_a, motion_b)
     load_grads(taps, reset_grads)
-    rows = cand_sum.shape[0]
-    split = rows // 2
-    last = rows + split
+    rows = reset_sum.shape[0]
 
     def finish(start, value):
-        parts[1, start : start + 2 * LANES] = (value + reset_sum[pl.ds(start, 2 * LANES)]).astype(BF16)
+        store_halves(parts, 0, rows, start, reset_sum[pl.ds(start, 2 * LANES)] + value)
 
     weight_products(pixels, taps, taps.shape[0] // 2, LANES, finish)
-    parts[0, 0:rows] = update_sum[...].astype(BF16)
-    for half in range(2):
-        parts[half, rows:last] = cand_sum[half * split : (half + 1) * split].astype(BF16)
-    parts[0, last:] = motion_w[...].astype(BF16)
-    parts[1, last:] = jnp.zeros((parts.shape[1] - last, LANES), BF16)
-    core = place[1] % 2
-    kept[...] = parts[core]
-    given[...] = parts[1 - core]
+    parts[0, rows // 2 :] = motion_w[...].astype(BF16)
+    parts[1, rows // 2 :] = jnp.zeros((parts.shape[1] - rows // 2, LANES), BF16)
+    share_cores(place, parts, kept, given)
+
+
+def join_kernel(kept, got, last_kept, last_got, half):
+    split = kept.shape[0]
+    half[:split] = (kept[...].astype(F32) + got[...].astype(F32)).astype(BF16)
+    half[split:] = (last_kept[...].astype(F32) + last_got[...].astype(F32)).astype(BF16)
 
 
 def right_kernel(place, own, back_a, back_b, grad_right):
@@ -603,7 +617,8 @@
 
 def exchanged_pair(value_a, value_b, axis):
     first, second = pairings(lax.axis_size(axis))
-    return lax.ppermute(value_a, axis, first), lax.ppermute(value_b, axis, second)
+    other = lax.ppermute(value_b, axis, second)
+    return lax.ppermute(value_a, axis, first), other
 
 
 def core_groups():
@@ -611,9 +626,11 @@
     return [[i for i in range(devices) if i % 2 == c] for c in range(2)]
 
 
-def shared_out(kept, given, axes):
-    got = swapped(given)
-    half = (kept.astype(F32) + got.astype(F32)).astype(BF16)
+def shared_out(kept, got, last_kept, last_given, axes):
+    total = kept.shape[0] + last_kept.shape[0]
+    (half,) = kernel_call(
+        join_kernel, [array((total, LANES), BF16)], [kept, got, last_kept, swapped(last_given)], 0, [], 0
+    )
     half = half.reshape(len(core_groups()[0]), -1, LANES)
     return lax.all_to_all(half, axes, 0, 0, tiled=True, axis_index_groups=core_groups())
 
@@ -651,14 +668,9 @@
     rows_index, cols_index = lax.axis_index("rows"), lax.axis_index("cols")
     place = jnp.stack([rows_index, cols_index]).astype(jnp.int32)
 
-    halos = packed(fmap_left, fmap_right, hidden_init, grad_hidden)
-    maps_a, maps_b = exchanged(halos, "cols")
+    maps_a, maps_b = exchanged(packed(fmap_left, fmap_right, hidden_init, grad_hidden), "cols")
     init_a, init_b = exchanged(hidden_init, "rows")
     motion_w = jnp.pad(motion_weight, ((0, LANES - feats_count), (0, 0)))
-    gate_wt = jnp.transpose(gate_weight.reshape(3, 3, 2 * state, 2 * state), (0, 1, 3, 2)).reshape(-1, 2 * state)
-    cand_wt = jnp.transpose(cand_weight.reshape(3, 3, 2 * state, state), (0, 1, 3, 2)).reshape(-1, 2 * state)
-    motion_w, gate_wt, cand_wt = lax.optimization_barrier((motion_w, gate_wt, cand_wt))
-
     field = lambda count, dtype: array((count, wide, LANES), dtype)
     band_flops = 2 * rows * wide * 512 * channels
     motion, motion_pre, feats, hidden, grads = kernel_call(
@@ -670,7 +682,17 @@
         2 * band_flops,
     )
     motion, init_a, init_b = lax.optimization_barrier((motion, init_a, init_b))
-    motions = (motion, *exchanged(motion, "rows"))
+    motion_a, motion_b = exchanged(motion, "rows")
+    gate_wt, cand_wt = kernel_call(
+        turn_kernel,
+        [array(gate_weight.shape, BF16), array((9 * state, 2 * state), BF16)],
+        [gate_weight, cand_weight],
+        0,
+        [],
+        0,
+    )
+    motion_a, motion_b, gate_wt, cand_wt = lax.optimization_barrier((motion_a, motion_b, gate_wt, cand_wt))
+    motions = (motion, motion_a, motion_b)
     unit = 2 * wide * 9 * 2 * state * state
     fields = [pltpu.VMEM((6, wide, 6 * LANES), BF16), pltpu.VMEM((4, wide, 6 * LANES), BF16)]
 
@@ -731,21 +753,25 @@
         8 * unit,
     )
     got_a, got_b = exchanged_pair(send_a, send_b, "rows")
-    cand_sum, update_sum, reset_sum = kernel_call(
+    depth = cand_weight.shape[0]
+    total = rows_axis * cols_axis * CHUNK_ROWS // 2
+    late = total - depth
+    kept, given, reset_sum = kernel_call(
         first_weights_kernel,
-        [weights, weights, weights],
+        [array((depth, LANES), BF16), array((depth, LANES), BF16), weights],
         [place, reset_hidden_0, hiddens_0, hidden_1, hidden_1a, hidden_1b, *motions,
          grad_cand_0, grad_update_0, grad_reset_1, cand_sum, update_sum],
         1,
-        [pixels, taps],
+        [pixels, taps, pltpu.VMEM((2, depth, LANES), BF16)],
         6 * unit,
     )
     (partial,) = kernel_call(
         own_cand_kernel, [partials], [grad_cand_0, cand_wt], 0, [pltpu.VMEM((2, wide, 3 * LANES), BF16)], 2 * unit
     )
-    got_a, got_b, cand_sum, update_sum, reset_sum = lax.optimization_barrier(
-        (got_a, got_b, cand_sum, update_sum, reset_sum)
-    )
+    got_a, got_b, kept, given, reset_sum, partial = lax.optimization_barrier(
+        (got_a, got_b, kept, given, reset_sum, partial)
+    )
+    got = swapped(given)
     grad_reset_0, grad_first, grad_feats, motion_sum = kernel_call(
         first_back_kernel,
         [field(2, BF16), array((2, cols, LANES), BF16), array((2, cols, LANES), F32), array((LANES, LANES), F32)],
@@ -755,13 +781,13 @@
         back_scratch + [pltpu.VMEM((2, wide, LANES), F32)],
         8 * unit,
     )
-    total = rows_axis * cols_axis * CHUNK_ROWS
-    kept, given = kernel_call(
+    reset_sum, got = lax.optimization_barrier((reset_sum, got))
+    last_kept, last_given = kernel_call(
         last_weights_kernel,
-        [array((total // 2, LANES), BF16), array((total // 2, LANES), BF16)],
-        [place, hiddens_0, *motions, grad_reset_0, reset_sum, update_sum, cand_sum, motion_sum],
+        [array((late, LANES), BF16), array((late, LANES), BF16)],
+        [place, hiddens_0, *motions, grad_reset_0, reset_sum, motion_sum],
         1,
-        [pixels, taps, pltpu.VMEM((2, total // 2, LANES), BF16)],
+        [pixels, taps, pltpu.VMEM((2, late, LANES), BF16)],
         2 * unit,
     )
     grad_left, back, own = kernel_call(
@@ -772,7 +798,7 @@
         [pltpu.VMEM((768, channels), BF16), pltpu.VMEM((768, channels), F32)],
         3 * band_flops,
     )
-    pieces = shared_out(kept, given, ("rows", "cols"))
+    pieces = shared_out(kept, got, last_kept, last_given, ("rows", "cols"))
     pieces, grad_left, back, own = lax.optimization_barrier((pieces, grad_left, back, own))
     back_a, back_b = exchanged(back, "cols")
     (grad_right,) = kernel_call(
@@ -782,7 +808,6 @@
     half, grad_right = lax.optimization_barrier((half, grad_right))
     normaliser = 1.0 / math.sqrt(rows * rows_axis * cols * cols_axis)
     other = swapped(half)
-    depth = cand_weight.shape[0]
     results = [array(gate_weight.shape, F32), array(cand_weight.shape, F32)]
     own_parts = half_call(
         lambda *refs: own_half_kernel(normaliser, *refs), place, [half], results, depth, {}

time: 153 us -> 152 us (level)
  waiting for transfers between devices: 32.5 us -> 30.9 us
    unnamed x24 -> x32, local copies, waits for them, and re-layouts: 1.03 us -> 3.79 us
    reshape x2 -> x0, local copies, waits for them, and re-layouts: 1.91 us -> none  [the longest x1 1.66 us: on_device(): gate_weight.reshape(3, 3, 2 * state, 2 * state)]
    pallas_call x15 -> x17, Pallas kernels: 41.8 us -> 41.5 us  [kernel_call(): pl.pallas_call(body, out_shape=outs, in_specs=[SMEM] * scalars + [VMEM] *...]
    ppermute x2 -> x3, starting transfers between devices: 6.2 us -> 5.96 us  [swapped(): lax.ppermute(value, 'cols', [(i, i ^ 1) for i in range(lax.axis_size('col...]
  transfers between devices with their start and end apart: 18 -> 19, of which waited for: 7 -> 8; matrix products, arithmetic and copies ran while one was open for 1% -> 0% of each run, Pallas kernels for 16% -> 18%
where the time goes in v5:
time: 152 us
  starting transfers between devices  68.2 us (45%)
  Pallas kernels  47.6 us (31%)
  waiting for transfers between devices  30.9 us (20%)
  local copies, waits for them, and re-layouts  3.8 us (2%)
    pallas_call x17, Pallas kernels, kernel_call(): pl.pallas_call(body, out_shape=outs, in_specs=[SMEM] * scalars + [VMEM] *...  41.5 us
    ppermute x10, starting transfers between devices, exchanged(): return (lax.ppermute(value, axis, first), lax.ppermute(value, axis, second))  29.6 us
    all_to_all x1, starting transfers between devices, shared_out(): lax.all_to_all(half, axes, 0, 0, tiled=True, axis_index_groups=core_group...  19.4 us
    ppermute x10, waiting for transfers between devices, exchanged(): return (lax.ppermute(value, axis, first), lax.ppermute(value, axis, second))  16.5 us
    all_to_all x1, waiting for transfers between devices, shared_out(): lax.all_to_all(half, axes, 0, 0, tiled=True, axis_index_groups=core_group...  10 us
    ppermute x2, starting transfers between devices, exchanged_pair(): return (lax.ppermute(value_a, axis, first), other)  6.14 us
    ppermute x3, starting transfers between devices, swapped(): lax.ppermute(value, 'cols', [(i, i ^ 1) for i in range(lax.axis_size('col...  5.96 us
    all_to_all x1, starting transfers between devices, gathered(): lax.all_to_all(spread, axes, 0, 0, tiled=True, axis_index_groups=core_gro...  5.49 us
  transfers between devices with their start and end apart: 19, of which 8 were waited for; matrix products, arithmetic and copies ran while one was open for 0% of the time, Pallas kernels for 18%

profile of v5, /device:TPU:1, one launch (start us, length us, event | category | flops | bytes accessed | tf_op | source)
XLA Modules:
  0.0 151.8 jit_solution(1601522381607699713)
XLA Ops:
  0.7 1.8 %shard_map.136 = bf16[2,288,256]{2,1,0:T(8,128)(2,1)} custom-call(bf16[2,512,256]{2,1,0:T(8,128)(2,1)} %left.5, bf16[2,512,256]{2,1,0:T(8,128)(2,1)} %right.5, bf16[2,512,128]{2,1,0:T(8,128)(2,1)} %hidden.3, bf16[2,512,128]{2,1,0:T(8,128)(2,1)} %grads.3), custom_call_target="tpu_custom_call" | custom-call | bytes 589824 | tf_op jit(solution)/shard_map/pallas_call | solution.py:117
  2.5 0.0 copy-start.2
  2.6 6.2 %collective-permute-start.1 = (bf16[2,288,256]{2,1,0:T(8,128)(2,1)}, bf16[2,288,256]{2,1,0:T(8,128)(2,1)S(1)}, u32[]{:S(2)}, u32[]{:S(2)}) collective-permute-start(bf16[2,288,256]{2,1,0:T(8,128)(2,1)} %shard_map.136), channel_id=1, source_target_pairs={{1,2},{2,1},{5,6},{6,5},{9,10},{10,9},{13,14},{14,13},{17,18},{18,... | collective-permute-start | bytes 884744 | tf_op jit(solution)/shard_map/ppermute | solution.py:615
  8.7 0.1 collective-permute-start
  8.8 1.4 collective-permute-start.3
  10.2 3.9 %collective-permute-start.2 = (bf16[2,512,128]{2,1,0:T(8,128)(2,1)S(1)}, bf16[2,512,128]{2,1,0:T(8,128)(2,1)}, u32[]{:S(2)}, u32[]{:S(2)}) collective-permute-start(bf16[2,512,128]{2,1,0:T(8,128)(2,1)S(1)} %copy-done.4), channel_id=1, source_target_pairs={{0,4},{8,12},{16,20},{24,28},{32,36},{40,44},{48,52},{56,60},{64,6... | collective-permute-start | bytes 786440 | tf_op jit(solution)/shard_map/ppermute | solution.py:615
  14.1 0.1 pad_add_fusion.place.refs_0_
  14.2 0.0 collective-permute-done.1.got_b
  14.2 0.0 collective-permute-done.got_a
  14.3 0.0 copy-start.7
  14.3 4.0 %shard_map.137 = (bf16[2,576,128]{2,1,0:T(8,128)(2,1)S(1)}, f32[2,544,128]{2,1,0:T(8,128)S(1)}, bf16[2,544,128]{2,1,0:T(8,128)(2,1)S(1)}, bf16[2,544,128]{2,1,0:T(8,128)(2,1)S(1)}, bf16[2,544,128]{2,1,0:T(8,128)(2,1)S(1)}) custom-call(s32[2]{0:T(128)S(1)} %pad_add_fusion.place.refs_0_, s32[2]{0:T(128)S(1)} %copy-done.10, s32[2,4]{1,0:T(2,128)S(1)} %copy-done.9, ...), custom_call_target="tpu_custom_call" | custom-call | flops 570425344 | bytes 3883056 | tf_op jit(solution)/shard_map/pallas_call | solution.py:46
  18.3 0.0 collective-permute-done.3.refs_3_
  18.3 1.8 %collective-permute-done.2.refs_2_ = bf16[2,512,128]{2,1,0:T(8,128)(2,1)} collective-permute-done((bf16[2,512,128]{2,1,0:T(8,128)(2,1)S(1)}, bf16[2,512,128]{2,1,0:T(8,128)(2,1)}, u32[]{:S(2)}, u32[]{:S(2)}) %collective-permute-start.2) | collective-permute-done | bytes 262176 | tf_op jit(solution)/shard_map/ppermute | solution.py:615
  20.2 0.7 collective-permute-start.5
  20.8 2.7 %collective-permute-start.4 = (bf16[2,576,128]{2,1,0:T(8,128)(2,1)S(1)}, bf16[2,576,128]{2,1,0:T(8,128)(2,1)S(1)}, u32[]{:S(2)}, u32[]{:S(2)}) collective-permute-start(bf16[2,576,128]{2,1,0:T(8,128)(2,1)S(1)} %get-tuple-element.88.motion), channel_id=1, source_target_pairs={{0,4},{8,12},{16,20},{24,28},{32,36},{40,44},{48,52},{56,60},{64,6... | collective-permute-start | bytes 884744 | tf_op jit(solution)/shard_map/ppermute | solution.py:615
  23.5 1.1 copy-done.5
  24.6 0.5 shard_map.138
  25.1 0.0 copy-start.6
  25.1 1.6 %shard_map.139 = (bf16[2,544,768]{2,1,0:T(8,128)(2,1)S(1)}, f32[4,544,256]{2,1,0:T(8,128)S(1)}) custom-call(bf16[2,544,128]{2,1,0:T(8,128)(2,1)S(1)} %get-tuple-element.84.hidden.refs_1_, bf16[2,576,128]{2,1,0:T(8,128)(2,1)S(1)} %get-tuple-element.88.motion, bf16[2304,256]{1,0:T(8,128)(2,1)S(1)} %copy-done.2), custom_call_target="tpu_custom_call" | custom-call | flops 1283457024 | bytes 5652480 | tf_op jit(solution)/shard_map/pallas_call | solution.py:46
  26.7 0.0 collective-permute-done.5.refs_5_.motion_b
  26.7 2.4 %collective-permute-done.4.refs_4_.motion_a = bf16[2,576,128]{2,1,0:T(8,128)(2,1)S(1)} collective-permute-done((bf16[2,576,128]{2,1,0:T(8,128)(2,1)S(1)}, bf16[2,576,128]{2,1,0:T(8,128)(2,1)S(1)}, u32[]{:S(2)}, u32[]{:S(2)}) %collective-permute-start.4) | collective-permute-done | bytes 294944 | tf_op jit(solution)/shard_map/ppermute | solution.py:615
  29.1 4.2 %shard_map.140 = (bf16[2,544,128]{2,1,0:T(8,128)(2,1)S(1)}, f32[4,544,128]{2,1,0:T(8,128)S(1)}, f32[4,544,128]{2,1,0:T(8,128)S(1)}, bf16[4,544,128]{2,1,0:T(8,12...) custom-call(s32[2]{0:T(128)S(1)} %pad_add_fusion.place.refs_0_, ...), custom_call_target="tpu_custom_call" | custom-call | flops 3208642560 | bytes 11239432 | tf_op jit(solution)/shard_map/pallas_call | solution.py:46
  33.4 0.7 collective-permute-start.7
  34.1 7.5 %collective-permute-start.6 = (bf16[2,544,128]{2,1,0:T(8,128)(2,1)S(1)}, bf16[2,544,128]{2,1,0:T(8,128)(2,1)S(1)}, u32[]{:S(2)}, u32[]{:S(2)}) collective-permute-start(bf16[2,544,128]{2,1,0:T(8,128)(2,1)S(1)} %get-tuple-element.95.hidden.refs_5_), channel_id=1, source_target_pairs={{0,4},{8,12},{16,20},{24,28},{32,36},{40,44},{48,52},{56,60},{64,6... | collective-permute-start | bytes 835592 | tf_op jit(solution)/shard_map/ppermute | solution.py:615
  41.5 1.6 %shard_map.141 = (bf16[2,544,768]{2,1,0:T(8,128)(2,1)S(1)}, f32[4,544,256]{2,1,0:T(8,128)S(1)}) custom-call(bf16[2,544,128]{2,1,0:T(8,128)(2,1)S(1)} %get-tuple-element.95.hidden.refs_5_, bf16[2,576,128]{2,1,0:T(8,128)(2,1)S(1)} %get-tuple-element.88.motion, bf16[2304,256]{1,0:T(8,128)(2,1)S(1)} %copy-done.2), custom_call_target="tpu_custom_call" | custom-call | flops 1283457024 | bytes 5652480 | tf_op jit(solution)/shard_map/pallas_call | solution.py:46
  43.1 0.0 collective-permute-done.7.hidden_b.refs_7_
  43.1 3.3 %collective-permute-done.6.hidden_a.refs_6_ = bf16[2,544,128]{2,1,0:T(8,128)(2,1)S(1)} collective-permute-done((bf16[2,544,128]{2,1,0:T(8,128)(2,1)S(1)}, bf16[2,544,128]{2,1,0:T(8,128)(2,1)S(1)}, u32[]{:S(2)}, u32[]{:S(2)}) %collective-permute-start.6) | collective-permute-done | bytes 278560 | tf_op jit(solution)/shard_map/ppermute | solution.py:615
  46.4 3.9 %shard_map.142 = (f32[4,544,128]{2,1,0:T(8,128)S(1)}, f32[4,544,128]{2,1,0:T(8,128)S(1)}, bf16[4,544,128]{2,1,0:T(8,128)(2,1)S(1)}, bf16[2,544,128]{2,1,0:T(8,12...) custom-call(s32[2]{0:T(128)S(1)} %pad_add_fusion.place.refs_0_, ...), custom_call_target="tpu_custom_call" | custom-call | flops 3208642560 | bytes 11550728 | tf_op jit(solution)/shard_map/pallas_call | solution.py:46
  50.4 1.3 collective-permute-start.8
  51.6 0.7 collective-permute-start.9
  52.3 1.0 shard_map.143.refs_1_
  53.3 3.0 %shard_map.144 = (f32[2304,128]{1,0:T(8,128)S(1)}, f32[2304,128]{1,0:T(8,128)S(1)}) custom-call(s32[2]{0:T(128)S(1)} %pad_add_fusion.place.refs_0_, bf16[4,544,128]{2,1,0:T(8,128)(2,1)S(1)} %get-tuple-element.103.resets, bf16[2,544,128]{2,1,0:T(8,128)(2,1)S(1)} %get-tuple-element.95.hidden.refs_5_, ...), custom_call_target="tpu_custom_call" | custom-call | flops 1283457024 | bytes 5193736 | tf_op jit(solution)/shard_map/pallas_call | solution.py:46
  56.3 2.5 %collective-permute-done.8.refs_2_ = bf16[3,544,128]{2,1,0:T(8,128)(2,1)S(1)} collective-permute-done((bf16[3,544,128]{2,1,0:T(8,128)(2,1)S(1)}, bf16[3,544,128]{2,1,0:T(8,128)(2,1)S(1)}, u32[]{:S(2)}, u32[]{:S(2)}) %collective-permute-start.8) | collective-permute-done | bytes 417824 | tf_op jit(solution)/shard_map/ppermute | solution.py:621
  58.8 0.0 collective-permute-done.9.refs_3_
  58.8 3.5 %shard_map.145 = (bf16[2,544,128]{2,1,0:T(8,128)(2,1)S(1)}, f32[2,544,128]{2,1,0:T(8,128)S(1)}, f32[2,544,128]{2,1,0:T(8,128)S(1)}, bf16[2,544,128]{2,1,0:T(8,12...) custom-call(s32[2]{0:T(128)S(1)} %pad_add_fusion.place.refs_0_, ...), custom_call_target="tpu_custom_call" | custom-call | flops 2566914048 | bytes 13467656 | tf_op jit(solution)/shard_map/pallas_call | solution.py:46
  62.3 4.9 %collective-permute-start.10 = (bf16[3,544,128]{2,1,0:T(8,128)(2,1)S(1)}, bf16[3,544,128]{2,1,0:T(8,128)(2,1)S(1)}, u32[]{:S(2)}, u32[]{:S(2)}) collective-permute-start(bf16[3,544,128]{2,1,0:T(8,128)(2,1)S(1)} %get-tuple-element.115), channel_id=1, source_target_pairs={{0,4},{8,12},{16,20},{24,28},{32,36},{40,44},{48,52},{56,60},{64,6... | collective-permute-start | bytes 1253384 | tf_op jit(solution)/shard_map/ppermute | solution.py:621
  67.2 0.9 collective-permute-start.11
  68.1 1.0 shard_map.147.partial
  69.1 4.3 %shard_map.146 = (bf16[2304,128]{1,0:T(8,128)(2,1)S(1)}, bf16[2304,128]{1,0:T(8,128)(2,1)S(1)}, f32[2304,128]{1,0:T(8,128)S(1)}) custom-call(s32[2]{0:T(128)S(1)} %pad_add_fusion.place.refs_0_, bf16[4,544,128]{2,1,0:T(8,128)(2,1)S(1)} %get-tuple-element.117.resets, bf16[4,544,128]{2,1,0:T(8,128)(2,1)S(1)} %get-tuple-element.112.refs_13_.older.hiddens, ...), custom_call_target="tpu_custom_call" | custom-call | flops 1925185536 | bytes 8388616 | tf_op jit(solution)/shard_map/pallas_call | solution.py:46
  73.5 4.3 %collective-permute-start.12 = (bf16[2304,128]{1,0:T(8,128)(2,1)S(1)}, bf16[2304,128]{1,0:T(8,128)(2,1)S(1)}, u32[]{:S(2)}, u32[]{:S(2)}) collective-permute-start(bf16[2304,128]{1,0:T(8,128)(2,1)S(1)} %get-tuple-element.128), channel_id=1, source_target_pairs={{0,1},{1,0},{2,3},{3,2},{4,5},{5,4},{6,7},{7,6},{8,9},{9,8},{10,11... | collective-permute-start | bytes 1769480 | tf_op jit(solution)/shard_map/ppermute | solution.py:649
  77.8 3.9 %shard_map.148 = (bf16[2,544,128]{2,1,0:T(8,128)(2,1)S(1)}, bf16[2,512,128]{2,1,0:T(8,128)(2,1)}, f32[2,512,128]{2,1,0:T(8,128)S(1)}, f32[128,128]{1,0:T(8,128)S(1)}) custom-call(s32[2]{0:T(128)S(1)} %pad_add_fusion.place.refs_0_, f32[4,544,256]{2,1,0:T(8,128)S(1)} %shard_map.147.partial, bf16[3,544,128]{2,1,0:T(8,128)(2,1)S(1)} %collective-permute-done.10.grad_a, ...), custom_call_target="tpu_custom_call" | custom-call | flops 2566914048 | bytes 11010056 | tf_op jit(solution)/shard_map/pallas_call | solution.py:46
  81.7 0.0 collective-permute-done.12.got
  81.7 2.0 %shard_map.149 = (bf16[1280,128]{1,0:T(8,128)(2,1)S(1)}, bf16[1280,128]{1,0:T(8,128)(2,1)S(1)}) custom-call(s32[2]{0:T(128)S(1)} %pad_add_fusion.place.refs_0_, bf16[4,544,128]{2,1,0:T(8,128)(2,1)S(1)} %get-tuple-element.112.refs_13_.older.hiddens, bf16[2,576,128]{2,1,0:T(8,128)(2,1)S(1)} %get-tuple-element.88.motion, ...), custom_call_target="tpu_custom_call" | custom-call | flops 641728512 | bytes 3620872 | tf_op jit(solution)/shard_map/pallas_call | solution.py:46
  83.7 0.1 collective-permute-start.13
  83.8 1.6 %collective-permute-done.13.last_got = bf16[1280,128]{1,0:T(8,128)(2,1)S(1)} collective-permute-done((bf16[1280,128]{1,0:T(8,128)(2,1)S(1)}, bf16[1280,128]{1,0:T(8,128)(2,1)S(1)}, u32[]{:S(2)}, u32[]{:S(2)}) %collective-permute-start.13) | collective-permute-done | bytes 327712 | tf_op jit(solution)/shard_map/ppermute | solution.py:649
  85.4 1.1 shard_map.150
  86.6 19.4 %all-to-all-start = ((bf16[64,56,128]{2,1,0:T(8,128)(2,1)}), bf16[64,56,128]{2,1,0:T(8,128)(2,1)S(1)}, u32[]{:S(2)}, u32[]{:S(2)}) async-start(bf16[64,56,128]{2,1,0:T(8,128)(2,1)} %bitcast.2), calls=%async_computation | async-start | bytes 1835008 | tf_op jit(solution)/shard_map/all_to_all | solution.py:635
  106.0 0.0 copy-start.8
  106.0 1.0 copy-done.8
  107.0 1.0 copy-done.12
  108.0 3.2 %shard_map.151 = (bf16[2,512,256]{2,1,0:T(8,128)(2,1)}, bf16[2,192,256]{2,1,0:T(8,128)(2,1)S(1)}, f32[2,512,256]{2,1,0:T(8,128)S(1)}) custom-call(s32[2]{0:T(128)S(1)} %pad_add_fusion.place.refs_0_, s32[2]{0:T(128)S(1)} %copy-done.10, s32[2,4]{1,0:T(2,128)S(1)} %copy-done.9, bf16[2,512,256]{2,1,0:T(8,128)(2,1)S(1)} %copy-done, ...), custom_call_target="tpu_custom_call" | custom-call | flops 855638016 | bytes 3932208 | tf_op jit(solution)/shard_map/pallas_call | solution.py:46
  111.3 0.7 copy-done.13
  111.9 10.0 %all-to-all-done.pieces = bf16[64,56,128]{2,1,0:T(8,128)(2,1)S(1)} async-done(((bf16[64,56,128]{2,1,0:T(8,128)(2,1)}), bf16[64,56,128]{2,1,0:T(8,128)(2,1)S(1)}, u32[]{:S(2)}, u32[]{:S(2)}) %all-to-all-start) | async-done | bytes 917536 | tf_op jit(solution)/shard_map/all_to_all | solution.py:635
  121.9 1.1 shard_map.152
  123.0 5.5 %all-to-all-start.1 = ((bf16[64,56,128]{2,1,0:T(8,128)(2,1)}), bf16[64,56,128]{2,1,0:T(8,128)(2,1)S(1)}, u32[]{:S(2)}, u32[]{:S(2)}) async-start(bf16[64,56,128]{2,1,0:T(8,128)(2,1)} %shard_map.152), calls=%async_computation.1 | async-start | bytes 1835008 | tf_op jit(solution)/shard_map/all_to_all | solution.py:644
  128.6 6.5 %collective-permute-start.15 = (bf16[2,192,256]{2,1,0:T(8,128)(2,1)S(1)}, bf16[2,192,256]{2,1,0:T(8,128)(2,1)S(1)}, u32[]{:S(2)}, u32[]{:S(2)}) collective-permute-start(bf16[2,192,256]{2,1,0:T(8,128)(2,1)S(1)} %copy-done.14), channel_id=1, source_target_pairs={{1,2},{2,1},{5,6},{6,5},{9,10},{10,9},{13,14},{14,13},{17,18},{18,... | collective-permute-start | bytes 589832 | tf_op jit(solution)/shard_map/ppermute | solution.py:615
  135.1 0.1 collective-permute-start.14
  135.2 8.9 %collective-permute-done.15.back_b = bf16[2,192,256]{2,1,0:T(8,128)(2,1)S(1)} collective-permute-done((bf16[2,192,256]{2,1,0:T(8,128)(2,1)S(1)}, bf16[2,192,256]{2,1,0:T(8,128)(2,1)S(1)}, u32[]{:S(2)}, u32[]{:S(2)}) %collective-permute-start.15) | collective-permute-done | bytes 196640 | tf_op jit(solution)/shard_map/ppermute | solution.py:615
  144.1 1.4 shard_map.153
  145.5 0.0 all-to-all-done.1
  145.5 1.6 %collective-permute-start.16 = (bf16[3584,128]{1,0:T(8,128)(2,1)S(1)}, bf16[3584,128]{1,0:T(8,128)(2,1)S(1)}, u32[]{:S(2)}, u32[]{:S(2)}) collective-permute-start(bf16[3584,128]{1,0:T(8,128)(2,1)S(1)} %bitcast.4), channel_id=1, source_target_pairs={{0,1},{1,0},{2,3},{3,2},{4,5},{5,4},{6,7},{7,6},{8,9},{9,8},{10,11... | collective-permute-start | bytes 2752520 | tf_op jit(solution)/shard_map/ppermute | solution.py:649
  147.1 1.8 %shard_map.154 = (f32[2304,256]{1,0:T(8,128)}, f32[2304,128]{1,0:T(8,128)}) custom-call(s32[2]{0:T(128)S(1)} %pad_add_fusion.place.refs_0_, bf16[3584,128]{1,0:T(8,128)(2,1)S(1)} %bitcast.5), custom_call_target="tpu_custom_call" | custom-call | bytes 1769472 | tf_op jit(solution)/shard_map/pallas_call | solution.py:163
  148.9 0.3 collective-permute-done.16.refs_2_
  149.2 2.4 %shard_map.155 = (f32[36,128]{1,0:T(8,128)}, f32[2304,256]{1,0:T(8,128)}, f32[2304,128]{1,0:T(8,128)}) custom-call(s32[2]{0:T(128)S(1)} %pad_add_fusion.place.refs_0_, bf16[3584,128]{1,0:T(8,128)(2,1)S(1)} %bitcast.6, bf16[3584,128]{1,0:T(8,128)(2,1)S(1)} %collective-permute-done.16.refs_2_, ...), custom_call_target="tpu_custom_call", output_to_operand_aliasing={{1}: (3, {}), {2}: (4, {})} | custom-call | bytes 1769472 | tf_op jit(solution)/shard_map/pallas_call | solution.py:163
  (28 shorter events, 0.1 us)
Async XLA Ops:
  0.6 8.2 %copy-start.4 = (bf16[2,512,128]{2,1,0:T(8,128)(2,1)S(1)}, bf16[2,512,128]{2,1,0:T(8,128)(2,1)}, u32[]{:S(2)}) copy-start(bf16[2,512,128]{2,1,0:T(8,128)(2,1)} %hidden.3) | copy-start | bytes 786436
  0.6 13.6 %copy-start.1 = (bf16[2,512,256]{2,1,0:T(8,128)(2,1)S(1)}, bf16[2,512,256]{2,1,0:T(8,128)(2,1)}, u32[]{:S(2)}) copy-start(bf16[2,512,256]{2,1,0:T(8,128)(2,1)} %right.5) | copy-start | bytes 1572868
  0.7 13.6 %copy-start = (bf16[2,512,256]{2,1,0:T(8,128)(2,1)S(1)}, bf16[2,512,256]{2,1,0:T(8,128)(2,1)}, u32[]{:S(2)}) copy-start(bf16[2,512,256]{2,1,0:T(8,128)(2,1)} %left.5) | copy-start | bytes 1572868
  0.7 13.6 %copy-start.3 = (bf16[2,512,128]{2,1,0:T(8,128)(2,1)S(1)}, bf16[2,512,128]{2,1,0:T(8,128)(2,1)}, u32[]{:S(2)}) copy-start(bf16[2,512,128]{2,1,0:T(8,128)(2,1)} %grads.3) | copy-start | bytes 786436
  0.7 13.4 %copy-start.15 = (bf16[36,128]{1,0:T(8,128)(2,1)S(1)}, bf16[36,128]{1,0:T(8,128)(2,1)}, u32[]{:S(2)}) copy-start(bf16[36,128]{1,0:T(8,128)(2,1)} %param.14) | copy-start | bytes 27652
  0.7 13.6 %copy-start.9 = (s32[2,4]{1,0:T(2,128)S(1)}, s32[2,4]{1,0:T(2,128)}, u32[]{:S(2)}) copy-start(s32[2,4]{1,0:T(2,128)} %offsets.3) | copy-start | bytes 100
  0.7 13.6 %copy-start.10 = (s32[2]{0:T(128)S(1)}, s32[2]{0:T(128)}, u32[]{:S(2)}) copy-start(s32[2]{0:T(128)} %disparity.3) | copy-start | bytes 28
  2.5 21.0 %copy-start.2 = (bf16[2304,256]{1,0:T(8,128)(2,1)S(1)}, bf16[2304,256]{1,0:T(8,128)(2,1)}, u32[]{:S(2)}) copy-start(bf16[2304,256]{1,0:T(8,128)(2,1)} %gate_w.7) | copy-start | bytes 3538948
  2.6 11.6 %collective-permute-start.1 = (bf16[2,288,256]{2,1,0:T(8,128)(2,1)}, bf16[2,288,256]{2,1,0:T(8,128)(2,1)S(1)}, u32[]{:S(2)}, u32[]{:S(2)}) collective-permute-start(bf16[2,288,256]{2,1,0:T(8,128)(2,1)} %shard_map.136), channel_id=1, source_target_pairs={{1,2},{2,1},{5,6},{6,5},{9,10},{10,9},{13,14},{14,13},{17,18},{18,... | collective-permute-start | bytes 884744 | tf_op jit(solution)/shard_map/ppermute | solution.py:615
  8.7 5.5 %collective-permute-start = (bf16[2,288,256]{2,1,0:T(8,128)(2,1)}, bf16[2,288,256]{2,1,0:T(8,128)(2,1)S(1)}, u32[]{:S(2)}, u32[]{:S(2)}) collective-permute-start(bf16[2,288,256]{2,1,0:T(8,128)(2,1)} %shard_map.136), channel_id=1, source_target_pairs={{0,1},{2,3},{1,0},{3,2},{4,5},{6,7},{5,4},{7,6},{8,9},{10,11},{9,8... | collective-permute-start | bytes 884744 | tf_op jit(solution)/shard_map/ppermute | solution.py:615
  8.8 9.5 %collective-permute-start.3 = (bf16[2,512,128]{2,1,0:T(8,128)(2,1)S(1)}, bf16[2,512,128]{2,1,0:T(8,128)(2,1)}, u32[]{:S(2)}, u32[]{:S(2)}) collective-permute-start(bf16[2,512,128]{2,1,0:T(8,128)(2,1)S(1)} %copy-done.4), channel_id=1, source_target_pairs={{4,8},{12,16},{20,24},{28,32},{36,40},{44,48},{52,56},{60,64},{68,... | collective-permute-start | bytes 786440 | tf_op jit(solution)/shard_map/ppermute | solution.py:615
  10.2 9.9 %collective-permute-start.2 = (bf16[2,512,128]{2,1,0:T(8,128)(2,1)S(1)}, bf16[2,512,128]{2,1,0:T(8,128)(2,1)}, u32[]{:S(2)}, u32[]{:S(2)}) collective-permute-start(bf16[2,512,128]{2,1,0:T(8,128)(2,1)S(1)} %copy-done.4), channel_id=1, source_target_pairs={{0,4},{8,12},{16,20},{24,28},{32,36},{40,44},{48,52},{56,60},{64,6... | collective-permute-start | bytes 786440 | tf_op jit(solution)/shard_map/ppermute | solution.py:615
  14.3 10.8 %copy-start.7 = (bf16[2,288,256]{2,1,0:T(8,128)(2,1)}, bf16[2,288,256]{2,1,0:T(8,128)(2,1)S(1)}, u32[]{:S(2)}) copy-start(bf16[2,288,256]{2,1,0:T(8,128)(2,1)S(1)} %collective-permute-done.got_a) | copy-start | bytes 884740
  20.2 6.5 %collective-permute-start.5 = (bf16[2,576,128]{2,1,0:T(8,128)(2,1)S(1)}, bf16[2,576,128]{2,1,0:T(8,128)(2,1)S(1)}, u32[]{:S(2)}, u32[]{:S(2)}) collective-permute-start(bf16[2,576,128]{2,1,0:T(8,128)(2,1)S(1)} %get-tuple-element.88.motion), channel_id=1, source_target_pairs={{4,8},{12,16},{20,24},{28,32},{36,40},{44,48},{52,56},{60,64},{68,... | collective-permute-start | bytes 884744 | tf_op jit(solution)/shard_map/ppermute | solution.py:615
  20.8 8.3 %collective-permute-start.4 = (bf16[2,576,128]{2,1,0:T(8,128)(2,1)S(1)}, bf16[2,576,128]{2,1,0:T(8,128)(2,1)S(1)}, u32[]{:S(2)}, u32[]{:S(2)}) collective-permute-start(bf16[2,576,128]{2,1,0:T(8,128)(2,1)S(1)} %get-tuple-element.88.motion), channel_id=1, source_target_pairs={{0,4},{8,12},{16,20},{24,28},{32,36},{40,44},{48,52},{56,60},{64,6... | collective-permute-start | bytes 884744 | tf_op jit(solution)/shard_map/ppermute | solution.py:615
  23.5 1.1 copy-start.5
  25.1 4.0 %copy-start.6 = (bf16[2304,128]{1,0:T(8,128)(2,1)S(1)}, bf16[2304,128]{1,0:T(8,128)(2,1)}, u32[]{:S(2)}) copy-start(bf16[2304,128]{1,0:T(8,128)(2,1)} %cand_w.3) | copy-start | bytes 1769476
  33.4 9.7 %collective-permute-start.7 = (bf16[2,544,128]{2,1,0:T(8,128)(2,1)S(1)}, bf16[2,544,128]{2,1,0:T(8,128)(2,1)S(1)}, u32[]{:S(2)}, u32[]{:S(2)}) collective-permute-start(bf16[2,544,128]{2,1,0:T(8,128)(2,1)S(1)} %get-tuple-element.95.hidden.refs_5_), channel_id=1, source_target_pairs={{4,8},{12,16},{20,24},{28,32},{36,40},{44,48},{52,56},{60,64},{68,... | collective-permute-start | bytes 835592 | tf_op jit(solution)/shard_map/ppermute | solution.py:615
  34.1 12.3 %collective-permute-start.6 = (bf16[2,544,128]{2,1,0:T(8,128)(2,1)S(1)}, bf16[2,544,128]{2,1,0:T(8,128)(2,1)S(1)}, u32[]{:S(2)}, u32[]{:S(2)}) collective-permute-start(bf16[2,544,128]{2,1,0:T(8,128)(2,1)S(1)} %get-tuple-element.95.hidden.refs_5_), channel_id=1, source_target_pairs={{0,4},{8,12},{16,20},{24,28},{32,36},{40,44},{48,52},{56,60},{64,6... | collective-permute-start | bytes 835592 | tf_op jit(solution)/shard_map/ppermute | solution.py:615
  50.4 8.5 %collective-permute-start.8 = (bf16[3,544,128]{2,1,0:T(8,128)(2,1)S(1)}, bf16[3,544,128]{2,1,0:T(8,128)(2,1)S(1)}, u32[]{:S(2)}, u32[]{:S(2)}) collective-permute-start(bf16[3,544,128]{2,1,0:T(8,128)(2,1)S(1)} %get-tuple-element.101), channel_id=1, source_target_pairs={{0,4},{8,12},{16,20},{24,28},{32,36},{40,44},{48,52},{56,60},{64,6... | collective-permute-start | bytes 1253384 | tf_op jit(solution)/shard_map/ppermute | solution.py:621
  51.6 7.2 %collective-permute-start.9 = (bf16[3,544,128]{2,1,0:T(8,128)(2,1)S(1)}, bf16[3,544,128]{2,1,0:T(8,128)(2,1)S(1)}, u32[]{:S(2)}, u32[]{:S(2)}) collective-permute-start(bf16[3,544,128]{2,1,0:T(8,128)(2,1)S(1)} %get-tuple-element.102), channel_id=1, source_target_pairs={{4,8},{12,16},{20,24},{28,32},{36,40},{44,48},{52,56},{60,64},{68,... | collective-permute-start | bytes 1253384 | tf_op jit(solution)/shard_map/ppermute | solution.py:620
  62.3 11.2 %collective-permute-start.10 = (bf16[3,544,128]{2,1,0:T(8,128)(2,1)S(1)}, bf16[3,544,128]{2,1,0:T(8,128)(2,1)S(1)}, u32[]{:S(2)}, u32[]{:S(2)}) collective-permute-start(bf16[3,544,128]{2,1,0:T(8,128)(2,1)S(1)} %get-tuple-element.115), channel_id=1, source_target_pairs={{0,4},{8,12},{16,20},{24,28},{32,36},{40,44},{48,52},{56,60},{64,6... | collective-permute-start | bytes 1253384 | tf_op jit(solution)/shard_map/ppermute | solution.py:621
  67.2 6.3 %collective-permute-start.11 = (bf16[3,544,128]{2,1,0:T(8,128)(2,1)S(1)}, bf16[3,544,128]{2,1,0:T(8,128)(2,1)S(1)}, u32[]{:S(2)}, u32[]{:S(2)}) collective-permute-start(bf16[3,544,128]{2,1,0:T(8,128)(2,1)S(1)} %get-tuple-element.116), channel_id=1, source_target_pairs={{4,8},{12,16},{20,24},{28,32},{36,40},{44,48},{52,56},{60,64},{68,... | collective-permute-start | bytes 1253384 | tf_op jit(solution)/shard_map/ppermute | solution.py:620
  73.5 8.2 %collective-permute-start.12 = (bf16[2304,128]{1,0:T(8,128)(2,1)S(1)}, bf16[2304,128]{1,0:T(8,128)(2,1)S(1)}, u32[]{:S(2)}, u32[]{:S(2)}) collective-permute-start(bf16[2304,128]{1,0:T(8,128)(2,1)S(1)} %get-tuple-element.128), channel_id=1, source_target_pairs={{0,1},{1,0},{2,3},{3,2},{4,5},{5,4},{6,7},{7,6},{8,9},{9,8},{10,11... | collective-permute-start | bytes 1769480 | tf_op jit(solution)/shard_map/ppermute | solution.py:649
  81.7 2.0 %copy-start.11 = (f32[2,512,128]{2,1,0:T(8,128)}, f32[2,512,128]{2,1,0:T(8,128)S(1)}, u32[]{:S(2)}) copy-start(f32[2,512,128]{2,1,0:T(8,128)S(1)} %get-tuple-element.143.grad_feats) | copy-start | bytes 1572868
  83.7 1.7 %collective-permute-start.13 = (bf16[1280,128]{1,0:T(8,128)(2,1)S(1)}, bf16[1280,128]{1,0:T(8,128)(2,1)S(1)}, u32[]{:S(2)}, u32[]{:S(2)}) collective-permute-start(bf16[1280,128]{1,0:T(8,128)(2,1)S(1)} %get-tuple-element.142), channel_id=1, source_target_pairs={{0,1},{1,0},{2,3},{3,2},{4,5},{5,4},{6,7},{7,6},{8,9},{9,8},{10,11... | collective-permute-start | bytes 983048 | tf_op jit(solution)/shard_map/ppermute | solution.py:649
  86.6 35.4 %all-to-all-start = ((bf16[64,56,128]{2,1,0:T(8,128)(2,1)}), bf16[64,56,128]{2,1,0:T(8,128)(2,1)S(1)}, u32[]{:S(2)}, u32[]{:S(2)}) async-start(bf16[64,56,128]{2,1,0:T(8,128)(2,1)} %bitcast.2), calls=%async_computation | async-start | bytes 1835008 | tf_op jit(solution)/shard_map/all_to_all | solution.py:635
  106.0 1.0 copy-start.8
  107.0 1.0 copy-start.12
  111.3 0.7 copy-start.13
  123.0 5.5 %copy-start.14 = (bf16[2,192,256]{2,1,0:T(8,128)(2,1)S(1)}, bf16[2,192,256]{2,1,0:T(8,128)(2,1)}, u32[]{:S(2)}) copy-start(bf16[2,192,256]{2,1,0:T(8,128)(2,1)} %copy-done.13) | copy-start | bytes 589828
  123.0 22.5 %all-to-all-start.1 = ((bf16[64,56,128]{2,1,0:T(8,128)(2,1)}), bf16[64,56,128]{2,1,0:T(8,128)(2,1)S(1)}, u32[]{:S(2)}, u32[]{:S(2)}) async-start(bf16[64,56,128]{2,1,0:T(8,128)(2,1)} %shard_map.152), calls=%async_computation.1 | async-start | bytes 1835008 | tf_op jit(solution)/shard_map/all_to_all | solution.py:644
  128.6 15.5 %collective-permute-start.15 = (bf16[2,192,256]{2,1,0:T(8,128)(2,1)S(1)}, bf16[2,192,256]{2,1,0:T(8,128)(2,1)S(1)}, u32[]{:S(2)}, u32[]{:S(2)}) collective-permute-start(bf16[2,192,256]{2,1,0:T(8,128)(2,1)S(1)} %copy-done.14), channel_id=1, source_target_pairs={{1,2},{2,1},{5,6},{6,5},{9,10},{10,9},{13,14},{14,13},{17,18},{18,... | collective-permute-start | bytes 589832 | tf_op jit(solution)/shard_map/ppermute | solution.py:615
  135.1 9.0 %collective-permute-start.14 = (bf16[2,192,256]{2,1,0:T(8,128)(2,1)S(1)}, bf16[2,192,256]{2,1,0:T(8,128)(2,1)S(1)}, u32[]{:S(2)}, u32[]{:S(2)}) collective-permute-start(bf16[2,192,256]{2,1,0:T(8,128)(2,1)S(1)} %copy-done.14), channel_id=1, source_target_pairs={{0,1},{2,3},{1,0},{3,2},{4,5},{6,7},{5,4},{7,6},{8,9},{10,11},{9,8... | collective-permute-start | bytes 589832 | tf_op jit(solution)/shard_map/ppermute | solution.py:615
  145.5 3.7 %collective-permute-start.16 = (bf16[3584,128]{1,0:T(8,128)(2,1)S(1)}, bf16[3584,128]{1,0:T(8,128)(2,1)S(1)}, u32[]{:S(2)}, u32[]{:S(2)}) collective-permute-start(bf16[3584,128]{1,0:T(8,128)(2,1)S(1)} %bitcast.4), channel_id=1, source_target_pairs={{0,1},{1,0},{2,3},{3,2},{4,5},{5,4},{6,7},{7,6},{8,9},{9,8},{10,11... | collective-permute-start | bytes 2752520 | tf_op jit(solution)/shard_map/ppermute | solution.py:649

commit v6 on v5

--- a/solution.py
+++ b/solution.py
@@ -125,7 +125,13 @@
     )(left, right, hidden, grads)
 
 
-def turn_kernel(gate_w, cand_w, gate_wt, cand_wt):
+def turn_kernel(gate_w, cand_w, gate_wt, cand_wt, cand_pair):
+    deep = cand_w.shape[0] // 3
+    nothing = jnp.zeros((deep, LANES), BF16)
+    for row in range(4):
+        here = slice(row * deep, (row + 1) * deep)
+        cand_pair[here, :LANES] = cand_w[here] if row < 3 else nothing
+        cand_pair[here, LANES:] = cand_w[(row - 1) * deep : row * deep] if row > 0 else nothing
     for tap in range(9):
         here = slice(tap * 2 * LANES, (tap + 1) * 2 * LANES)
         gate_wt[here] = gate_w[here].T
@@ -293,10 +299,10 @@
     fill_neighbours(lambda r, v: store_taps(fields, r, lane, 2 * LANES, v, True), odd, first, second, wide)
 
 
-def candidate_part(resets, cand_w, row, here):
-    deep = cand_w.shape[0] // 3
-    total = sum(dot(resets[row + a, here], cand_w[a * deep : (a + 1) * deep]) for a in range(3))
-    return jnp.tanh(total)
+def candidates(resets, cand_pair, here):
+    deep = cand_pair.shape[0] // 4
+    total = sum(dot(resets[row, here], cand_pair[row * deep : (row + 1) * deep]) for row in range(4))
+    return jnp.tanh(total[:, :LANES]), jnp.tanh(total[:, LANES:])
 
 
 def first_kernel(cols_axis, place, hidden, init_a, init_b, motion_a, motion_b, gate_w, cand_w, own, partial,
@@ -320,10 +326,9 @@
         hiddens[1 + row] = hidden[row]
     gates(fields, own, partial, resets, gate_w, update, reset, reset_hidden, wide)
     inside = image_columns(place, wide, wide - 2 * HALO, cols_axis)
-    for row in range(2):
-        for start in range(0, wide, block):
-            here = pl.ds(start, block)
-            new = candidate_part(resets, cand_w, row, here)
+    for start in range(0, wide, block):
+        here = pl.ds(start, block)
+        for row, new in enumerate(candidates(resets, cand_w, here)):
             candidate[row, here] = new
             gate = update[row + 1, here]
             old = hidden[row, here].astype(F32)
@@ -351,10 +356,9 @@
     load_field(odd, fields, LANES, motion_a, motion_b)
     load_field(odd, fields, 0, hidden_a, hidden_b)
     gates(fields, own, partial, resets, gate_w, update, reset, reset_hidden, wide)
-    for row in range(2):
-        for start in range(0, wide, block):
-            here = pl.ds(start, block)
-            new = candidate_part(resets, cand_w, row, here)
+    for start in range(0, wide, block):
+        here = pl.ds(start, block)
+        for row, new in enumerate(candidates(resets, cand_w, here)):
             gradients_out(grad_hidden[row, here].astype(F32), update[row + 1, here], new,
                           hidden[row, here].astype(F32), row, here, grad_cand, grad_update, send_a, send_b)
     send_updates(odd, grad_update, send_a, send_b)
@@ -424,7 +428,8 @@
 
 def first_back_kernel(place, partial, grad_a, grad_b, grad_update, hiddens, reset,
                       cand_wt, gate_wt, update, grad_state, motion_so_far, pre, feats, weight,
-                      grad_reset, grad_first, grad_feats, motion_w, cand_taps, gate_taps, inner, grad_motion):
+                      motion, motion_a, motion_b, reset_sum, grad_first, grad_feats, kept, given,
+                      cand_taps, gate_taps, inner, grad_motion, grad_reset, pixels, taps, parts):
     def finish(row, start, here, terms):
         gate = update[row + 1, here]
         grad = grad_state[row, here] * (1.0 - gate) + terms
@@ -443,7 +448,7 @@
         grad_pre = (grad_motion[row, inner_cols] * slope).astype(BF16)
         total = total + dot_tn(feats[row, inner_cols], grad_pre)
         grad_feats[row] = dot_nt(grad_pre, weight[...])
-    motion_w[...] = total
+    last_weights(place, hiddens, motion, motion_a, motion_b, grad_reset, reset_sum, total, kept, given, pixels, taps, parts)
 
 
 def load_pixels(odd, pixels, hiddens, motion, motion_a, motion_b):
@@ -545,8 +550,8 @@
     weight_products(pixels, taps, wide, LANES, reset_finish)
 
 
-def last_weights_kernel(place, hiddens, motion, motion_a, motion_b, reset_grads, reset_sum, motion_w,
-                        kept, given, pixels, taps, parts):
+def last_weights(place, hiddens, motion, motion_a, motion_b, reset_grads, reset_sum, motion_w,
+                 kept, given, pixels, taps, parts):
     odd = place[0] % 2 == 1
     load_pixels(odd, pixels, [hiddens[row] for row in range(4)], motion, motion_a, motion_b)
     load_grads(taps, reset_grads)
@@ -556,7 +561,7 @@
         store_halves(parts, 0, rows, start, reset_sum[pl.ds(start, 2 * LANES)] + value)
 
     weight_products(pixels, taps, taps.shape[0] // 2, LANES, finish)
-    parts[0, rows // 2 :] = motion_w[...].astype(BF16)
+    parts[0, rows // 2 :] = motion_w.astype(BF16)
     parts[1, rows // 2 :] = jnp.zeros((parts.shape[1] - rows // 2, LANES), BF16)
     share_cores(place, parts, kept, given)
 
@@ -683,15 +688,17 @@
     )
     motion, init_a, init_b = lax.optimization_barrier((motion, init_a, init_b))
     motion_a, motion_b = exchanged(motion, "rows")
-    gate_wt, cand_wt = kernel_call(
+    gate_wt, cand_wt, cand_pair = kernel_call(
         turn_kernel,
-        [array(gate_weight.shape, BF16), array((9 * state, 2 * state), BF16)],
+        [array(gate_weight.shape, BF16), array((9 * state, 2 * state), BF16), array((24 * state, 2 * state), BF16)],
         [gate_weight, cand_weight],
         0,
         [],
         0,
     )
-    motion_a, motion_b, gate_wt, cand_wt = lax.optimization_barrier((motion_a, motion_b, gate_wt, cand_wt))
+    motion_a, motion_b, gate_wt, cand_wt, cand_pair = lax.optimization_barrier(
+        (motion_a, motion_b, gate_wt, cand_wt, cand_pair)
+    )
     motions = (motion, motion_a, motion_b)
     unit = 2 * wide * 9 * 2 * state * state
     fields = [pltpu.VMEM((6, wide, 6 * LANES), BF16), pltpu.VMEM((4, wide, 6 * LANES), BF16)]
@@ -704,7 +711,7 @@
     hidden_1, update_0, reset_0, reset_hidden_0, candidate_0, hiddens_0 = kernel_call(
         lambda *refs: first_kernel(cols_axis, *refs),
         [field(2, BF16), field(4, F32), field(4, F32), field(4, BF16), field(2, F32), field(4, BF16)],
-        [place, hidden, init_a, init_b, *motions[1:], gate_weight, cand_weight, own_taps, partial],
+        [place, hidden, init_a, init_b, *motions[1:], gate_weight, cand_pair, own_taps, partial],
         1,
         fields,
         10 * unit,
@@ -716,7 +723,7 @@
     update_1, reset_1, reset_hidden_1, grad_cand_1, grad_update_1, send_a, send_b = kernel_call(
         second_kernel,
         [field(4, F32), field(4, F32), field(4, BF16), field(2, BF16), field(2, BF16), field(3, BF16), field(3, BF16)],
-        [place, hidden_1, hidden_1a, hidden_1b, *motions[1:], gate_weight, cand_weight, own_taps, partial, grads],
+        [place, hidden_1, hidden_1a, hidden_1b, *motions[1:], gate_weight, cand_pair, own_taps, partial, grads],
         1,
         fields,
         10 * unit,
@@ -772,24 +779,17 @@
         (got_a, got_b, kept, given, reset_sum, partial)
     )
     got = swapped(given)
-    grad_reset_0, grad_first, grad_feats, motion_sum = kernel_call(
+    grad_first, grad_feats, last_kept, last_given = kernel_call(
         first_back_kernel,
-        [field(2, BF16), array((2, cols, LANES), BF16), array((2, cols, LANES), F32), array((LANES, LANES), F32)],
+        [array((2, cols, LANES), BF16), array((2, cols, LANES), F32), array((late, LANES), BF16), array((late, LANES), BF16)],
         [place, partial, got_a, got_b, grad_update_0, hiddens_0, reset_0, cand_wt, gate_wt,
-         update_0, grad_state, grad_motion_1, motion_pre, feats, motion_w],
+         update_0, grad_state, grad_motion_1, motion_pre, feats, motion_w, *motions, reset_sum],
         1,
-        back_scratch + [pltpu.VMEM((2, wide, LANES), F32)],
-        8 * unit,
-    )
-    reset_sum, got = lax.optimization_barrier((reset_sum, got))
-    last_kept, last_given = kernel_call(
-        last_weights_kernel,
-        [array((late, LANES), BF16), array((late, LANES), BF16)],
-        [place, hiddens_0, *motions, grad_reset_0, reset_sum, motion_sum],
-        1,
-        [pixels, taps, pltpu.VMEM((2, late, LANES), BF16)],
-        2 * unit,
-    )
+        back_scratch + [pltpu.VMEM((2, wide, LANES), F32), pltpu.VMEM((2, wide, LANES), BF16), pixels, taps,
+                        pltpu.VMEM((2, late, LANES), BF16)],
+        10 * unit,
+    )
+    last_kept, last_given, got = lax.optimization_barrier((last_kept, last_given, got))
     grad_left, back, own = kernel_call(
         band_back_kernel,
         [array((2, cols, channels), BF16), array((2, DISP, channels), BF16), array((2, cols, channels), F32)],

time: 152 us -> 150 us (0.987)
  Pallas kernels: 47.6 us -> 45.7 us
    pallas_call x17 -> x16, Pallas kernels: 41.5 us -> 39.6 us  [kernel_call(): pl.pallas_call(body, out_shape=outs, in_specs=[SMEM] * scalars + [VMEM] *...]
    unnamed x32 -> x30, local copies, waits for them, and re-layouts: 3.79 us -> 3.79 us
  transfers between devices with their start and end apart: 19 -> 19, of which waited for: 8 -> 8; matrix products, arithmetic and copies ran while one was open for 0% -> 0% of each run, Pallas kernels for 18% -> 19%
where the time goes in v6:
time: 150 us
  starting transfers between devices  68 us (45%)
  Pallas kernels  45.7 us (30%)
  waiting for transfers between devices  31 us (21%)
  local copies, waits for them, and re-layouts  3.79 us (3%)
    pallas_call x16, Pallas kernels, kernel_call(): pl.pallas_call(body, out_shape=outs, in_specs=[SMEM] * scalars + [VMEM] *...  39.6 us
    ppermute x10, starting transfers between devices, exchanged(): return (lax.ppermute(value, axis, first), lax.ppermute(value, axis, second))  29.6 us
    all_to_all x1, starting transfers between devices, shared_out(): lax.all_to_all(half, axes, 0, 0, tiled=True, axis_index_groups=core_group...  19.2 us
    ppermute x10, waiting for transfers between devices, exchanged(): return (lax.ppermute(value, axis, first), lax.ppermute(value, axis, second))  16.4 us
    all_to_all x1, waiting for transfers between devices, shared_out(): lax.all_to_all(half, axes, 0, 0, tiled=True, axis_index_groups=core_group...  10.3 us
    ppermute x2, starting transfers between devices, exchanged_pair(): return (lax.ppermute(value_a, axis, first), other)  6.13 us
    ppermute x3, starting transfers between devices, swapped(): lax.ppermute(value, 'cols', [(i, i ^ 1) for i in range(lax.axis_size('col...  5.99 us
    all_to_all x1, starting transfers between devices, gathered(): lax.all_to_all(spread, axes, 0, 0, tiled=True, axis_index_groups=core_gro...  5.49 us
  transfers between devices with their start and end apart: 19, of which 8 were waited for; matrix products, arithmetic and copies ran while one was open for 0% of the time, Pallas kernels for 19%

profile of v6, /device:TPU:1, one launch (start us, length us, event | category | flops | bytes accessed | tf_op | source)
XLA Modules:
  0.0 149.8 jit_solution(959675796860488185)
XLA Ops:
  0.7 1.8 %shard_map.136 = bf16[2,288,256]{2,1,0:T(8,128)(2,1)} custom-call(bf16[2,512,256]{2,1,0:T(8,128)(2,1)} %left.5, bf16[2,512,256]{2,1,0:T(8,128)(2,1)} %right.5, bf16[2,512,128]{2,1,0:T(8,128)(2,1)} %hidden.3, bf16[2,512,128]{2,1,0:T(8,128)(2,1)} %grads.3), custom_call_target="tpu_custom_call" | custom-call | bytes 589824 | tf_op jit(solution)/shard_map/pallas_call | solution.py:117
  2.5 0.0 copy-start.2
  2.6 6.2 %collective-permute-start.1 = (bf16[2,288,256]{2,1,0:T(8,128)(2,1)}, bf16[2,288,256]{2,1,0:T(8,128)(2,1)S(1)}, u32[]{:S(2)}, u32[]{:S(2)}) collective-permute-start(bf16[2,288,256]{2,1,0:T(8,128)(2,1)} %shard_map.136), channel_id=1, source_target_pairs={{1,2},{2,1},{5,6},{6,5},{9,10},{10,9},{13,14},{14,13},{17,18},{18,... | collective-permute-start | bytes 884744 | tf_op jit(solution)/shard_map/ppermute | solution.py:620
  8.7 0.1 collective-permute-start
  8.8 1.4 collective-permute-start.3
  10.2 3.9 %collective-permute-start.2 = (bf16[2,512,128]{2,1,0:T(8,128)(2,1)S(1)}, bf16[2,512,128]{2,1,0:T(8,128)(2,1)}, u32[]{:S(2)}, u32[]{:S(2)}) collective-permute-start(bf16[2,512,128]{2,1,0:T(8,128)(2,1)S(1)} %copy-done.4), channel_id=1, source_target_pairs={{0,4},{8,12},{16,20},{24,28},{32,36},{40,44},{48,52},{56,60},{64,6... | collective-permute-start | bytes 786440 | tf_op jit(solution)/shard_map/ppermute | solution.py:620
  14.1 0.1 pad_add_fusion.place.refs_0_
  14.2 0.0 collective-permute-done.1.got_b
  14.2 0.0 collective-permute-done.got_a
  14.3 0.0 copy-start.6
  14.3 4.0 %shard_map.137 = (bf16[2,576,128]{2,1,0:T(8,128)(2,1)S(1)}, f32[2,544,128]{2,1,0:T(8,128)S(1)}, bf16[2,544,128]{2,1,0:T(8,128)(2,1)S(1)}, bf16[2,544,128]{2,1,0:T(8,128)(2,1)S(1)}, bf16[2,544,128]{2,1,0:T(8,128)(2,1)S(1)}) custom-call(s32[2]{0:T(128)S(1)} %pad_add_fusion.place.refs_0_, s32[2]{0:T(128)S(1)} %copy-done.9, s32[2,4]{1,0:T(2,128)S(1)} %copy-done.8, ...), custom_call_target="tpu_custom_call" | custom-call | flops 570425344 | bytes 3883056 | tf_op jit(solution)/shard_map/pallas_call | solution.py:46
  18.3 0.0 collective-permute-done.3.refs_3_
  18.3 1.8 %collective-permute-done.2.refs_2_ = bf16[2,512,128]{2,1,0:T(8,128)(2,1)} collective-permute-done((bf16[2,512,128]{2,1,0:T(8,128)(2,1)S(1)}, bf16[2,512,128]{2,1,0:T(8,128)(2,1)}, u32[]{:S(2)}, u32[]{:S(2)}) %collective-permute-start.2) | collective-permute-done | bytes 262176 | tf_op jit(solution)/shard_map/ppermute | solution.py:620
  20.2 0.7 collective-permute-start.5
  20.8 2.7 %collective-permute-start.4 = (bf16[2,576,128]{2,1,0:T(8,128)(2,1)S(1)}, bf16[2,576,128]{2,1,0:T(8,128)(2,1)S(1)}, u32[]{:S(2)}, u32[]{:S(2)}) collective-permute-start(bf16[2,576,128]{2,1,0:T(8,128)(2,1)S(1)} %get-tuple-element.89.motion), channel_id=1, source_target_pairs={{0,4},{8,12},{16,20},{24,28},{32,36},{40,44},{48,52},{56,60},{64,6... | collective-permute-start | bytes 884744 | tf_op jit(solution)/shard_map/ppermute | solution.py:620
  23.5 1.1 copy-done.5
  24.6 0.7 shard_map.138
  25.2 1.6 %shard_map.139 = (bf16[2,544,768]{2,1,0:T(8,128)(2,1)S(1)}, f32[4,544,256]{2,1,0:T(8,128)S(1)}) custom-call(bf16[2,544,128]{2,1,0:T(8,128)(2,1)S(1)} %get-tuple-element.85.hidden.refs_1_, bf16[2,576,128]{2,1,0:T(8,128)(2,1)S(1)} %get-tuple-element.89.motion, bf16[2304,256]{1,0:T(8,128)(2,1)S(1)} %copy-done.2), custom_call_target="tpu_custom_call" | custom-call | flops 1283457024 | bytes 5652480 | tf_op jit(solution)/shard_map/pallas_call | solution.py:46
  26.8 0.0 collective-permute-done.5.refs_5_.motion_b
  26.8 2.3 %collective-permute-done.4.refs_4_.motion_a = bf16[2,576,128]{2,1,0:T(8,128)(2,1)S(1)} collective-permute-done((bf16[2,576,128]{2,1,0:T(8,128)(2,1)S(1)}, bf16[2,576,128]{2,1,0:T(8,128)(2,1)S(1)}, u32[]{:S(2)}, u32[]{:S(2)}) %collective-permute-start.4) | collective-permute-done | bytes 294944 | tf_op jit(solution)/shard_map/ppermute | solution.py:620
  29.1 3.8 %shard_map.140 = (bf16[2,544,128]{2,1,0:T(8,128)(2,1)S(1)}, f32[4,544,128]{2,1,0:T(8,128)S(1)}, f32[4,544,128]{2,1,0:T(8,128)S(1)}, bf16[4,544,128]{2,1,0:T(8,12...) custom-call(s32[2]{0:T(128)S(1)} %pad_add_fusion.place.refs_0_, ...), custom_call_target="tpu_custom_call" | custom-call | flops 3208642560 | bytes 12222472 | tf_op jit(solution)/shard_map/pallas_call | solution.py:46
  32.9 0.7 collective-permute-start.7
  33.6 7.5 %collective-permute-start.6 = (bf16[2,544,128]{2,1,0:T(8,128)(2,1)S(1)}, bf16[2,544,128]{2,1,0:T(8,128)(2,1)S(1)}, u32[]{:S(2)}, u32[]{:S(2)}) collective-permute-start(bf16[2,544,128]{2,1,0:T(8,128)(2,1)S(1)} %get-tuple-element.98.hidden.refs_5_), channel_id=1, source_target_pairs={{0,4},{8,12},{16,20},{24,28},{32,36},{40,44},{48,52},{56,60},{64,6... | collective-permute-start | bytes 835592 | tf_op jit(solution)/shard_map/ppermute | solution.py:620
  41.1 1.6 %shard_map.141 = (bf16[2,544,768]{2,1,0:T(8,128)(2,1)S(1)}, f32[4,544,256]{2,1,0:T(8,128)S(1)}) custom-call(bf16[2,544,128]{2,1,0:T(8,128)(2,1)S(1)} %get-tuple-element.98.hidden.refs_5_, bf16[2,576,128]{2,1,0:T(8,128)(2,1)S(1)} %get-tuple-element.89.motion, bf16[2304,256]{1,0:T(8,128)(2,1)S(1)} %copy-done.2), custom_call_target="tpu_custom_call" | custom-call | flops 1283457024 | bytes 5652480 | tf_op jit(solution)/shard_map/pallas_call | solution.py:46
  42.6 0.0 collective-permute-done.7.hidden_b.refs_7_
  42.6 3.3 %collective-permute-done.6.hidden_a.refs_6_ = bf16[2,544,128]{2,1,0:T(8,128)(2,1)S(1)} collective-permute-done((bf16[2,544,128]{2,1,0:T(8,128)(2,1)S(1)}, bf16[2,544,128]{2,1,0:T(8,128)(2,1)S(1)}, u32[]{:S(2)}, u32[]{:S(2)}) %collective-permute-start.6) | collective-permute-done | bytes 278560 | tf_op jit(solution)/shard_map/ppermute | solution.py:620
  46.0 3.6 %shard_map.142 = (f32[4,544,128]{2,1,0:T(8,128)S(1)}, f32[4,544,128]{2,1,0:T(8,128)S(1)}, bf16[4,544,128]{2,1,0:T(8,128)(2,1)S(1)}, bf16[2,544,128]{2,1,0:T(8,12...) custom-call(s32[2]{0:T(128)S(1)} %pad_add_fusion.place.refs_0_, ...), custom_call_target="tpu_custom_call" | custom-call | flops 3208642560 | bytes 12533768 | tf_op jit(solution)/shard_map/pallas_call | solution.py:46
  49.5 1.3 collective-permute-start.8
  50.8 0.7 collective-permute-start.9
  51.5 1.0 shard_map.143.refs_1_
  52.5 3.0 %shard_map.144 = (f32[2304,128]{1,0:T(8,128)S(1)}, f32[2304,128]{1,0:T(8,128)S(1)}) custom-call(s32[2]{0:T(128)S(1)} %pad_add_fusion.place.refs_0_, bf16[4,544,128]{2,1,0:T(8,128)(2,1)S(1)} %get-tuple-element.106.resets, bf16[2,544,128]{2,1,0:T(8,128)(2,1)S(1)} %get-tuple-element.98.hidden.refs_5_, ...), custom_call_target="tpu_custom_call" | custom-call | flops 1283457024 | bytes 5193736 | tf_op jit(solution)/shard_map/pallas_call | solution.py:46
  55.6 2.5 %collective-permute-done.8.refs_2_ = bf16[3,544,128]{2,1,0:T(8,128)(2,1)S(1)} collective-permute-done((bf16[3,544,128]{2,1,0:T(8,128)(2,1)S(1)}, bf16[3,544,128]{2,1,0:T(8,128)(2,1)S(1)}, u32[]{:S(2)}, u32[]{:S(2)}) %collective-permute-start.8) | collective-permute-done | bytes 417824 | tf_op jit(solution)/shard_map/ppermute | solution.py:626
  58.0 0.0 collective-permute-done.9.refs_3_
  58.0 3.5 %shard_map.145 = (bf16[2,544,128]{2,1,0:T(8,128)(2,1)S(1)}, f32[2,544,128]{2,1,0:T(8,128)S(1)}, f32[2,544,128]{2,1,0:T(8,128)S(1)}, bf16[2,544,128]{2,1,0:T(8,12...) custom-call(s32[2]{0:T(128)S(1)} %pad_add_fusion.place.refs_0_, ...), custom_call_target="tpu_custom_call" | custom-call | flops 2566914048 | bytes 13467656 | tf_op jit(solution)/shard_map/pallas_call | solution.py:46
  61.5 4.9 %collective-permute-start.10 = (bf16[3,544,128]{2,1,0:T(8,128)(2,1)S(1)}, bf16[3,544,128]{2,1,0:T(8,128)(2,1)S(1)}, u32[]{:S(2)}, u32[]{:S(2)}) collective-permute-start(bf16[3,544,128]{2,1,0:T(8,128)(2,1)S(1)} %get-tuple-element.118), channel_id=1, source_target_pairs={{0,4},{8,12},{16,20},{24,28},{32,36},{40,44},{48,52},{56,60},{64,6... | collective-permute-start | bytes 1253384 | tf_op jit(solution)/shard_map/ppermute | solution.py:626
  66.4 0.9 collective-permute-start.11
  67.3 1.0 shard_map.147.partial
  68.4 4.3 %shard_map.146 = (bf16[2304,128]{1,0:T(8,128)(2,1)S(1)}, bf16[2304,128]{1,0:T(8,128)(2,1)S(1)}, f32[2304,128]{1,0:T(8,128)S(1)}) custom-call(s32[2]{0:T(128)S(1)} %pad_add_fusion.place.refs_0_, bf16[4,544,128]{2,1,0:T(8,128)(2,1)S(1)} %get-tuple-element.120.resets, bf16[4,544,128]{2,1,0:T(8,128)(2,1)S(1)} %get-tuple-element.115.refs_13_.older.hiddens, ...), custom_call_target="tpu_custom_call" | custom-call | flops 1925185536 | bytes 8388616 | tf_op jit(solution)/shard_map/pallas_call | solution.py:46
  72.6 0.0 collective-permute-done.10.grad_a
  72.7 0.0 collective-permute-done.11.grad_b
  72.7 4.3 %collective-permute-start.12 = (bf16[2304,128]{1,0:T(8,128)(2,1)S(1)}, bf16[2304,128]{1,0:T(8,128)(2,1)S(1)}, u32[]{:S(2)}, u32[]{:S(2)}) collective-permute-start(bf16[2304,128]{1,0:T(8,128)(2,1)S(1)} %get-tuple-element.141), channel_id=1, source_target_pairs={{0,1},{1,0},{2,3},{3,2},{4,5},{5,4},{6,7},{7,6},{8,9},{9,8},{10,11... | collective-permute-start | bytes 1769480 | tf_op jit(solution)/shard_map/ppermute | solution.py:654
  77.0 4.7 %shard_map.148 = (bf16[2,512,128]{2,1,0:T(8,128)(2,1)}, f32[2,512,128]{2,1,0:T(8,128)S(1)}, bf16[1280,128]{1,0:T(8,128)(2,1)S(1)}, bf16[1280,128]{1,0:T(8,128)(2,1)S(1)}) custom-call(s32[2]{0:T(128)S(1)} %pad_add_fusion.place.refs_0_, f32[4,544,256]{2,1,0:T(8,128)S(1)} %shard_map.147.partial, bf16[3,544,128]{2,1,0:T(8,128)(2,1)S(1)} %collective-permute-done.10.grad_a, ...), custom_call_target="tpu_custom_call" | custom-call | flops 3208642560 | bytes 13385736 | tf_op jit(solution)/shard_map/pallas_call | solution.py:46
  81.7 0.0 collective-permute-done.12.got
  81.7 0.1 collective-permute-start.13
  81.8 1.6 %collective-permute-done.13.last_got = bf16[1280,128]{1,0:T(8,128)(2,1)S(1)} collective-permute-done((bf16[1280,128]{1,0:T(8,128)(2,1)S(1)}, bf16[1280,128]{1,0:T(8,128)(2,1)S(1)}, u32[]{:S(2)}, u32[]{:S(2)}) %collective-permute-start.13) | collective-permute-done | bytes 327712 | tf_op jit(solution)/shard_map/ppermute | solution.py:654
  83.4 1.1 shard_map.149
  84.6 19.2 %all-to-all-start = ((bf16[64,56,128]{2,1,0:T(8,128)(2,1)}), bf16[64,56,128]{2,1,0:T(8,128)(2,1)S(1)}, u32[]{:S(2)}, u32[]{:S(2)}) async-start(bf16[64,56,128]{2,1,0:T(8,128)(2,1)} %bitcast.2), calls=%async_computation | async-start | bytes 1835008 | tf_op jit(solution)/shard_map/all_to_all | solution.py:640
  103.8 0.0 copy-start.7
  103.8 1.0 copy-done.7
  104.7 1.0 copy-done.11
  105.8 3.2 %shard_map.150 = (bf16[2,512,256]{2,1,0:T(8,128)(2,1)}, bf16[2,192,256]{2,1,0:T(8,128)(2,1)S(1)}, f32[2,512,256]{2,1,0:T(8,128)S(1)}) custom-call(s32[2]{0:T(128)S(1)} %pad_add_fusion.place.refs_0_, s32[2]{0:T(128)S(1)} %copy-done.9, s32[2,4]{1,0:T(2,128)S(1)} %copy-done.8, bf16[2,512,256]{2,1,0:T(8,128)(2,1)S(1)} %copy-done, ...), custom_call_target="tpu_custom_call" | custom-call | flops 855638016 | bytes 3932208 | tf_op jit(solution)/shard_map/pallas_call | solution.py:46
  109.0 0.7 copy-done.12
  109.7 10.3 %all-to-all-done.pieces = bf16[64,56,128]{2,1,0:T(8,128)(2,1)S(1)} async-done(((bf16[64,56,128]{2,1,0:T(8,128)(2,1)}), bf16[64,56,128]{2,1,0:T(8,128)(2,1)S(1)}, u32[]{:S(2)}, u32[]{:S(2)}) %all-to-all-start) | async-done | bytes 917536 | tf_op jit(solution)/shard_map/all_to_all | solution.py:640
  119.9 1.1 shard_map.151
  121.1 5.5 %all-to-all-start.1 = ((bf16[64,56,128]{2,1,0:T(8,128)(2,1)}), bf16[64,56,128]{2,1,0:T(8,128)(2,1)S(1)}, u32[]{:S(2)}, u32[]{:S(2)}) async-start(bf16[64,56,128]{2,1,0:T(8,128)(2,1)} %shard_map.151), calls=%async_computation.1 | async-start | bytes 1835008 | tf_op jit(solution)/shard_map/all_to_all | solution.py:649
  126.6 6.5 %collective-permute-start.15 = (bf16[2,192,256]{2,1,0:T(8,128)(2,1)S(1)}, bf16[2,192,256]{2,1,0:T(8,128)(2,1)S(1)}, u32[]{:S(2)}, u32[]{:S(2)}) collective-permute-start(bf16[2,192,256]{2,1,0:T(8,128)(2,1)S(1)} %copy-done.13), channel_id=1, source_target_pairs={{1,2},{2,1},{5,6},{6,5},{9,10},{10,9},{13,14},{14,13},{17,18},{18,... | collective-permute-start | bytes 589832 | tf_op jit(solution)/shard_map/ppermute | solution.py:620
  133.1 0.1 collective-permute-start.14
  133.2 8.9 %collective-permute-done.15.back_b = bf16[2,192,256]{2,1,0:T(8,128)(2,1)S(1)} collective-permute-done((bf16[2,192,256]{2,1,0:T(8,128)(2,1)S(1)}, bf16[2,192,256]{2,1,0:T(8,128)(2,1)S(1)}, u32[]{:S(2)}, u32[]{:S(2)}) %collective-permute-start.15) | collective-permute-done | bytes 196640 | tf_op jit(solution)/shard_map/ppermute | solution.py:620
  142.1 1.4 shard_map.152
  143.5 0.0 all-to-all-done.1
  143.5 1.6 %collective-permute-start.16 = (bf16[3584,128]{1,0:T(8,128)(2,1)S(1)}, bf16[3584,128]{1,0:T(8,128)(2,1)S(1)}, u32[]{:S(2)}, u32[]{:S(2)}) collective-permute-start(bf16[3584,128]{1,0:T(8,128)(2,1)S(1)} %bitcast.4), channel_id=1, source_target_pairs={{0,1},{1,0},{2,3},{3,2},{4,5},{5,4},{6,7},{7,6},{8,9},{9,8},{10,11... | collective-permute-start | bytes 2752520 | tf_op jit(solution)/shard_map/ppermute | solution.py:654
  145.1 1.8 %shard_map.153 = (f32[2304,256]{1,0:T(8,128)}, f32[2304,128]{1,0:T(8,128)}) custom-call(s32[2]{0:T(128)S(1)} %pad_add_fusion.place.refs_0_, bf16[3584,128]{1,0:T(8,128)(2,1)S(1)} %bitcast.5), custom_call_target="tpu_custom_call" | custom-call | bytes 1769472 | tf_op jit(solution)/shard_map/pallas_call | solution.py:169
  146.9 0.3 collective-permute-done.16.refs_2_
  147.2 2.4 %shard_map.154 = (f32[36,128]{1,0:T(8,128)}, f32[2304,256]{1,0:T(8,128)}, f32[2304,128]{1,0:T(8,128)}) custom-call(s32[2]{0:T(128)S(1)} %pad_add_fusion.place.refs_0_, bf16[3584,128]{1,0:T(8,128)(2,1)S(1)} %bitcast.6, bf16[3584,128]{1,0:T(8,128)(2,1)S(1)} %collective-permute-done.16.refs_2_, ...), custom_call_target="tpu_custom_call", output_to_operand_aliasing={{1}: (3, {}), {2}: (4, {})} | custom-call | bytes 1769472 | tf_op jit(solution)/shard_map/pallas_call | solution.py:169
  (25 shorter events, 0.1 us)
Async XLA Ops:
  0.6 8.2 %copy-start.4 = (bf16[2,512,128]{2,1,0:T(8,128)(2,1)S(1)}, bf16[2,512,128]{2,1,0:T(8,128)(2,1)}, u32[]{:S(2)}) copy-start(bf16[2,512,128]{2,1,0:T(8,128)(2,1)} %hidden.3) | copy-start | bytes 786436
  0.6 13.6 %copy-start.1 = (bf16[2,512,256]{2,1,0:T(8,128)(2,1)S(1)}, bf16[2,512,256]{2,1,0:T(8,128)(2,1)}, u32[]{:S(2)}) copy-start(bf16[2,512,256]{2,1,0:T(8,128)(2,1)} %right.5) | copy-start | bytes 1572868
  0.7 13.6 %copy-start = (bf16[2,512,256]{2,1,0:T(8,128)(2,1)S(1)}, bf16[2,512,256]{2,1,0:T(8,128)(2,1)}, u32[]{:S(2)}) copy-start(bf16[2,512,256]{2,1,0:T(8,128)(2,1)} %left.5) | copy-start | bytes 1572868
  0.7 13.6 %copy-start.3 = (bf16[2,512,128]{2,1,0:T(8,128)(2,1)S(1)}, bf16[2,512,128]{2,1,0:T(8,128)(2,1)}, u32[]{:S(2)}) copy-start(bf16[2,512,128]{2,1,0:T(8,128)(2,1)} %grads.3) | copy-start | bytes 786436
  0.7 13.4 %copy-start.14 = (bf16[36,128]{1,0:T(8,128)(2,1)S(1)}, bf16[36,128]{1,0:T(8,128)(2,1)}, u32[]{:S(2)}) copy-start(bf16[36,128]{1,0:T(8,128)(2,1)} %param.14) | copy-start | bytes 27652
  0.7 13.6 %copy-start.8 = (s32[2,4]{1,0:T(2,128)S(1)}, s32[2,4]{1,0:T(2,128)}, u32[]{:S(2)}) copy-start(s32[2,4]{1,0:T(2,128)} %offsets.3) | copy-start | bytes 100
  0.7 13.6 %copy-start.9 = (s32[2]{0:T(128)S(1)}, s32[2]{0:T(128)}, u32[]{:S(2)}) copy-start(s32[2]{0:T(128)} %disparity.3) | copy-start | bytes 28
  2.5 21.0 %copy-start.2 = (bf16[2304,256]{1,0:T(8,128)(2,1)S(1)}, bf16[2304,256]{1,0:T(8,128)(2,1)}, u32[]{:S(2)}) copy-start(bf16[2304,256]{1,0:T(8,128)(2,1)} %gate_w.7) | copy-start | bytes 3538948
  2.6 11.6 %collective-permute-start.1 = (bf16[2,288,256]{2,1,0:T(8,128)(2,1)}, bf16[2,288,256]{2,1,0:T(8,128)(2,1)S(1)}, u32[]{:S(2)}, u32[]{:S(2)}) collective-permute-start(bf16[2,288,256]{2,1,0:T(8,128)(2,1)} %shard_map.136), channel_id=1, source_target_pairs={{1,2},{2,1},{5,6},{6,5},{9,10},{10,9},{13,14},{14,13},{17,18},{18,... | collective-permute-start | bytes 884744 | tf_op jit(solution)/shard_map/ppermute | solution.py:620
  8.7 5.5 %collective-permute-start = (bf16[2,288,256]{2,1,0:T(8,128)(2,1)}, bf16[2,288,256]{2,1,0:T(8,128)(2,1)S(1)}, u32[]{:S(2)}, u32[]{:S(2)}) collective-permute-start(bf16[2,288,256]{2,1,0:T(8,128)(2,1)} %shard_map.136), channel_id=1, source_target_pairs={{0,1},{2,3},{1,0},{3,2},{4,5},{6,7},{5,4},{7,6},{8,9},{10,11},{9,8... | collective-permute-start | bytes 884744 | tf_op jit(solution)/shard_map/ppermute | solution.py:620
  8.8 9.5 %collective-permute-start.3 = (bf16[2,512,128]{2,1,0:T(8,128)(2,1)S(1)}, bf16[2,512,128]{2,1,0:T(8,128)(2,1)}, u32[]{:S(2)}, u32[]{:S(2)}) collective-permute-start(bf16[2,512,128]{2,1,0:T(8,128)(2,1)S(1)} %copy-done.4), channel_id=1, source_target_pairs={{4,8},{12,16},{20,24},{28,32},{36,40},{44,48},{52,56},{60,64},{68,... | collective-permute-start | bytes 786440 | tf_op jit(solution)/shard_map/ppermute | solution.py:620
  10.2 9.9 %collective-permute-start.2 = (bf16[2,512,128]{2,1,0:T(8,128)(2,1)S(1)}, bf16[2,512,128]{2,1,0:T(8,128)(2,1)}, u32[]{:S(2)}, u32[]{:S(2)}) collective-permute-start(bf16[2,512,128]{2,1,0:T(8,128)(2,1)S(1)} %copy-done.4), channel_id=1, source_target_pairs={{0,4},{8,12},{16,20},{24,28},{32,36},{40,44},{48,52},{56,60},{64,6... | collective-permute-start | bytes 786440 | tf_op jit(solution)/shard_map/ppermute | solution.py:620
  14.3 11.0 %copy-start.6 = (bf16[2,288,256]{2,1,0:T(8,128)(2,1)}, bf16[2,288,256]{2,1,0:T(8,128)(2,1)S(1)}, u32[]{:S(2)}) copy-start(bf16[2,288,256]{2,1,0:T(8,128)(2,1)S(1)} %collective-permute-done.got_a) | copy-start | bytes 884740
  20.2 6.7 %collective-permute-start.5 = (bf16[2,576,128]{2,1,0:T(8,128)(2,1)S(1)}, bf16[2,576,128]{2,1,0:T(8,128)(2,1)S(1)}, u32[]{:S(2)}, u32[]{:S(2)}) collective-permute-start(bf16[2,576,128]{2,1,0:T(8,128)(2,1)S(1)} %get-tuple-element.89.motion), channel_id=1, source_target_pairs={{4,8},{12,16},{20,24},{28,32},{36,40},{44,48},{52,56},{60,64},{68,... | collective-permute-start | bytes 884744 | tf_op jit(solution)/shard_map/ppermute | solution.py:620
  20.8 8.3 %collective-permute-start.4 = (bf16[2,576,128]{2,1,0:T(8,128)(2,1)S(1)}, bf16[2,576,128]{2,1,0:T(8,128)(2,1)S(1)}, u32[]{:S(2)}, u32[]{:S(2)}) collective-permute-start(bf16[2,576,128]{2,1,0:T(8,128)(2,1)S(1)} %get-tuple-element.89.motion), channel_id=1, source_target_pairs={{0,4},{8,12},{16,20},{24,28},{32,36},{40,44},{48,52},{56,60},{64,6... | collective-permute-start | bytes 884744 | tf_op jit(solution)/shard_map/ppermute | solution.py:620
  23.5 1.1 copy-start.5
  32.9 9.7 %collective-permute-start.7 = (bf16[2,544,128]{2,1,0:T(8,128)(2,1)S(1)}, bf16[2,544,128]{2,1,0:T(8,128)(2,1)S(1)}, u32[]{:S(2)}, u32[]{:S(2)}) collective-permute-start(bf16[2,544,128]{2,1,0:T(8,128)(2,1)S(1)} %get-tuple-element.98.hidden.refs_5_), channel_id=1, source_target_pairs={{4,8},{12,16},{20,24},{28,32},{36,40},{44,48},{52,56},{60,64},{68,... | collective-permute-start | bytes 835592 | tf_op jit(solution)/shard_map/ppermute | solution.py:620
  33.6 12.3 %collective-permute-start.6 = (bf16[2,544,128]{2,1,0:T(8,128)(2,1)S(1)}, bf16[2,544,128]{2,1,0:T(8,128)(2,1)S(1)}, u32[]{:S(2)}, u32[]{:S(2)}) collective-permute-start(bf16[2,544,128]{2,1,0:T(8,128)(2,1)S(1)} %get-tuple-element.98.hidden.refs_5_), channel_id=1, source_target_pairs={{0,4},{8,12},{16,20},{24,28},{32,36},{40,44},{48,52},{56,60},{64,6... | collective-permute-start | bytes 835592 | tf_op jit(solution)/shard_map/ppermute | solution.py:620
  49.5 8.5 %collective-permute-start.8 = (bf16[3,544,128]{2,1,0:T(8,128)(2,1)S(1)}, bf16[3,544,128]{2,1,0:T(8,128)(2,1)S(1)}, u32[]{:S(2)}, u32[]{:S(2)}) collective-permute-start(bf16[3,544,128]{2,1,0:T(8,128)(2,1)S(1)} %get-tuple-element.104), channel_id=1, source_target_pairs={{0,4},{8,12},{16,20},{24,28},{32,36},{40,44},{48,52},{56,60},{64,6... | collective-permute-start | bytes 1253384 | tf_op jit(solution)/shard_map/ppermute | solution.py:626
  50.8 7.2 %collective-permute-start.9 = (bf16[3,544,128]{2,1,0:T(8,128)(2,1)S(1)}, bf16[3,544,128]{2,1,0:T(8,128)(2,1)S(1)}, u32[]{:S(2)}, u32[]{:S(2)}) collective-permute-start(bf16[3,544,128]{2,1,0:T(8,128)(2,1)S(1)} %get-tuple-element.105), channel_id=1, source_target_pairs={{4,8},{12,16},{20,24},{28,32},{36,40},{44,48},{52,56},{60,64},{68,... | collective-permute-start | bytes 1253384 | tf_op jit(solution)/shard_map/ppermute | solution.py:625
  61.5 11.1 %collective-permute-start.10 = (bf16[3,544,128]{2,1,0:T(8,128)(2,1)S(1)}, bf16[3,544,128]{2,1,0:T(8,128)(2,1)S(1)}, u32[]{:S(2)}, u32[]{:S(2)}) collective-permute-start(bf16[3,544,128]{2,1,0:T(8,128)(2,1)S(1)} %get-tuple-element.118), channel_id=1, source_target_pairs={{0,4},{8,12},{16,20},{24,28},{32,36},{40,44},{48,52},{56,60},{64,6... | collective-permute-start | bytes 1253384 | tf_op jit(solution)/shard_map/ppermute | solution.py:626
  66.4 6.3 %collective-permute-start.11 = (bf16[3,544,128]{2,1,0:T(8,128)(2,1)S(1)}, bf16[3,544,128]{2,1,0:T(8,128)(2,1)S(1)}, u32[]{:S(2)}, u32[]{:S(2)}) collective-permute-start(bf16[3,544,128]{2,1,0:T(8,128)(2,1)S(1)} %get-tuple-element.119), channel_id=1, source_target_pairs={{4,8},{12,16},{20,24},{28,32},{36,40},{44,48},{52,56},{60,64},{68,... | collective-permute-start | bytes 1253384 | tf_op jit(solution)/shard_map/ppermute | solution.py:625
  72.7 9.0 %collective-permute-start.12 = (bf16[2304,128]{1,0:T(8,128)(2,1)S(1)}, bf16[2304,128]{1,0:T(8,128)(2,1)S(1)}, u32[]{:S(2)}, u32[]{:S(2)}) collective-permute-start(bf16[2304,128]{1,0:T(8,128)(2,1)S(1)} %get-tuple-element.141), channel_id=1, source_target_pairs={{0,1},{1,0},{2,3},{3,2},{4,5},{5,4},{6,7},{7,6},{8,9},{9,8},{10,11... | collective-permute-start | bytes 1769480 | tf_op jit(solution)/shard_map/ppermute | solution.py:654
  81.7 2.9 %copy-start.10 = (f32[2,512,128]{2,1,0:T(8,128)}, f32[2,512,128]{2,1,0:T(8,128)S(1)}, u32[]{:S(2)}) copy-start(f32[2,512,128]{2,1,0:T(8,128)S(1)} %get-tuple-element.145.grad_feats) | copy-start | bytes 1572868
  81.7 1.7 %collective-permute-start.13 = (bf16[1280,128]{1,0:T(8,128)(2,1)S(1)}, bf16[1280,128]{1,0:T(8,128)(2,1)S(1)}, u32[]{:S(2)}, u32[]{:S(2)}) collective-permute-start(bf16[1280,128]{1,0:T(8,128)(2,1)S(1)} %get-tuple-element.144), channel_id=1, source_target_pairs={{0,1},{1,0},{2,3},{3,2},{4,5},{5,4},{6,7},{7,6},{8,9},{9,8},{10,11... | collective-permute-start | bytes 983048 | tf_op jit(solution)/shard_map/ppermute | solution.py:654
  84.6 35.4 %all-to-all-start = ((bf16[64,56,128]{2,1,0:T(8,128)(2,1)}), bf16[64,56,128]{2,1,0:T(8,128)(2,1)S(1)}, u32[]{:S(2)}, u32[]{:S(2)}) async-start(bf16[64,56,128]{2,1,0:T(8,128)(2,1)} %bitcast.2), calls=%async_computation | async-start | bytes 1835008 | tf_op jit(solution)/shard_map/all_to_all | solution.py:640
  103.8 1.0 copy-start.7
  104.7 1.0 copy-start.11
  109.0 0.7 copy-start.12
  121.1 5.5 %copy-start.13 = (bf16[2,192,256]{2,1,0:T(8,128)(2,1)S(1)}, bf16[2,192,256]{2,1,0:T(8,128)(2,1)}, u32[]{:S(2)}) copy-start(bf16[2,192,256]{2,1,0:T(8,128)(2,1)} %copy-done.12) | copy-start | bytes 589828
  121.1 22.5 %all-to-all-start.1 = ((bf16[64,56,128]{2,1,0:T(8,128)(2,1)}), bf16[64,56,128]{2,1,0:T(8,128)(2,1)S(1)}, u32[]{:S(2)}, u32[]{:S(2)}) async-start(bf16[64,56,128]{2,1,0:T(8,128)(2,1)} %shard_map.151), calls=%async_computation.1 | async-start | bytes 1835008 | tf_op jit(solution)/shard_map/all_to_all | solution.py:649
  126.6 15.5 %collective-permute-start.15 = (bf16[2,192,256]{2,1,0:T(8,128)(2,1)S(1)}, bf16[2,192,256]{2,1,0:T(8,128)(2,1)S(1)}, u32[]{:S(2)}, u32[]{:S(2)}) collective-permute-start(bf16[2,192,256]{2,1,0:T(8,128)(2,1)S(1)} %copy-done.13), channel_id=1, source_target_pairs={{1,2},{2,1},{5,6},{6,5},{9,10},{10,9},{13,14},{14,13},{17,18},{18,... | collective-permute-start | bytes 589832 | tf_op jit(solution)/shard_map/ppermute | solution.py:620
  133.1 9.0 %collective-permute-start.14 = (bf16[2,192,256]{2,1,0:T(8,128)(2,1)S(1)}, bf16[2,192,256]{2,1,0:T(8,128)(2,1)S(1)}, u32[]{:S(2)}, u32[]{:S(2)}) collective-permute-start(bf16[2,192,256]{2,1,0:T(8,128)(2,1)S(1)} %copy-done.13), channel_id=1, source_target_pairs={{0,1},{2,3},{1,0},{3,2},{4,5},{6,7},{5,4},{7,6},{8,9},{10,11},{9,8... | collective-permute-start | bytes 589832 | tf_op jit(solution)/shard_map/ppermute | solution.py:620
  143.5 3.7 %collective-permute-start.16 = (bf16[3584,128]{1,0:T(8,128)(2,1)S(1)}, bf16[3584,128]{1,0:T(8,128)(2,1)S(1)}, u32[]{:S(2)}, u32[]{:S(2)}) collective-permute-start(bf16[3584,128]{1,0:T(8,128)(2,1)S(1)} %bitcast.4), channel_id=1, source_target_pairs={{0,1},{1,0},{2,3},{3,2},{4,5},{5,4},{6,7},{7,6},{8,9},{9,8},{10,11... | collective-permute-start | bytes 2752520 | tf_op jit(solution)/shard_map/ppermute | solution.py:654

commit v7 on v6

--- a/solution.py
+++ b/solution.py
@@ -566,9 +566,13 @@
     share_cores(place, parts, kept, given)
 
 
-def join_kernel(kept, got, last_kept, last_got, half):
-    split = kept.shape[0]
-    half[:split] = (kept[...].astype(F32) + got[...].astype(F32)).astype(BF16)
+def add_kernel(kept, got, out):
+    out[...] = (kept[...].astype(F32) + got[...].astype(F32)).astype(BF16)
+
+
+def join_kernel(early, last_kept, last_got, half):
+    split = early.shape[0]
+    half[:split] = early[...]
     half[split:] = (last_kept[...].astype(F32) + last_got[...].astype(F32)).astype(BF16)
 
 
@@ -633,9 +637,10 @@
 
 def shared_out(kept, got, last_kept, last_given, axes):
     total = kept.shape[0] + last_kept.shape[0]
-    (half,) = kernel_call(
-        join_kernel, [array((total, LANES), BF16)], [kept, got, last_kept, swapped(last_given)], 0, [], 0
-    )
+    (early,) = kernel_call(add_kernel, [array(kept.shape, BF16)], [kept, got], 0, [], 0)
+    last_got = swapped(last_given)
+    early, last_got = lax.optimization_barrier((early, last_got))
+    (half,) = kernel_call(join_kernel, [array((total, LANES), BF16)], [early, last_kept, last_got], 0, [], 0)
     half = half.reshape(len(core_groups()[0]), -1, LANES)
     return lax.all_to_all(half, axes, 0, 0, tiled=True, axis_index_groups=core_groups())
 

time: 150 us -> 150 us (level)
    pallas_call x16 -> x17, Pallas kernels: 39.6 us -> 39.7 us  [kernel_call(): pl.pallas_call(body, out_shape=outs, in_specs=[SMEM] * scalars + [VMEM] *...]
where the time goes in v7:
time: 150 us
  starting transfers between devices  68 us (45%)
  Pallas kernels  45.8 us (31%)
  waiting for transfers between devices  30.9 us (21%)
  local copies, waits for them, and re-layouts  3.79 us (3%)
    pallas_call x17, Pallas kernels, kernel_call(): pl.pallas_call(body, out_shape=outs, in_specs=[SMEM] * scalars + [VMEM] *...  39.7 us
    ppermute x10, starting transfers between devices, exchanged(): return (lax.ppermute(value, axis, first), lax.ppermute(value, axis, second))  29.6 us
    all_to_all x1, starting transfers between devices, shared_out(): lax.all_to_all(half, axes, 0, 0, tiled=True, axis_index_groups=core_group...  19.2 us
    ppermute x10, waiting for transfers between devices, exchanged(): return (lax.ppermute(value, axis, first), lax.ppermute(value, axis, second))  16.4 us
    all_to_all x1, waiting for transfers between devices, shared_out(): lax.all_to_all(half, axes, 0, 0, tiled=True, axis_index_groups=core_group...  10.3 us
    ppermute x2, starting transfers between devices, exchanged_pair(): return (lax.ppermute(value_a, axis, first), other)  6.13 us
    ppermute x3, starting transfers between devices, swapped(): lax.ppermute(value, 'cols', [(i, i ^ 1) for i in range(lax.axis_size('col...  5.96 us
    all_to_all x1, starting transfers between devices, gathered(): lax.all_to_all(spread, axes, 0, 0, tiled=True, axis_index_groups=core_gro...  5.49 us
  transfers between devices with their start and end apart: 19, of which 8 were waited for; matrix products, arithmetic and copies ran while one was open for 0% of the time, Pallas kernels for 19%

profile of v7, /device:TPU:1, one launch (start us, length us, event | category | flops | bytes accessed | tf_op | source)
XLA Modules:
  0.0 149.7 jit_solution(11310690342158493214)
XLA Ops:
  0.7 1.8 %shard_map.136 = bf16[2,288,256]{2,1,0:T(8,128)(2,1)} custom-call(bf16[2,512,256]{2,1,0:T(8,128)(2,1)} %left.5, bf16[2,512,256]{2,1,0:T(8,128)(2,1)} %right.5, bf16[2,512,128]{2,1,0:T(8,128)(2,1)} %hidden.3, bf16[2,512,128]{2,1,0:T(8,128)(2,1)} %grads.3), custom_call_target="tpu_custom_call" | custom-call | bytes 589824 | tf_op jit(solution)/shard_map/pallas_call | solution.py:117
  2.5 0.0 copy-start.2
  2.6 6.2 %collective-permute-start.1 = (bf16[2,288,256]{2,1,0:T(8,128)(2,1)}, bf16[2,288,256]{2,1,0:T(8,128)(2,1)S(1)}, u32[]{:S(2)}, u32[]{:S(2)}) collective-permute-start(bf16[2,288,256]{2,1,0:T(8,128)(2,1)} %shard_map.136), channel_id=1, source_target_pairs={{1,2},{2,1},{5,6},{6,5},{9,10},{10,9},{13,14},{14,13},{17,18},{18,... | collective-permute-start | bytes 884744 | tf_op jit(solution)/shard_map/ppermute | solution.py:624
  8.7 0.1 collective-permute-start
  8.8 1.4 collective-permute-start.3
  10.2 3.9 %collective-permute-start.2 = (bf16[2,512,128]{2,1,0:T(8,128)(2,1)S(1)}, bf16[2,512,128]{2,1,0:T(8,128)(2,1)}, u32[]{:S(2)}, u32[]{:S(2)}) collective-permute-start(bf16[2,512,128]{2,1,0:T(8,128)(2,1)S(1)} %copy-done.4), channel_id=1, source_target_pairs={{0,4},{8,12},{16,20},{24,28},{32,36},{40,44},{48,52},{56,60},{64,6... | collective-permute-start | bytes 786440 | tf_op jit(solution)/shard_map/ppermute | solution.py:624
  14.1 0.1 pad_add_fusion.place.refs_0_
  14.2 0.0 collective-permute-done.1.got_b
  14.2 0.0 collective-permute-done.got_a
  14.3 0.0 copy-start.6
  14.3 4.0 %shard_map.137 = (bf16[2,576,128]{2,1,0:T(8,128)(2,1)S(1)}, f32[2,544,128]{2,1,0:T(8,128)S(1)}, bf16[2,544,128]{2,1,0:T(8,128)(2,1)S(1)}, bf16[2,544,128]{2,1,0:T(8,128)(2,1)S(1)}, bf16[2,544,128]{2,1,0:T(8,128)(2,1)S(1)}) custom-call(s32[2]{0:T(128)S(1)} %pad_add_fusion.place.refs_0_, s32[2]{0:T(128)S(1)} %copy-done.9, s32[2,4]{1,0:T(2,128)S(1)} %copy-done.8, ...), custom_call_target="tpu_custom_call" | custom-call | flops 570425344 | bytes 3883056 | tf_op jit(solution)/shard_map/pallas_call | solution.py:46
  18.3 0.0 collective-permute-done.3.refs_3_
  18.3 1.8 %collective-permute-done.2.refs_2_ = bf16[2,512,128]{2,1,0:T(8,128)(2,1)} collective-permute-done((bf16[2,512,128]{2,1,0:T(8,128)(2,1)S(1)}, bf16[2,512,128]{2,1,0:T(8,128)(2,1)}, u32[]{:S(2)}, u32[]{:S(2)}) %collective-permute-start.2) | collective-permute-done | bytes 262176 | tf_op jit(solution)/shard_map/ppermute | solution.py:624
  20.2 0.7 collective-permute-start.5
  20.8 2.7 %collective-permute-start.4 = (bf16[2,576,128]{2,1,0:T(8,128)(2,1)S(1)}, bf16[2,576,128]{2,1,0:T(8,128)(2,1)S(1)}, u32[]{:S(2)}, u32[]{:S(2)}) collective-permute-start(bf16[2,576,128]{2,1,0:T(8,128)(2,1)S(1)} %get-tuple-element.91.motion), channel_id=1, source_target_pairs={{0,4},{8,12},{16,20},{24,28},{32,36},{40,44},{48,52},{56,60},{64,6... | collective-permute-start | bytes 884744 | tf_op jit(solution)/shard_map/ppermute | solution.py:624
  23.5 1.1 copy-done.5
  24.6 0.7 shard_map.138
  25.2 1.6 %shard_map.139 = (bf16[2,544,768]{2,1,0:T(8,128)(2,1)S(1)}, f32[4,544,256]{2,1,0:T(8,128)S(1)}) custom-call(bf16[2,544,128]{2,1,0:T(8,128)(2,1)S(1)} %get-tuple-element.87.hidden.refs_1_, bf16[2,576,128]{2,1,0:T(8,128)(2,1)S(1)} %get-tuple-element.91.motion, bf16[2304,256]{1,0:T(8,128)(2,1)S(1)} %copy-done.2), custom_call_target="tpu_custom_call" | custom-call | flops 1283457024 | bytes 5652480 | tf_op jit(solution)/shard_map/pallas_call | solution.py:46
  26.8 0.0 collective-permute-done.5.refs_5_.motion_b
  26.8 2.3 %collective-permute-done.4.refs_4_.motion_a = bf16[2,576,128]{2,1,0:T(8,128)(2,1)S(1)} collective-permute-done((bf16[2,576,128]{2,1,0:T(8,128)(2,1)S(1)}, bf16[2,576,128]{2,1,0:T(8,128)(2,1)S(1)}, u32[]{:S(2)}, u32[]{:S(2)}) %collective-permute-start.4) | collective-permute-done | bytes 294944 | tf_op jit(solution)/shard_map/ppermute | solution.py:624
  29.1 3.8 %shard_map.140 = (bf16[2,544,128]{2,1,0:T(8,128)(2,1)S(1)}, f32[4,544,128]{2,1,0:T(8,128)S(1)}, f32[4,544,128]{2,1,0:T(8,128)S(1)}, bf16[4,544,128]{2,1,0:T(8,12...) custom-call(s32[2]{0:T(128)S(1)} %pad_add_fusion.place.refs_0_, ...), custom_call_target="tpu_custom_call" | custom-call | flops 3208642560 | bytes 12222472 | tf_op jit(solution)/shard_map/pallas_call | solution.py:46
  32.9 0.7 collective-permute-start.7
  33.6 7.5 %collective-permute-start.6 = (bf16[2,544,128]{2,1,0:T(8,128)(2,1)S(1)}, bf16[2,544,128]{2,1,0:T(8,128)(2,1)S(1)}, u32[]{:S(2)}, u32[]{:S(2)}) collective-permute-start(bf16[2,544,128]{2,1,0:T(8,128)(2,1)S(1)} %get-tuple-element.100.hidden.refs_5_), channel_id=1, source_target_pairs={{0,4},{8,12},{16,20},{24,28},{32,36},{40,44},{48,52},{56,60},{64,6... | collective-permute-start | bytes 835592 | tf_op jit(solution)/shard_map/ppermute | solution.py:624
  41.1 1.6 %shard_map.141 = (bf16[2,544,768]{2,1,0:T(8,128)(2,1)S(1)}, f32[4,544,256]{2,1,0:T(8,128)S(1)}) custom-call(bf16[2,544,128]{2,1,0:T(8,128)(2,1)S(1)} %get-tuple-element.100.hidden.refs_5_, bf16[2,576,128]{2,1,0:T(8,128)(2,1)S(1)} %get-tuple-element.91.motion, bf16[2304,256]{1,0:T(8,128)(2,1)S(1)} %copy-done.2), custom_call_target="tpu_custom_call" | custom-call | flops 1283457024 | bytes 5652480 | tf_op jit(solution)/shard_map/pallas_call | solution.py:46
  42.6 0.0 collective-permute-done.7.hidden_b.refs_7_
  42.6 3.3 %collective-permute-done.6.hidden_a.refs_6_ = bf16[2,544,128]{2,1,0:T(8,128)(2,1)S(1)} collective-permute-done((bf16[2,544,128]{2,1,0:T(8,128)(2,1)S(1)}, bf16[2,544,128]{2,1,0:T(8,128)(2,1)S(1)}, u32[]{:S(2)}, u32[]{:S(2)}) %collective-permute-start.6) | collective-permute-done | bytes 278560 | tf_op jit(solution)/shard_map/ppermute | solution.py:624
  46.0 3.6 %shard_map.142 = (f32[4,544,128]{2,1,0:T(8,128)S(1)}, f32[4,544,128]{2,1,0:T(8,128)S(1)}, bf16[4,544,128]{2,1,0:T(8,128)(2,1)S(1)}, bf16[2,544,128]{2,1,0:T(8,12...) custom-call(s32[2]{0:T(128)S(1)} %pad_add_fusion.place.refs_0_, ...), custom_call_target="tpu_custom_call" | custom-call | flops 3208642560 | bytes 12533768 | tf_op jit(solution)/shard_map/pallas_call | solution.py:46
  49.5 1.3 collective-permute-start.8
  50.8 0.7 collective-permute-start.9
  51.5 1.0 shard_map.143.refs_1_
  52.5 3.0 %shard_map.144 = (f32[2304,128]{1,0:T(8,128)S(1)}, f32[2304,128]{1,0:T(8,128)S(1)}) custom-call(s32[2]{0:T(128)S(1)} %pad_add_fusion.place.refs_0_, bf16[4,544,128]{2,1,0:T(8,128)(2,1)S(1)} %get-tuple-element.108.resets, bf16[2,544,128]{2,1,0:T(8,128)(2,1)S(1)} %get-tuple-element.100.hidden.refs_5_, ...), custom_call_target="tpu_custom_call" | custom-call | flops 1283457024 | bytes 5193736 | tf_op jit(solution)/shard_map/pallas_call | solution.py:46
  55.6 2.5 %collective-permute-done.8.refs_2_ = bf16[3,544,128]{2,1,0:T(8,128)(2,1)S(1)} collective-permute-done((bf16[3,544,128]{2,1,0:T(8,128)(2,1)S(1)}, bf16[3,544,128]{2,1,0:T(8,128)(2,1)S(1)}, u32[]{:S(2)}, u32[]{:S(2)}) %collective-permute-start.8) | collective-permute-done | bytes 417824 | tf_op jit(solution)/shard_map/ppermute | solution.py:630
  58.0 0.0 collective-permute-done.9.refs_3_
  58.0 3.5 %shard_map.145 = (bf16[2,544,128]{2,1,0:T(8,128)(2,1)S(1)}, f32[2,544,128]{2,1,0:T(8,128)S(1)}, f32[2,544,128]{2,1,0:T(8,128)S(1)}, bf16[2,544,128]{2,1,0:T(8,12...) custom-call(s32[2]{0:T(128)S(1)} %pad_add_fusion.place.refs_0_, ...), custom_call_target="tpu_custom_call" | custom-call | flops 2566914048 | bytes 13467656 | tf_op jit(solution)/shard_map/pallas_call | solution.py:46
  61.5 4.9 %collective-permute-start.10 = (bf16[3,544,128]{2,1,0:T(8,128)(2,1)S(1)}, bf16[3,544,128]{2,1,0:T(8,128)(2,1)S(1)}, u32[]{:S(2)}, u32[]{:S(2)}) collective-permute-start(bf16[3,544,128]{2,1,0:T(8,128)(2,1)S(1)} %get-tuple-element.120), channel_id=1, source_target_pairs={{0,4},{8,12},{16,20},{24,28},{32,36},{40,44},{48,52},{56,60},{64,6... | collective-permute-start | bytes 1253384 | tf_op jit(solution)/shard_map/ppermute | solution.py:630
  66.4 0.9 collective-permute-start.11
  67.3 1.0 shard_map.147.partial
  68.4 4.3 %shard_map.146 = (bf16[2304,128]{1,0:T(8,128)(2,1)S(1)}, bf16[2304,128]{1,0:T(8,128)(2,1)S(1)}, f32[2304,128]{1,0:T(8,128)S(1)}) custom-call(s32[2]{0:T(128)S(1)} %pad_add_fusion.place.refs_0_, bf16[4,544,128]{2,1,0:T(8,128)(2,1)S(1)} %get-tuple-element.122.resets, bf16[4,544,128]{2,1,0:T(8,128)(2,1)S(1)} %get-tuple-element.117.refs_13_.older.hiddens, ...), custom_call_target="tpu_custom_call" | custom-call | flops 1925185536 | bytes 8388616 | tf_op jit(solution)/shard_map/pallas_call | solution.py:46
  72.7 0.0 collective-permute-done.11.grad_b
  72.7 4.3 %collective-permute-start.12 = (bf16[2304,128]{1,0:T(8,128)(2,1)S(1)}, bf16[2304,128]{1,0:T(8,128)(2,1)S(1)}, u32[]{:S(2)}, u32[]{:S(2)}) collective-permute-start(bf16[2304,128]{1,0:T(8,128)(2,1)S(1)} %get-tuple-element.143), channel_id=1, source_target_pairs={{0,1},{1,0},{2,3},{3,2},{4,5},{5,4},{6,7},{7,6},{8,9},{9,8},{10,11... | collective-permute-start | bytes 1769480 | tf_op jit(solution)/shard_map/ppermute | solution.py:659
  77.0 4.7 %shard_map.148 = (bf16[2,512,128]{2,1,0:T(8,128)(2,1)}, f32[2,512,128]{2,1,0:T(8,128)S(1)}, bf16[1280,128]{1,0:T(8,128)(2,1)S(1)}, bf16[1280,128]{1,0:T(8,128)(2,1)S(1)}) custom-call(s32[2]{0:T(128)S(1)} %pad_add_fusion.place.refs_0_, f32[4,544,256]{2,1,0:T(8,128)S(1)} %shard_map.147.partial, bf16[3,544,128]{2,1,0:T(8,128)(2,1)S(1)} %collective-permute-done.10.grad_a, ...), custom_call_target="tpu_custom_call" | custom-call | flops 3208642560 | bytes 13385736 | tf_op jit(solution)/shard_map/pallas_call | solution.py:46
  81.7 0.0 collective-permute-done.12.got
  81.7 0.1 collective-permute-start.13
  81.8 0.1 shard_map.149.early
  82.0 1.5 collective-permute-done.13.last_got
  83.4 1.0 shard_map.150
  84.5 19.2 %all-to-all-start = ((bf16[64,56,128]{2,1,0:T(8,128)(2,1)}), bf16[64,56,128]{2,1,0:T(8,128)(2,1)S(1)}, u32[]{:S(2)}, u32[]{:S(2)}) async-start(bf16[64,56,128]{2,1,0:T(8,128)(2,1)} %bitcast.2), calls=%async_computation | async-start | bytes 1835008 | tf_op jit(solution)/shard_map/all_to_all | solution.py:645
  103.7 0.0 copy-start.7
  103.7 1.0 copy-done.7
  104.6 1.0 copy-done.11
  105.7 3.2 %shard_map.151 = (bf16[2,512,256]{2,1,0:T(8,128)(2,1)}, bf16[2,192,256]{2,1,0:T(8,128)(2,1)S(1)}, f32[2,512,256]{2,1,0:T(8,128)S(1)}) custom-call(s32[2]{0:T(128)S(1)} %pad_add_fusion.place.refs_0_, s32[2]{0:T(128)S(1)} %copy-done.9, s32[2,4]{1,0:T(2,128)S(1)} %copy-done.8, bf16[2,512,256]{2,1,0:T(8,128)(2,1)S(1)} %copy-done, ...), custom_call_target="tpu_custom_call" | custom-call | flops 855638016 | bytes 3932208 | tf_op jit(solution)/shard_map/pallas_call | solution.py:46
  108.9 0.7 copy-done.12
  109.6 10.3 %all-to-all-done.pieces = bf16[64,56,128]{2,1,0:T(8,128)(2,1)S(1)} async-done(((bf16[64,56,128]{2,1,0:T(8,128)(2,1)}), bf16[64,56,128]{2,1,0:T(8,128)(2,1)S(1)}, u32[]{:S(2)}, u32[]{:S(2)}) %all-to-all-start) | async-done | bytes 917536 | tf_op jit(solution)/shard_map/all_to_all | solution.py:645
  119.8 1.1 shard_map.152
  121.0 5.5 %all-to-all-start.1 = ((bf16[64,56,128]{2,1,0:T(8,128)(2,1)}), bf16[64,56,128]{2,1,0:T(8,128)(2,1)S(1)}, u32[]{:S(2)}, u32[]{:S(2)}) async-start(bf16[64,56,128]{2,1,0:T(8,128)(2,1)} %shard_map.152), calls=%async_computation.1 | async-start | bytes 1835008 | tf_op jit(solution)/shard_map/all_to_all | solution.py:654
  126.5 6.5 %collective-permute-start.15 = (bf16[2,192,256]{2,1,0:T(8,128)(2,1)S(1)}, bf16[2,192,256]{2,1,0:T(8,128)(2,1)S(1)}, u32[]{:S(2)}, u32[]{:S(2)}) collective-permute-start(bf16[2,192,256]{2,1,0:T(8,128)(2,1)S(1)} %copy-done.13), channel_id=1, source_target_pairs={{1,2},{2,1},{5,6},{6,5},{9,10},{10,9},{13,14},{14,13},{17,18},{18,... | collective-permute-start | bytes 589832 | tf_op jit(solution)/shard_map/ppermute | solution.py:624
  133.0 0.1 collective-permute-start.14
  133.1 8.9 %collective-permute-done.15.back_b = bf16[2,192,256]{2,1,0:T(8,128)(2,1)S(1)} collective-permute-done((bf16[2,192,256]{2,1,0:T(8,128)(2,1)S(1)}, bf16[2,192,256]{2,1,0:T(8,128)(2,1)S(1)}, u32[]{:S(2)}, u32[]{:S(2)}) %collective-permute-start.15) | collective-permute-done | bytes 196640 | tf_op jit(solution)/shard_map/ppermute | solution.py:624
  142.0 1.4 shard_map.153
  143.4 0.0 all-to-all-done.1
  143.4 1.6 %collective-permute-start.16 = (bf16[3584,128]{1,0:T(8,128)(2,1)S(1)}, bf16[3584,128]{1,0:T(8,128)(2,1)S(1)}, u32[]{:S(2)}, u32[]{:S(2)}) collective-permute-start(bf16[3584,128]{1,0:T(8,128)(2,1)S(1)} %bitcast.4), channel_id=1, source_target_pairs={{0,1},{1,0},{2,3},{3,2},{4,5},{5,4},{6,7},{7,6},{8,9},{9,8},{10,11... | collective-permute-start | bytes 2752520 | tf_op jit(solution)/shard_map/ppermute | solution.py:659
  145.0 1.8 %shard_map.154 = (f32[2304,256]{1,0:T(8,128)}, f32[2304,128]{1,0:T(8,128)}) custom-call(s32[2]{0:T(128)S(1)} %pad_add_fusion.place.refs_0_, bf16[3584,128]{1,0:T(8,128)(2,1)S(1)} %bitcast.5), custom_call_target="tpu_custom_call" | custom-call | bytes 1769472 | tf_op jit(solution)/shard_map/pallas_call | solution.py:169
  146.8 0.3 collective-permute-done.16.refs_2_
  147.1 2.4 %shard_map.155 = (f32[36,128]{1,0:T(8,128)}, f32[2304,256]{1,0:T(8,128)}, f32[2304,128]{1,0:T(8,128)}) custom-call(s32[2]{0:T(128)S(1)} %pad_add_fusion.place.refs_0_, bf16[3584,128]{1,0:T(8,128)(2,1)S(1)} %bitcast.6, bf16[3584,128]{1,0:T(8,128)(2,1)S(1)} %collective-permute-done.16.refs_2_, ...), custom_call_target="tpu_custom_call", output_to_operand_aliasing={{1}: (3, {}), {2}: (4, {})} | custom-call | bytes 1769472 | tf_op jit(solution)/shard_map/pallas_call | solution.py:169
  (26 shorter events, 0.1 us)
Async XLA Ops:
  0.6 8.2 %copy-start.4 = (bf16[2,512,128]{2,1,0:T(8,128)(2,1)S(1)}, bf16[2,512,128]{2,1,0:T(8,128)(2,1)}, u32[]{:S(2)}) copy-start(bf16[2,512,128]{2,1,0:T(8,128)(2,1)} %hidden.3) | copy-start | bytes 786436
  0.6 13.6 %copy-start.1 = (bf16[2,512,256]{2,1,0:T(8,128)(2,1)S(1)}, bf16[2,512,256]{2,1,0:T(8,128)(2,1)}, u32[]{:S(2)}) copy-start(bf16[2,512,256]{2,1,0:T(8,128)(2,1)} %right.5) | copy-start | bytes 1572868
  0.7 13.6 %copy-start = (bf16[2,512,256]{2,1,0:T(8,128)(2,1)S(1)}, bf16[2,512,256]{2,1,0:T(8,128)(2,1)}, u32[]{:S(2)}) copy-start(bf16[2,512,256]{2,1,0:T(8,128)(2,1)} %left.5) | copy-start | bytes 1572868
  0.7 13.6 %copy-start.3 = (bf16[2,512,128]{2,1,0:T(8,128)(2,1)S(1)}, bf16[2,512,128]{2,1,0:T(8,128)(2,1)}, u32[]{:S(2)}) copy-start(bf16[2,512,128]{2,1,0:T(8,128)(2,1)} %grads.3) | copy-start | bytes 786436
  0.7 13.4 %copy-start.14 = (bf16[36,128]{1,0:T(8,128)(2,1)S(1)}, bf16[36,128]{1,0:T(8,128)(2,1)}, u32[]{:S(2)}) copy-start(bf16[36,128]{1,0:T(8,128)(2,1)} %param.14) | copy-start | bytes 27652
  0.7 13.6 %copy-start.8 = (s32[2,4]{1,0:T(2,128)S(1)}, s32[2,4]{1,0:T(2,128)}, u32[]{:S(2)}) copy-start(s32[2,4]{1,0:T(2,128)} %offsets.3) | copy-start | bytes 100
  0.7 13.6 %copy-start.9 = (s32[2]{0:T(128)S(1)}, s32[2]{0:T(128)}, u32[]{:S(2)}) copy-start(s32[2]{0:T(128)} %disparity.3) | copy-start | bytes 28
  2.5 21.0 %copy-start.2 = (bf16[2304,256]{1,0:T(8,128)(2,1)S(1)}, bf16[2304,256]{1,0:T(8,128)(2,1)}, u32[]{:S(2)}) copy-start(bf16[2304,256]{1,0:T(8,128)(2,1)} %gate_w.7) | copy-start | bytes 3538948
  2.6 11.6 %collective-permute-start.1 = (bf16[2,288,256]{2,1,0:T(8,128)(2,1)}, bf16[2,288,256]{2,1,0:T(8,128)(2,1)S(1)}, u32[]{:S(2)}, u32[]{:S(2)}) collective-permute-start(bf16[2,288,256]{2,1,0:T(8,128)(2,1)} %shard_map.136), channel_id=1, source_target_pairs={{1,2},{2,1},{5,6},{6,5},{9,10},{10,9},{13,14},{14,13},{17,18},{18,... | collective-permute-start | bytes 884744 | tf_op jit(solution)/shard_map/ppermute | solution.py:624
  8.7 5.5 %collective-permute-start = (bf16[2,288,256]{2,1,0:T(8,128)(2,1)}, bf16[2,288,256]{2,1,0:T(8,128)(2,1)S(1)}, u32[]{:S(2)}, u32[]{:S(2)}) collective-permute-start(bf16[2,288,256]{2,1,0:T(8,128)(2,1)} %shard_map.136), channel_id=1, source_target_pairs={{0,1},{2,3},{1,0},{3,2},{4,5},{6,7},{5,4},{7,6},{8,9},{10,11},{9,8... | collective-permute-start | bytes 884744 | tf_op jit(solution)/shard_map/ppermute | solution.py:624
  8.8 9.5 %collective-permute-start.3 = (bf16[2,512,128]{2,1,0:T(8,128)(2,1)S(1)}, bf16[2,512,128]{2,1,0:T(8,128)(2,1)}, u32[]{:S(2)}, u32[]{:S(2)}) collective-permute-start(bf16[2,512,128]{2,1,0:T(8,128)(2,1)S(1)} %copy-done.4), channel_id=1, source_target_pairs={{4,8},{12,16},{20,24},{28,32},{36,40},{44,48},{52,56},{60,64},{68,... | collective-permute-start | bytes 786440 | tf_op jit(solution)/shard_map/ppermute | solution.py:624
  10.2 9.9 %collective-permute-start.2 = (bf16[2,512,128]{2,1,0:T(8,128)(2,1)S(1)}, bf16[2,512,128]{2,1,0:T(8,128)(2,1)}, u32[]{:S(2)}, u32[]{:S(2)}) collective-permute-start(bf16[2,512,128]{2,1,0:T(8,128)(2,1)S(1)} %copy-done.4), channel_id=1, source_target_pairs={{0,4},{8,12},{16,20},{24,28},{32,36},{40,44},{48,52},{56,60},{64,6... | collective-permute-start | bytes 786440 | tf_op jit(solution)/shard_map/ppermute | solution.py:624
  14.3 11.0 %copy-start.6 = (bf16[2,288,256]{2,1,0:T(8,128)(2,1)}, bf16[2,288,256]{2,1,0:T(8,128)(2,1)S(1)}, u32[]{:S(2)}) copy-start(bf16[2,288,256]{2,1,0:T(8,128)(2,1)S(1)} %collective-permute-done.got_a) | copy-start | bytes 884740
  20.2 6.7 %collective-permute-start.5 = (bf16[2,576,128]{2,1,0:T(8,128)(2,1)S(1)}, bf16[2,576,128]{2,1,0:T(8,128)(2,1)S(1)}, u32[]{:S(2)}, u32[]{:S(2)}) collective-permute-start(bf16[2,576,128]{2,1,0:T(8,128)(2,1)S(1)} %get-tuple-element.91.motion), channel_id=1, source_target_pairs={{4,8},{12,16},{20,24},{28,32},{36,40},{44,48},{52,56},{60,64},{68,... | collective-permute-start | bytes 884744 | tf_op jit(solution)/shard_map/ppermute | solution.py:624
  20.8 8.3 %collective-permute-start.4 = (bf16[2,576,128]{2,1,0:T(8,128)(2,1)S(1)}, bf16[2,576,128]{2,1,0:T(8,128)(2,1)S(1)}, u32[]{:S(2)}, u32[]{:S(2)}) collective-permute-start(bf16[2,576,128]{2,1,0:T(8,128)(2,1)S(1)} %get-tuple-element.91.motion), channel_id=1, source_target_pairs={{0,4},{8,12},{16,20},{24,28},{32,36},{40,44},{48,52},{56,60},{64,6... | collective-permute-start | bytes 884744 | tf_op jit(solution)/shard_map/ppermute | solution.py:624
  23.5 1.1 copy-start.5
  32.9 9.7 %collective-permute-start.7 = (bf16[2,544,128]{2,1,0:T(8,128)(2,1)S(1)}, bf16[2,544,128]{2,1,0:T(8,128)(2,1)S(1)}, u32[]{:S(2)}, u32[]{:S(2)}) collective-permute-start(bf16[2,544,128]{2,1,0:T(8,128)(2,1)S(1)} %get-tuple-element.100.hidden.refs_5_), channel_id=1, source_target_pairs={{4,8},{12,16},{20,24},{28,32},{36,40},{44,48},{52,56},{60,64},{68,... | collective-permute-start | bytes 835592 | tf_op jit(solution)/shard_map/ppermute | solution.py:624
  33.6 12.3 %collective-permute-start.6 = (bf16[2,544,128]{2,1,0:T(8,128)(2,1)S(1)}, bf16[2,544,128]{2,1,0:T(8,128)(2,1)S(1)}, u32[]{:S(2)}, u32[]{:S(2)}) collective-permute-start(bf16[2,544,128]{2,1,0:T(8,128)(2,1)S(1)} %get-tuple-element.100.hidden.refs_5_), channel_id=1, source_target_pairs={{0,4},{8,12},{16,20},{24,28},{32,36},{40,44},{48,52},{56,60},{64,6... | collective-permute-start | bytes 835592 | tf_op jit(solution)/shard_map/ppermute | solution.py:624
  49.5 8.5 %collective-permute-start.8 = (bf16[3,544,128]{2,1,0:T(8,128)(2,1)S(1)}, bf16[3,544,128]{2,1,0:T(8,128)(2,1)S(1)}, u32[]{:S(2)}, u32[]{:S(2)}) collective-permute-start(bf16[3,544,128]{2,1,0:T(8,128)(2,1)S(1)} %get-tuple-element.106), channel_id=1, source_target_pairs={{0,4},{8,12},{16,20},{24,28},{32,36},{40,44},{48,52},{56,60},{64,6... | collective-permute-start | bytes 1253384 | tf_op jit(solution)/shard_map/ppermute | solution.py:630
  50.8 7.2 %collective-permute-start.9 = (bf16[3,544,128]{2,1,0:T(8,128)(2,1)S(1)}, bf16[3,544,128]{2,1,0:T(8,128)(2,1)S(1)}, u32[]{:S(2)}, u32[]{:S(2)}) collective-permute-start(bf16[3,544,128]{2,1,0:T(8,128)(2,1)S(1)} %get-tuple-element.107), channel_id=1, source_target_pairs={{4,8},{12,16},{20,24},{28,32},{36,40},{44,48},{52,56},{60,64},{68,... | collective-permute-start | bytes 1253384 | tf_op jit(solution)/shard_map/ppermute | solution.py:629
  61.5 11.2 %collective-permute-start.10 = (bf16[3,544,128]{2,1,0:T(8,128)(2,1)S(1)}, bf16[3,544,128]{2,1,0:T(8,128)(2,1)S(1)}, u32[]{:S(2)}, u32[]{:S(2)}) collective-permute-start(bf16[3,544,128]{2,1,0:T(8,128)(2,1)S(1)} %get-tuple-element.120), channel_id=1, source_target_pairs={{0,4},{8,12},{16,20},{24,28},{32,36},{40,44},{48,52},{56,60},{64,6... | collective-permute-start | bytes 1253384 | tf_op jit(solution)/shard_map/ppermute | solution.py:630
  66.4 6.3 %collective-permute-start.11 = (bf16[3,544,128]{2,1,0:T(8,128)(2,1)S(1)}, bf16[3,544,128]{2,1,0:T(8,128)(2,1)S(1)}, u32[]{:S(2)}, u32[]{:S(2)}) collective-permute-start(bf16[3,544,128]{2,1,0:T(8,128)(2,1)S(1)} %get-tuple-element.121), channel_id=1, source_target_pairs={{4,8},{12,16},{20,24},{28,32},{36,40},{44,48},{52,56},{60,64},{68,... | collective-permute-start | bytes 1253384 | tf_op jit(solution)/shard_map/ppermute | solution.py:629
  72.7 9.0 %collective-permute-start.12 = (bf16[2304,128]{1,0:T(8,128)(2,1)S(1)}, bf16[2304,128]{1,0:T(8,128)(2,1)S(1)}, u32[]{:S(2)}, u32[]{:S(2)}) collective-permute-start(bf16[2304,128]{1,0:T(8,128)(2,1)S(1)} %get-tuple-element.143), channel_id=1, source_target_pairs={{0,1},{1,0},{2,3},{3,2},{4,5},{5,4},{6,7},{7,6},{8,9},{9,8},{10,11... | collective-permute-start | bytes 1769480 | tf_op jit(solution)/shard_map/ppermute | solution.py:659
  81.7 2.8 %copy-start.10 = (f32[2,512,128]{2,1,0:T(8,128)}, f32[2,512,128]{2,1,0:T(8,128)S(1)}, u32[]{:S(2)}) copy-start(f32[2,512,128]{2,1,0:T(8,128)S(1)} %get-tuple-element.149.grad_feats) | copy-start | bytes 1572868
  81.7 1.7 %collective-permute-start.13 = (bf16[1280,128]{1,0:T(8,128)(2,1)S(1)}, bf16[1280,128]{1,0:T(8,128)(2,1)S(1)}, u32[]{:S(2)}, u32[]{:S(2)}) collective-permute-start(bf16[1280,128]{1,0:T(8,128)(2,1)S(1)} %get-tuple-element.145), channel_id=1, source_target_pairs={{0,1},{1,0},{2,3},{3,2},{4,5},{5,4},{6,7},{7,6},{8,9},{9,8},{10,11... | collective-permute-start | bytes 983048 | tf_op jit(solution)/shard_map/ppermute | solution.py:659
  84.5 35.4 %all-to-all-start = ((bf16[64,56,128]{2,1,0:T(8,128)(2,1)}), bf16[64,56,128]{2,1,0:T(8,128)(2,1)S(1)}, u32[]{:S(2)}, u32[]{:S(2)}) async-start(bf16[64,56,128]{2,1,0:T(8,128)(2,1)} %bitcast.2), calls=%async_computation | async-start | bytes 1835008 | tf_op jit(solution)/shard_map/all_to_all | solution.py:645
  103.7 1.0 copy-start.7
  104.6 1.0 copy-start.11
  108.9 0.7 copy-start.12
  121.0 5.5 %copy-start.13 = (bf16[2,192,256]{2,1,0:T(8,128)(2,1)S(1)}, bf16[2,192,256]{2,1,0:T(8,128)(2,1)}, u32[]{:S(2)}) copy-start(bf16[2,192,256]{2,1,0:T(8,128)(2,1)} %copy-done.12) | copy-start | bytes 589828
  121.0 22.5 %all-to-all-start.1 = ((bf16[64,56,128]{2,1,0:T(8,128)(2,1)}), bf16[64,56,128]{2,1,0:T(8,128)(2,1)S(1)}, u32[]{:S(2)}, u32[]{:S(2)}) async-start(bf16[64,56,128]{2,1,0:T(8,128)(2,1)} %shard_map.152), calls=%async_computation.1 | async-start | bytes 1835008 | tf_op jit(solution)/shard_map/all_to_all | solution.py:654
  126.5 15.5 %collective-permute-start.15 = (bf16[2,192,256]{2,1,0:T(8,128)(2,1)S(1)}, bf16[2,192,256]{2,1,0:T(8,128)(2,1)S(1)}, u32[]{:S(2)}, u32[]{:S(2)}) collective-permute-start(bf16[2,192,256]{2,1,0:T(8,128)(2,1)S(1)} %copy-done.13), channel_id=1, source_target_pairs={{1,2},{2,1},{5,6},{6,5},{9,10},{10,9},{13,14},{14,13},{17,18},{18,... | collective-permute-start | bytes 589832 | tf_op jit(solution)/shard_map/ppermute | solution.py:624
  133.0 9.0 %collective-permute-start.14 = (bf16[2,192,256]{2,1,0:T(8,128)(2,1)S(1)}, bf16[2,192,256]{2,1,0:T(8,128)(2,1)S(1)}, u32[]{:S(2)}, u32[]{:S(2)}) collective-permute-start(bf16[2,192,256]{2,1,0:T(8,128)(2,1)S(1)} %copy-done.13), channel_id=1, source_target_pairs={{0,1},{2,3},{1,0},{3,2},{4,5},{6,7},{5,4},{7,6},{8,9},{10,11},{9,8... | collective-permute-start | bytes 589832 | tf_op jit(solution)/shard_map/ppermute | solution.py:624
  143.4 3.7 %collective-permute-start.16 = (bf16[3584,128]{1,0:T(8,128)(2,1)S(1)}, bf16[3584,128]{1,0:T(8,128)(2,1)S(1)}, u32[]{:S(2)}, u32[]{:S(2)}) collective-permute-start(bf16[3584,128]{1,0:T(8,128)(2,1)S(1)} %bitcast.4), channel_id=1, source_target_pairs={{0,1},{1,0},{2,3},{3,2},{4,5},{5,4},{6,7},{7,6},{8,9},{9,8},{10,11... | collective-permute-start | bytes 2752520 | tf_op jit(solution)/shard_map/ppermute | solution.py:659
